TPU v7x, 256 devices: a whole 4x4x8 slice. The times are simulated.
256 devices in a mesh: section: 4 (over x), expert: 32 (over z, y), dp: 2 (over core).
Axes of the slice: x: 4, y: 4, z: 8, core: 2. Of those that a mesh axis runs over, the one named last changes fastest.
Arguments:
- tokens: bfloat16 [2048, 4096], P(('expert', 'dp')), may hold values from -6 to 6
- routing: int32 [2048, 8], P(('expert', 'dp')), may hold values from 0 to 63, all different within a row; in each aligned block of 32 rows (0 to 31, 32 to 63, ...) at most 8 rows name the same one
- gate_weights: float32 [2048, 8], P(('expert', 'dp')), may hold values from 0.05 to 0.3
- w_gate: bfloat16 [64, 4096, 1536], P(('expert', 'dp'), None, 'section'), may hold values from -0.09375 to 0.09375
- w_up: bfloat16 [64, 4096, 1536], P(('expert', 'dp'), None, 'section'), may hold values from -0.09375 to 0.09375
- w_down: bfloat16 [64, 1536, 4096], P(('expert', 'dp'), 'section'), may hold values from -0.15625 to 0.15625
Outputs:
- combined: bfloat16 [2048, 4096], P(('expert', 'dp'), 'section')
Inputs may be any that keep to these rules, and one draw needn't show every extreme that they name: `routing`: each row names 8 different experts. In each aligned block of 32 rows (the rows of one device) no expert is named by more than 8 rows, and in some block an expert is named by exactly 8 rows.
All inputs are finite; a program needn't handle non-finite values.
Results may differ from a plain program's by a relative error of at most 0.011.
Values may be sent and summed in bfloat16 or wider, within the bound.
No kernel may reach another device: no remote copies, remote signals or barrier semaphores. Data moves between devices by JAX's collectives and lax.ppermute only.
A program may use at most 128 MiB of HBM per device.

v0:
```python
import jax
import jax.numpy as jnp
from jax import lax
from jax.sharding import PartitionSpec as P


def on_device(tokens, routing, gate_weights, w_gate, w_up, w_down):
    tok_count, model_width = tokens.shape
    fanout = routing.shape[1]
    experts = lax.axis_size(("expert", "dp"))
    capacity = min(tok_count, max(2, 2 * tok_count * fanout // experts))
    one_hot = (routing[:, :, None] == jnp.arange(experts, dtype=jnp.int32)[None, None, :]).astype(
        jnp.int32
    )
    flattened = one_hot.reshape(tok_count * fanout, experts)
    earlier = jnp.cumsum(flattened, axis=0) - flattened
    slot_rank = jnp.sum(earlier * flattened, axis=1).reshape(tok_count, fanout)
    slot_index = routing * capacity + slot_rank
    copies = jnp.broadcast_to(tokens[:, None, :], (tok_count, fanout, model_width)).reshape(
        tok_count * fanout, model_width
    )
    outgoing = (
        jnp.zeros((experts * capacity, model_width), tokens.dtype)
        .at[slot_index.reshape(-1)]
        .set(copies)
    )
    outgoing = outgoing.reshape(experts, capacity, model_width)
    received = lax.all_to_all(outgoing, ("expert", "dp"), split_axis=0, concat_axis=0, tiled=True)
    gate_proj = jnp.einsum("scd,df->scf", received, w_gate[0], preferred_element_type=jnp.float32)
    up_proj = jnp.einsum("scd,df->scf", received, w_up[0], preferred_element_type=jnp.float32)
    hidden = (jax.nn.silu(gate_proj) * up_proj).astype(jnp.bfloat16)
    partial_value = jnp.einsum("scf,fd->scd", hidden, w_down[0], preferred_element_type=jnp.float32)
    returned_part = lax.all_to_all(
        partial_value.astype(jnp.bfloat16),
        ("expert", "dp"),
        split_axis=0,
        concat_axis=0,
        tiled=True,
    ).astype(partial_value.dtype)
    out_width = returned_part.shape[2]
    picked = returned_part.reshape(experts * capacity, out_width)[slot_index]
    weighted = jnp.sum(picked * gate_weights[:, :, None], axis=1)
    result = lax.psum_scatter(weighted, "section", scatter_dimension=1, tiled=True)
    return result.astype(jnp.bfloat16)


def solution(mesh):
    placed = (
        P(("expert", "dp"), None),
        P(("expert", "dp"), None),
        P(("expert", "dp"), None),
        P(("expert", "dp"), None, "section"),
        P(("expert", "dp"), None, "section"),
        P(("expert", "dp"), "section", None),
    )
    return jax.shard_map(
        on_device,
        mesh=mesh,
        in_specs=placed,
        out_specs=P(("expert", "dp"), "section"),
        check_vma=False,
    )
```

profile of v0, /device:TPU:1, one launch (start us, length us, event | category | flops | bytes accessed | tf_op | source)
XLA Modules:
  0.0 288.5 jit_solution(15244828590709159340)
XLA Ops:
  6.5 0.9 copy.8
  7.4 0.1 eq.30
  7.5 0.1 eq.26
  7.6 0.6 reduce-window.6
  8.3 0.2 slice_reduce_fusion
  8.5 0.1 fusion.21
  8.6 0.1 reshape.67
  8.7 0.1 reshape.68
  8.8 6.4 %scatter_custom_fusion = bf16[512,4096]{1,0:T(8,128)(2,1)} fusion(s32[256]{0:T(256)S(1)} %bitcast.52, bf16[]{:T(256)} %constant.6.clone.1, bf16[32,4096]{1,0:T(8,128)(2,1)} %param.6), kind=kCustom, calls=%fused_computation.11 | custom fusion | bytes 4456450 | tf_op jit(solution)/shard_map/scatter | solution.py:25
  15.2 108.0 %all_to_all.10 = bf16[64,8,4096]{2,1,0:T(8,128)(2,1)S(1)} all-to-all(bf16[64,8,4096]{2,1,0:T(8,128)(2,1)} %bitcast.51), channel_id=1, replica_groups=mesh['section'=4,'expert'=32,'dp'=2] {'expert','dp'}, dimensions={0} | all-to-all | bytes 8388608 | tf_op jit(solution)/shard_map/all_to_all | solution.py:28
  123.2 2.0 copy-done.1
  125.2 3.3 %fusion.4 = f32[64,8,384]{2,1,0:T(8,128)} fusion(bf16[64,8,4096]{2,1,0:T(8,128)(2,1)S(1)} %all_to_all.10, bf16[1,4096,384]{2,1,0:T(8,128)(2,1)S(1)} %copy-done.3), kind=kOutput, calls=%fused_computation.9 | convolution fusion | flops 1610612736 | bytes 8126464 | tf_op jit(solution)/shard_map/scd,df->scf/dot_general | solution.py:29
  128.5 9.7 %convolution_convert_fusion = bf16[64,8,4096]{2,1,0:T(8,128)(2,1)} fusion(bf16[1,384,4096]{2,1,0:T(8,128)(2,1)S(1)} %copy-done, bf16[64,8,4096]{2,1,0:T(8,128)(2,1)} %copy-done.1, bf16[1,4096,384]{2,1,0:T(8,128)(2,1)} %param.10, f32[64,8,384]{2,1,0:T(8,128)} %fusion.4), kind=kOutput, calls=%fused_computation.2 | convolution fusion | flops 3224502272 | bytes 15466496 | tf_op jit(solution)/shard_map/scf,fd->scd/dot_general | solution.py:32
  138.2 7.3 %all-to-all-start.1 = ((bf16[64,8,4096]{2,1,0:T(8,128)(2,1)}), bf16[64,8,4096]{2,1,0:T(8,128)(2,1)}, u32[]{:S(2)}, u32[]{:S(2)}) async-start(bf16[64,8,4096]{2,1,0:T(8,128)(2,1)} %convolution_convert_fusion), calls=%async_computation.1 | async-start | bytes 8388608 | tf_op jit(solution)/shard_map/all_to_all | solution.py:33
  145.5 0.3 reduce-scatter.2.cloned.1.call-start
  145.8 0.1 reshape.77
  145.9 0.1 copy.12
  146.0 94.2 %all-to-all-done.1 = bf16[64,8,4096]{2,1,0:T(8,128)(2,1)} async-done(((bf16[64,8,4096]{2,1,0:T(8,128)(2,1)}), bf16[64,8,4096]{2,1,0:T(8,128)(2,1)}, u32[]{:S(2)}, u32[]{:S(2)}) %all-to-all-start.1) | async-done | bytes 4194336 | tf_op jit(solution)/shard_map/all_to_all | solution.py:33
  240.1 6.5 %bitcast_convert_fusion = f32[512,4096]{1,0:T(8,128)} fusion(bf16[64,8,4096]{2,1,0:T(8,128)(2,1)} %all-to-all-done.1), kind=kLoop, calls=%fused_computation.3 | loop fusion | flops 2097152 | bytes 12582912 | tf_op jit(solution)/shard_map/reshape | solution.py:41
  246.6 9.0 %gather_fusion = f32[256,4096]{1,0:T(8,128)} fusion(f32[512,4096]{1,0:T(8,128)} %bitcast_convert_fusion, s32[1024]{0:T(1024)S(1)} %pad_clamp_fusion), kind=kCustom, calls=%fused_computation | custom fusion | bytes 8389632 | tf_op jit(solution)/shard_map/gather | solution.py:41
  255.7 4.3 %fusion = f32[32,4096]{1,0:T(8,128)} fusion(f32[256,4096]{1,0:T(8,128)} %gather_fusion, f32[32,8]{1,0:T(8,128)S(1)} %copy.12), kind=kLoop, calls=%fused_computation.5 | loop fusion | flops 1966080 | bytes 4719616 | tf_op jit(solution)/shard_map/reduce_sum | solution.py:42
  260.0 0.0 reduce-scatter.2.cloned.1.call-update
  260.0 20.1 %reduce-scatter.2.cloned.1.call-done = f32[32,1024]{1,0:T(8,128)} async-done(((f32[32,4096]{1,0:T(8,128)}), f32[32,1024]{1,0:T(8,128)}) %reduce-scatter.2.cloned.1.call-update) | async-done | bytes 131088 | tf_op jit(solution)/shard_map/reduce_scatter | solution.py:43
  280.1 1.5 convert_element_type.22
  (13 shorter events, 0.1 us)
Async XLA Ops:
  6.5 121.9 %copy-start = (bf16[1,384,4096]{2,1,0:T(8,128)(2,1)S(1)}, bf16[1,384,4096]{2,1,0:T(8,128)(2,1)}, u32[]{:S(2)}) copy-start(bf16[1,384,4096]{2,1,0:T(8,128)(2,1)} %param.11) | copy-start | bytes 9437188
  15.2 110.0 %copy-start.3 = (bf16[1,4096,384]{2,1,0:T(8,128)(2,1)S(1)}, bf16[1,4096,384]{2,1,0:T(8,128)(2,1)}, u32[]{:S(2)}) copy-start(bf16[1,4096,384]{2,1,0:T(8,128)(2,1)} %param.9) | copy-start | bytes 9437188
  123.2 2.0 copy-start.1
  138.2 7.7 %copy-start.2 = (f32[32,8]{0,1:T(8,128)S(1)}, f32[32,8]{0,1:T(8,128)}, u32[]{:S(2)}) copy-start(f32[32,8]{0,1:T(8,128)} %param.8) | copy-start | bytes 3076
  138.2 102.0 %all-to-all-start.1 = ((bf16[64,8,4096]{2,1,0:T(8,128)(2,1)}), bf16[64,8,4096]{2,1,0:T(8,128)(2,1)}, u32[]{:S(2)}, u32[]{:S(2)}) async-start(bf16[64,8,4096]{2,1,0:T(8,128)(2,1)} %convolution_convert_fusion), calls=%async_computation.1 | async-start | bytes 8388608 | tf_op jit(solution)/shard_map/all_to_all | solution.py:33
  145.5 134.6 %reduce-scatter.2.cloned.1.call-start = ((), (), s32[]{:S(2)}) async-start(), calls=%async_computation.3 | async-start | bytes 655360 | tf_op jit(solution)/shard_map/reduce_scatter | solution.py:43
Sparse Core Ops, SparseCore 0:
  260.2 19.9 reduce-scatter.1
where the time goes:
time: 290 us; the launch traced here: 289 us
  waiting for transfers between devices  114 us (39%)
  blocking collectives  108 us (37%)
  local copies, waits for them, and re-layouts  19 us (7%)
  between operations  13.5 us (5%)
  other arithmetic  13.2 us (5%)
  matrix products  13 us (4%)
  starting transfers between devices  7.61 us (3%)
    all_to_all x1, blocking collectives, on_device(): lax.all_to_all(outgoing, ('expert', 'dp'), split_axis=0, concat_axis=0, t...  108 us
    all_to_all x1, waiting for transfers between devices, on_device(): lax.all_to_all(partial_value.astype(jnp.bfloat16), ('expert', 'dp'), spli...  94.2 us
    reduce_scatter x1, waiting for transfers between devices, on_device(): lax.psum_scatter(weighted, 'section', scatter_dimension=1, tiled=True)  20.1 us
    dot_general x1, matrix products, on_device(): jnp.einsum('scf,fd->scd', hidden, w_down[0], preferred_element_type=jnp.f...  9.69 us
    gather x1, local copies, waits for them, and re-layouts, on_device(): picked = returned_part.reshape(experts * capacity, out_width)[slot_index]  9.04 us
    all_to_all x1, starting transfers between devices, on_device(): lax.all_to_all(partial_value.astype(jnp.bfloat16), ('expert', 'dp'), spli...  7.35 us
    reshape x1, other arithmetic, on_device(): picked = returned_part.reshape(experts * capacity, out_width)[slot_index]  6.49 us
    scatter x1, local copies, waits for them, and re-layouts, on_device(): outgoing = jnp.zeros((experts * capacity, model_width), tokens.dtype).at[...  6.4 us
  transfers between devices with their start and end apart: 2, of which 2 were waited for; matrix products, arithmetic and copies ran while one was open for 0% of the time, Pallas kernels for 0%

commit v1 on v0

v1 whole, which is shorter than its diff:
```python
import jax
import jax.numpy as jnp
from jax import lax
from jax.sharding import PartitionSpec as P

ED = ("expert", "dp")
BF = jnp.bfloat16
F32 = jnp.float32


def dot(a, b):
    return jnp.dot(a, b, preferred_element_type=F32)


def on_device(tokens, routing, gate_weights, w_gate, w_up, w_down):
    toks, width = tokens.shape
    fanout = routing.shape[1]
    experts = lax.axis_size(ED)
    sections = lax.axis_size("section")
    cap = min(toks, max(2, 2 * toks * fanout // experts))
    quarter = width // sections
    s = lax.axis_index("section")
    right = [(k, (k + 1) % sections) for k in range(sections)]
    left = [(k, (k - 1) % sections) for k in range(sections)]

    def to_right(v):
        return lax.ppermute(v, "section", right)

    def to_left(v):
        return lax.ppermute(v, "section", left)

    match = routing[:, :, None] == jnp.arange(experts, dtype=jnp.int32)[None, None, :]
    named = jnp.any(match, axis=1)
    weight = jnp.sum(jnp.where(match, gate_weights[:, :, None], 0.0), axis=1)
    counts = named.astype(jnp.int32)
    rank = jnp.cumsum(counts, axis=0) - counts
    place = named[:, :, None] & (rank[:, :, None] == jnp.arange(cap, dtype=jnp.int32)[None, None, :])
    pick = place.astype(BF).reshape(toks, experts * cap)
    spread = jnp.where(place, weight[:, :, None], 0.0).reshape(toks, experts * cap)
    spread_hi = spread.astype(BF)
    spread_lo = (spread - spread_hi.astype(F32)).astype(BF)
    spread2 = jnp.concatenate([spread_hi, spread_lo], axis=0)

    own_cols = lax.dynamic_slice_in_dim(tokens, s * quarter, quarter, axis=1)
    outgoing = lax.dot_general(
        pick, own_cols, (((0,), (0,)), ((), ())), preferred_element_type=F32
    ).astype(BF)
    received = lax.all_to_all(
        outgoing.reshape(experts, cap, quarter), ED, split_axis=0, concat_axis=0, tiled=True
    ).reshape(experts * cap, quarter)
    rows = experts * cap
    half = rows // 2

    def k_part(block, q):
        q = q % sections
        g = lax.dynamic_slice_in_dim(w_gate[0], q * quarter, quarter, axis=0)
        u = lax.dynamic_slice_in_dim(w_up[0], q * quarter, quarter, axis=0)
        return dot(block, g), dot(block, u)

    a, b = received[:half], received[half:]
    r_a = to_right(a)
    l_b = to_left(b)
    r_b = to_right(b)
    l_a = to_left(a)
    rr_a = to_right(r_a)
    ll_b = to_left(l_b)
    from_left = jnp.concatenate([r_a, r_b], axis=0)
    from_right = jnp.concatenate([l_a, l_b], axis=0)
    across = jnp.concatenate([rr_a, ll_b], axis=0)
    gate, up = k_part(received, s)
    for block, q in ((from_left, s + 3), (from_right, s + 1), (across, s + 2)):
        g, u = k_part(block, q)
        gate, up = gate + g, up + u
    hidden = (jax.nn.silu(gate) * up).astype(BF)

    def down(h, q):
        q = q % sections
        return dot(h, lax.dynamic_slice_in_dim(w_down[0], q * quarter, quarter, axis=1))

    h_a, h_b = hidden[:half], hidden[half:]
    far_a = to_right(down(h_a, s + 2).astype(BF))
    far_b = to_left(down(h_b, s + 2).astype(BF))
    near_b = to_right(down(h_b, s + 1).astype(BF))
    near_a = to_left(down(h_a, s + 3).astype(BF))
    relay_a = to_right((down(h_a, s + 1) + far_a.astype(F32)).astype(BF))
    relay_b = to_left((down(h_b, s + 3) + far_b.astype(F32)).astype(BF))
    own_a = down(h_a, s) + near_a.astype(F32) + relay_a.astype(F32)
    own_b = down(h_b, s) + near_b.astype(F32) + relay_b.astype(F32)
    summed = jnp.concatenate([own_a, own_b], axis=0).astype(BF)
    returned = lax.all_to_all(
        summed.reshape(experts, cap, quarter), ED, split_axis=0, concat_axis=0, tiled=True
    ).reshape(rows, quarter)
    both = dot(spread2, returned)
    return (both[:toks] + both[toks:]).astype(BF)


def solution(mesh):
    placed = (
        P(ED, None),
        P(ED, None),
        P(ED, None),
        P(ED, None, "section"),
        P(ED, None, "section"),
        P(ED, "section", None),
    )
    return jax.shard_map(
        on_device,
        mesh=mesh,
        in_specs=placed,
        out_specs=P(ED, "section"),
        check_vma=False,
    )
```

time: 290 us -> 169 us (0.58)
  blocking collectives: 108 us -> 0 us
  starting transfers between devices: 7.61 us -> 44.8 us
  local copies, waits for them, and re-layouts: 19 us -> 4.07 us
  between operations: 13.5 us -> 0.41 us
  waiting for transfers between devices: 114 us -> 101 us
  other arithmetic: 13.2 us -> 2.57 us
  matrix products: 13 us -> 16 us
    all_to_all x1 -> x0, blocking collectives: 108 us -> none  [on_device(): lax.all_to_all(outgoing, ('expert', 'dp'), split_axis=0, concat_axis=0, t...]
    ppermute x0 -> x12, waiting for transfers between devices: none -> 45.1 us  [the longest x6 38.2 us: to_right(): return lax.ppermute(v, 'section', right)]
    all_to_all x1 -> x2, waiting for transfers between devices: 94.2 us -> 55.7 us  [the longest x1 27.9 us: on_device(): lax.all_to_all(summed.reshape(experts, cap, quarter), ED, split_axis=0, c...]
    all_to_all x1 -> x2, starting transfers between devices: 7.35 us -> 28.4 us  [the longest x1 15 us: on_device(): lax.all_to_all(summed.reshape(experts, cap, quarter), ED, split_axis=0, c...]
    reduce_scatter x1 -> x0, waiting for transfers between devices: 20.1 us -> none  [on_device(): lax.psum_scatter(weighted, 'section', scatter_dimension=1, tiled=True)]
    ppermute x0 -> x12, starting transfers between devices: none -> 16.4 us  [the longest x6 14.1 us: to_left(): return lax.ppermute(v, 'section', left)]
    gather x1 -> x0, local copies, waits for them, and re-layouts: 9.04 us -> none  [on_device(): picked = returned_part.reshape(experts * capacity, out_width)[slot_index]]
    reshape x1 -> x0, other arithmetic: 6.49 us -> none  [on_device(): picked = returned_part.reshape(experts * capacity, out_width)[slot_index]]
  transfers between devices with their start and end apart: 2 -> 14, of which waited for: 2 -> 9; matrix products, arithmetic and copies ran while one was open for 0% -> 6% of each run, Pallas kernels for 0% -> 0%
where the time goes in v1:
time: 169 us
  waiting for transfers between devices  101 us (60%)
  starting transfers between devices  44.8 us (27%)
  matrix products  16 us (9%)
  local copies, waits for them, and re-layouts  4.07 us (2%)
  other arithmetic  2.57 us (2%)
    ppermute x6, waiting for transfers between devices, to_right(): return lax.ppermute(v, 'section', right)  38.2 us
    all_to_all x1, waiting for transfers between devices, on_device(): lax.all_to_all(summed.reshape(experts, cap, quarter), ED, split_axis=0, c...  27.9 us
    all_to_all x1, waiting for transfers between devices, on_device(): lax.all_to_all(outgoing.reshape(experts, cap, quarter), ED, split_axis=0,...  27.8 us
    all_to_all x1, starting transfers between devices, on_device(): lax.all_to_all(summed.reshape(experts, cap, quarter), ED, split_axis=0, c...  15 us
    ppermute x6, starting transfers between devices, to_left(): return lax.ppermute(v, 'section', left)  14.1 us
    dot_general x17, matrix products, dot(): return jnp.dot(a, b, preferred_element_type=F32)  13.7 us
    all_to_all x1, starting transfers between devices, on_device(): lax.all_to_all(outgoing.reshape(experts, cap, quarter), ED, split_axis=0,...  13.3 us
    ppermute x6, waiting for transfers between devices, to_left(): return lax.ppermute(v, 'section', left)  6.89 us
  transfers between devices with their start and end apart: 14, of which 9 were waited for; matrix products, arithmetic and copies ran while one was open for 6% of the time, Pallas kernels for 0%

profile of v1, /device:TPU:1, one launch (start us, length us, event | category | flops | bytes accessed | tf_op | source)
XLA Modules:
  0.0 168.6 jit_solution(7242543927806840576)
XLA Ops:
  0.0 0.9 copy.18
  2.9 2.3 %fusion = bf16[64,8,1024]{2,1,0:T(8,128)(2,1)} fusion(pred[32,512]{1,0:T(32,128)(4,1)S(1)} %get-tuple-element.6, bf16[32,4096]{1,0:T(8,128)(2,1)} %param.6, s32[]{:T(128)S(6)} %select_n.73), kind=kOutput, calls=%fused_computation.1 | convolution fusion | flops 34078720 | bytes 1130500 | tf_op jit(solution)/shard_map/dot_general | solution.py:45
  5.2 13.3 %all-to-all-start = ((bf16[64,8,1024]{2,1,0:T(8,128)(2,1)}), bf16[64,8,1024]{2,1,0:T(8,128)(2,1)}, u32[]{:S(2)}, u32[]{:S(2)}) async-start(bf16[64,8,1024]{2,1,0:T(8,128)(2,1)} %fusion), calls=%async_computation | async-start | bytes 2097152 | tf_op jit(solution)/shard_map/all_to_all | solution.py:48
  18.6 27.8 %all-to-all-done = bf16[64,8,1024]{2,1,0:T(8,128)(2,1)} async-done(((bf16[64,8,1024]{2,1,0:T(8,128)(2,1)}), bf16[64,8,1024]{2,1,0:T(8,128)(2,1)}, u32[]{:S(2)}, u32[]{:S(2)}) %all-to-all-start) | async-done | bytes 1048608 | tf_op jit(solution)/shard_map/all_to_all | solution.py:48
  46.5 1.4 slice_bitcast_fusion
  47.9 1.3 collective-permute-start.1
  49.2 1.5 collective-permute-start.3
  50.6 2.7 %collective-permute-start.2 = (bf16[256,1024]{1,0:T(8,128)(2,1)S(1)}, bf16[256,1024]{1,0:T(8,128)(2,1)S(1)}, u32[]{:S(2)}, u32[]{:S(2)}) collective-permute-start(bf16[256,1024]{1,0:T(8,128)(2,1)S(1)} %get-tuple-element.8), channel_id=1, source_target_pairs={{0,192},{64,0},{128,64},{192,128},{1,193},{65,1},{129,65},{193,129... | collective-permute-start | bytes 1572872 | tf_op jit(solution)/shard_map/ppermute | solution.py:30
  53.3 2.2 %fusion.3 = f32[512,384]{1,0:T(8,128)S(1)} fusion(bf16[64,8,1024]{2,1,0:T(8,128)(2,1)} %all-to-all-done, bf16[1,4096,384]{2,1,0:T(8,128)(2,1)} %param.10, s32[]{:T(128)S(6)} %select_n.75), kind=kOutput, calls=%fused_computation.15 | convolution fusion | flops 402653184 | bytes 2621444 | tf_op jit(solution)/shard_map/dot_general | solution.py:12
  55.5 2.1 %fusion.5 = f32[512,384]{1,0:T(8,128)S(1)} fusion(bf16[64,8,1024]{2,1,0:T(8,128)(2,1)} %all-to-all-done, bf16[1,4096,384]{2,1,0:T(8,128)(2,1)S(1)} %copy-done.1, s32[]{:T(128)S(6)} %select_n.75), kind=kOutput, calls=%fused_computation.17 | convolution fusion | flops 402653184 | bytes 2621444 | tf_op jit(solution)/shard_map/dot_general | solution.py:12
  57.6 14.9 %collective-permute-done = bf16[256,1024]{1,0:T(8,128)(2,1)S(1)} collective-permute-done((bf16[256,1024]{1,0:T(8,128)(2,1)S(1)}, bf16[256,1024]{1,0:T(8,128)(2,1)S(1)}, u32[]{:S(2)}, u32[]{:S(2)}) %collective-permute-start) | collective-permute-done | bytes 524320 | tf_op jit(solution)/shard_map/ppermute | solution.py:27
  74.1 2.9 %collective-permute-start.5 = (bf16[256,1024]{1,0:T(8,128)(2,1)S(1)}, bf16[256,1024]{1,0:T(8,128)(2,1)S(1)}, u32[]{:S(2)}, u32[]{:S(2)}) collective-permute-start(bf16[256,1024]{1,0:T(8,128)(2,1)S(1)} %collective-permute-done.3), channel_id=1, source_target_pairs={{0,192},{64,0},{128,64},{192,128},{1,193},{65,1},{129,65},{193,129... | collective-permute-start | bytes 1572872 | tf_op jit(solution)/shard_map/ppermute | solution.py:30
  78.5 6.3 %collective-permute-done.4 = bf16[256,1024]{1,0:T(8,128)(2,1)S(1)} collective-permute-done((bf16[256,1024]{1,0:T(8,128)(2,1)S(1)}, bf16[256,1024]{1,0:T(8,128)(2,1)S(1)}, u32[]{:S(2)}, u32[]{:S(2)}) %collective-permute-start.4) | collective-permute-done | bytes 524320 | tf_op jit(solution)/shard_map/ppermute | solution.py:27
  84.8 0.8 collective-permute-done.5
  88.9 2.8 %collective-permute-start.10 = (bf16[256,1024]{1,0:T(8,128)(2,1)S(1)}, bf16[256,1024]{1,0:T(8,128)(2,1)S(1)}, u32[]{:S(2)}, u32[]{:S(2)}) collective-permute-start(bf16[256,1024]{1,0:T(8,128)(2,1)S(1)} %convolution_convert_fusion.1), channel_id=1, source_target_pairs={{0,192},{64,0},{128,64},{192,128},{1,193},{65,1},{129,65},{193,129... | collective-permute-start | bytes 1572872 | tf_op jit(solution)/shard_map/ppermute | solution.py:30
  92.6 1.5 collective-permute-start.6
  94.1 5.8 %collective-permute-done.7 = bf16[256,1024]{1,0:T(8,128)(2,1)S(1)} collective-permute-done((bf16[256,1024]{1,0:T(8,128)(2,1)S(1)}, bf16[256,1024]{1,0:T(8,128)(2,1)S(1)}, u32[]{:S(2)}, u32[]{:S(2)}) %collective-permute-start.7) | collective-permute-done | bytes 524320 | tf_op jit(solution)/shard_map/ppermute | solution.py:27
  101.5 2.7 %collective-permute-start.11 = (bf16[256,1024]{1,0:T(8,128)(2,1)S(1)}, bf16[256,1024]{1,0:T(8,128)(2,1)S(1)}, u32[]{:S(2)}, u32[]{:S(2)}) collective-permute-start(bf16[256,1024]{1,0:T(8,128)(2,1)S(1)} %add_convert_fusion.1), channel_id=1, source_target_pairs={{0,192},{64,0},{128,64},{192,128},{1,193},{65,1},{129,65},{193,129... | collective-permute-start | bytes 1572872 | tf_op jit(solution)/shard_map/ppermute | solution.py:30
  104.6 6.0 %collective-permute-done.6 = bf16[256,1024]{1,0:T(8,128)(2,1)S(1)} collective-permute-done((bf16[256,1024]{1,0:T(8,128)(2,1)S(1)}, bf16[256,1024]{1,0:T(8,128)(2,1)S(1)}, u32[]{:S(2)}, u32[]{:S(2)}) %collective-permute-start.6) | collective-permute-done | bytes 524320 | tf_op jit(solution)/shard_map/ppermute | solution.py:30
  111.2 11.0 %collective-permute-done.9 = bf16[256,1024]{1,0:T(8,128)(2,1)S(1)} collective-permute-done((bf16[256,1024]{1,0:T(8,128)(2,1)S(1)}, bf16[256,1024]{1,0:T(8,128)(2,1)S(1)}, u32[]{:S(2)}, u32[]{:S(2)}) %collective-permute-start.9) | collective-permute-done | bytes 524320 | tf_op jit(solution)/shard_map/ppermute | solution.py:27
  122.4 1.1 maximum_bitcast_fusion
  123.5 15.0 %all-to-all-start.1 = ((bf16[64,8,1024]{2,1,0:T(8,128)(2,1)}), bf16[64,8,1024]{2,1,0:T(8,128)(2,1)}, u32[]{:S(2)}, u32[]{:S(2)}) async-start(bf16[64,8,1024]{2,1,0:T(8,128)(2,1)} %maximum_bitcast_fusion), calls=%async_computation.1 | async-start | bytes 2097152 | tf_op jit(solution)/shard_map/all_to_all | solution.py:90
  138.6 27.9 %all-to-all-done.1 = bf16[64,8,1024]{2,1,0:T(8,128)(2,1)} async-done(((bf16[64,8,1024]{2,1,0:T(8,128)(2,1)}), bf16[64,8,1024]{2,1,0:T(8,128)(2,1)}, u32[]{:S(2)}, u32[]{:S(2)}) %all-to-all-start.1) | async-done | bytes 1048608 | tf_op jit(solution)/shard_map/all_to_all | solution.py:90
  166.5 1.5 fusion.1
  (59 shorter events, 12.4 us)
Async XLA Ops:
  0.0 87.2 %copy-start = (bf16[1,384,4096]{2,1,0:T(8,128)(2,1)S(1)}, bf16[1,384,4096]{2,1,0:T(8,128)(2,1)}, u32[]{:S(2)}) copy-start(bf16[1,384,4096]{2,1,0:T(8,128)(2,1)} %param.11) | copy-start | bytes 9437188
  5.2 41.3 %all-to-all-start = ((bf16[64,8,1024]{2,1,0:T(8,128)(2,1)}), bf16[64,8,1024]{2,1,0:T(8,128)(2,1)}, u32[]{:S(2)}, u32[]{:S(2)}) async-start(bf16[64,8,1024]{2,1,0:T(8,128)(2,1)} %fusion), calls=%async_computation | async-start | bytes 2097152 | tf_op jit(solution)/shard_map/all_to_all | solution.py:48
  46.5 9.0 %copy-start.1 = (bf16[1,4096,384]{2,1,0:T(8,128)(2,1)S(1)}, bf16[1,4096,384]{2,1,0:T(8,128)(2,1)}, u32[]{:S(2)}) copy-start(bf16[1,4096,384]{2,1,0:T(8,128)(2,1)} %param.9) | copy-start | bytes 9437188
  47.9 24.7 %collective-permute-start.1 = (bf16[256,1024]{1,0:T(8,128)(2,1)S(1)}, bf16[256,1024]{1,0:T(8,128)(2,1)S(1)}, u32[]{:S(2)}, u32[]{:S(2)}) collective-permute-start(bf16[256,1024]{1,0:T(8,128)(2,1)S(1)} %get-tuple-element.7), channel_id=1, source_target_pairs={{0,64},{64,128},{128,192},{192,0},{1,65},{65,129},{129,193},{193,1... | collective-permute-start | bytes 1572872 | tf_op jit(solution)/shard_map/ppermute | solution.py:27
  49.2 24.9 %collective-permute-start.3 = (bf16[256,1024]{1,0:T(8,128)(2,1)S(1)}, bf16[256,1024]{1,0:T(8,128)(2,1)S(1)}, u32[]{:S(2)}, u32[]{:S(2)}) collective-permute-start(bf16[256,1024]{1,0:T(8,128)(2,1)S(1)} %get-tuple-element.7), channel_id=1, source_target_pairs={{0,192},{64,0},{128,64},{192,128},{1,193},{65,1},{129,65},{193,129... | collective-permute-start | bytes 1572872 | tf_op jit(solution)/shard_map/ppermute | solution.py:30
  50.6 21.8 %collective-permute-start = (bf16[256,1024]{1,0:T(8,128)(2,1)S(1)}, bf16[256,1024]{1,0:T(8,128)(2,1)S(1)}, u32[]{:S(2)}, u32[]{:S(2)}) collective-permute-start(bf16[256,1024]{1,0:T(8,128)(2,1)S(1)} %get-tuple-element.8), channel_id=1, source_target_pairs={{0,64},{64,128},{128,192},{192,0},{1,65},{65,129},{129,193},{193,1... | collective-permute-start | bytes 1572872 | tf_op jit(solution)/shard_map/ppermute | solution.py:27
  50.6 21.9 %collective-permute-start.2 = (bf16[256,1024]{1,0:T(8,128)(2,1)S(1)}, bf16[256,1024]{1,0:T(8,128)(2,1)S(1)}, u32[]{:S(2)}, u32[]{:S(2)}) collective-permute-start(bf16[256,1024]{1,0:T(8,128)(2,1)S(1)} %get-tuple-element.8), channel_id=1, source_target_pairs={{0,192},{64,0},{128,64},{192,128},{1,193},{65,1},{129,65},{193,129... | collective-permute-start | bytes 1572872 | tf_op jit(solution)/shard_map/ppermute | solution.py:30
  55.5 17.1 %copy-start.2 = (bf16[1,4096,384]{2,1,0:T(8,128)(2,1)S(1)}, bf16[1,4096,384]{2,1,0:T(8,128)(2,1)}, u32[]{:S(2)}) copy-start(bf16[1,4096,384]{2,1,0:T(8,128)(2,1)} %param.10) | copy-start | bytes 9437188
  72.5 12.3 %collective-permute-start.4 = (bf16[256,1024]{1,0:T(8,128)(2,1)S(1)}, bf16[256,1024]{1,0:T(8,128)(2,1)S(1)}, u32[]{:S(2)}, u32[]{:S(2)}) collective-permute-start(bf16[256,1024]{1,0:T(8,128)(2,1)S(1)} %collective-permute-done), channel_id=1, source_target_pairs={{0,64},{64,128},{128,192},{192,0},{1,65},{65,129},{129,193},{193,1... | collective-permute-start | bytes 1572872 | tf_op jit(solution)/shard_map/ppermute | solution.py:27
  74.1 11.6 %collective-permute-start.5 = (bf16[256,1024]{1,0:T(8,128)(2,1)S(1)}, bf16[256,1024]{1,0:T(8,128)(2,1)S(1)}, u32[]{:S(2)}, u32[]{:S(2)}) collective-permute-start(bf16[256,1024]{1,0:T(8,128)(2,1)S(1)} %collective-permute-done.3), channel_id=1, source_target_pairs={{0,192},{64,0},{128,64},{192,128},{1,193},{65,1},{129,65},{193,129... | collective-permute-start | bytes 1572872 | tf_op jit(solution)/shard_map/ppermute | solution.py:30
  87.7 12.2 %collective-permute-start.7 = (bf16[256,1024]{1,0:T(8,128)(2,1)S(1)}, bf16[256,1024]{1,0:T(8,128)(2,1)S(1)}, u32[]{:S(2)}, u32[]{:S(2)}) collective-permute-start(bf16[256,1024]{1,0:T(8,128)(2,1)S(1)} %convolution_convert_fusion.3), channel_id=1, source_target_pairs={{0,64},{64,128},{128,192},{192,0},{1,65},{65,129},{129,193},{193,1... | collective-permute-start | bytes 1572872 | tf_op jit(solution)/shard_map/ppermute | solution.py:27
  88.9 12.1 %collective-permute-start.10 = (bf16[256,1024]{1,0:T(8,128)(2,1)S(1)}, bf16[256,1024]{1,0:T(8,128)(2,1)S(1)}, u32[]{:S(2)}, u32[]{:S(2)}) collective-permute-start(bf16[256,1024]{1,0:T(8,128)(2,1)S(1)} %convolution_convert_fusion.1), channel_id=1, source_target_pairs={{0,192},{64,0},{128,64},{192,128},{1,193},{65,1},{129,65},{193,129... | collective-permute-start | bytes 1572872 | tf_op jit(solution)/shard_map/ppermute | solution.py:30
  92.6 18.1 %collective-permute-start.6 = (bf16[256,1024]{1,0:T(8,128)(2,1)S(1)}, bf16[256,1024]{1,0:T(8,128)(2,1)S(1)}, u32[]{:S(2)}, u32[]{:S(2)}) collective-permute-start(bf16[256,1024]{1,0:T(8,128)(2,1)S(1)} %convolution_convert_fusion.4), channel_id=1, source_target_pairs={{0,192},{64,0},{128,64},{192,128},{1,193},{65,1},{129,65},{193,129... | collective-permute-start | bytes 1572872 | tf_op jit(solution)/shard_map/ppermute | solution.py:30
  100.4 10.6 %collective-permute-start.8 = (bf16[256,1024]{1,0:T(8,128)(2,1)S(1)}, bf16[256,1024]{1,0:T(8,128)(2,1)S(1)}, u32[]{:S(2)}, u32[]{:S(2)}) collective-permute-start(bf16[256,1024]{1,0:T(8,128)(2,1)S(1)} %add_convert_fusion.3), channel_id=1, source_target_pairs={{0,64},{64,128},{128,192},{192,0},{1,65},{65,129},{129,193},{193,1... | collective-permute-start | bytes 1572872 | tf_op jit(solution)/shard_map/ppermute | solution.py:27
  100.9 21.3 %collective-permute-start.9 = (bf16[256,1024]{1,0:T(8,128)(2,1)S(1)}, bf16[256,1024]{1,0:T(8,128)(2,1)S(1)}, u32[]{:S(2)}, u32[]{:S(2)}) collective-permute-start(bf16[256,1024]{1,0:T(8,128)(2,1)S(1)} %convolution_convert_fusion.2), channel_id=1, source_target_pairs={{0,64},{64,128},{128,192},{192,0},{1,65},{65,129},{129,193},{193,1... | collective-permute-start | bytes 1572872 | tf_op jit(solution)/shard_map/ppermute | solution.py:27
  101.5 20.7 %collective-permute-start.11 = (bf16[256,1024]{1,0:T(8,128)(2,1)S(1)}, bf16[256,1024]{1,0:T(8,128)(2,1)S(1)}, u32[]{:S(2)}, u32[]{:S(2)}) collective-permute-start(bf16[256,1024]{1,0:T(8,128)(2,1)S(1)} %add_convert_fusion.1), channel_id=1, source_target_pairs={{0,192},{64,0},{128,64},{192,128},{1,193},{65,1},{129,65},{193,129... | collective-permute-start | bytes 1572872 | tf_op jit(solution)/shard_map/ppermute | solution.py:30
  123.5 42.9 %all-to-all-start.1 = ((bf16[64,8,1024]{2,1,0:T(8,128)(2,1)}), bf16[64,8,1024]{2,1,0:T(8,128)(2,1)}, u32[]{:S(2)}, u32[]{:S(2)}) async-start(bf16[64,8,1024]{2,1,0:T(8,128)(2,1)} %maximum_bitcast_fusion), calls=%async_computation.1 | async-start | bytes 2097152 | tf_op jit(solution)/shard_map/all_to_all | solution.py:90

commit v2 on v1

v2 whole, which is shorter than its diff:
```python
import jax
import jax.numpy as jnp
from jax import lax
from jax.sharding import PartitionSpec as P

ED = ("expert", "dp")
BF = jnp.bfloat16
F32 = jnp.float32
CHUNKS = 2


def dot(a, b):
    return jnp.dot(a, b, preferred_element_type=F32)


def on_device(tokens, routing, gate_weights, w_gate, w_up, w_down):
    toks, width = tokens.shape
    fanout = routing.shape[1]
    experts = lax.axis_size(ED)
    sections = lax.axis_size("section")
    cap = min(toks, max(2, 2 * toks * fanout // experts))
    quarter = width // sections
    s = lax.axis_index("section")
    right = [(k, (k + 1) % sections) for k in range(sections)]
    left = [(k, (k - 1) % sections) for k in range(sections)]

    def to_right(v):
        return lax.ppermute(v, "section", right)

    def to_left(v):
        return lax.ppermute(v, "section", left)

    match = routing[:, :, None] == jnp.arange(experts, dtype=jnp.int32)[None, None, :]
    named = jnp.any(match, axis=1)
    weight = jnp.sum(jnp.where(match, gate_weights[:, :, None], 0.0), axis=1)
    counts = named.astype(jnp.int32)
    rank = jnp.cumsum(counts, axis=0) - counts
    place = named[:, :, None] & (rank[:, :, None] == jnp.arange(cap, dtype=jnp.int32)[None, None, :])
    pick = place.astype(BF).reshape(toks, experts * cap)
    spread = jnp.where(place, weight[:, :, None], 0.0).reshape(toks, experts * cap)
    spread_hi = spread.astype(BF)
    spread_lo = (spread - spread_hi.astype(F32)).astype(BF)
    spread2 = jnp.concatenate([spread_hi, spread_lo], axis=0)

    rows = experts * cap
    half = rows // 2
    part = quarter // CHUNKS

    def exchange(v):
        return lax.all_to_all(
            v.reshape(experts, cap, part), ED, split_axis=0, concat_axis=0, tiled=True
        ).reshape(rows, part)

    def span(q, c):
        return (q % sections) * quarter + c * part

    received = []
    for c in range(CHUNKS):
        cols = lax.dynamic_slice_in_dim(tokens, span(s, c), part, axis=1)
        outgoing = lax.dot_general(
            pick, cols, (((0,), (0,)), ((), ())), preferred_element_type=F32
        ).astype(BF)
        received.append(exchange(outgoing))

    def k_part(block, q, c):
        g = lax.dynamic_slice_in_dim(w_gate[0], span(q, c), part, axis=0)
        u = lax.dynamic_slice_in_dim(w_up[0], span(q, c), part, axis=0)
        return dot(block, g), dot(block, u)

    gate = up = jnp.zeros((), F32)
    for c in range(CHUNKS):
        block = received[c]
        from_left = to_right(block)
        from_right = to_left(block)
        across = jnp.concatenate([to_right(from_left[:half]), to_left(from_right[half:])], axis=0)
        for piece, q in ((block, s), (from_left, s + 3), (from_right, s + 1), (across, s + 2)):
            g, u = k_part(piece, q, c)
            gate, up = gate + g, up + u
    hidden = (jax.nn.silu(gate) * up).astype(BF)

    def down(h, q, c):
        return dot(h, lax.dynamic_slice_in_dim(w_down[0], span(q, c), part, axis=1))

    h_a, h_b = hidden[:half], hidden[half:]
    returned = []
    for c in range(CHUNKS):
        got_l = to_right(
            jnp.concatenate([down(h_a, s + 2, c), down(h_b, s + 1, c)], axis=0).astype(BF)
        )
        got_r = to_left(
            jnp.concatenate([down(h_a, s + 3, c), down(h_b, s + 2, c)], axis=0).astype(BF)
        )
        relay_a = to_right((down(h_a, s + 1, c) + got_l[:half].astype(F32)).astype(BF))
        relay_b = to_left((down(h_b, s + 3, c) + got_r[half:].astype(F32)).astype(BF))
        near = jnp.concatenate([got_r[:half], got_l[half:]], axis=0).astype(F32)
        relayed = jnp.concatenate([relay_a, relay_b], axis=0).astype(F32)
        returned.append(exchange((down(hidden, s, c) + near + relayed).astype(BF)))
    both = dot(spread2, jnp.concatenate(returned, axis=1))
    return (both[:toks] + both[toks:]).astype(BF)


def solution(mesh):
    placed = (
        P(ED, None),
        P(ED, None),
        P(ED, None),
        P(ED, None, "section"),
        P(ED, None, "section"),
        P(ED, "section", None),
    )
    return jax.shard_map(
        on_device,
        mesh=mesh,
        in_specs=placed,
        out_specs=P(ED, "section"),
        check_vma=False,
    )
```

time: 169 us -> 178 us (1.053)
  waiting for transfers between devices: 101 us -> 82.1 us
  matrix products: 16 us -> 29.4 us
  starting transfers between devices: 44.8 us -> 52.3 us
  local copies, waits for them, and re-layouts: 4.07 us -> 7.07 us
  other arithmetic: 2.57 us -> 4.95 us
    dot_general x17 -> x31, matrix products: 13.7 us -> 25.6 us  [dot(): return jnp.dot(a, b, preferred_element_type=F32)]
    ppermute x6 -> x8, waiting for transfers between devices: 38.2 us -> 28.2 us  [to_right(): return lax.ppermute(v, 'section', right)]
    ppermute x6 -> x8, waiting for transfers between devices: 6.89 us -> 0.2 us  [to_left(): return lax.ppermute(v, 'section', left)]
    all_to_all x2 -> x4, starting transfers between devices: 28.4 us -> 32.6 us  [exchange(): lax.all_to_all(v.reshape(experts, cap, part), ED, split_axis=0, concat_ax...]
    slice x1 -> x8, local copies, waits for them, and re-layouts: 1.42 us -> 3.95 us  [the longest x4 1.97 us: on_device(): near = jnp.concatenate([got_r[:half], got_l[half:]], axis=0).astype(F32)]
    ppermute x6 -> x8, starting transfers between devices: 14.1 us -> 16.4 us  [to_left(): return lax.ppermute(v, 'section', left)]
    all_to_all x2 -> x4, waiting for transfers between devices: 55.7 us -> 53.7 us  [exchange(): lax.all_to_all(v.reshape(experts, cap, part), ED, split_axis=0, concat_ax...]
    dot_general x1 -> x2, matrix products: 2.34 us -> 3.82 us  [on_device(): lax.dot_general(pick, cols, (((0,), (0,)), ((), ())), preferred_element_t...]
  transfers between devices with their start and end apart: 14 -> 20, of which waited for: 9 -> 10; matrix products, arithmetic and copies ran while one was open for 6% -> 15% of each run, Pallas kernels for 0% -> 0%
where the time goes in v2:
time: 178 us; the launch traced here: 176 us
  waiting for transfers between devices  82.1 us (46%)
  starting transfers between devices  52.3 us (29%)
  matrix products  29.4 us (17%)
  local copies, waits for them, and re-layouts  7.07 us (4%)
  other arithmetic  4.95 us (3%)
    all_to_all x4, waiting for transfers between devices, exchange(): lax.all_to_all(v.reshape(experts, cap, part), ED, split_axis=0, concat_ax...  53.7 us
    all_to_all x4, starting transfers between devices, exchange(): lax.all_to_all(v.reshape(experts, cap, part), ED, split_axis=0, concat_ax...  32.6 us
    ppermute x8, waiting for transfers between devices, to_right(): return lax.ppermute(v, 'section', right)  28.2 us
    dot_general x31, matrix products, dot(): return jnp.dot(a, b, preferred_element_type=F32)  25.6 us
    ppermute x8, starting transfers between devices, to_left(): return lax.ppermute(v, 'section', left)  16.4 us
    dot_general x2, matrix products, on_device(): lax.dot_general(pick, cols, (((0,), (0,)), ((), ())), preferred_element_t...  3.82 us
  transfers between devices with their start and end apart: 20, of which 10 were waited for; matrix products, arithmetic and copies ran while one was open for 15% of the time, Pallas kernels for 0%

profile of v2, /device:TPU:1, one launch (start us, length us, event | category | flops | bytes accessed | tf_op | source)
XLA Modules:
  0.0 176.4 jit_solution(940690028748118678)
XLA Ops:
  4.8 1.9 %fusion.8 = bf16[64,8,512]{2,1,0:T(8,128)(2,1)} fusion(pred[32,512]{1,0:T(32,128)(4,1)S(1)} %get-tuple-element.6, bf16[32,4096]{1,0:T(8,128)(2,1)} %param.6, s32[]{:T(128)S(6)} %select_n.135), kind=kOutput, calls=%fused_computation.16 | convolution fusion | flops 17039360 | bytes 573444 | tf_op jit(solution)/shard_map/dot_general | solution.py:60
  6.7 13.3 %all-to-all-start = ((bf16[64,8,512]{2,1,0:T(8,128)(2,1)}), bf16[64,8,512]{2,1,0:T(8,128)(2,1)}, u32[]{:S(2)}, u32[]{:S(2)}) async-start(bf16[64,8,512]{2,1,0:T(8,128)(2,1)} %fusion.8), calls=%async_computation | async-start | bytes 1048576 | tf_op jit(solution)/shard_map/all_to_all | solution.py:50
  20.1 1.9 %fusion.9 = bf16[64,8,512]{2,1,0:T(8,128)(2,1)} fusion(pred[32,512]{1,0:T(32,128)(4,1)S(1)} %get-tuple-element.6, bf16[32,4096]{1,0:T(8,128)(2,1)} %param.6, s32[]{:T(128)S(6)} %select_n.142), kind=kOutput, calls=%fused_computation.17 | convolution fusion | flops 17039360 | bytes 573444 | tf_op jit(solution)/shard_map/dot_general | solution.py:60
  22.0 15.7 %all-to-all-done = bf16[64,8,512]{2,1,0:T(8,128)(2,1)} async-done(((bf16[64,8,512]{2,1,0:T(8,128)(2,1)}), bf16[64,8,512]{2,1,0:T(8,128)(2,1)}, u32[]{:S(2)}, u32[]{:S(2)}) %all-to-all-start) | async-done | bytes 524320 | tf_op jit(solution)/shard_map/all_to_all | solution.py:50
  37.7 5.9 %all-to-all-start.1 = ((bf16[64,8,512]{2,1,0:T(8,128)(2,1)}), bf16[64,8,512]{2,1,0:T(8,128)(2,1)}, u32[]{:S(2)}, u32[]{:S(2)}) async-start(bf16[64,8,512]{2,1,0:T(8,128)(2,1)} %fusion.9), calls=%async_computation.1 | async-start | bytes 1048576 | tf_op jit(solution)/shard_map/all_to_all | solution.py:50
  46.4 14.8 %all-to-all-done.1 = bf16[64,8,512]{2,1,0:T(8,128)(2,1)} async-done(((bf16[64,8,512]{2,1,0:T(8,128)(2,1)}), bf16[64,8,512]{2,1,0:T(8,128)(2,1)}, u32[]{:S(2)}, u32[]{:S(2)}) %all-to-all-start.1) | async-done | bytes 524320 | tf_op jit(solution)/shard_map/all_to_all | solution.py:50
  63.9 1.6 fusion.53
  65.5 1.6 fusion.47
  67.1 1.6 fusion.66
  72.3 2.7 %collective-permute-start.3 = (bf16[256,512]{1,0:T(8,128)(2,1)S(1)}, bf16[256,512]{1,0:T(8,128)(2,1)S(1)}, u32[]{:S(2)}, u32[]{:S(2)}) collective-permute-start(bf16[256,512]{1,0:T(8,128)(2,1)S(1)} %slice.65), channel_id=1, source_target_pairs={{0,192},{64,0},{128,64},{192,128},{1,193},{65,1},{129,65},{193,129... | collective-permute-start | bytes 786440 | tf_op jit(solution)/shard_map/ppermute | solution.py:31
  75.9 2.9 %collective-permute-start.7 = (bf16[256,512]{1,0:T(8,128)(2,1)S(1)}, bf16[256,512]{1,0:T(8,128)(2,1)S(1)}, u32[]{:S(2)}, u32[]{:S(2)}) collective-permute-start(bf16[256,512]{1,0:T(8,128)(2,1)S(1)} %slice.67), channel_id=1, source_target_pairs={{0,192},{64,0},{128,64},{192,128},{1,193},{65,1},{129,65},{193,129... | collective-permute-start | bytes 786440 | tf_op jit(solution)/shard_map/ppermute | solution.py:31
  78.8 1.5 convolution_add_fusion.2
  83.2 3.8 %collective-permute-done.6 = bf16[256,512]{1,0:T(8,128)(2,1)S(1)} collective-permute-done((bf16[256,512]{1,0:T(8,128)(2,1)S(1)}, bf16[256,512]{1,0:T(8,128)(2,1)S(1)}, u32[]{:S(2)}, u32[]{:S(2)}) %collective-permute-start.6) | collective-permute-done | bytes 262176 | tf_op jit(solution)/shard_map/ppermute | solution.py:28
  94.6 2.4 %collective-permute-start.8 = (bf16[512,512]{1,0:T(8,128)(2,1)S(1)}, bf16[512,512]{1,0:T(8,128)(2,1)S(1)}, u32[]{:S(2)}, u32[]{:S(2)}) collective-permute-start(bf16[512,512]{1,0:T(8,128)(2,1)S(1)} %pad_maximum_fusion), channel_id=1, source_target_pairs={{0,192},{64,0},{128,64},{192,128},{1,193},{65,1},{129,65},{193,129... | collective-permute-start | bytes 1572872 | tf_op jit(solution)/shard_map/ppermute | solution.py:31
  98.4 9.1 %collective-permute-done.9 = bf16[512,512]{1,0:T(8,128)(2,1)S(1)} collective-permute-done((bf16[512,512]{1,0:T(8,128)(2,1)S(1)}, bf16[512,512]{1,0:T(8,128)(2,1)S(1)}, u32[]{:S(2)}, u32[]{:S(2)}) %collective-permute-start.9) | collective-permute-done | bytes 524320 | tf_op jit(solution)/shard_map/ppermute | solution.py:28
  108.2 2.7 %collective-permute-start.11 = (bf16[256,512]{1,0:T(8,128)(2,1)S(1)}, bf16[256,512]{1,0:T(8,128)(2,1)S(1)}, u32[]{:S(2)}, u32[]{:S(2)}) collective-permute-start(bf16[256,512]{1,0:T(8,128)(2,1)S(1)} %add_convert_fusion.4), channel_id=1, source_target_pairs={{0,192},{64,0},{128,64},{192,128},{1,193},{65,1},{129,65},{193,129... | collective-permute-start | bytes 786440 | tf_op jit(solution)/shard_map/ppermute | solution.py:31
  112.2 12.2 %collective-permute-done.10 = bf16[256,512]{1,0:T(8,128)(2,1)S(1)} collective-permute-done((bf16[256,512]{1,0:T(8,128)(2,1)S(1)}, bf16[256,512]{1,0:T(8,128)(2,1)S(1)}, u32[]{:S(2)}, u32[]{:S(2)}) %collective-permute-start.10) | collective-permute-done | bytes 262176 | tf_op jit(solution)/shard_map/ppermute | solution.py:28
  125.7 7.4 %all-to-all-start.2 = ((bf16[64,8,512]{2,1,0:T(8,128)(2,1)}), bf16[64,8,512]{2,1,0:T(8,128)(2,1)}, u32[]{:S(2)}, u32[]{:S(2)}) async-start(bf16[64,8,512]{2,1,0:T(8,128)(2,1)} %fusion.14), calls=%async_computation.2 | async-start | bytes 1048576 | tf_op jit(solution)/shard_map/all_to_all | solution.py:50
  135.7 2.7 %collective-permute-start.15 = (bf16[256,512]{1,0:T(8,128)(2,1)S(1)}, bf16[256,512]{1,0:T(8,128)(2,1)S(1)}, u32[]{:S(2)}, u32[]{:S(2)}) collective-permute-start(bf16[256,512]{1,0:T(8,128)(2,1)S(1)} %add_convert_fusion.2), channel_id=1, source_target_pairs={{0,192},{64,0},{128,64},{192,128},{1,193},{65,1},{129,65},{193,129... | collective-permute-start | bytes 786440 | tf_op jit(solution)/shard_map/ppermute | solution.py:31
  140.4 2.5 %collective-permute-done.14 = bf16[256,512]{1,0:T(8,128)(2,1)S(1)} collective-permute-done((bf16[256,512]{1,0:T(8,128)(2,1)S(1)}, bf16[256,512]{1,0:T(8,128)(2,1)S(1)}, u32[]{:S(2)}, u32[]{:S(2)}) %collective-permute-start.14) | collective-permute-done | bytes 262176 | tf_op jit(solution)/shard_map/ppermute | solution.py:28
  144.3 6.4 %all-to-all-done.2 = bf16[64,8,512]{2,1,0:T(8,128)(2,1)} async-done(((bf16[64,8,512]{2,1,0:T(8,128)(2,1)}), bf16[64,8,512]{2,1,0:T(8,128)(2,1)}, u32[]{:S(2)}, u32[]{:S(2)}) %all-to-all-start.2) | async-done | bytes 524320 | tf_op jit(solution)/shard_map/all_to_all | solution.py:50
  150.7 5.9 %all-to-all-start.3 = ((bf16[64,8,512]{2,1,0:T(8,128)(2,1)}), bf16[64,8,512]{2,1,0:T(8,128)(2,1)}, u32[]{:S(2)}, u32[]{:S(2)}) async-start(bf16[64,8,512]{2,1,0:T(8,128)(2,1)} %fusion.15), calls=%async_computation.3 | async-start | bytes 1048576 | tf_op jit(solution)/shard_map/all_to_all | solution.py:50
  157.5 16.8 %all-to-all-done.3 = bf16[64,8,512]{2,1,0:T(8,128)(2,1)} async-done(((bf16[64,8,512]{2,1,0:T(8,128)(2,1)}), bf16[64,8,512]{2,1,0:T(8,128)(2,1)}, u32[]{:S(2)}, u32[]{:S(2)}) %all-to-all-start.3) | async-done | bytes 524320 | tf_op jit(solution)/shard_map/all_to_all | solution.py:50
  174.2 1.5 fusion.10
  (94 shorter events, 37.0 us)
Async XLA Ops:
  0.0 92.4 %copy-start = (bf16[1,384,4096]{2,1,0:T(8,128)(2,1)S(1)}, bf16[1,384,4096]{2,1,0:T(8,128)(2,1)}, u32[]{:S(2)}) copy-start(bf16[1,384,4096]{2,1,0:T(8,128)(2,1)} %param.11) | copy-start | bytes 9437188
  3.3 63.8 %copy-start.3 = (f32[32,512]{1,0:T(8,128)}, f32[32,512]{1,0:T(8,128)S(1)}, u32[]{:S(2)}) copy-start(f32[32,512]{1,0:T(8,128)S(1)} %copy.25) | copy-start | bytes 196612
  6.7 31.0 %all-to-all-start = ((bf16[64,8,512]{2,1,0:T(8,128)(2,1)}), bf16[64,8,512]{2,1,0:T(8,128)(2,1)}, u32[]{:S(2)}, u32[]{:S(2)}) async-start(bf16[64,8,512]{2,1,0:T(8,128)(2,1)} %fusion.8), calls=%async_computation | async-start | bytes 1048576 | tf_op jit(solution)/shard_map/all_to_all | solution.py:50
  37.7 23.6 %all-to-all-start.1 = ((bf16[64,8,512]{2,1,0:T(8,128)(2,1)}), bf16[64,8,512]{2,1,0:T(8,128)(2,1)}, u32[]{:S(2)}, u32[]{:S(2)}) async-start(bf16[64,8,512]{2,1,0:T(8,128)(2,1)} %fusion.9), calls=%async_computation.1 | async-start | bytes 1048576 | tf_op jit(solution)/shard_map/all_to_all | solution.py:50
  43.7 26.6 %collective-permute-start = (bf16[512,512]{1,0:T(8,128)(2,1)}, bf16[512,512]{1,0:T(8,128)(2,1)}, u32[]{:S(2)}, u32[]{:S(2)}) collective-permute-start(bf16[512,512]{1,0:T(8,128)(2,1)} %bitcast.4), channel_id=1, source_target_pairs={{0,64},{64,128},{128,192},{192,0},{1,65},{65,129},{129,193},{193,1... | collective-permute-start | bytes 1572872 | tf_op jit(solution)/shard_map/ppermute | solution.py:28
  44.9 26.4 %collective-permute-start.1 = (bf16[512,512]{1,0:T(8,128)(2,1)}, bf16[512,512]{1,0:T(8,128)(2,1)}, u32[]{:S(2)}, u32[]{:S(2)}) collective-permute-start(bf16[512,512]{1,0:T(8,128)(2,1)} %bitcast.4), channel_id=1, source_target_pairs={{0,192},{64,0},{128,64},{192,128},{1,193},{65,1},{129,65},{193,129... | collective-permute-start | bytes 1572872 | tf_op jit(solution)/shard_map/ppermute | solution.py:31
  61.2 5.9 %copy-start.1 = (bf16[1,4096,384]{2,1,0:T(8,128)(2,1)S(1)}, bf16[1,4096,384]{2,1,0:T(8,128)(2,1)}, u32[]{:S(2)}) copy-start(bf16[1,4096,384]{2,1,0:T(8,128)(2,1)} %param.9) | copy-start | bytes 9437188
  61.2 14.5 %collective-permute-start.4 = (bf16[512,512]{1,0:T(8,128)(2,1)}, bf16[512,512]{1,0:T(8,128)(2,1)S(1)}, u32[]{:S(2)}, u32[]{:S(2)}) collective-permute-start(bf16[512,512]{1,0:T(8,128)(2,1)} %bitcast.10), channel_id=1, source_target_pairs={{0,64},{64,128},{128,192},{192,0},{1,65},{65,129},{129,193},{193,1... | collective-permute-start | bytes 1572872 | tf_op jit(solution)/shard_map/ppermute | solution.py:28
  62.4 13.4 %collective-permute-start.5 = (bf16[512,512]{1,0:T(8,128)(2,1)}, bf16[512,512]{1,0:T(8,128)(2,1)S(1)}, u32[]{:S(2)}, u32[]{:S(2)}) collective-permute-start(bf16[512,512]{1,0:T(8,128)(2,1)} %bitcast.10), channel_id=1, source_target_pairs={{0,192},{64,0},{128,64},{192,128},{1,193},{65,1},{129,65},{193,129... | collective-permute-start | bytes 1572872 | tf_op jit(solution)/shard_map/ppermute | solution.py:31
  67.1 11.7 %copy-start.2 = (bf16[1,4096,384]{2,1,0:T(8,128)(2,1)S(1)}, bf16[1,4096,384]{2,1,0:T(8,128)(2,1)}, u32[]{:S(2)}) copy-start(bf16[1,4096,384]{2,1,0:T(8,128)(2,1)} %param.10) | copy-start | bytes 9437188
  71.2 11.5 %collective-permute-start.2 = (bf16[256,512]{1,0:T(8,128)(2,1)S(1)}, bf16[256,512]{1,0:T(8,128)(2,1)S(1)}, u32[]{:S(2)}, u32[]{:S(2)}) collective-permute-start(bf16[256,512]{1,0:T(8,128)(2,1)S(1)} %slice.64), channel_id=1, source_target_pairs={{0,64},{64,128},{128,192},{192,0},{1,65},{65,129},{129,193},{193,1... | collective-permute-start | bytes 786440 | tf_op jit(solution)/shard_map/ppermute | solution.py:28
  72.3 10.4 %collective-permute-start.3 = (bf16[256,512]{1,0:T(8,128)(2,1)S(1)}, bf16[256,512]{1,0:T(8,128)(2,1)S(1)}, u32[]{:S(2)}, u32[]{:S(2)}) collective-permute-start(bf16[256,512]{1,0:T(8,128)(2,1)S(1)} %slice.65), channel_id=1, source_target_pairs={{0,192},{64,0},{128,64},{192,128},{1,193},{65,1},{129,65},{193,129... | collective-permute-start | bytes 786440 | tf_op jit(solution)/shard_map/ppermute | solution.py:31
  75.8 11.2 %collective-permute-start.6 = (bf16[256,512]{1,0:T(8,128)(2,1)S(1)}, bf16[256,512]{1,0:T(8,128)(2,1)S(1)}, u32[]{:S(2)}, u32[]{:S(2)}) collective-permute-start(bf16[256,512]{1,0:T(8,128)(2,1)S(1)} %slice.66), channel_id=1, source_target_pairs={{0,64},{64,128},{128,192},{192,0},{1,65},{65,129},{129,193},{193,1... | collective-permute-start | bytes 786440 | tf_op jit(solution)/shard_map/ppermute | solution.py:28
  75.9 11.6 %collective-permute-start.7 = (bf16[256,512]{1,0:T(8,128)(2,1)S(1)}, bf16[256,512]{1,0:T(8,128)(2,1)S(1)}, u32[]{:S(2)}, u32[]{:S(2)}) collective-permute-start(bf16[256,512]{1,0:T(8,128)(2,1)S(1)} %slice.67), channel_id=1, source_target_pairs={{0,192},{64,0},{128,64},{192,128},{1,193},{65,1},{129,65},{193,129... | collective-permute-start | bytes 786440 | tf_op jit(solution)/shard_map/ppermute | solution.py:31
  94.0 13.5 %collective-permute-start.9 = (bf16[512,512]{1,0:T(8,128)(2,1)S(1)}, bf16[512,512]{1,0:T(8,128)(2,1)S(1)}, u32[]{:S(2)}, u32[]{:S(2)}) collective-permute-start(bf16[512,512]{1,0:T(8,128)(2,1)S(1)} %pad_maximum_fusion.1), channel_id=1, source_target_pairs={{0,64},{64,128},{128,192},{192,0},{1,65},{65,129},{129,193},{193,1... | collective-permute-start | bytes 1572872 | tf_op jit(solution)/shard_map/ppermute | solution.py:28
  94.6 13.4 %collective-permute-start.8 = (bf16[512,512]{1,0:T(8,128)(2,1)S(1)}, bf16[512,512]{1,0:T(8,128)(2,1)S(1)}, u32[]{:S(2)}, u32[]{:S(2)}) collective-permute-start(bf16[512,512]{1,0:T(8,128)(2,1)S(1)} %pad_maximum_fusion), channel_id=1, source_target_pairs={{0,192},{64,0},{128,64},{192,128},{1,193},{65,1},{129,65},{193,129... | collective-permute-start | bytes 1572872 | tf_op jit(solution)/shard_map/ppermute | solution.py:31
  98.1 35.0 %collective-permute-start.13 = (bf16[512,512]{1,0:T(8,128)(2,1)}, bf16[512,512]{1,0:T(8,128)(2,1)}, u32[]{:S(2)}, u32[]{:S(2)}) collective-permute-start(bf16[512,512]{1,0:T(8,128)(2,1)} %pad_maximum_fusion.3), channel_id=1, source_target_pairs={{0,64},{64,128},{128,192},{192,0},{1,65},{65,129},{129,193},{193,1... | collective-permute-start | bytes 1572872 | tf_op jit(solution)/shard_map/ppermute | solution.py:28
  107.8 16.5 %collective-permute-start.10 = (bf16[256,512]{1,0:T(8,128)(2,1)S(1)}, bf16[256,512]{1,0:T(8,128)(2,1)S(1)}, u32[]{:S(2)}, u32[]{:S(2)}) collective-permute-start(bf16[256,512]{1,0:T(8,128)(2,1)S(1)} %add_convert_fusion.5), channel_id=1, source_target_pairs={{0,64},{64,128},{128,192},{192,0},{1,65},{65,129},{129,193},{193,1... | collective-permute-start | bytes 786440 | tf_op jit(solution)/shard_map/ppermute | solution.py:28
  108.2 16.1 %collective-permute-start.11 = (bf16[256,512]{1,0:T(8,128)(2,1)S(1)}, bf16[256,512]{1,0:T(8,128)(2,1)S(1)}, u32[]{:S(2)}, u32[]{:S(2)}) collective-permute-start(bf16[256,512]{1,0:T(8,128)(2,1)S(1)} %add_convert_fusion.4), channel_id=1, source_target_pairs={{0,192},{64,0},{128,64},{192,128},{1,193},{65,1},{129,65},{193,129... | collective-permute-start | bytes 786440 | tf_op jit(solution)/shard_map/ppermute | solution.py:31
  112.1 22.3 %collective-permute-start.12 = (bf16[512,512]{1,0:T(8,128)(2,1)}, bf16[512,512]{1,0:T(8,128)(2,1)}, u32[]{:S(2)}, u32[]{:S(2)}) collective-permute-start(bf16[512,512]{1,0:T(8,128)(2,1)} %pad_maximum_fusion.2), channel_id=1, source_target_pairs={{0,192},{64,0},{128,64},{192,128},{1,193},{65,1},{129,65},{193,129... | collective-permute-start | bytes 1572872 | tf_op jit(solution)/shard_map/ppermute | solution.py:31
  125.7 25.0 %all-to-all-start.2 = ((bf16[64,8,512]{2,1,0:T(8,128)(2,1)}), bf16[64,8,512]{2,1,0:T(8,128)(2,1)}, u32[]{:S(2)}, u32[]{:S(2)}) async-start(bf16[64,8,512]{2,1,0:T(8,128)(2,1)} %fusion.14), calls=%async_computation.2 | async-start | bytes 1048576 | tf_op jit(solution)/shard_map/all_to_all | solution.py:50
  134.3 8.5 %collective-permute-start.14 = (bf16[256,512]{1,0:T(8,128)(2,1)S(1)}, bf16[256,512]{1,0:T(8,128)(2,1)S(1)}, u32[]{:S(2)}, u32[]{:S(2)}) collective-permute-start(bf16[256,512]{1,0:T(8,128)(2,1)S(1)} %add_convert_fusion.3), channel_id=1, source_target_pairs={{0,64},{64,128},{128,192},{192,0},{1,65},{65,129},{129,193},{193,1... | collective-permute-start | bytes 786440 | tf_op jit(solution)/shard_map/ppermute | solution.py:28
  135.7 7.3 %collective-permute-start.15 = (bf16[256,512]{1,0:T(8,128)(2,1)S(1)}, bf16[256,512]{1,0:T(8,128)(2,1)S(1)}, u32[]{:S(2)}, u32[]{:S(2)}) collective-permute-start(bf16[256,512]{1,0:T(8,128)(2,1)S(1)} %add_convert_fusion.2), channel_id=1, source_target_pairs={{0,192},{64,0},{128,64},{192,128},{1,193},{65,1},{129,65},{193,129... | collective-permute-start | bytes 786440 | tf_op jit(solution)/shard_map/ppermute | solution.py:31
  150.7 23.6 %all-to-all-start.3 = ((bf16[64,8,512]{2,1,0:T(8,128)(2,1)}), bf16[64,8,512]{2,1,0:T(8,128)(2,1)}, u32[]{:S(2)}, u32[]{:S(2)}) async-start(bf16[64,8,512]{2,1,0:T(8,128)(2,1)} %fusion.15), calls=%async_computation.3 | async-start | bytes 1048576 | tf_op jit(solution)/shard_map/all_to_all | solution.py:50

commit v3 on v1

v3 whole, which is shorter than its diff:
```python
import jax
import jax.numpy as jnp
from jax import lax
from jax.experimental import pallas as pl
from jax.experimental.pallas import tpu as pltpu
from jax.sharding import PartitionSpec as P

ED = ("expert", "dp")
BF = jnp.bfloat16
F32 = jnp.float32
OUT_WIDTHS = (640, 384)
BACK_WIDTHS = (384, 640)
VMEM = pl.BlockSpec(memory_space=pltpu.VMEM)
SMEM = pl.BlockSpec(memory_space=pltpu.SMEM)
ANY = pl.BlockSpec(memory_space=pl.ANY)
PARAMS = pltpu.CompilerParams(vmem_limit_bytes=40 * 1024 * 1024)


def dot(a, b):
    return jnp.dot(a, b, preferred_element_type=F32)


def cost(flops, read):
    return pl.CostEstimate(flops=flops, bytes_accessed=read, transcendentals=0)


def tie(value, *others):
    return lax.optimization_barrier((value,) + others)[0]


def make_slots(section, tokens, routing, gate_weights, cap, experts, widths):
    toks, fanout = routing.shape
    slots = experts * cap
    quarter = sum(widths)

    def kernel(s_ref, routing_ref, weights_ref, tokens_ref, *outs):
        slot = lax.broadcasted_iota(jnp.int32, (toks, slots), 1)
        expert, order = lax.div(slot, cap), lax.rem(slot, cap)
        named = jnp.zeros((toks, slots), F32)
        weight = jnp.zeros((toks, slots), F32)
        for k in range(fanout):
            hit = routing_ref[:, k : k + 1] == expert
            named = jnp.where(hit, 1.0, named)
            weight = jnp.where(hit, weights_ref[:, k : k + 1], weight)
        before = (
            lax.broadcasted_iota(jnp.int32, (toks, toks), 0)
            > lax.broadcasted_iota(jnp.int32, (toks, toks), 1)
        )
        earlier = dot(jnp.where(before, 1.0, 0.0).astype(BF), named.astype(BF))
        place = jnp.where(earlier == order.astype(F32), named, 0.0)
        rows = lax.dot_general(
            place.astype(BF),
            tokens_ref[...],
            (((0,), (0,)), ((), ())),
            preferred_element_type=F32,
        ).astype(BF)
        start = 0
        for out, width in zip(outs, widths):
            out[...] = rows[:, start : start + width]
            start += width
        spread = place * weight
        high = spread.astype(BF)
        outs[-1][...] = jnp.concatenate([high, (spread - high.astype(F32)).astype(BF)], axis=0)

    return pl.pallas_call(
        kernel,
        grid_spec=pltpu.PrefetchScalarGridSpec(
            num_scalar_prefetch=1,
            grid=(1,),
            in_specs=[
                pl.BlockSpec((toks, fanout), lambda i, s: (0, 0)),
                pl.BlockSpec((toks, fanout), lambda i, s: (0, 0)),
                pl.BlockSpec((toks, quarter), lambda i, s: (0, s[0])),
            ],
            out_specs=[pl.BlockSpec((slots, w), lambda i, s: (0, 0)) for w in widths]
            + [pl.BlockSpec((2 * toks, slots), lambda i, s: (0, 0))],
        ),
        out_shape=[jax.ShapeDtypeStruct((slots, w), BF) for w in widths]
        + [jax.ShapeDtypeStruct((2 * toks, slots), BF)],
        compiler_params=PARAMS,
        cost_estimate=cost(2 * slots * toks * quarter, 2 * slots * quarter),
        name="slots",
    )(section, routing, gate_weights, tokens)


def gate_up(offsets, blocks, w_gate, w_up, total=None, down=None):
    rows = blocks[0].shape[0]
    widths = [b.shape[1] for b in blocks]
    hid = w_gate.shape[2]
    n = len(blocks)
    has_total = total is not None
    if down is not None:
        w_down, down_offsets, down_widths = down
        m = len(down_widths)

    def kernel(*refs):
        refs = list(refs)
        off_ref = refs.pop(0)
        down_off_ref = refs.pop(0) if down is not None else None
        block_refs = [refs.pop(0) for _ in range(n)]
        total_ref = refs.pop(0) if has_total else None
        g_ref, u_ref = refs.pop(0), refs.pop(0)
        d_ref = refs.pop(0) if down is not None else None
        outs = [refs.pop(0) for _ in range(1 if down is None else 1 + m)]
        wbuf, sem = refs.pop(0), refs.pop(0)
        copies = []
        start = 0
        for i, width in enumerate(widths):
            at = pl.ds(pl.multiple_of(off_ref[i], 128), width)
            pair = (
                pltpu.make_async_copy(
                    g_ref.at[0, at, :], wbuf.at[pl.ds(start, width), pl.ds(0, hid)], sem.at[2 * i]
                ),
                pltpu.make_async_copy(
                    u_ref.at[0, at, :],
                    wbuf.at[pl.ds(start, width), pl.ds(hid, hid)],
                    sem.at[2 * i + 1],
                ),
            )
            for c in pair:
                c.start()
            copies.append((pair, start, width))
            start += width
        downs = []
        if down is not None:
            dbuf, dsem = refs.pop(0), refs.pop(0)
            place = 0
            for i, width in enumerate(down_widths):
                c = pltpu.make_async_copy(
                    d_ref.at[0, :, pl.ds(pl.multiple_of(down_off_ref[i], 128), width)],
                    dbuf.at[:, pl.ds(place, width)],
                    dsem.at[i],
                )
                c.start()
                downs.append(c)
                place += width
        acc = total_ref[...] if has_total else None
        for (pair, start, width), block_ref in zip(copies, block_refs):
            for c in pair:
                c.wait()
            term = dot(block_ref[...], wbuf[start : start + width, :])
            acc = term if acc is None else acc + term
        if down is None:
            outs[0][...] = acc
            return
        gate, up = acc[:, :hid], acc[:, hid:]
        hidden = (gate / (1.0 + jnp.exp(-gate)) * up).astype(BF)
        outs[0][...] = hidden
        place = 0
        for c, width, out in zip(downs, down_widths, outs[1:]):
            c.wait()
            out[...] = dot(hidden, dbuf[:, place : place + width]).astype(BF)
            place += width

    scratch = [pltpu.VMEM((sum(widths), 2 * hid), BF), pltpu.SemaphoreType.DMA((2 * n,))]
    ins = [offsets] + ([down_offsets] if down is not None else []) + list(blocks)
    specs = [SMEM] * (1 if down is None else 2) + [VMEM] * n
    if has_total:
        ins.append(total)
        specs.append(VMEM)
    ins += [w_gate, w_up]
    specs += [ANY, ANY]
    flops = 2 * rows * sum(widths) * 2 * hid
    read = 2 * sum(widths) * (2 * hid + rows) + 4 * rows * 2 * hid
    if down is None:
        shapes = [jax.ShapeDtypeStruct((rows, 2 * hid), F32)]
    else:
        ins.append(w_down)
        specs.append(ANY)
        shapes = [jax.ShapeDtypeStruct((rows, hid), BF)]
        shapes += [jax.ShapeDtypeStruct((rows, w), BF) for w in down_widths]
        scratch += [pltpu.VMEM((hid, sum(down_widths)), BF), pltpu.SemaphoreType.DMA((m,))]
        flops += 2 * rows * hid * sum(down_widths)
        read += 2 * sum(down_widths) * (rows + hid)
    out = pl.pallas_call(
        kernel,
        in_specs=specs,
        out_specs=[VMEM] * len(shapes),
        out_shape=shapes,
        scratch_shapes=scratch,
        compiler_params=PARAMS,
        cost_estimate=cost(flops, read),
        name="gate_up" if down is None else "gate_up_down",
    )(*ins)
    return out[0] if down is None else out


def project(offsets, widths, hidden, w_down, addends=()):
    rows, hid = hidden.shape
    n = len(widths)
    k = len(addends)

    def kernel(off_ref, h_ref, d_ref, *refs):
        adds, outs, (dbuf, sem) = refs[:k], refs[k : k + n], refs[k + n :]
        copies = []
        place = 0
        for i, width in enumerate(widths):
            c = pltpu.make_async_copy(
                d_ref.at[0, :, pl.ds(pl.multiple_of(off_ref[i], 128), width)],
                dbuf.at[:, pl.ds(place, width)],
                sem.at[i],
            )
            c.start()
            copies.append((c, place, width))
            place += width
        for (c, place, width), out in zip(copies, outs):
            c.wait()
            value = dot(h_ref[...], dbuf[:, place : place + width])
            for a in adds:
                value = value + a[...].astype(F32)
            out[...] = value.astype(BF)

    return pl.pallas_call(
        kernel,
        in_specs=[SMEM, VMEM, ANY] + [VMEM] * k,
        out_specs=[VMEM] * n,
        out_shape=[jax.ShapeDtypeStruct((rows, w), BF) for w in widths],
        scratch_shapes=[pltpu.VMEM((hid, sum(widths)), BF), pltpu.SemaphoreType.DMA((n,))],
        compiler_params=PARAMS,
        cost_estimate=cost(
            2 * rows * hid * sum(widths), 2 * (rows * hid + sum(widths) * (hid + rows * (1 + k)))
        ),
        name="down",
    )(offsets, hidden, w_down, *addends)


def combine(spread, parts, toks):
    widths = [p.shape[1] for p in parts]

    def kernel(spread_ref, *refs):
        start = 0
        for ref, width in zip(refs[:-1], widths):
            both = dot(spread_ref[...], ref[...])
            refs[-1][:, start : start + width] = (both[:toks] + both[toks:]).astype(BF)
            start += width

    return pl.pallas_call(
        kernel,
        in_specs=[VMEM] * (1 + len(parts)),
        out_specs=VMEM,
        out_shape=jax.ShapeDtypeStruct((toks, sum(widths)), BF),
        compiler_params=PARAMS,
        name="combine",
    )(spread, *parts)


def on_device(tokens, routing, gate_weights, w_gate, w_up, w_down):
    toks, width = tokens.shape
    fanout = routing.shape[1]
    experts = lax.axis_size(ED)
    sections = lax.axis_size("section")
    cap = min(toks, max(2, 2 * toks * fanout // experts))
    quarter = width // sections
    s = lax.axis_index("section").astype(jnp.int32)
    right = [(k, (k + 1) % sections) for k in range(sections)]
    left = [(k, (k - 1) % sections) for k in range(sections)]

    def to_right(v):
        return lax.ppermute(v, "section", right)

    def to_left(v):
        return lax.ppermute(v, "section", left)

    def exchange(v):
        rows, w = v.shape
        return lax.all_to_all(
            v.reshape(experts, cap, w), ED, split_axis=0, concat_axis=0, tiled=True
        ).reshape(rows, w)

    def places(*pairs):
        return jnp.stack([lax.rem(s + d, sections) * quarter + c for d, c in pairs])

    o1, o2 = 0, OUT_WIDTHS[0]
    out1, out2, spread = make_slots(
        s.reshape(1), tokens, routing, gate_weights, cap, experts, OUT_WIDTHS
    )
    got1 = exchange(out1)
    got2 = exchange(tie(out2, got1))
    r1 = to_right(got1)
    l1 = to_left(got1)
    rr1 = to_right(r1)
    got2 = tie(got2, r1, l1)
    l2 = to_left(got2)
    r2 = to_right(got2)
    ll2 = to_left(l2)
    total = gate_up(places((0, o1), (3, o1), (1, o1)), (got1, r1, l1), w_gate, w_up)
    total = gate_up(places((2, o1), (0, o2), (1, o2)), (rr1, got2, l2), w_gate, w_up, total)
    b1, b2 = 0, BACK_WIDTHS[0]
    w1, w2 = BACK_WIDTHS
    hidden, far1, near1 = gate_up(
        places((3, o2), (2, o2)),
        (r2, ll2),
        w_gate,
        w_up,
        total,
        (w_down, places((2, b1), (3, b1)), (w1, w1)),
    )
    far1 = to_right(far1)
    near1 = to_left(near1)
    far2, near2 = project(places((2, b2), (1, b2)), (w2, w2), hidden, w_down)
    far2 = to_left(far2)
    (relay1,) = project(places((1, b1)), (w1,), hidden, w_down, (far1,))
    relay1 = to_right(relay1)
    near2 = to_right(tie(near2, relay1))
    (sum1,) = project(places((0, b1)), (w1,), hidden, w_down, (near1, relay1))
    back1 = exchange(sum1)
    (relay2,) = project(places((3, b2)), (w2,), hidden, w_down, (far2,))
    relay2 = to_left(relay2)
    (sum2,) = project(places((0, b2)), (w2,), hidden, w_down, (near2, relay2))
    back2 = exchange(sum2)
    return combine(spread, (back1, back2), toks)


def solution(mesh):
    placed = (
        P(ED, None),
        P(ED, None),
        P(ED, None),
        P(ED, None, "section"),
        P(ED, None, "section"),
        P(ED, "section", None),
    )
    return jax.shard_map(
        on_device,
        mesh=mesh,
        in_specs=placed,
        out_specs=P(ED, "section"),
        check_vma=False,
    )
```

time: 169 us -> 194 us (1.15)
  blocking collectives: 0 us -> 65.5 us
  waiting for transfers between devices: 101 us -> 57.9 us
  Pallas kernels: 0 us -> 24.9 us
  matrix products: 16 us -> 0 us
  starting transfers between devices: 44.8 us -> 34.9 us
  local copies, waits for them, and re-layouts: 4.07 us -> 9.41 us
  other arithmetic: 2.57 us -> 0.3 us
    all_to_all x0 -> x2, blocking collectives: none -> 65.5 us  [exchange(): lax.all_to_all(v.reshape(experts, cap, w), ED, split_axis=0, concat_axis=...]
    all_to_all x2, waiting for transfers between devices: 55.7 us -> 0.01 us  [exchange(): lax.all_to_all(v.reshape(experts, cap, w), ED, split_axis=0, concat_axis=...]
    ppermute x6, waiting for transfers between devices: 6.89 us -> 35 us  [to_left(): return lax.ppermute(v, 'section', left)]
    pallas_call x0 -> x10, Pallas kernels: none -> 24.9 us  [the longest x3 12.4 us: gate_up(): pl.pallas_call(kernel, in_specs=specs, out_specs=[VMEM] * len(shapes), ou...]
    dot_general x18 -> x0, matrix products: 16 us -> none  [the longest x17 13.7 us: dot(): return jnp.dot(a, b, preferred_element_type=F32)]
    ppermute x6, waiting for transfers between devices: 38.2 us -> 23 us  [to_right(): return lax.ppermute(v, 'section', right)]
    all_to_all x2, starting transfers between devices: 28.4 us -> 20.2 us  [exchange(): lax.all_to_all(v.reshape(experts, cap, w), ED, split_axis=0, concat_axis=...]
    unnamed x11 -> x26, local copies, waits for them, and re-layouts: 1.79 us -> 9.41 us
  transfers between devices with their start and end apart: 14 -> 14, of which waited for: 9 -> 7; matrix products, arithmetic and copies ran while one was open for 6% -> 0% of each run, Pallas kernels for 0% -> 9%
where the time goes in v3:
time: 194 us; the launch traced here: 193 us
  blocking collectives  65.5 us (34%)
  waiting for transfers between devices  57.9 us (30%)
  starting transfers between devices  34.9 us (18%)
  Pallas kernels  24.9 us (13%)
  local copies, waits for them, and re-layouts  9.41 us (5%)
    all_to_all x2, blocking collectives, exchange(): lax.all_to_all(v.reshape(experts, cap, w), ED, split_axis=0, concat_axis=...  65.5 us
    ppermute x6, waiting for transfers between devices, to_left(): return lax.ppermute(v, 'section', left)  35 us
    ppermute x6, waiting for transfers between devices, to_right(): return lax.ppermute(v, 'section', right)  23 us
    all_to_all x2, starting transfers between devices, exchange(): lax.all_to_all(v.reshape(experts, cap, w), ED, split_axis=0, concat_axis=...  20.2 us
    ppermute x6, starting transfers between devices, to_left(): return lax.ppermute(v, 'section', left)  13.2 us
    pallas_call x3, Pallas kernels, gate_up(): pl.pallas_call(kernel, in_specs=specs, out_specs=[VMEM] * len(shapes), ou...  12.4 us
    unnamed x26, local copies, waits for them, and re-layouts  9.41 us
    pallas_call x5, Pallas kernels, project(): pl.pallas_call(kernel, in_specs=[SMEM, VMEM, ANY] + [VMEM] * k, out_specs...  9.12 us
  transfers between devices with their start and end apart: 14, of which 7 were waited for; matrix products, arithmetic and copies ran while one was open for 0% of the time, Pallas kernels for 9%

profile of v3, /device:TPU:1, one launch (start us, length us, event | category | flops | bytes accessed | tf_op | source)
XLA Modules:
  0.0 193.1 jit_solution(2677262912386042131)
XLA Ops:
  4.0 33.3 %all_to_all.20 = bf16[64,8,640]{2,1,0:T(8,128)(2,1)S(1)} all-to-all(bf16[64,8,640]{2,1,0:T(8,128)(2,1)S(1)} %bitcast.30), channel_id=1, replica_groups=mesh['section'=4,'expert'=32,'dp'=2] {'expert','dp'}, dimensions={0} | all-to-all | bytes 1310720 | tf_op jit(solution)/shard_map/all_to_all | solution.py:266
  37.3 5.9 %all-to-all-start.1 = ((bf16[64,8,384]{2,1,0:T(8,128)(2,1)}), bf16[64,8,384]{2,1,0:T(8,128)(2,1)S(1)}, u32[]{:S(2)}, u32[]{:S(2)}) async-start(bf16[64,8,384]{2,1,0:T(8,128)(2,1)} %bitcast.8), calls=%async_computation.1 | async-start | bytes 786432 | tf_op jit(solution)/shard_map/all_to_all | solution.py:266
  45.9 14.5 %collective-permute-done.refs_2_ = bf16[512,640]{1,0:T(8,128)(2,1)} collective-permute-done((bf16[512,640]{1,0:T(8,128)(2,1)S(1)}, bf16[512,640]{1,0:T(8,128)(2,1)}, u32[]{:S(2)}, u32[]{:S(2)}) %collective-permute-start) | collective-permute-done | bytes 655392 | tf_op jit(solution)/shard_map/ppermute | solution.py:259
  60.4 2.2 %collective-permute-start.3 = (bf16[512,384]{1,0:T(8,128)(2,1)S(1)}, bf16[512,384]{1,0:T(8,128)(2,1)}, u32[]{:S(2)}, u32[]{:S(2)}) collective-permute-start(bf16[512,384]{1,0:T(8,128)(2,1)S(1)} %bitcast.26), channel_id=1, source_target_pairs={{0,192},{64,0},{128,64},{192,128},{1,193},{65,1},{129,65},{193,129... | collective-permute-start | bytes 1179656 | tf_op jit(solution)/shard_map/ppermute | solution.py:262
  62.8 7.0 %collective-permute-done.3.refs_3_ = bf16[512,384]{1,0:T(8,128)(2,1)} collective-permute-done((bf16[512,384]{1,0:T(8,128)(2,1)S(1)}, bf16[512,384]{1,0:T(8,128)(2,1)}, u32[]{:S(2)}, u32[]{:S(2)}) %collective-permute-start.3) | collective-permute-done | bytes 393248 | tf_op jit(solution)/shard_map/ppermute | solution.py:262
  69.8 3.1 %collective-permute-start.4 = (bf16[512,384]{1,0:T(8,128)(2,1)}, bf16[512,384]{1,0:T(8,128)(2,1)}, u32[]{:S(2)}, u32[]{:S(2)}) collective-permute-start(bf16[512,384]{1,0:T(8,128)(2,1)} %collective-permute-done.3.refs_3_), channel_id=1, source_target_pairs={{0,192},{64,0},{128,64},{192,128},{1,193},{65,1},{129,65},{193,129... | collective-permute-start | bytes 1179656 | tf_op jit(solution)/shard_map/ppermute | solution.py:262
  73.1 1.9 copy-done.1
  75.0 1.9 copy-done.3
  76.9 4.2 %gate_up.2.refs_4_ = f32[512,768]{1,0:T(8,128)S(1)} custom-call(s32[3]{0:T(128)S(1)} %pad_add_fusion.3.refs_0_, bf16[512,640]{1,0:T(8,128)(2,1)S(1)} %bitcast.23, bf16[512,640]{1,0:T(8,128)(2,1)} %collective-permute-done.refs_2_, bf16[512,640]{1,0:T(8,128)(2,1)S(1)} %collective-permute-done.1.refs_3_, bf16[1,4096,384]{2,1,0:T(8,128)(2,1)S(1)} %copy-done.1, ...), custom_call_target="tpu_custom_call" | custom-call | flops 1509949440 | bytes 6488064 | tf_op jit(solution)/shard_map/gate_up/pallas_call | solution.py:175
  81.1 4.1 %gate_up.3.refs_4_ = f32[512,768]{1,0:T(8,128)S(1)} custom-call(s32[3]{0:T(128)S(1)} %pad_add_fusion.2.refs_0_, bf16[512,640]{1,0:T(8,128)(2,1)} %collective-permute-done.5.refs_1_, bf16[512,384]{1,0:T(8,128)(2,1)S(1)} %bitcast.28, bf16[512,384]{1,0:T(8,128)(2,1)} %collective-permute-done.3.refs_3_, f32[512,768]{1,0:T(8,128)S(1)} %gate_up.2.refs_4_, ...), custom_call_target="tpu_custom_call" | custom-call | flops 1107296256 | bytes 5177344 | tf_op jit(solution)/shard_map/gate_up/pallas_call | solution.py:175
  85.1 1.8 collective-permute-done.2.refs_2_
  86.9 4.2 %gate_up_down.1 = (bf16[512,384]{1,0:T(8,128)(2,1)S(1)}, bf16[512,384]{1,0:T(8,128)(2,1)}, bf16[512,384]{1,0:T(8,128)(2,1)S(1)}) custom-call(s32[2]{0:T(128)S(1)} %get-tuple-element.27.refs_0_, s32[2]{0:T(128)S(1)} %get-tuple-element.28.refs_1_, bf16[512,384]{1,0:T(8,128)(2,1)} %collective-permute-done.2.refs_2_, ...), custom_call_target="tpu_custom_call" | custom-call | flops 905969664 | bytes 4915200 | tf_op jit(solution)/shard_map/gate_up_down/pallas_call | solution.py:175
  91.9 2.8 %down.7 = (bf16[512,640]{1,0:T(8,128)(2,1)}, bf16[512,640]{1,0:T(8,128)(2,1)}) custom-call(s32[2]{0:T(128)S(1)} %pad_add_fusion.4.off_ref, bf16[512,384]{1,0:T(8,128)(2,1)S(1)} %get-tuple-element.21.h_ref, bf16[1,384,4096]{2,1,0:T(8,128)(2,1)S(1)} %copy-done), custom_call_target="tpu_custom_call" | custom-call | flops 503316480 | bytes 2686976 | tf_op jit(solution)/shard_map/down/pallas_call | solution.py:213
  94.7 2.8 %collective-permute-start.10 = (bf16[512,640]{1,0:T(8,128)(2,1)}, bf16[512,640]{1,0:T(8,128)(2,1)}, u32[]{:S(2)}, u32[]{:S(2)}) collective-permute-start(bf16[512,640]{1,0:T(8,128)(2,1)} %get-tuple-element.26), channel_id=1, source_target_pairs={{0,192},{64,0},{128,64},{192,128},{1,193},{65,1},{129,65},{193,129... | collective-permute-start | bytes 1966088 | tf_op jit(solution)/shard_map/ppermute | solution.py:262
  97.6 3.6 %collective-permute-done.7.refs_0_ = bf16[512,384]{1,0:T(8,128)(2,1)} collective-permute-done((bf16[512,384]{1,0:T(8,128)(2,1)}, bf16[512,384]{1,0:T(8,128)(2,1)}, u32[]{:S(2)}, u32[]{:S(2)}) %collective-permute-start.7) | collective-permute-done | bytes 393248 | tf_op jit(solution)/shard_map/ppermute | solution.py:259
  102.7 14.3 %collective-permute-done.6.refs_0_ = bf16[512,384]{1,0:T(8,128)(2,1)S(1)} collective-permute-done((bf16[512,384]{1,0:T(8,128)(2,1)S(1)}, bf16[512,384]{1,0:T(8,128)(2,1)S(1)}, u32[]{:S(2)}, u32[]{:S(2)}) %collective-permute-start.6) | collective-permute-done | bytes 393248 | tf_op jit(solution)/shard_map/ppermute | solution.py:262
  118.2 14.4 %all-to-all-start.2 = ((bf16[64,8,384]{2,1,0:T(8,128)(2,1)}), bf16[64,8,384]{2,1,0:T(8,128)(2,1)}, u32[]{:S(2)}, u32[]{:S(2)}) async-start(bf16[64,8,384]{2,1,0:T(8,128)(2,1)} %bitcast.29), calls=%async_computation.2 | async-start | bytes 786432 | tf_op jit(solution)/shard_map/all_to_all | solution.py:266
  132.6 2.6 %down.8 = bf16[512,640]{1,0:T(8,128)(2,1)} custom-call(s32[1]{0:T(128)} %bitcast.18.off_ref, bf16[512,384]{1,0:T(8,128)(2,1)S(1)} %get-tuple-element.21.h_ref, bf16[1,384,4096]{2,1,0:T(8,128)(2,1)S(1)} %copy-done, bf16[512,640]{1,0:T(8,128)(2,1)} %collective-permute-done.10.refs_0_), custom_call_target="tpu_custom_call" | custom-call | flops 251658240 | bytes 2195456 | tf_op jit(solution)/shard_map/down/pallas_call | solution.py:213
  135.2 3.5 %collective-permute-start.11 = (bf16[512,640]{1,0:T(8,128)(2,1)}, bf16[512,640]{1,0:T(8,128)(2,1)}, u32[]{:S(2)}, u32[]{:S(2)}) collective-permute-start(bf16[512,640]{1,0:T(8,128)(2,1)} %down.8), channel_id=1, source_target_pairs={{0,192},{64,0},{128,64},{192,128},{1,193},{65,1},{129,65},{193,129... | collective-permute-start | bytes 1966088 | tf_op jit(solution)/shard_map/ppermute | solution.py:262
  138.7 13.7 %collective-permute-done.11.refs_1_ = bf16[512,640]{1,0:T(8,128)(2,1)} collective-permute-done((bf16[512,640]{1,0:T(8,128)(2,1)}, bf16[512,640]{1,0:T(8,128)(2,1)}, u32[]{:S(2)}, u32[]{:S(2)}) %collective-permute-start.11) | collective-permute-done | bytes 655392 | tf_op jit(solution)/shard_map/ppermute | solution.py:262
  152.3 3.1 %collective-permute-done.9.refs_0_ = bf16[512,640]{1,0:T(8,128)(2,1)} collective-permute-done((bf16[512,640]{1,0:T(8,128)(2,1)}, bf16[512,640]{1,0:T(8,128)(2,1)}, u32[]{:S(2)}, u32[]{:S(2)}) %collective-permute-start.9) | collective-permute-done | bytes 655392 | tf_op jit(solution)/shard_map/ppermute | solution.py:259
  155.4 1.9 down.9
  158.2 32.2 %all_to_all.21 = bf16[64,8,640]{2,1,0:T(8,128)(2,1)S(1)} all-to-all(bf16[64,8,640]{2,1,0:T(8,128)(2,1)} %bitcast.25), channel_id=1, replica_groups=mesh['section'=4,'expert'=32,'dp'=2] {'expert','dp'}, dimensions={0} | all-to-all | bytes 1310720 | tf_op jit(solution)/shard_map/all_to_all | solution.py:266
  191.2 1.9 combine.1
  (46 shorter events, 12.4 us)
Async XLA Ops:
  1.5 0.9 copy-start.7
  4.0 33.3 %copy-start.8 = (bf16[64,512]{1,0:T(8,128)(2,1)}, bf16[64,512]{1,0:T(8,128)(2,1)S(1)}, u32[]{:S(2)}) copy-start(bf16[64,512]{1,0:T(8,128)(2,1)S(1)} %get-tuple-element.16.spread_ref) | copy-start | bytes 196612
  37.3 23.1 %all-to-all-start.1 = ((bf16[64,8,384]{2,1,0:T(8,128)(2,1)}), bf16[64,8,384]{2,1,0:T(8,128)(2,1)S(1)}, u32[]{:S(2)}, u32[]{:S(2)}) async-start(bf16[64,8,384]{2,1,0:T(8,128)(2,1)} %bitcast.8), calls=%async_computation.1 | async-start | bytes 786432 | tf_op jit(solution)/shard_map/all_to_all | solution.py:266
  43.1 17.2 %collective-permute-start = (bf16[512,640]{1,0:T(8,128)(2,1)S(1)}, bf16[512,640]{1,0:T(8,128)(2,1)}, u32[]{:S(2)}, u32[]{:S(2)}) collective-permute-start(bf16[512,640]{1,0:T(8,128)(2,1)S(1)} %bitcast.21), channel_id=1, source_target_pairs={{0,64},{64,128},{128,192},{192,0},{1,65},{65,129},{129,193},{193,1... | collective-permute-start | bytes 1966088 | tf_op jit(solution)/shard_map/ppermute | solution.py:259
  44.4 16.0 %collective-permute-start.1 = (bf16[512,640]{1,0:T(8,128)(2,1)S(1)}, bf16[512,640]{1,0:T(8,128)(2,1)S(1)}, u32[]{:S(2)}, u32[]{:S(2)}) collective-permute-start(bf16[512,640]{1,0:T(8,128)(2,1)S(1)} %bitcast.22), channel_id=1, source_target_pairs={{0,192},{64,0},{128,64},{192,128},{1,193},{65,1},{129,65},{193,129... | collective-permute-start | bytes 1966088 | tf_op jit(solution)/shard_map/ppermute | solution.py:262
  60.4 9.4 %collective-permute-start.3 = (bf16[512,384]{1,0:T(8,128)(2,1)S(1)}, bf16[512,384]{1,0:T(8,128)(2,1)}, u32[]{:S(2)}, u32[]{:S(2)}) collective-permute-start(bf16[512,384]{1,0:T(8,128)(2,1)S(1)} %bitcast.26), channel_id=1, source_target_pairs={{0,192},{64,0},{128,64},{192,128},{1,193},{65,1},{129,65},{193,129... | collective-permute-start | bytes 1179656 | tf_op jit(solution)/shard_map/ppermute | solution.py:262
  62.6 18.4 %collective-permute-start.5 = (bf16[512,640]{1,0:T(8,128)(2,1)}, bf16[512,640]{1,0:T(8,128)(2,1)}, u32[]{:S(2)}, u32[]{:S(2)}) collective-permute-start(bf16[512,640]{1,0:T(8,128)(2,1)} %collective-permute-done.refs_2_), channel_id=1, source_target_pairs={{0,64},{64,128},{128,192},{192,0},{1,65},{65,129},{129,193},{193,1... | collective-permute-start | bytes 1966088 | tf_op jit(solution)/shard_map/ppermute | solution.py:259
  62.7 24.2 %collective-permute-start.2 = (bf16[512,384]{1,0:T(8,128)(2,1)S(1)}, bf16[512,384]{1,0:T(8,128)(2,1)}, u32[]{:S(2)}, u32[]{:S(2)}) collective-permute-start(bf16[512,384]{1,0:T(8,128)(2,1)S(1)} %bitcast.27), channel_id=1, source_target_pairs={{0,64},{64,128},{128,192},{192,0},{1,65},{65,129},{129,193},{193,1... | collective-permute-start | bytes 1179656 | tf_op jit(solution)/shard_map/ppermute | solution.py:259
  69.8 17.1 %collective-permute-start.4 = (bf16[512,384]{1,0:T(8,128)(2,1)}, bf16[512,384]{1,0:T(8,128)(2,1)}, u32[]{:S(2)}, u32[]{:S(2)}) collective-permute-start(bf16[512,384]{1,0:T(8,128)(2,1)} %collective-permute-done.3.refs_3_), channel_id=1, source_target_pairs={{0,192},{64,0},{128,64},{192,128},{1,193},{65,1},{129,65},{193,129... | collective-permute-start | bytes 1179656 | tf_op jit(solution)/shard_map/ppermute | solution.py:262
  73.1 1.9 copy-start.1
  75.0 1.9 copy-start.3
  76.9 4.2 %copy-start.2 = (bf16[1,4096,384]{2,1,0:T(8,128)(2,1)S(1)}, bf16[1,4096,384]{2,1,0:T(8,128)(2,1)}, u32[]{:S(2)}) copy-start(bf16[1,4096,384]{2,1,0:T(8,128)(2,1)} %refs_5_.5) | copy-start | bytes 9437188
  76.9 4.2 %copy-start.4 = (bf16[1,4096,384]{2,1,0:T(8,128)(2,1)S(1)}, bf16[1,4096,384]{2,1,0:T(8,128)(2,1)}, u32[]{:S(2)}) copy-start(bf16[1,4096,384]{2,1,0:T(8,128)(2,1)} %refs_6_.3) | copy-start | bytes 9437188
  81.0 5.9 %copy-start = (bf16[1,384,4096]{2,1,0:T(8,128)(2,1)S(1)}, bf16[1,384,4096]{2,1,0:T(8,128)(2,1)}, u32[]{:S(2)}) copy-start(bf16[1,384,4096]{2,1,0:T(8,128)(2,1)} %d_ref.9) | copy-start | bytes 9437188
  91.9 9.3 %collective-permute-start.7 = (bf16[512,384]{1,0:T(8,128)(2,1)}, bf16[512,384]{1,0:T(8,128)(2,1)}, u32[]{:S(2)}, u32[]{:S(2)}) collective-permute-start(bf16[512,384]{1,0:T(8,128)(2,1)} %get-tuple-element.23), channel_id=1, source_target_pairs={{0,64},{64,128},{128,192},{192,0},{1,65},{65,129},{129,193},{193,1... | collective-permute-start | bytes 1179656 | tf_op jit(solution)/shard_map/ppermute | solution.py:259
  91.9 5.6 %copy-start.11 = (bf16[512,384]{1,0:T(8,128)(2,1)S(1)}, bf16[512,384]{1,0:T(8,128)(2,1)}, u32[]{:S(2)}) copy-start(bf16[512,384]{1,0:T(8,128)(2,1)} %copy-done.10) | copy-start | bytes 1179652
  94.7 37.9 %collective-permute-start.10 = (bf16[512,640]{1,0:T(8,128)(2,1)}, bf16[512,640]{1,0:T(8,128)(2,1)}, u32[]{:S(2)}, u32[]{:S(2)}) collective-permute-start(bf16[512,640]{1,0:T(8,128)(2,1)} %get-tuple-element.26), channel_id=1, source_target_pairs={{0,192},{64,0},{128,64},{192,128},{1,193},{65,1},{129,65},{193,129... | collective-permute-start | bytes 1966088 | tf_op jit(solution)/shard_map/ppermute | solution.py:262
  97.5 19.6 %collective-permute-start.6 = (bf16[512,384]{1,0:T(8,128)(2,1)S(1)}, bf16[512,384]{1,0:T(8,128)(2,1)S(1)}, u32[]{:S(2)}, u32[]{:S(2)}) collective-permute-start(bf16[512,384]{1,0:T(8,128)(2,1)S(1)} %copy-done.11), channel_id=1, source_target_pairs={{0,192},{64,0},{128,64},{192,128},{1,193},{65,1},{129,65},{193,129... | collective-permute-start | bytes 1179656 | tf_op jit(solution)/shard_map/ppermute | solution.py:262
  102.6 14.4 %collective-permute-start.8 = (bf16[512,384]{1,0:T(8,128)(2,1)S(1)}, bf16[512,384]{1,0:T(8,128)(2,1)S(1)}, u32[]{:S(2)}, u32[]{:S(2)}) collective-permute-start(bf16[512,384]{1,0:T(8,128)(2,1)S(1)} %down.5), channel_id=1, source_target_pairs={{0,64},{64,128},{128,192},{192,0},{1,65},{65,129},{129,193},{193,1... | collective-permute-start | bytes 1179656 | tf_op jit(solution)/shard_map/ppermute | solution.py:259
  118.2 39.9 %all-to-all-start.2 = ((bf16[64,8,384]{2,1,0:T(8,128)(2,1)}), bf16[64,8,384]{2,1,0:T(8,128)(2,1)}, u32[]{:S(2)}, u32[]{:S(2)}) async-start(bf16[64,8,384]{2,1,0:T(8,128)(2,1)} %bitcast.29), calls=%async_computation.2 | async-start | bytes 786432 | tf_op jit(solution)/shard_map/all_to_all | solution.py:266
  135.2 17.1 %collective-permute-start.11 = (bf16[512,640]{1,0:T(8,128)(2,1)}, bf16[512,640]{1,0:T(8,128)(2,1)}, u32[]{:S(2)}, u32[]{:S(2)}) collective-permute-start(bf16[512,640]{1,0:T(8,128)(2,1)} %down.8), channel_id=1, source_target_pairs={{0,192},{64,0},{128,64},{192,128},{1,193},{65,1},{129,65},{193,129... | collective-permute-start | bytes 1966088 | tf_op jit(solution)/shard_map/ppermute | solution.py:262
  138.7 16.7 %collective-permute-start.9 = (bf16[512,640]{1,0:T(8,128)(2,1)}, bf16[512,640]{1,0:T(8,128)(2,1)}, u32[]{:S(2)}, u32[]{:S(2)}) collective-permute-start(bf16[512,640]{1,0:T(8,128)(2,1)} %get-tuple-element.25), channel_id=1, source_target_pairs={{0,64},{64,128},{128,192},{192,0},{1,65},{65,129},{129,193},{193,1... | collective-permute-start | bytes 1966088 | tf_op jit(solution)/shard_map/ppermute | solution.py:259
  157.3 0.8 copy-start.5
  190.4 0.8 copy-start.9
  (2 other events, 1.5 us)

commit v4 on v1

v4 whole, which is shorter than its diff:
```python
import jax
import jax.numpy as jnp
from jax import lax
from jax.experimental import pallas as pl
from jax.experimental.pallas import tpu as pltpu
from jax.sharding import PartitionSpec as P

ED = ("expert", "dp")
BF = jnp.bfloat16
F32 = jnp.float32
SMEM = pl.BlockSpec(memory_space=pltpu.SMEM)
ANY = pl.BlockSpec(memory_space=pl.ANY)
PARAMS = pltpu.CompilerParams(vmem_limit_bytes=56 * 1024 * 1024)


def dot(a, b):
    return jnp.dot(a, b, preferred_element_type=F32)


def cost(flops, read):
    return pl.CostEstimate(flops=flops, bytes_accessed=read, transcendentals=0)


def tie(value, *others):
    return lax.optimization_barrier((value,) + others)[0]


def make_slots(section, tokens, routing, gate_weights, cap, experts, widths):
    toks, fanout = routing.shape
    slots = experts * cap
    quarter = sum(widths)

    def kernel(s_ref, routing_ref, weights_ref, tokens_ref, *outs):
        slot = lax.broadcasted_iota(jnp.int32, (toks, slots), 1)
        expert, order = lax.div(slot, cap), lax.rem(slot, cap)
        named = jnp.zeros((toks, slots), F32)
        weight = jnp.zeros((toks, slots), F32)
        for k in range(fanout):
            hit = routing_ref[:, k : k + 1] == expert
            named = jnp.where(hit, 1.0, named)
            weight = jnp.where(hit, weights_ref[:, k : k + 1], weight)
        before = (
            lax.broadcasted_iota(jnp.int32, (toks, toks), 0)
            > lax.broadcasted_iota(jnp.int32, (toks, toks), 1)
        )
        earlier = dot(jnp.where(before, 1.0, 0.0).astype(BF), named.astype(BF))
        place = jnp.where(earlier == order.astype(F32), named, 0.0)
        rows = lax.dot_general(
            place.astype(BF),
            tokens_ref[...],
            (((0,), (0,)), ((), ())),
            preferred_element_type=F32,
        ).astype(BF)
        start = 0
        for out, width in zip(outs, widths):
            out[...] = rows[:, start : start + width]
            start += width
        spread = place * weight
        high = spread.astype(BF)
        outs[-1][...] = jnp.concatenate([high, (spread - high.astype(F32)).astype(BF)], axis=0)

    return pl.pallas_call(
        kernel,
        grid_spec=pltpu.PrefetchScalarGridSpec(
            num_scalar_prefetch=1,
            grid=(1,),
            in_specs=[
                pl.BlockSpec((toks, fanout), lambda i, s: (0, 0)),
                pl.BlockSpec((toks, fanout), lambda i, s: (0, 0)),
                pl.BlockSpec((toks, quarter), lambda i, s: (0, s[0])),
            ],
            out_specs=[pl.BlockSpec((slots, w), lambda i, s: (0, 0)) for w in widths]
            + [pl.BlockSpec((2 * toks, slots), lambda i, s: (0, 0))],
        ),
        out_shape=[jax.ShapeDtypeStruct((slots, w), BF) for w in widths]
        + [jax.ShapeDtypeStruct((2 * toks, slots), BF)],
        compiler_params=PARAMS,
        cost_estimate=cost(2 * slots * toks * quarter, 2 * slots * quarter),
        name="slots",
    )(section, routing, gate_weights, tokens)


def split_down(section, w_down, sections):
    _, hid, width = w_down.shape
    quarter = width // sections
    count = sections - 1

    def kernel(s_ref, d_ref, *refs):
        outs, sem = refs[:count], refs[count]
        copies = []
        for d in range(count):
            start = pl.multiple_of(lax.rem(s_ref[0] + d + 1, sections) * quarter, 128)
            copies.append(
                pltpu.make_async_copy(d_ref.at[0, :, pl.ds(start, quarter)], outs[d], sem.at[d])
            )
        for c in copies:
            c.start()
        for c in copies:
            c.wait()

    return pl.pallas_call(
        kernel,
        in_specs=[SMEM, ANY],
        out_specs=[ANY] * count,
        out_shape=[jax.ShapeDtypeStruct((hid, quarter), BF)] * count,
        scratch_shapes=[pltpu.SemaphoreType.DMA((count,))],
        compiler_params=PARAMS,
        cost_estimate=cost(0, 4 * count * hid * quarter),
        name="split_down",
    )(section, w_down)


def on_device(tokens, routing, gate_weights, w_gate, w_up, w_down):
    toks, width = tokens.shape
    fanout = routing.shape[1]
    experts = lax.axis_size(ED)
    sections = lax.axis_size("section")
    cap = min(toks, max(2, 2 * toks * fanout // experts))
    quarter = width // sections
    s = lax.axis_index("section").astype(jnp.int32)

    def send(v, d):
        return lax.ppermute(v, "section", [(k, (k + d) % sections) for k in range(sections)])

    def to_right(v):
        return send(v, 1)

    def to_left(v):
        return send(v, sections - 1)

    def exchange(v):
        rows, w = v.shape
        return lax.all_to_all(
            v.reshape(experts, cap, w), ED, split_axis=0, concat_axis=0, tiled=True
        ).reshape(rows, w)

    def gather(a, b):
        r_a, l_b = to_right(a), to_left(b)
        b_later, a_later, _, _ = lax.optimization_barrier((b, a, r_a, l_b))
        rr_a, ll_b = to_right(r_a), to_left(l_b)
        r_b, l_a = to_right(b_later), to_left(a_later)
        return (r_a, r_b), (l_a, l_b), (rr_a, ll_b)

    cut = split_down(s.reshape(1), w_down, sections)
    downs = [send(c, d + 1) for d, c in enumerate(cut)]
    own_down = lax.dynamic_slice_in_dim(w_down[0], s * quarter, quarter, axis=1)

    outgoing, spread = make_slots(
        s.reshape(1), tokens, routing, gate_weights, cap, experts, (quarter,)
    )
    received = exchange(tie(outgoing, *cut))
    received, *downs = lax.optimization_barrier((received, *downs))
    rows = experts * cap
    half = rows // 2

    def k_part(halves, d):
        block = jnp.concatenate(halves, axis=0)
        start = lax.rem(s + d, sections) * quarter
        g = lax.dynamic_slice_in_dim(w_gate[0], start, quarter, axis=0)
        u = lax.dynamic_slice_in_dim(w_up[0], start, quarter, axis=0)
        return dot(block, g), dot(block, u)

    own = (received[:half], received[half:])
    gate, up = k_part(own, 0)
    for halves, d in zip(gather(*own), (3, 1, 2)):
        g, u = k_part(halves, d)
        gate, up = gate + g, up + u
    hidden = (jax.nn.silu(gate) * up).astype(BF)
    out = dot(hidden, own_down)
    for d, down in enumerate(downs):
        out = out + dot(send(hidden, d + 1), down)
    returned = exchange(out.astype(BF))
    both = dot(spread, returned)
    return (both[:toks] + both[toks:]).astype(BF)


def solution(mesh):
    placed = (
        P(ED, None),
        P(ED, None),
        P(ED, None),
        P(ED, None, "section"),
        P(ED, None, "section"),
        P(ED, "section", None),
    )
    return jax.shard_map(
        on_device,
        mesh=mesh,
        in_specs=placed,
        out_specs=P(ED, "section"),
        check_vma=False,
    )
```

time: 169 us -> 245 us (1.45)
  Pallas kernels: 0 us -> 75.2 us
  blocking collectives: 0 us -> 45.3 us
  waiting for transfers between devices: 101 us -> 65.7 us
  starting transfers between devices: 44.8 us -> 30.8 us
  local copies, waits for them, and re-layouts: 4.07 us -> 8.31 us
    pallas_call x0 -> x2, Pallas kernels: none -> 75.2 us  [the longest x1 72.6 us: split_down(): pl.pallas_call(kernel, in_specs=[SMEM, ANY], out_specs=[ANY] * count, out...]
    all_to_all x2 -> x1, waiting for transfers between devices: 55.7 us -> 0.01 us  [exchange(): lax.all_to_all(v.reshape(experts, cap, w), ED, split_axis=0, concat_axis=...]
    all_to_all x0 -> x1, blocking collectives: none -> 45.3 us  [exchange(): lax.all_to_all(v.reshape(experts, cap, w), ED, split_axis=0, concat_axis=...]
    ppermute x12, waiting for transfers between devices: 45.1 us -> 65.7 us  [send(): lax.ppermute(v, 'section', [(k, (k + d) % sections) for k in range(sectio...]
    all_to_all x2 -> x1, starting transfers between devices: 28.4 us -> 13.4 us  [exchange(): lax.all_to_all(v.reshape(experts, cap, w), ED, split_axis=0, concat_axis=...]
    dot_general x17 -> x13, matrix products: 13.7 us -> 18.1 us  [dot(): return jnp.dot(a, b, preferred_element_type=F32)]
    unnamed x11 -> x13, local copies, waits for them, and re-layouts: 1.79 us -> 5.08 us
  transfers between devices with their start and end apart: 14 -> 13, of which waited for: 9 -> 8; matrix products, arithmetic and copies ran while one was open for 6% -> 7% of each run, Pallas kernels for 0% -> 0%
where the time goes in v4:
time: 245 us; the launch traced here: 244 us
  Pallas kernels  75.2 us (31%)
  waiting for transfers between devices  65.7 us (27%)
  blocking collectives  45.3 us (18%)
  starting transfers between devices  30.8 us (13%)
  matrix products  18.1 us (7%)
  local copies, waits for them, and re-layouts  8.31 us (3%)
    pallas_call x1, Pallas kernels, split_down(): pl.pallas_call(kernel, in_specs=[SMEM, ANY], out_specs=[ANY] * count, out...  72.6 us
    ppermute x12, waiting for transfers between devices, send(): lax.ppermute(v, 'section', [(k, (k + d) % sections) for k in range(sectio...  65.7 us
    all_to_all x1, blocking collectives, exchange(): lax.all_to_all(v.reshape(experts, cap, w), ED, split_axis=0, concat_axis=...  45.3 us
    dot_general x13, matrix products, dot(): return jnp.dot(a, b, preferred_element_type=F32)  18.1 us
    ppermute x12, starting transfers between devices, send(): lax.ppermute(v, 'section', [(k, (k + d) % sections) for k in range(sectio...  17.5 us
    all_to_all x1, starting transfers between devices, exchange(): lax.all_to_all(v.reshape(experts, cap, w), ED, split_axis=0, concat_axis=...  13.4 us
    unnamed x13, local copies, waits for them, and re-layouts  5.08 us
  transfers between devices with their start and end apart: 13, of which 8 were waited for; matrix products, arithmetic and copies ran while one was open for 7% of the time, Pallas kernels for 0%

profile of v4, /device:TPU:1, one launch (start us, length us, event | category | flops | bytes accessed | tf_op | source)
XLA Modules:
  0.0 244.3 jit_solution(661752681419884016)
XLA Ops:
  2.9 72.6 %split_down.1 = (bf16[384,1024]{1,0:T(8,128)(2,1)}, bf16[384,1024]{1,0:T(8,128)(2,1)}, bf16[384,1024]{1,0:T(8,128)(2,1)}) custom-call(s32[1]{0:T(128)} %bitcast.s_ref, bf16[1,384,4096]{2,1,0:T(8,128)(2,1)} %d_ref.1), custom_call_target="tpu_custom_call" | custom-call | bytes 4718592 | tf_op jit(solution)/shard_map/split_down/pallas_call | solution.py:101
  75.5 2.6 %slots.1 = (bf16[512,1024]{1,0:T(8,128)(2,1)}, bf16[64,512]{1,0:T(8,128)(2,1)}) custom-call(s32[1]{0:T(128)} %bitcast.s_ref, s32[32,8]{1,0:T(8,128)} %copy.7.routing_ref, f32[32,8]{1,0:T(8,128)} %copy.8.weights_ref, bf16[32,4096]{1,0:T(8,128)(2,1)} %tokens_ref.1), custom_call_target="tpu_custom_call" | custom-call | flops 33554432 | bytes 1048576 | tf_op jit(solution)/shard_map/slots/pallas_call | solution.py:62
  78.0 13.4 %all-to-all-start = ((bf16[64,8,1024]{2,1,0:T(8,128)(2,1)}), bf16[64,8,1024]{2,1,0:T(8,128)(2,1)}, u32[]{:S(2)}, u32[]{:S(2)}) async-start(bf16[64,8,1024]{2,1,0:T(8,128)(2,1)} %bitcast.53), calls=%async_computation | async-start | bytes 2097152 | tf_op jit(solution)/shard_map/all_to_all | solution.py:133
  92.7 2.5 %collective-permute-start.1 = (bf16[384,1024]{1,0:T(8,128)(2,1)}, bf16[384,1024]{1,0:T(8,128)(2,1)}, u32[]{:S(2)}, u32[]{:S(2)}) collective-permute-start(bf16[384,1024]{1,0:T(8,128)(2,1)} %get-tuple-element.20), channel_id=1, source_target_pairs={{0,128},{64,192},{128,0},{192,64},{1,129},{65,193},{129,1},{193,65... | collective-permute-start | bytes 2359304 | tf_op jit(solution)/shard_map/ppermute | solution.py:123
  96.3 15.3 %collective-permute-done = bf16[384,1024]{1,0:T(8,128)(2,1)} collective-permute-done((bf16[384,1024]{1,0:T(8,128)(2,1)}, bf16[384,1024]{1,0:T(8,128)(2,1)}, u32[]{:S(2)}, u32[]{:S(2)}) %collective-permute-start) | collective-permute-done | bytes 786464 | tf_op jit(solution)/shard_map/ppermute | solution.py:123
  111.6 17.8 %collective-permute-done.1 = bf16[384,1024]{1,0:T(8,128)(2,1)} collective-permute-done((bf16[384,1024]{1,0:T(8,128)(2,1)}, bf16[384,1024]{1,0:T(8,128)(2,1)}, u32[]{:S(2)}, u32[]{:S(2)}) %collective-permute-start.1) | collective-permute-done | bytes 786464 | tf_op jit(solution)/shard_map/ppermute | solution.py:123
  129.4 2.1 fusion.40
  132.7 2.5 %collective-permute-start.4 = (bf16[256,1024]{1,0:T(8,128)(2,1)S(1)}, bf16[256,1024]{1,0:T(8,128)(2,1)}, u32[]{:S(2)}, u32[]{:S(2)}) collective-permute-start(bf16[256,1024]{1,0:T(8,128)(2,1)S(1)} %get-tuple-element.24), channel_id=1, source_target_pairs={{0,192},{64,0},{128,64},{192,128},{1,193},{65,1},{129,65},{193,129... | collective-permute-start | bytes 1572872 | tf_op jit(solution)/shard_map/ppermute | solution.py:123
  135.2 10.3 %collective-permute-done.3 = bf16[256,1024]{1,0:T(8,128)(2,1)} collective-permute-done((bf16[256,1024]{1,0:T(8,128)(2,1)}, bf16[256,1024]{1,0:T(8,128)(2,1)}, u32[]{:S(2)}, u32[]{:S(2)}) %collective-permute-start.3) | collective-permute-done | bytes 524320 | tf_op jit(solution)/shard_map/ppermute | solution.py:123
  145.8 3.5 %collective-permute-start.6 = (bf16[256,1024]{1,0:T(8,128)(2,1)}, bf16[256,1024]{1,0:T(8,128)(2,1)}, u32[]{:S(2)}, u32[]{:S(2)}) collective-permute-start(bf16[256,1024]{1,0:T(8,128)(2,1)} %get-tuple-element.25), channel_id=1, source_target_pairs={{0,192},{64,0},{128,64},{192,128},{1,193},{65,1},{129,65},{193,129... | collective-permute-start | bytes 1572872 | tf_op jit(solution)/shard_map/ppermute | solution.py:123
  149.3 2.7 %collective-permute-start.8 = (bf16[256,1024]{1,0:T(8,128)(2,1)}, bf16[256,1024]{1,0:T(8,128)(2,1)S(1)}, u32[]{:S(2)}, u32[]{:S(2)}) collective-permute-start(bf16[256,1024]{1,0:T(8,128)(2,1)} %collective-permute-done.4), channel_id=1, source_target_pairs={{0,192},{64,0},{128,64},{192,128},{1,193},{65,1},{129,65},{193,129... | collective-permute-start | bytes 1572872 | tf_op jit(solution)/shard_map/ppermute | solution.py:123
  153.1 6.2 %collective-permute-done.6 = bf16[256,1024]{1,0:T(8,128)(2,1)} collective-permute-done((bf16[256,1024]{1,0:T(8,128)(2,1)}, bf16[256,1024]{1,0:T(8,128)(2,1)}, u32[]{:S(2)}, u32[]{:S(2)}) %collective-permute-start.6) | collective-permute-done | bytes 524320 | tf_op jit(solution)/shard_map/ppermute | solution.py:123
  161.5 2.0 fusion.8
  165.0 1.9 fusion.1
  167.0 6.6 %collective-permute-done.7 = bf16[256,1024]{1,0:T(8,128)(2,1)S(1)} collective-permute-done((bf16[256,1024]{1,0:T(8,128)(2,1)}, bf16[256,1024]{1,0:T(8,128)(2,1)S(1)}, u32[]{:S(2)}, u32[]{:S(2)}) %collective-permute-start.7) | collective-permute-done | bytes 524320 | tf_op jit(solution)/shard_map/ppermute | solution.py:123
  174.3 1.9 fusion
  178.6 2.7 %collective-permute-start.11 = (bf16[512,384]{1,0:T(8,128)(2,1)}, bf16[512,384]{1,0:T(8,128)(2,1)S(1)}, u32[]{:S(2)}, u32[]{:S(2)}) collective-permute-start(bf16[512,384]{1,0:T(8,128)(2,1)} %multiply_convert_fusion), channel_id=1, source_target_pairs={{0,192},{64,0},{128,64},{192,128},{1,193},{65,1},{129,65},{193,129... | collective-permute-start | bytes 1179656 | tf_op jit(solution)/shard_map/ppermute | solution.py:123
  181.3 2.0 fusion.5
  183.3 6.9 %collective-permute-done.9 = bf16[512,384]{1,0:T(8,128)(2,1)S(1)} collective-permute-done((bf16[512,384]{1,0:T(8,128)(2,1)}, bf16[512,384]{1,0:T(8,128)(2,1)S(1)}, u32[]{:S(2)}, u32[]{:S(2)}) %collective-permute-start.9) | collective-permute-done | bytes 393248 | tf_op jit(solution)/shard_map/ppermute | solution.py:123
  190.2 1.8 fusion.41
  192.0 2.2 collective-permute-done.10
  194.3 1.8 fusion.42
  196.1 1.9 fusion.2
  198.0 45.3 %all_to_all.10 = bf16[64,8,1024]{2,1,0:T(8,128)(2,1)S(1)} all-to-all(bf16[64,8,1024]{2,1,0:T(8,128)(2,1)S(1)} %fusion.2), channel_id=1, replica_groups=mesh['section'=4,'expert'=32,'dp'=2] {'expert','dp'}, dimensions={0} | all-to-all | bytes 2097152 | tf_op jit(solution)/shard_map/all_to_all | solution.py:133
  (36 shorter events, 15.6 us)
Async XLA Ops:
  0.0 163.5 %copy-start = (bf16[1,4096,384]{2,1,0:T(8,128)(2,1)S(1)}, bf16[1,4096,384]{2,1,0:T(8,128)(2,1)}, u32[]{:S(2)}) copy-start(bf16[1,4096,384]{2,1,0:T(8,128)(2,1)} %param.9) | copy-start | bytes 9437188
  78.0 51.4 %all-to-all-start = ((bf16[64,8,1024]{2,1,0:T(8,128)(2,1)}), bf16[64,8,1024]{2,1,0:T(8,128)(2,1)}, u32[]{:S(2)}, u32[]{:S(2)}) async-start(bf16[64,8,1024]{2,1,0:T(8,128)(2,1)} %bitcast.53), calls=%async_computation | async-start | bytes 2097152 | tf_op jit(solution)/shard_map/all_to_all | solution.py:133
  91.4 20.2 %collective-permute-start = (bf16[384,1024]{1,0:T(8,128)(2,1)}, bf16[384,1024]{1,0:T(8,128)(2,1)}, u32[]{:S(2)}, u32[]{:S(2)}) collective-permute-start(bf16[384,1024]{1,0:T(8,128)(2,1)} %get-tuple-element.19), channel_id=1, source_target_pairs={{0,64},{64,128},{128,192},{192,0},{1,65},{65,129},{129,193},{193,1... | collective-permute-start | bytes 2359304 | tf_op jit(solution)/shard_map/ppermute | solution.py:123
  92.7 36.7 %collective-permute-start.1 = (bf16[384,1024]{1,0:T(8,128)(2,1)}, bf16[384,1024]{1,0:T(8,128)(2,1)}, u32[]{:S(2)}, u32[]{:S(2)}) collective-permute-start(bf16[384,1024]{1,0:T(8,128)(2,1)} %get-tuple-element.20), channel_id=1, source_target_pairs={{0,128},{64,192},{128,0},{192,64},{1,129},{65,193},{129,1},{193,65... | collective-permute-start | bytes 2359304 | tf_op jit(solution)/shard_map/ppermute | solution.py:123
  95.1 34.3 %collective-permute-start.2 = (bf16[384,1024]{1,0:T(8,128)(2,1)}, bf16[384,1024]{1,0:T(8,128)(2,1)}, u32[]{:S(2)}, u32[]{:S(2)}) collective-permute-start(bf16[384,1024]{1,0:T(8,128)(2,1)} %get-tuple-element.21), channel_id=1, source_target_pairs={{0,192},{64,0},{128,64},{192,128},{1,193},{65,1},{129,65},{193,129... | collective-permute-start | bytes 2359304 | tf_op jit(solution)/shard_map/ppermute | solution.py:123
  131.5 1.2 copy-start.2
  131.5 14.0 %collective-permute-start.3 = (bf16[256,1024]{1,0:T(8,128)(2,1)}, bf16[256,1024]{1,0:T(8,128)(2,1)}, u32[]{:S(2)}, u32[]{:S(2)}) collective-permute-start(bf16[256,1024]{1,0:T(8,128)(2,1)} %get-tuple-element.25), channel_id=1, source_target_pairs={{0,64},{64,128},{128,192},{192,0},{1,65},{65,129},{129,193},{193,1... | collective-permute-start | bytes 1572872 | tf_op jit(solution)/shard_map/ppermute | solution.py:123
  132.7 13.1 %collective-permute-start.4 = (bf16[256,1024]{1,0:T(8,128)(2,1)S(1)}, bf16[256,1024]{1,0:T(8,128)(2,1)}, u32[]{:S(2)}, u32[]{:S(2)}) collective-permute-start(bf16[256,1024]{1,0:T(8,128)(2,1)S(1)} %get-tuple-element.24), channel_id=1, source_target_pairs={{0,192},{64,0},{128,64},{192,128},{1,193},{65,1},{129,65},{193,129... | collective-permute-start | bytes 1572872 | tf_op jit(solution)/shard_map/ppermute | solution.py:123
  145.8 13.5 %collective-permute-start.6 = (bf16[256,1024]{1,0:T(8,128)(2,1)}, bf16[256,1024]{1,0:T(8,128)(2,1)}, u32[]{:S(2)}, u32[]{:S(2)}) collective-permute-start(bf16[256,1024]{1,0:T(8,128)(2,1)} %get-tuple-element.25), channel_id=1, source_target_pairs={{0,192},{64,0},{128,64},{192,128},{1,193},{65,1},{129,65},{193,129... | collective-permute-start | bytes 1572872 | tf_op jit(solution)/shard_map/ppermute | solution.py:123
  149.3 14.9 %collective-permute-start.5 = (bf16[256,1024]{1,0:T(8,128)(2,1)}, bf16[256,1024]{1,0:T(8,128)(2,1)S(1)}, u32[]{:S(2)}, u32[]{:S(2)}) collective-permute-start(bf16[256,1024]{1,0:T(8,128)(2,1)} %copy-done.2), channel_id=1, source_target_pairs={{0,64},{64,128},{128,192},{192,0},{1,65},{65,129},{129,193},{193,1... | collective-permute-start | bytes 1572872 | tf_op jit(solution)/shard_map/ppermute | solution.py:123
  149.3 24.3 %collective-permute-start.7 = (bf16[256,1024]{1,0:T(8,128)(2,1)}, bf16[256,1024]{1,0:T(8,128)(2,1)S(1)}, u32[]{:S(2)}, u32[]{:S(2)}) collective-permute-start(bf16[256,1024]{1,0:T(8,128)(2,1)} %collective-permute-done.3), channel_id=1, source_target_pairs={{0,64},{64,128},{128,192},{192,0},{1,65},{65,129},{129,193},{193,1... | collective-permute-start | bytes 1572872 | tf_op jit(solution)/shard_map/ppermute | solution.py:123
  149.3 27.0 %collective-permute-start.8 = (bf16[256,1024]{1,0:T(8,128)(2,1)}, bf16[256,1024]{1,0:T(8,128)(2,1)S(1)}, u32[]{:S(2)}, u32[]{:S(2)}) collective-permute-start(bf16[256,1024]{1,0:T(8,128)(2,1)} %collective-permute-done.4), channel_id=1, source_target_pairs={{0,192},{64,0},{128,64},{192,128},{1,193},{65,1},{129,65},{193,129... | collective-permute-start | bytes 1572872 | tf_op jit(solution)/shard_map/ppermute | solution.py:123
  161.5 2.8 %copy-start.1 = (bf16[1,4096,384]{2,1,0:T(8,128)(2,1)S(1)}, bf16[1,4096,384]{2,1,0:T(8,128)(2,1)}, u32[]{:S(2)}) copy-start(bf16[1,4096,384]{2,1,0:T(8,128)(2,1)} %param.10) | copy-start | bytes 9437188
  178.6 11.6 %collective-permute-start.9 = (bf16[512,384]{1,0:T(8,128)(2,1)}, bf16[512,384]{1,0:T(8,128)(2,1)S(1)}, u32[]{:S(2)}, u32[]{:S(2)}) collective-permute-start(bf16[512,384]{1,0:T(8,128)(2,1)} %multiply_convert_fusion), channel_id=1, source_target_pairs={{0,64},{64,128},{128,192},{192,0},{1,65},{65,129},{129,193},{193,1... | collective-permute-start | bytes 1179656 | tf_op jit(solution)/shard_map/ppermute | solution.py:123
  178.6 17.5 %collective-permute-start.11 = (bf16[512,384]{1,0:T(8,128)(2,1)}, bf16[512,384]{1,0:T(8,128)(2,1)S(1)}, u32[]{:S(2)}, u32[]{:S(2)}) collective-permute-start(bf16[512,384]{1,0:T(8,128)(2,1)} %multiply_convert_fusion), channel_id=1, source_target_pairs={{0,192},{64,0},{128,64},{192,128},{1,193},{65,1},{129,65},{193,129... | collective-permute-start | bytes 1179656 | tf_op jit(solution)/shard_map/ppermute | solution.py:123
  181.3 13.0 %collective-permute-start.10 = (bf16[512,384]{1,0:T(8,128)(2,1)}, bf16[512,384]{1,0:T(8,128)(2,1)S(1)}, u32[]{:S(2)}, u32[]{:S(2)}) collective-permute-start(bf16[512,384]{1,0:T(8,128)(2,1)} %multiply_convert_fusion), channel_id=1, source_target_pairs={{0,128},{64,192},{128,0},{192,64},{1,129},{65,193},{129,1},{193,65... | collective-permute-start | bytes 1179656 | tf_op jit(solution)/shard_map/ppermute | solution.py:123
  196.1 47.3 %copy-start.3 = (bf16[64,512]{1,0:T(8,128)(2,1)S(1)}, bf16[64,512]{1,0:T(8,128)(2,1)}, u32[]{:S(2)}) copy-start(bf16[64,512]{1,0:T(8,128)(2,1)} %get-tuple-element.17) | copy-start | bytes 196612

commit v5 on v4

--- a/solution.py
+++ b/solution.py
@@ -35,10 +35,11 @@
         expert, order = lax.div(slot, cap), lax.rem(slot, cap)
         named = jnp.zeros((toks, slots), F32)
         weight = jnp.zeros((toks, slots), F32)
+        routes, gates = routing_ref[...].T, weights_ref[...].T
         for k in range(fanout):
-            hit = routing_ref[:, k : k + 1] == expert
+            hit = routes[:, k : k + 1] == expert
             named = jnp.where(hit, 1.0, named)
-            weight = jnp.where(hit, weights_ref[:, k : k + 1], weight)
+            weight = jnp.where(hit, gates[:, k : k + 1], weight)
         before = (
             lax.broadcasted_iota(jnp.int32, (toks, toks), 0)
             > lax.broadcasted_iota(jnp.int32, (toks, toks), 1)
@@ -65,8 +66,8 @@
             num_scalar_prefetch=1,
             grid=(1,),
             in_specs=[
-                pl.BlockSpec((toks, fanout), lambda i, s: (0, 0)),
-                pl.BlockSpec((toks, fanout), lambda i, s: (0, 0)),
+                pl.BlockSpec((fanout, toks), lambda i, s: (0, 0)),
+                pl.BlockSpec((fanout, toks), lambda i, s: (0, 0)),
                 pl.BlockSpec((toks, quarter), lambda i, s: (0, s[0])),
             ],
             out_specs=[pl.BlockSpec((slots, w), lambda i, s: (0, 0)) for w in widths]
@@ -77,7 +78,7 @@
         compiler_params=PARAMS,
         cost_estimate=cost(2 * slots * toks * quarter, 2 * slots * quarter),
         name="slots",
-    )(section, routing, gate_weights, tokens)
+    )(section, routing.T, gate_weights.T, tokens)
 
 
 def split_down(section, w_down, sections):
@@ -85,29 +86,62 @@
     quarter = width // sections
     count = sections - 1
 
-    def kernel(s_ref, d_ref, *refs):
-        outs, sem = refs[:count], refs[count]
-        copies = []
-        for d in range(count):
-            start = pl.multiple_of(lax.rem(s_ref[0] + d + 1, sections) * quarter, 128)
-            copies.append(
-                pltpu.make_async_copy(d_ref.at[0, :, pl.ds(start, quarter)], outs[d], sem.at[d])
-            )
-        for c in copies:
-            c.start()
-        for c in copies:
-            c.wait()
+    def kernel(s_ref, *refs):
+        for src, out in zip(refs[:count], refs[count:]):
+            out[...] = src[0]
+
+    def columns(d):
+        return pl.BlockSpec((1, hid, quarter), lambda i, at: (0, 0, lax.rem(at[0] + d, sections)))
 
     return pl.pallas_call(
         kernel,
-        in_specs=[SMEM, ANY],
-        out_specs=[ANY] * count,
+        grid_spec=pltpu.PrefetchScalarGridSpec(
+            num_scalar_prefetch=1,
+            grid=(1,),
+            in_specs=[columns(d + 1) for d in range(count)],
+            out_specs=[pl.BlockSpec((hid, quarter), lambda i, at: (0, 0))] * count,
+        ),
         out_shape=[jax.ShapeDtypeStruct((hid, quarter), BF)] * count,
-        scratch_shapes=[pltpu.SemaphoreType.DMA((count,))],
         compiler_params=PARAMS,
         cost_estimate=cost(0, 4 * count * hid * quarter),
         name="split_down",
-    )(section, w_down)
+    )(section, *([w_down] * count))
+
+
+def project(section, hiddens, downs, w_down, sections):
+    rows, hid = hiddens[0].shape
+    quarter = downs[0].shape[1]
+    n = len(hiddens)
+    tile = rows // 2
+
+    def kernel(s_ref, *refs):
+        hs, ws, out = refs[:n], refs[n : 2 * n], refs[2 * n]
+
+        def body(i, carry):
+            at = pl.ds(pl.multiple_of(i * tile, tile), tile)
+            total = dot(hs[0][at, :], ws[0][0])
+            for h, w in zip(hs[1:], ws[1:]):
+                total = total + dot(h[at, :], w[...])
+            out[at, :] = total.astype(BF)
+            return carry
+
+        lax.fori_loop(0, rows // tile, body, 0)
+
+    return pl.pallas_call(
+        kernel,
+        grid_spec=pltpu.PrefetchScalarGridSpec(
+            num_scalar_prefetch=1,
+            grid=(1,),
+            in_specs=[pl.BlockSpec((rows, hid), lambda i, at: (0, 0))] * n
+            + [pl.BlockSpec((1, hid, quarter), lambda i, at: (0, 0, at[0]))]
+            + [pl.BlockSpec((hid, quarter), lambda i, at: (0, 0))] * (n - 1),
+            out_specs=pl.BlockSpec((rows, quarter), lambda i, at: (0, 0)),
+        ),
+        out_shape=jax.ShapeDtypeStruct((rows, quarter), BF),
+        compiler_params=PARAMS,
+        cost_estimate=cost(2 * rows * hid * quarter * n, 2 * n * hid * (rows + quarter)),
+        name="down",
+    )(section, *hiddens, w_down, *downs)
 
 
 def on_device(tokens, routing, gate_weights, w_gate, w_up, w_down):
@@ -134,22 +168,12 @@
             v.reshape(experts, cap, w), ED, split_axis=0, concat_axis=0, tiled=True
         ).reshape(rows, w)
 
-    def gather(a, b):
-        r_a, l_b = to_right(a), to_left(b)
-        b_later, a_later, _, _ = lax.optimization_barrier((b, a, r_a, l_b))
-        rr_a, ll_b = to_right(r_a), to_left(l_b)
-        r_b, l_a = to_right(b_later), to_left(a_later)
-        return (r_a, r_b), (l_a, l_b), (rr_a, ll_b)
-
     cut = split_down(s.reshape(1), w_down, sections)
     downs = [send(c, d + 1) for d, c in enumerate(cut)]
-    own_down = lax.dynamic_slice_in_dim(w_down[0], s * quarter, quarter, axis=1)
-
     outgoing, spread = make_slots(
         s.reshape(1), tokens, routing, gate_weights, cap, experts, (quarter,)
     )
     received = exchange(tie(outgoing, *cut))
-    received, *downs = lax.optimization_barrier((received, *downs))
     rows = experts * cap
     half = rows // 2
 
@@ -160,16 +184,18 @@
         u = lax.dynamic_slice_in_dim(w_up[0], start, quarter, axis=0)
         return dot(block, g), dot(block, u)
 
-    own = (received[:half], received[half:])
-    gate, up = k_part(own, 0)
-    for halves, d in zip(gather(*own), (3, 1, 2)):
+    a, b = received[:half], received[half:]
+    r_a, l_b = to_right(a), to_left(b)
+    gate, up = k_part((a, b), 0)
+    a_later, b_later, gate, up, *downs = lax.optimization_barrier((a, b, gate, up, *downs))
+    r_b, l_a = to_right(b_later), to_left(a_later)
+    across = (to_right(r_a), to_left(l_b))
+    for halves, d in (((r_a, r_b), 3), ((l_a, l_b), 1), (across, 2)):
         g, u = k_part(halves, d)
         gate, up = gate + g, up + u
     hidden = (jax.nn.silu(gate) * up).astype(BF)
-    out = dot(hidden, own_down)
-    for d, down in enumerate(downs):
-        out = out + dot(send(hidden, d + 1), down)
-    returned = exchange(out.astype(BF))
+    hiddens = [hidden] + [send(hidden, d + 1) for d in range(len(downs))]
+    returned = exchange(project(s.reshape(1), hiddens, downs, w_down, sections))
     both = dot(spread, returned)
     return (both[:toks] + both[toks:]).astype(BF)
 

time: 245 us -> 163 us (0.67)
  Pallas kernels: 75.2 us -> 11.7 us
  blocking collectives: 45.3 us -> 38.6 us
  matrix products: 18.1 us -> 11.9 us
  waiting for transfers between devices: 65.7 us -> 62.8 us
    pallas_call x1 -> x2, Pallas kernels: 72.6 us -> 9.04 us  [the longest x1 5.82 us: project(): pl.pallas_call(kernel, grid_spec=pltpu.PrefetchScalarGridSpec(num_scalar_...]
    ppermute x12, waiting for transfers between devices: 65.7 us -> 39.8 us  [send(): lax.ppermute(v, 'section', [(k, (k + d) % sections) for k in range(sectio...]
    all_to_all x1, waiting for transfers between devices: 0.01 us -> 23 us  [exchange(): lax.all_to_all(v.reshape(experts, cap, w), ED, split_axis=0, concat_axis=...]
    all_to_all x1, blocking collectives: 45.3 us -> 38.6 us  [exchange(): lax.all_to_all(v.reshape(experts, cap, w), ED, split_axis=0, concat_axis=...]
    dot_general x13 -> x9, matrix products: 18.1 us -> 11.9 us  [dot(): return jnp.dot(a, b, preferred_element_type=F32)]
    unnamed x13 -> x21, local copies, waits for them, and re-layouts: 5.08 us -> 3.32 us
  transfers between devices with their start and end apart: 13 -> 13, of which waited for: 8 -> 7; matrix products, arithmetic and copies ran while one was open for 7% -> 10% of each run, Pallas kernels for 0% -> 0%
where the time goes in v5:
time: 163 us; the launch traced here: 162 us
  waiting for transfers between devices  62.8 us (39%)
  blocking collectives  38.6 us (24%)
  starting transfers between devices  29.7 us (18%)
  matrix products  11.9 us (7%)
  Pallas kernels  11.7 us (7%)
  local copies, waits for them, and re-layouts  6.7 us (4%)
    ppermute x12, waiting for transfers between devices, send(): lax.ppermute(v, 'section', [(k, (k + d) % sections) for k in range(sectio...  39.8 us
    all_to_all x1, blocking collectives, exchange(): lax.all_to_all(v.reshape(experts, cap, w), ED, split_axis=0, concat_axis=...  38.6 us
    all_to_all x1, waiting for transfers between devices, exchange(): lax.all_to_all(v.reshape(experts, cap, w), ED, split_axis=0, concat_axis=...  23 us
    ppermute x12, starting transfers between devices, send(): lax.ppermute(v, 'section', [(k, (k + d) % sections) for k in range(sectio...  16.3 us
    all_to_all x1, starting transfers between devices, exchange(): lax.all_to_all(v.reshape(experts, cap, w), ED, split_axis=0, concat_axis=...  13.3 us
    dot_general x9, matrix products, dot(): return jnp.dot(a, b, preferred_element_type=F32)  11.9 us
    pallas_call x1, Pallas kernels, project(): pl.pallas_call(kernel, grid_spec=pltpu.PrefetchScalarGridSpec(num_scalar_...  5.82 us
    unnamed x21, local copies, waits for them, and re-layouts  3.32 us
  transfers between devices with their start and end apart: 13, of which 7 were waited for; matrix products, arithmetic and copies ran while one was open for 10% of the time, Pallas kernels for 0%

profile of v5, /device:TPU:1, one launch (start us, length us, event | category | flops | bytes accessed | tf_op | source)
XLA Modules:
  0.0 162.2 jit_solution(16878798512818596609)
XLA Ops:
  0.0 3.2 %split_down.1 = (bf16[384,1024]{1,0:T(8,128)(2,1)}, bf16[384,1024]{1,0:T(8,128)(2,1)}, bf16[384,1024]{1,0:T(8,128)(2,1)}) custom-call(s32[1]{0:T(128)} %bitcast.s_ref, bf16[1,384,4096]{2,1,0:T(8,128)(2,1)} %refs_4_.1, bf16[1,384,4096]{2,1,0:T(8,128)(2,1)} %refs_4_.1, bf16[1,384,4096]{2,1,0:T(8,128)(2,1)} %refs_4_.1), custom_call_target="tpu_custom_call" | custom-call | bytes 4718592 | tf_op jit(solution)/shard_map/split_down/pallas_call | solution.py:96
  3.2 2.6 %slots.1 = (bf16[512,1024]{1,0:T(8,128)(2,1)}, bf16[64,512]{1,0:T(8,128)(2,1)}) custom-call(s32[1]{0:T(128)} %bitcast.s_ref, s32[8,32]{1,0:T(8,128)} %bitcast.47, f32[8,32]{1,0:T(8,128)} %bitcast.48, bf16[32,4096]{1,0:T(8,128)(2,1)} %tokens_ref.1), custom_call_target="tpu_custom_call" | custom-call | flops 33554432 | bytes 1048576 | tf_op jit(solution)/shard_map/slots/pallas_call | solution.py:63
  5.8 13.3 %all-to-all-start = ((bf16[64,8,1024]{2,1,0:T(8,128)(2,1)}), bf16[64,8,1024]{2,1,0:T(8,128)(2,1)}, u32[]{:S(2)}, u32[]{:S(2)}) async-start(bf16[64,8,1024]{2,1,0:T(8,128)(2,1)} %bitcast.46), calls=%async_computation | async-start | bytes 2097152 | tf_op jit(solution)/shard_map/all_to_all | solution.py:167
  19.2 1.3 collective-permute-start
  20.5 2.5 %collective-permute-start.1 = (bf16[384,1024]{1,0:T(8,128)(2,1)}, bf16[384,1024]{1,0:T(8,128)(2,1)}, u32[]{:S(2)}, u32[]{:S(2)}) collective-permute-start(bf16[384,1024]{1,0:T(8,128)(2,1)} %get-tuple-element.21), channel_id=1, source_target_pairs={{0,128},{64,192},{128,0},{192,64},{1,129},{65,193},{129,1},{193,65... | collective-permute-start | bytes 2359304 | tf_op jit(solution)/shard_map/ppermute | solution.py:157
  22.9 1.2 collective-permute-start.2
  24.1 23.0 %all-to-all-done = bf16[64,8,1024]{2,1,0:T(8,128)(2,1)} async-done(((bf16[64,8,1024]{2,1,0:T(8,128)(2,1)}), bf16[64,8,1024]{2,1,0:T(8,128)(2,1)}, u32[]{:S(2)}, u32[]{:S(2)}) %all-to-all-start) | async-done | bytes 1048608 | tf_op jit(solution)/shard_map/all_to_all | solution.py:167
  47.1 2.2 %slice_bitcast_fusion = (bf16[256,1024]{1,0:T(8,128)(2,1)}, bf16[256,1024]{1,0:T(8,128)(2,1)}) fusion(bf16[64,8,1024]{2,1,0:T(8,128)(2,1)} %all-to-all-done), kind=kLoop, calls=%fused_computation.28 | loop fusion | bytes 2097152 | tf_op jit(solution)/shard_map/slice | solution.py:187
  49.3 2.5 %collective-permute-start.6 = (bf16[256,1024]{1,0:T(8,128)(2,1)}, bf16[256,1024]{1,0:T(8,128)(2,1)}, u32[]{:S(2)}, u32[]{:S(2)}) collective-permute-start(bf16[256,1024]{1,0:T(8,128)(2,1)} %get-tuple-element.25), channel_id=1, source_target_pairs={{0,192},{64,0},{128,64},{192,128},{1,193},{65,1},{129,65},{193,129... | collective-permute-start | bytes 1572872 | tf_op jit(solution)/shard_map/ppermute | solution.py:157
  51.8 3.0 %fusion.12 = f32[512,384]{1,0:T(8,128)} fusion(bf16[1,4096,384]{2,1,0:T(8,128)(2,1)} %param.10, s32[]{:T(128)S(6)} %select_n.16, bf16[256,1024]{1,0:T(8,128)(2,1)} %get-tuple-element.25, bf16[256,1024]{1,0:T(8,128)(2,1)} %get-tuple-element.26), kind=kOutput, calls=%fused_computation.15 | convolution fusion | flops 404750336 | bytes 2621444 | tf_op jit(solution)/shard_map/dot_general | solution.py:17
  54.9 2.8 %fusion.14 = f32[512,384]{1,0:T(8,128)} fusion(bf16[1,4096,384]{2,1,0:T(8,128)(2,1)S(1)} %copy-done, s32[]{:T(128)S(6)} %select_n.16, bf16[256,1024]{1,0:T(8,128)(2,1)} %get-tuple-element.25, bf16[256,1024]{1,0:T(8,128)(2,1)} %get-tuple-element.26), kind=kOutput, calls=%fused_computation.17 | convolution fusion | flops 404750336 | bytes 2621444 | tf_op jit(solution)/shard_map/dot_general | solution.py:17
  57.7 2.8 %collective-permute-start.5 = (bf16[256,1024]{1,0:T(8,128)(2,1)}, bf16[256,1024]{1,0:T(8,128)(2,1)}, u32[]{:S(2)}, u32[]{:S(2)}) collective-permute-start(bf16[256,1024]{1,0:T(8,128)(2,1)} %get-tuple-element.26), channel_id=1, source_target_pairs={{0,192},{64,0},{128,64},{192,128},{1,193},{65,1},{129,65},{193,129... | collective-permute-start | bytes 1572872 | tf_op jit(solution)/shard_map/ppermute | solution.py:157
  60.5 7.5 %collective-permute-done.6 = bf16[256,1024]{1,0:T(8,128)(2,1)} collective-permute-done((bf16[256,1024]{1,0:T(8,128)(2,1)}, bf16[256,1024]{1,0:T(8,128)(2,1)}, u32[]{:S(2)}, u32[]{:S(2)}) %collective-permute-start.6) | collective-permute-done | bytes 524320 | tf_op jit(solution)/shard_map/ppermute | solution.py:157
  67.9 3.4 %collective-permute-start.8 = (bf16[256,1024]{1,0:T(8,128)(2,1)}, bf16[256,1024]{1,0:T(8,128)(2,1)S(1)}, u32[]{:S(2)}, u32[]{:S(2)}) collective-permute-start(bf16[256,1024]{1,0:T(8,128)(2,1)} %collective-permute-done.6), channel_id=1, source_target_pairs={{0,192},{64,0},{128,64},{192,128},{1,193},{65,1},{129,65},{193,129... | collective-permute-start | bytes 1572872 | tf_op jit(solution)/shard_map/ppermute | solution.py:157
  71.3 1.1 constant_dynamic-update-slice_fusion.1
  72.4 6.7 %collective-permute-done.5 = bf16[256,1024]{1,0:T(8,128)(2,1)} collective-permute-done((bf16[256,1024]{1,0:T(8,128)(2,1)}, bf16[256,1024]{1,0:T(8,128)(2,1)}, u32[]{:S(2)}, u32[]{:S(2)}) %collective-permute-start.5) | collective-permute-done | bytes 524320 | tf_op jit(solution)/shard_map/ppermute | solution.py:157
  81.3 2.0 %fusion.3 = f32[512,384]{1,0:T(8,128)S(1)} fusion(bf16[512,1024]{1,0:T(8,128)(2,1)S(1)} %constant_dynamic-update-slice_fusion.2, bf16[1,4096,384]{2,1,0:T(8,128)(2,1)} %param.10, s32[]{:T(128)S(6)} %select_n.18), kind=kOutput, calls=%fused_computation.6 | convolution fusion | flops 402653184 | bytes 2621444 | tf_op jit(solution)/shard_map/dot_general | solution.py:17
  85.6 5.7 %collective-permute-done.7 = bf16[256,1024]{1,0:T(8,128)(2,1)S(1)} collective-permute-done((bf16[256,1024]{1,0:T(8,128)(2,1)}, bf16[256,1024]{1,0:T(8,128)(2,1)S(1)}, u32[]{:S(2)}, u32[]{:S(2)}) %collective-permute-start.7) | collective-permute-done | bytes 524320 | tf_op jit(solution)/shard_map/ppermute | solution.py:157
  93.3 2.1 %collective-permute-start.11 = (bf16[512,384]{1,0:T(8,128)(2,1)S(1)}, bf16[512,384]{1,0:T(8,128)(2,1)S(1)}, u32[]{:S(2)}, u32[]{:S(2)}) collective-permute-start(bf16[512,384]{1,0:T(8,128)(2,1)S(1)} %multiply_convert_fusion.refs_0_), channel_id=1, source_target_pairs={{0,192},{64,0},{128,64},{192,128},{1,193},{65,1},{129,65},{193,129... | collective-permute-start | bytes 1179656 | tf_op jit(solution)/shard_map/ppermute | solution.py:157
  96.1 8.1 %collective-permute-done.11.refs_3_ = bf16[512,384]{1,0:T(8,128)(2,1)S(1)} collective-permute-done((bf16[512,384]{1,0:T(8,128)(2,1)S(1)}, bf16[512,384]{1,0:T(8,128)(2,1)S(1)}, u32[]{:S(2)}, u32[]{:S(2)}) %collective-permute-start.11) | collective-permute-done | bytes 393248 | tf_op jit(solution)/shard_map/ppermute | solution.py:157
  104.2 2.6 %collective-permute-done.10.refs_2_ = bf16[512,384]{1,0:T(8,128)(2,1)S(1)} collective-permute-done((bf16[512,384]{1,0:T(8,128)(2,1)S(1)}, bf16[512,384]{1,0:T(8,128)(2,1)S(1)}, u32[]{:S(2)}, u32[]{:S(2)}) %collective-permute-start.10) | collective-permute-done | bytes 393248 | tf_op jit(solution)/shard_map/ppermute | solution.py:157
  106.9 9.2 %collective-permute-done.9.refs_1_ = bf16[512,384]{1,0:T(8,128)(2,1)S(1)} collective-permute-done((bf16[512,384]{1,0:T(8,128)(2,1)S(1)}, bf16[512,384]{1,0:T(8,128)(2,1)S(1)}, u32[]{:S(2)}, u32[]{:S(2)}) %collective-permute-start.9) | collective-permute-done | bytes 393248 | tf_op jit(solution)/shard_map/ppermute | solution.py:157
  116.8 5.8 %down.1 = bf16[512,1024]{1,0:T(8,128)(2,1)} custom-call(s32[1]{0:T(128)} %bitcast.s_ref, bf16[512,384]{1,0:T(8,128)(2,1)} %copy-done.3, bf16[512,384]{1,0:T(8,128)(2,1)} %copy-done.6, bf16[512,384]{1,0:T(8,128)(2,1)} %copy-done.5, bf16[512,384]{1,0:T(8,128)(2,1)} %copy-done.4, bf16[1,384,4096]{2,1,0:T(8,128)(2,1)} %refs_4_.1, ...), custom_call_target="tpu_custom_call" | custom-call | flops 1610612736 | bytes 4718592 | tf_op jit(solution)/shard_map/down/pallas_call | solution.py:130
  122.6 38.6 %all_to_all.10 = bf16[64,8,1024]{2,1,0:T(8,128)(2,1)S(1)} all-to-all(bf16[64,8,1024]{2,1,0:T(8,128)(2,1)} %bitcast.45), channel_id=1, replica_groups=mesh['section'=4,'expert'=32,'dp'=2] {'expert','dp'}, dimensions={0} | all-to-all | bytes 2097152 | tf_op jit(solution)/shard_map/all_to_all | solution.py:167
  (41 shorter events, 8.7 us)
Async XLA Ops:
  0.0 54.9 %copy-start = (bf16[1,4096,384]{2,1,0:T(8,128)(2,1)S(1)}, bf16[1,4096,384]{2,1,0:T(8,128)(2,1)}, u32[]{:S(2)}) copy-start(bf16[1,4096,384]{2,1,0:T(8,128)(2,1)} %param.9) | copy-start | bytes 9437188
  5.8 41.3 %all-to-all-start = ((bf16[64,8,1024]{2,1,0:T(8,128)(2,1)}), bf16[64,8,1024]{2,1,0:T(8,128)(2,1)}, u32[]{:S(2)}, u32[]{:S(2)}) async-start(bf16[64,8,1024]{2,1,0:T(8,128)(2,1)} %bitcast.46), calls=%async_computation | async-start | bytes 2097152 | tf_op jit(solution)/shard_map/all_to_all | solution.py:167
  19.2 38.5 %collective-permute-start = (bf16[384,1024]{1,0:T(8,128)(2,1)}, bf16[384,1024]{1,0:T(8,128)(2,1)}, u32[]{:S(2)}, u32[]{:S(2)}) collective-permute-start(bf16[384,1024]{1,0:T(8,128)(2,1)} %get-tuple-element.20), channel_id=1, source_target_pairs={{0,64},{64,128},{128,192},{192,0},{1,65},{65,129},{129,193},{193,1... | collective-permute-start | bytes 2359304 | tf_op jit(solution)/shard_map/ppermute | solution.py:157
  20.5 37.2 %collective-permute-start.1 = (bf16[384,1024]{1,0:T(8,128)(2,1)}, bf16[384,1024]{1,0:T(8,128)(2,1)}, u32[]{:S(2)}, u32[]{:S(2)}) collective-permute-start(bf16[384,1024]{1,0:T(8,128)(2,1)} %get-tuple-element.21), channel_id=1, source_target_pairs={{0,128},{64,192},{128,0},{192,64},{1,129},{65,193},{129,1},{193,65... | collective-permute-start | bytes 2359304 | tf_op jit(solution)/shard_map/ppermute | solution.py:157
  22.9 34.8 %collective-permute-start.2 = (bf16[384,1024]{1,0:T(8,128)(2,1)}, bf16[384,1024]{1,0:T(8,128)(2,1)}, u32[]{:S(2)}, u32[]{:S(2)}) collective-permute-start(bf16[384,1024]{1,0:T(8,128)(2,1)} %get-tuple-element.22), channel_id=1, source_target_pairs={{0,192},{64,0},{128,64},{192,128},{1,193},{65,1},{129,65},{193,129... | collective-permute-start | bytes 2359304 | tf_op jit(solution)/shard_map/ppermute | solution.py:157
  49.3 18.6 %collective-permute-start.6 = (bf16[256,1024]{1,0:T(8,128)(2,1)}, bf16[256,1024]{1,0:T(8,128)(2,1)}, u32[]{:S(2)}, u32[]{:S(2)}) collective-permute-start(bf16[256,1024]{1,0:T(8,128)(2,1)} %get-tuple-element.25), channel_id=1, source_target_pairs={{0,192},{64,0},{128,64},{192,128},{1,193},{65,1},{129,65},{193,129... | collective-permute-start | bytes 1572872 | tf_op jit(solution)/shard_map/ppermute | solution.py:157
  51.8 19.5 %collective-permute-start.3 = (bf16[256,1024]{1,0:T(8,128)(2,1)}, bf16[256,1024]{1,0:T(8,128)(2,1)}, u32[]{:S(2)}, u32[]{:S(2)}) collective-permute-start(bf16[256,1024]{1,0:T(8,128)(2,1)} %get-tuple-element.26), channel_id=1, source_target_pairs={{0,64},{64,128},{128,192},{192,0},{1,65},{65,129},{129,193},{193,1... | collective-permute-start | bytes 1572872 | tf_op jit(solution)/shard_map/ppermute | solution.py:157
  57.7 21.4 %collective-permute-start.5 = (bf16[256,1024]{1,0:T(8,128)(2,1)}, bf16[256,1024]{1,0:T(8,128)(2,1)}, u32[]{:S(2)}, u32[]{:S(2)}) collective-permute-start(bf16[256,1024]{1,0:T(8,128)(2,1)} %get-tuple-element.26), channel_id=1, source_target_pairs={{0,192},{64,0},{128,64},{192,128},{1,193},{65,1},{129,65},{193,129... | collective-permute-start | bytes 1572872 | tf_op jit(solution)/shard_map/ppermute | solution.py:157
  60.5 23.6 %collective-permute-start.4 = (bf16[256,1024]{1,0:T(8,128)(2,1)}, bf16[256,1024]{1,0:T(8,128)(2,1)S(1)}, u32[]{:S(2)}, u32[]{:S(2)}) collective-permute-start(bf16[256,1024]{1,0:T(8,128)(2,1)} %get-tuple-element.25), channel_id=1, source_target_pairs={{0,64},{64,128},{128,192},{192,0},{1,65},{65,129},{129,193},{193,1... | collective-permute-start | bytes 1572872 | tf_op jit(solution)/shard_map/ppermute | solution.py:157
  67.9 23.4 %collective-permute-start.8 = (bf16[256,1024]{1,0:T(8,128)(2,1)}, bf16[256,1024]{1,0:T(8,128)(2,1)S(1)}, u32[]{:S(2)}, u32[]{:S(2)}) collective-permute-start(bf16[256,1024]{1,0:T(8,128)(2,1)} %collective-permute-done.6), channel_id=1, source_target_pairs={{0,192},{64,0},{128,64},{192,128},{1,193},{65,1},{129,65},{193,129... | collective-permute-start | bytes 1572872 | tf_op jit(solution)/shard_map/ppermute | solution.py:157
  71.3 19.9 %collective-permute-start.7 = (bf16[256,1024]{1,0:T(8,128)(2,1)}, bf16[256,1024]{1,0:T(8,128)(2,1)S(1)}, u32[]{:S(2)}, u32[]{:S(2)}) collective-permute-start(bf16[256,1024]{1,0:T(8,128)(2,1)} %collective-permute-done.3), channel_id=1, source_target_pairs={{0,64},{64,128},{128,192},{192,0},{1,65},{65,129},{129,193},{193,1... | collective-permute-start | bytes 1572872 | tf_op jit(solution)/shard_map/ppermute | solution.py:157
  81.3 2.8 %copy-start.2 = (bf16[1,4096,384]{2,1,0:T(8,128)(2,1)S(1)}, bf16[1,4096,384]{2,1,0:T(8,128)(2,1)}, u32[]{:S(2)}) copy-start(bf16[1,4096,384]{2,1,0:T(8,128)(2,1)} %param.10) | copy-start | bytes 9437188
  84.1 7.3 %copy-start.1 = (f32[512,384]{1,0:T(8,128)S(1)}, f32[512,384]{1,0:T(8,128)}, u32[]{:S(2)}) copy-start(f32[512,384]{1,0:T(8,128)} %fusion.14) | copy-start | bytes 2359300
  91.3 1.1 copy-start.8
  93.3 22.8 %copy-start.3 = (bf16[512,384]{1,0:T(8,128)(2,1)}, bf16[512,384]{1,0:T(8,128)(2,1)S(1)}, u32[]{:S(2)}) copy-start(bf16[512,384]{1,0:T(8,128)(2,1)S(1)} %multiply_convert_fusion.refs_0_) | copy-start | bytes 1179652
  93.3 67.9 %copy-start.7 = (bf16[64,512]{1,0:T(8,128)(2,1)S(1)}, bf16[64,512]{1,0:T(8,128)(2,1)}, u32[]{:S(2)}) copy-start(bf16[64,512]{1,0:T(8,128)(2,1)} %get-tuple-element.18) | copy-start | bytes 196612
  93.3 10.9 %collective-permute-start.11 = (bf16[512,384]{1,0:T(8,128)(2,1)S(1)}, bf16[512,384]{1,0:T(8,128)(2,1)S(1)}, u32[]{:S(2)}, u32[]{:S(2)}) collective-permute-start(bf16[512,384]{1,0:T(8,128)(2,1)S(1)} %multiply_convert_fusion.refs_0_), channel_id=1, source_target_pairs={{0,192},{64,0},{128,64},{192,128},{1,193},{65,1},{129,65},{193,129... | collective-permute-start | bytes 1179656 | tf_op jit(solution)/shard_map/ppermute | solution.py:157
  95.4 11.5 %collective-permute-start.10 = (bf16[512,384]{1,0:T(8,128)(2,1)S(1)}, bf16[512,384]{1,0:T(8,128)(2,1)S(1)}, u32[]{:S(2)}, u32[]{:S(2)}) collective-permute-start(bf16[512,384]{1,0:T(8,128)(2,1)S(1)} %multiply_convert_fusion.refs_0_), channel_id=1, source_target_pairs={{0,128},{64,192},{128,0},{192,64},{1,129},{65,193},{129,1},{193,65... | collective-permute-start | bytes 1179656 | tf_op jit(solution)/shard_map/ppermute | solution.py:157
  95.6 20.5 %collective-permute-start.9 = (bf16[512,384]{1,0:T(8,128)(2,1)S(1)}, bf16[512,384]{1,0:T(8,128)(2,1)S(1)}, u32[]{:S(2)}, u32[]{:S(2)}) collective-permute-start(bf16[512,384]{1,0:T(8,128)(2,1)S(1)} %multiply_convert_fusion.refs_0_), channel_id=1, source_target_pairs={{0,64},{64,128},{128,192},{192,0},{1,65},{65,129},{129,193},{193,1... | collective-permute-start | bytes 1179656 | tf_op jit(solution)/shard_map/ppermute | solution.py:157
  104.2 11.8 %copy-start.4 = (bf16[512,384]{1,0:T(8,128)(2,1)}, bf16[512,384]{1,0:T(8,128)(2,1)S(1)}, u32[]{:S(2)}) copy-start(bf16[512,384]{1,0:T(8,128)(2,1)S(1)} %collective-permute-done.11.refs_3_) | copy-start | bytes 1179652
  106.9 9.2 %copy-start.5 = (bf16[512,384]{1,0:T(8,128)(2,1)}, bf16[512,384]{1,0:T(8,128)(2,1)S(1)}, u32[]{:S(2)}) copy-start(bf16[512,384]{1,0:T(8,128)(2,1)S(1)} %collective-permute-done.10.refs_2_) | copy-start | bytes 1179652
  116.1 0.7 copy-start.6

commit v6 on v5

--- a/solution.py
+++ b/solution.py
@@ -25,12 +25,14 @@
     return lax.optimization_barrier((value,) + others)[0]
 
 
-def make_slots(section, tokens, routing, gate_weights, cap, experts, widths):
+def make_slots(section, tokens, routing, gate_weights, cap, experts, share):
     toks, fanout = routing.shape
     slots = experts * cap
-    quarter = sum(widths)
-
-    def kernel(s_ref, routing_ref, weights_ref, tokens_ref, *outs):
+    width = tokens.shape[1]
+    tail = width - share * (width // share)
+
+    def kernel(s_ref, routing_ref, weights_ref, *refs):
+        sources, outs = refs[:2], refs[2:]
         slot = lax.broadcasted_iota(jnp.int32, (toks, slots), 1)
         expert, order = lax.div(slot, cap), lax.rem(slot, cap)
         named = jnp.zeros((toks, slots), F32)
@@ -46,16 +48,13 @@
         )
         earlier = dot(jnp.where(before, 1.0, 0.0).astype(BF), named.astype(BF))
         place = jnp.where(earlier == order.astype(F32), named, 0.0)
-        rows = lax.dot_general(
-            place.astype(BF),
-            tokens_ref[...],
-            (((0,), (0,)), ((), ())),
-            preferred_element_type=F32,
-        ).astype(BF)
-        start = 0
-        for out, width in zip(outs, widths):
-            out[...] = rows[:, start : start + width]
-            start += width
+        for source, out in zip(sources, outs):
+            out[...] = lax.dot_general(
+                place.astype(BF),
+                source[...],
+                (((0,), (0,)), ((), ())),
+                preferred_element_type=F32,
+            ).astype(BF)
         spread = place * weight
         high = spread.astype(BF)
         outs[-1][...] = jnp.concatenate([high, (spread - high.astype(F32)).astype(BF)], axis=0)
@@ -68,17 +67,18 @@
             in_specs=[
                 pl.BlockSpec((fanout, toks), lambda i, s: (0, 0)),
                 pl.BlockSpec((fanout, toks), lambda i, s: (0, 0)),
-                pl.BlockSpec((toks, quarter), lambda i, s: (0, s[0])),
+                pl.BlockSpec((toks, share), lambda i, s: (0, s[0])),
+                pl.BlockSpec((toks, tail), lambda i, s: (0, width // tail - 1)),
             ],
-            out_specs=[pl.BlockSpec((slots, w), lambda i, s: (0, 0)) for w in widths]
+            out_specs=[pl.BlockSpec((slots, w), lambda i, s: (0, 0)) for w in (share, tail)]
             + [pl.BlockSpec((2 * toks, slots), lambda i, s: (0, 0))],
         ),
-        out_shape=[jax.ShapeDtypeStruct((slots, w), BF) for w in widths]
+        out_shape=[jax.ShapeDtypeStruct((slots, w), BF) for w in (share, tail)]
         + [jax.ShapeDtypeStruct((2 * toks, slots), BF)],
         compiler_params=PARAMS,
-        cost_estimate=cost(2 * slots * toks * quarter, 2 * slots * quarter),
+        cost_estimate=cost(2 * slots * toks * (share + tail), 2 * slots * (share + tail)),
         name="slots",
-    )(section, routing.T, gate_weights.T, tokens)
+    )(section, routing.T, gate_weights.T, tokens, tokens)
 
 
 def split_down(section, w_down, sections):
@@ -112,30 +112,25 @@
     rows, hid = hiddens[0].shape
     quarter = downs[0].shape[1]
     n = len(hiddens)
-    tile = rows // 2
+    tile = min(256, quarter)
+    tiles = quarter // tile
 
     def kernel(s_ref, *refs):
         hs, ws, out = refs[:n], refs[n : 2 * n], refs[2 * n]
-
-        def body(i, carry):
-            at = pl.ds(pl.multiple_of(i * tile, tile), tile)
-            total = dot(hs[0][at, :], ws[0][0])
-            for h, w in zip(hs[1:], ws[1:]):
-                total = total + dot(h[at, :], w[...])
-            out[at, :] = total.astype(BF)
-            return carry
-
-        lax.fori_loop(0, rows // tile, body, 0)
+        total = dot(hs[0][...], ws[0][0])
+        for h, w in zip(hs[1:], ws[1:]):
+            total = total + dot(h[...], w[...])
+        out[...] = total.astype(BF)
 
     return pl.pallas_call(
         kernel,
         grid_spec=pltpu.PrefetchScalarGridSpec(
             num_scalar_prefetch=1,
-            grid=(1,),
+            grid=(tiles,),
             in_specs=[pl.BlockSpec((rows, hid), lambda i, at: (0, 0))] * n
-            + [pl.BlockSpec((1, hid, quarter), lambda i, at: (0, 0, at[0]))]
-            + [pl.BlockSpec((hid, quarter), lambda i, at: (0, 0))] * (n - 1),
-            out_specs=pl.BlockSpec((rows, quarter), lambda i, at: (0, 0)),
+            + [pl.BlockSpec((1, hid, tile), lambda i, at: (0, 0, at[0] * tiles + i))]
+            + [pl.BlockSpec((hid, tile), lambda i, at: (0, i))] * (n - 1),
+            out_specs=pl.BlockSpec((rows, tile), lambda i, at: (0, i)),
         ),
         out_shape=jax.ShapeDtypeStruct((rows, quarter), BF),
         compiler_params=PARAMS,
@@ -170,28 +165,35 @@
 
     cut = split_down(s.reshape(1), w_down, sections)
     downs = [send(c, d + 1) for d, c in enumerate(cut)]
-    outgoing, spread = make_slots(
-        s.reshape(1), tokens, routing, gate_weights, cap, experts, (quarter,)
+    share = quarter - quarter // 8
+    outgoing, straight, spread = make_slots(
+        s.reshape(1), tokens, routing, gate_weights, cap, experts, share
     )
     received = exchange(tie(outgoing, *cut))
     rows = experts * cap
     half = rows // 2
 
+    def k_rows(block, start):
+        g = lax.dynamic_slice_in_dim(w_gate[0], start, block.shape[1], axis=0)
+        u = lax.dynamic_slice_in_dim(w_up[0], start, block.shape[1], axis=0)
+        return dot(block, g), dot(block, u)
+
     def k_part(halves, d):
-        block = jnp.concatenate(halves, axis=0)
-        start = lax.rem(s + d, sections) * quarter
-        g = lax.dynamic_slice_in_dim(w_gate[0], start, quarter, axis=0)
-        u = lax.dynamic_slice_in_dim(w_up[0], start, quarter, axis=0)
-        return dot(block, g), dot(block, u)
+        return k_rows(jnp.concatenate(halves, axis=0), lax.rem(s + d, sections) * share)
 
     a, b = received[:half], received[half:]
     r_a, l_b = to_right(a), to_left(b)
     gate, up = k_part((a, b), 0)
-    a_later, b_later, gate, up, *downs = lax.optimization_barrier((a, b, gate, up, *downs))
+    a_later, b_later, straight, gate, up, *downs = lax.optimization_barrier(
+        (a, b, straight, gate, up, *downs)
+    )
     r_b, l_a = to_right(b_later), to_left(a_later)
     across = (to_right(r_a), to_left(l_b))
-    for halves, d in (((r_a, r_b), 3), ((l_a, l_b), 1), (across, 2)):
-        g, u = k_part(halves, d)
+    straight = exchange(straight)
+    parts = [k_part(halves, d) for halves, d in (((r_a, r_b), 3), ((l_a, l_b), 1))]
+    parts.append(k_rows(straight, share * sections))
+    parts.append(k_part(across, 2))
+    for g, u in parts:
         gate, up = gate + g, up + u
     hidden = (jax.nn.silu(gate) * up).astype(BF)
     hiddens = [hidden] + [send(hidden, d + 1) for d in range(len(downs))]

time: 163 us -> 170 us (1.043)
  waiting for transfers between devices: 62.8 us -> 48.3 us
  starting transfers between devices: 29.7 us -> 40.1 us
  matrix products: 11.9 us -> 22 us
  blocking collectives: 38.6 us -> 40.5 us
    ppermute x12, waiting for transfers between devices: 39.8 us -> 27.9 us  [send(): lax.ppermute(v, 'section', [(k, (k + d) % sections) for k in range(sectio...]
    all_to_all x1 -> x2, starting transfers between devices: 13.3 us -> 24 us  [exchange(): lax.all_to_all(v.reshape(experts, cap, w), ED, split_axis=0, concat_axis=...]
    dot_general x9 -> x11, matrix products: 11.9 us -> 22 us  [dot(): return jnp.dot(a, b, preferred_element_type=F32)]
    all_to_all x1 -> x2, waiting for transfers between devices: 23 us -> 20.4 us  [exchange(): lax.all_to_all(v.reshape(experts, cap, w), ED, split_axis=0, concat_axis=...]
    all_to_all x1, blocking collectives: 38.6 us -> 40.5 us  [exchange(): lax.all_to_all(v.reshape(experts, cap, w), ED, split_axis=0, concat_axis=...]
  transfers between devices with their start and end apart: 13 -> 14, of which waited for: 7 -> 8; matrix products, arithmetic and copies ran while one was open for 10% -> 11% of each run, Pallas kernels for 0% -> 0%
where the time goes in v6:
time: 170 us; the launch traced here: 169 us
  waiting for transfers between devices  48.3 us (28%)
  blocking collectives  40.5 us (24%)
  starting transfers between devices  40.1 us (24%)
  matrix products  22 us (13%)
  Pallas kernels  11.8 us (7%)
  local copies, waits for them, and re-layouts  5.12 us (3%)
    all_to_all x1, blocking collectives, exchange(): lax.all_to_all(v.reshape(experts, cap, w), ED, split_axis=0, concat_axis=...  40.5 us
    ppermute x12, waiting for transfers between devices, send(): lax.ppermute(v, 'section', [(k, (k + d) % sections) for k in range(sectio...  27.9 us
    all_to_all x2, starting transfers between devices, exchange(): lax.all_to_all(v.reshape(experts, cap, w), ED, split_axis=0, concat_axis=...  24 us
    dot_general x11, matrix products, dot(): return jnp.dot(a, b, preferred_element_type=F32)  22 us
    all_to_all x2, waiting for transfers between devices, exchange(): lax.all_to_all(v.reshape(experts, cap, w), ED, split_axis=0, concat_axis=...  20.4 us
    ppermute x12, starting transfers between devices, send(): lax.ppermute(v, 'section', [(k, (k + d) % sections) for k in range(sectio...  16.1 us
    pallas_call x1, Pallas kernels, project(): pl.pallas_call(kernel, grid_spec=pltpu.PrefetchScalarGridSpec(num_scalar_...  5.98 us
  transfers between devices with their start and end apart: 14, of which 8 were waited for; matrix products, arithmetic and copies ran while one was open for 11% of the time, Pallas kernels for 0%

profile of v6, /device:TPU:1, one launch (start us, length us, event | category | flops | bytes accessed | tf_op | source)
XLA Modules:
  0.0 168.7 jit_solution(13615258526978492500)
XLA Ops:
  0.0 3.1 %split_down.1 = (bf16[384,1024]{1,0:T(8,128)(2,1)}, bf16[384,1024]{1,0:T(8,128)(2,1)}, bf16[384,1024]{1,0:T(8,128)(2,1)}) custom-call(s32[1]{0:T(128)} %bitcast.s_ref, bf16[1,384,4096]{2,1,0:T(8,128)(2,1)} %refs_4_.1, bf16[1,384,4096]{2,1,0:T(8,128)(2,1)} %refs_4_.1, bf16[1,384,4096]{2,1,0:T(8,128)(2,1)} %refs_4_.1), custom_call_target="tpu_custom_call" | custom-call | bytes 4718592 | tf_op jit(solution)/shard_map/split_down/pallas_call | solution.py:96
  3.1 2.7 %slots.1 = (bf16[512,896]{1,0:T(8,128)(2,1)}, bf16[512,512]{1,0:T(8,128)(2,1)}, bf16[64,512]{1,0:T(8,128)(2,1)}) custom-call(s32[1]{0:T(128)} %bitcast.s_ref, s32[8,32]{1,0:T(8,128)} %bitcast.60, f32[8,32]{1,0:T(8,128)} %bitcast.61, bf16[32,4096]{1,0:T(8,128)(2,1)} %refs_1_.2, bf16[32,4096]{1,0:T(8,128)(2,1)} %refs_1_.2), custom_call_target="tpu_custom_call" | custom-call | flops 46137344 | bytes 1441792 | tf_op jit(solution)/shard_map/slots/pallas_call | solution.py:62
  5.8 13.2 %all-to-all-start = ((bf16[64,8,896]{2,1,0:T(8,128)(2,1)}), bf16[64,8,896]{2,1,0:T(8,128)(2,1)S(1)}, u32[]{:S(2)}, u32[]{:S(2)}) async-start(bf16[64,8,896]{2,1,0:T(8,128)(2,1)} %bitcast.58), calls=%async_computation | async-start | bytes 1835008 | tf_op jit(solution)/shard_map/all_to_all | solution.py:162
  20.3 2.5 %collective-permute-start.1 = (bf16[384,1024]{1,0:T(8,128)(2,1)}, bf16[384,1024]{1,0:T(8,128)(2,1)S(1)}, u32[]{:S(2)}, u32[]{:S(2)}) collective-permute-start(bf16[384,1024]{1,0:T(8,128)(2,1)} %get-tuple-element.23), channel_id=1, source_target_pairs={{0,128},{64,192},{128,0},{192,64},{1,129},{65,193},{129,1},{193,65... | collective-permute-start | bytes 2359304 | tf_op jit(solution)/shard_map/ppermute | solution.py:152
  23.9 20.4 %all-to-all-done = bf16[64,8,896]{2,1,0:T(8,128)(2,1)S(1)} async-done(((bf16[64,8,896]{2,1,0:T(8,128)(2,1)}), bf16[64,8,896]{2,1,0:T(8,128)(2,1)S(1)}, u32[]{:S(2)}, u32[]{:S(2)}) %all-to-all-start) | async-done | bytes 917536 | tf_op jit(solution)/shard_map/all_to_all | solution.py:162
  48.0 2.9 %fusion.16 = f32[512,384]{1,0:T(8,128)} fusion(bf16[1,4096,384]{2,1,0:T(8,128)(2,1)} %param.9, s32[]{:T(128)S(6)} %select_n.16, bf16[256,896]{1,0:T(8,128)(2,1)} %get-tuple-element.28, bf16[256,896]{1,0:T(8,128)(2,1)} %get-tuple-element.29), kind=kOutput, calls=%fused_computation.18 | convolution fusion | flops 354156544 | bytes 2392068 | tf_op jit(solution)/shard_map/dot_general | solution.py:17
  50.9 2.9 %fusion.14 = f32[512,384]{1,0:T(8,128)} fusion(bf16[1,4096,384]{2,1,0:T(8,128)(2,1)} %param.10, s32[]{:T(128)S(6)} %select_n.16, bf16[256,896]{1,0:T(8,128)(2,1)} %get-tuple-element.28, bf16[256,896]{1,0:T(8,128)(2,1)} %get-tuple-element.29), kind=kOutput, calls=%fused_computation.16 | convolution fusion | flops 354156544 | bytes 2392068 | tf_op jit(solution)/shard_map/dot_general | solution.py:17
  53.9 3.2 %collective-permute-done.1.refs_6_ = bf16[384,1024]{1,0:T(8,128)(2,1)S(1)} collective-permute-done((bf16[384,1024]{1,0:T(8,128)(2,1)}, bf16[384,1024]{1,0:T(8,128)(2,1)S(1)}, u32[]{:S(2)}, u32[]{:S(2)}) %collective-permute-start.1) | collective-permute-done | bytes 786464 | tf_op jit(solution)/shard_map/ppermute | solution.py:152
  57.1 2.7 %collective-permute-start.5 = (bf16[256,896]{1,0:T(8,128)(2,1)}, bf16[256,896]{1,0:T(8,128)(2,1)}, u32[]{:S(2)}, u32[]{:S(2)}) collective-permute-start(bf16[256,896]{1,0:T(8,128)(2,1)} %get-tuple-element.29), channel_id=1, source_target_pairs={{0,192},{64,0},{128,64},{192,128},{1,193},{65,1},{129,65},{193,129... | collective-permute-start | bytes 1376264 | tf_op jit(solution)/shard_map/ppermute | solution.py:152
  59.8 10.8 %all-to-all-start.1 = ((bf16[64,8,512]{2,1,0:T(8,128)(2,1)}), bf16[64,8,512]{2,1,0:T(8,128)(2,1)S(1)}, u32[]{:S(2)}, u32[]{:S(2)}) async-start(bf16[64,8,512]{2,1,0:T(8,128)(2,1)} %bitcast.59), calls=%async_computation.1 | async-start | bytes 1048576 | tf_op jit(solution)/shard_map/all_to_all | solution.py:162
  71.9 1.7 %collective-permute-start.8 = (bf16[256,896]{1,0:T(8,128)(2,1)}, bf16[256,896]{1,0:T(8,128)(2,1)S(1)}, u32[]{:S(2)}, u32[]{:S(2)}) collective-permute-start(bf16[256,896]{1,0:T(8,128)(2,1)} %collective-permute-done.6), channel_id=1, source_target_pairs={{0,192},{64,0},{128,64},{192,128},{1,193},{65,1},{129,65},{193,129... | collective-permute-start | bytes 1376264 | tf_op jit(solution)/shard_map/ppermute | solution.py:152
  78.3 1.8 %fusion.10 = f32[512,384]{1,0:T(8,128)S(1)} fusion(bf16[512,896]{1,0:T(8,128)(2,1)S(1)} %constant_dynamic-update-slice_fusion.2, bf16[1,4096,384]{2,1,0:T(8,128)(2,1)} %param.9, s32[]{:T(128)S(6)} %select_n.18), kind=kOutput, calls=%fused_computation.12 | convolution fusion | flops 352321536 | bytes 2392068 | tf_op jit(solution)/shard_map/dot_general | solution.py:17
  80.1 3.7 %collective-permute-done.4 = bf16[256,896]{1,0:T(8,128)(2,1)S(1)} collective-permute-done((bf16[256,896]{1,0:T(8,128)(2,1)}, bf16[256,896]{1,0:T(8,128)(2,1)S(1)}, u32[]{:S(2)}, u32[]{:S(2)}) %collective-permute-start.4) | collective-permute-done | bytes 458784 | tf_op jit(solution)/shard_map/ppermute | solution.py:152
  83.8 2.7 %fusion.5 = f32[512,384]{1,0:T(8,128)} fusion(bf16[512,896]{1,0:T(8,128)(2,1)S(1)} %constant_dynamic-update-slice_fusion.2, bf16[1,4096,384]{2,1,0:T(8,128)(2,1)} %param.10, s32[]{:T(128)S(6)} %select_n.18), kind=kOutput, calls=%fused_computation.7 | convolution fusion | flops 352321536 | bytes 2392068 | tf_op jit(solution)/shard_map/dot_general | solution.py:17
  86.4 1.8 %fusion.12 = f32[512,384]{1,0:T(8,128)S(1)} fusion(bf16[512,896]{1,0:T(8,128)(2,1)S(1)} %constant_dynamic-update-slice_fusion, bf16[1,4096,384]{2,1,0:T(8,128)(2,1)} %param.9, s32[]{:T(128)S(6)} %select_n.17), kind=kOutput, calls=%fused_computation.14 | convolution fusion | flops 352321536 | bytes 2392068 | tf_op jit(solution)/shard_map/dot_general | solution.py:17
  88.2 2.7 %fusion.7 = f32[512,384]{1,0:T(8,128)} fusion(bf16[512,896]{1,0:T(8,128)(2,1)S(1)} %constant_dynamic-update-slice_fusion, bf16[1,4096,384]{2,1,0:T(8,128)(2,1)} %param.10, s32[]{:T(128)S(6)} %select_n.17), kind=kOutput, calls=%fused_computation.9 | convolution fusion | flops 352321536 | bytes 2392068 | tf_op jit(solution)/shard_map/dot_general | solution.py:17
  90.9 2.7 %collective-permute-done.7 = bf16[256,896]{1,0:T(8,128)(2,1)S(1)} collective-permute-done((bf16[256,896]{1,0:T(8,128)(2,1)}, bf16[256,896]{1,0:T(8,128)(2,1)S(1)}, u32[]{:S(2)}, u32[]{:S(2)}) %collective-permute-start.7) | collective-permute-done | bytes 458784 | tf_op jit(solution)/shard_map/ppermute | solution.py:152
  95.1 2.2 %convolution_add_fusion.1 = f32[512,384]{1,0:T(8,128)S(1)} fusion(bf16[512,896]{1,0:T(8,128)(2,1)S(1)} %constant_dynamic-update-slice_fusion.4, f32[512,384]{1,0:T(8,128)S(1)} %fusion.28, f32[512,384]{1,0:T(8,128)S(1)} %fusion.10, f32[512,384]{1,0:T(8,128)} %fusion.16, f32[512,384]{1,0:T(8,128)S(1)} %fusion.12, bf16[1,4096,384]{2,1,0:T(8,128)(2,1)} %param.9, ...), kind=kOutput, calls=%fused_computation.1 | convolution fusion | flops 353107968 | bytes 5537796 | tf_op jit(solution)/shard_map/dot_general | solution.py:17
  98.8 1.9 %multiply_convert_fusion.refs_0_ = bf16[512,384]{1,0:T(8,128)(2,1)S(1)} fusion(f32[512,384]{1,0:T(8,128)S(1)} %convolution_add_fusion.1, bf16[512,896]{1,0:T(8,128)(2,1)S(1)} %constant_dynamic-update-slice_fusion.4, f32[512,384]{1,0:T(8,128)S(1)} %fusion.26, f32[512,384]{1,0:T(8,128)S(1)} %copy-done.3, f32[512,384]{1,0:T(8,128)S(1)} %copy-done.10, ...), kind=kOutput, calls=%fused_computation.5 | convolution fusion | flops 354287616 | bytes 5931012 | tf_op jit(solution)/shard_map/dot_general | solution.py:17
  100.9 1.6 collective-permute-start.10
  103.6 8.8 %collective-permute-done.9.refs_1_ = bf16[512,384]{1,0:T(8,128)(2,1)S(1)} collective-permute-done((bf16[512,384]{1,0:T(8,128)(2,1)S(1)}, bf16[512,384]{1,0:T(8,128)(2,1)S(1)}, u32[]{:S(2)}, u32[]{:S(2)}) %collective-permute-start.9) | collective-permute-done | bytes 393248 | tf_op jit(solution)/shard_map/ppermute | solution.py:152
  112.4 6.5 %collective-permute-done.10.refs_2_ = bf16[512,384]{1,0:T(8,128)(2,1)S(1)} collective-permute-done((bf16[512,384]{1,0:T(8,128)(2,1)S(1)}, bf16[512,384]{1,0:T(8,128)(2,1)S(1)}, u32[]{:S(2)}, u32[]{:S(2)}) %collective-permute-start.10) | collective-permute-done | bytes 393248 | tf_op jit(solution)/shard_map/ppermute | solution.py:152
  121.2 6.0 %down.1 = bf16[512,1024]{1,0:T(8,128)(2,1)} custom-call(s32[1]{0:T(128)} %bitcast.s_ref, bf16[512,384]{1,0:T(8,128)(2,1)} %copy-done.5, bf16[512,384]{1,0:T(8,128)(2,1)} %copy-done.6, bf16[512,384]{1,0:T(8,128)(2,1)} %copy-done.7, bf16[512,384]{1,0:T(8,128)(2,1)} %copy-done.8, bf16[1,384,4096]{2,1,0:T(8,128)(2,1)} %refs_4_.1, bf16[384,1024]{1,0:T(8,128)(2,1)} %copy-done, ...), custom_call_target="tpu_custom_call" | custom-call | flops 1610612736 | bytes 4718592 | tf_op jit(solution)/shard_map/down/pallas_call | solution.py:125
  127.2 40.5 %all_to_all.15 = bf16[64,8,1024]{2,1,0:T(8,128)(2,1)S(1)} all-to-all(bf16[64,8,1024]{2,1,0:T(8,128)(2,1)} %bitcast.57), channel_id=1, replica_groups=mesh['section'=4,'expert'=32,'dp'=2] {'expert','dp'}, dimensions={0} | all-to-all | bytes 2097152 | tf_op jit(solution)/shard_map/all_to_all | solution.py:162
  (49 shorter events, 19.6 us)
Async XLA Ops:
  5.8 38.5 %all-to-all-start = ((bf16[64,8,896]{2,1,0:T(8,128)(2,1)}), bf16[64,8,896]{2,1,0:T(8,128)(2,1)S(1)}, u32[]{:S(2)}, u32[]{:S(2)}) async-start(bf16[64,8,896]{2,1,0:T(8,128)(2,1)} %bitcast.58), calls=%async_computation | async-start | bytes 1835008 | tf_op jit(solution)/shard_map/all_to_all | solution.py:162
  19.0 34.9 %collective-permute-start = (bf16[384,1024]{1,0:T(8,128)(2,1)}, bf16[384,1024]{1,0:T(8,128)(2,1)S(1)}, u32[]{:S(2)}, u32[]{:S(2)}) collective-permute-start(bf16[384,1024]{1,0:T(8,128)(2,1)} %get-tuple-element.22), channel_id=1, source_target_pairs={{0,64},{64,128},{128,192},{192,0},{1,65},{65,129},{129,193},{193,1... | collective-permute-start | bytes 2359304 | tf_op jit(solution)/shard_map/ppermute | solution.py:152
  20.3 36.8 %collective-permute-start.1 = (bf16[384,1024]{1,0:T(8,128)(2,1)}, bf16[384,1024]{1,0:T(8,128)(2,1)S(1)}, u32[]{:S(2)}, u32[]{:S(2)}) collective-permute-start(bf16[384,1024]{1,0:T(8,128)(2,1)} %get-tuple-element.23), channel_id=1, source_target_pairs={{0,128},{64,192},{128,0},{192,64},{1,129},{65,193},{129,1},{193,65... | collective-permute-start | bytes 2359304 | tf_op jit(solution)/shard_map/ppermute | solution.py:152
  22.7 34.3 %collective-permute-start.2 = (bf16[384,1024]{1,0:T(8,128)(2,1)}, bf16[384,1024]{1,0:T(8,128)(2,1)S(1)}, u32[]{:S(2)}, u32[]{:S(2)}) collective-permute-start(bf16[384,1024]{1,0:T(8,128)(2,1)} %get-tuple-element.24), channel_id=1, source_target_pairs={{0,192},{64,0},{128,64},{192,128},{1,193},{65,1},{129,65},{193,129... | collective-permute-start | bytes 2359304 | tf_op jit(solution)/shard_map/ppermute | solution.py:152
  45.3 25.7 %collective-permute-start.3 = (bf16[256,896]{1,0:T(8,128)(2,1)}, bf16[256,896]{1,0:T(8,128)(2,1)}, u32[]{:S(2)}, u32[]{:S(2)}) collective-permute-start(bf16[256,896]{1,0:T(8,128)(2,1)} %get-tuple-element.29), channel_id=1, source_target_pairs={{0,64},{64,128},{128,192},{192,0},{1,65},{65,129},{129,193},{193,1... | collective-permute-start | bytes 1376264 | tf_op jit(solution)/shard_map/ppermute | solution.py:152
  46.5 25.4 %collective-permute-start.6 = (bf16[256,896]{1,0:T(8,128)(2,1)}, bf16[256,896]{1,0:T(8,128)(2,1)}, u32[]{:S(2)}, u32[]{:S(2)}) collective-permute-start(bf16[256,896]{1,0:T(8,128)(2,1)} %get-tuple-element.28), channel_id=1, source_target_pairs={{0,192},{64,0},{128,64},{192,128},{1,193},{65,1},{129,65},{193,129... | collective-permute-start | bytes 1376264 | tf_op jit(solution)/shard_map/ppermute | solution.py:152
  53.9 23.4 %copy-start = (bf16[384,1024]{1,0:T(8,128)(2,1)}, bf16[384,1024]{1,0:T(8,128)(2,1)S(1)}, u32[]{:S(2)}) copy-start(bf16[384,1024]{1,0:T(8,128)(2,1)S(1)} %collective-permute-done.refs_5_) | copy-start | bytes 2359300
  57.0 26.7 %copy-start.1 = (bf16[384,1024]{1,0:T(8,128)(2,1)}, bf16[384,1024]{1,0:T(8,128)(2,1)S(1)}, u32[]{:S(2)}) copy-start(bf16[384,1024]{1,0:T(8,128)(2,1)S(1)} %collective-permute-done.1.refs_6_) | copy-start | bytes 2359300
  57.1 26.7 %copy-start.2 = (bf16[384,1024]{1,0:T(8,128)(2,1)}, bf16[384,1024]{1,0:T(8,128)(2,1)S(1)}, u32[]{:S(2)}) copy-start(bf16[384,1024]{1,0:T(8,128)(2,1)S(1)} %collective-permute-done.2.refs_7_) | copy-start | bytes 2359300
  57.1 19.1 %collective-permute-start.5 = (bf16[256,896]{1,0:T(8,128)(2,1)}, bf16[256,896]{1,0:T(8,128)(2,1)}, u32[]{:S(2)}, u32[]{:S(2)}) collective-permute-start(bf16[256,896]{1,0:T(8,128)(2,1)} %get-tuple-element.29), channel_id=1, source_target_pairs={{0,192},{64,0},{128,64},{192,128},{1,193},{65,1},{129,65},{193,129... | collective-permute-start | bytes 1376264 | tf_op jit(solution)/shard_map/ppermute | solution.py:152
  59.8 33.9 %all-to-all-start.1 = ((bf16[64,8,512]{2,1,0:T(8,128)(2,1)}), bf16[64,8,512]{2,1,0:T(8,128)(2,1)S(1)}, u32[]{:S(2)}, u32[]{:S(2)}) async-start(bf16[64,8,512]{2,1,0:T(8,128)(2,1)} %bitcast.59), calls=%async_computation.1 | async-start | bytes 1048576 | tf_op jit(solution)/shard_map/all_to_all | solution.py:162
  70.6 13.1 %collective-permute-start.4 = (bf16[256,896]{1,0:T(8,128)(2,1)}, bf16[256,896]{1,0:T(8,128)(2,1)S(1)}, u32[]{:S(2)}, u32[]{:S(2)}) collective-permute-start(bf16[256,896]{1,0:T(8,128)(2,1)} %get-tuple-element.28), channel_id=1, source_target_pairs={{0,64},{64,128},{128,192},{192,0},{1,65},{65,129},{129,193},{193,1... | collective-permute-start | bytes 1376264 | tf_op jit(solution)/shard_map/ppermute | solution.py:152
  71.0 22.6 %collective-permute-start.7 = (bf16[256,896]{1,0:T(8,128)(2,1)}, bf16[256,896]{1,0:T(8,128)(2,1)S(1)}, u32[]{:S(2)}, u32[]{:S(2)}) collective-permute-start(bf16[256,896]{1,0:T(8,128)(2,1)} %collective-permute-done.3), channel_id=1, source_target_pairs={{0,64},{64,128},{128,192},{192,0},{1,65},{65,129},{129,193},{193,1... | collective-permute-start | bytes 1376264 | tf_op jit(solution)/shard_map/ppermute | solution.py:152
  71.9 21.6 %collective-permute-start.8 = (bf16[256,896]{1,0:T(8,128)(2,1)}, bf16[256,896]{1,0:T(8,128)(2,1)S(1)}, u32[]{:S(2)}, u32[]{:S(2)}) collective-permute-start(bf16[256,896]{1,0:T(8,128)(2,1)} %collective-permute-done.6), channel_id=1, source_target_pairs={{0,192},{64,0},{128,64},{192,128},{1,193},{65,1},{129,65},{193,129... | collective-permute-start | bytes 1376264 | tf_op jit(solution)/shard_map/ppermute | solution.py:152
  95.1 3.7 %copy-start.3 = (f32[512,384]{1,0:T(8,128)S(1)}, f32[512,384]{1,0:T(8,128)}, u32[]{:S(2)}) copy-start(f32[512,384]{1,0:T(8,128)} %fusion.5) | copy-start | bytes 2359300
  95.1 3.7 %copy-start.4 = (f32[512,384]{1,0:T(8,128)S(1)}, f32[512,384]{1,0:T(8,128)}, u32[]{:S(2)}) copy-start(f32[512,384]{1,0:T(8,128)} %fusion.7) | copy-start | bytes 2359300
  95.1 3.7 %copy-start.10 = (f32[512,384]{1,0:T(8,128)S(1)}, f32[512,384]{1,0:T(8,128)}, u32[]{:S(2)}) copy-start(f32[512,384]{1,0:T(8,128)} %fusion.14) | copy-start | bytes 2359300
  100.8 19.7 %copy-start.5 = (bf16[512,384]{1,0:T(8,128)(2,1)}, bf16[512,384]{1,0:T(8,128)(2,1)S(1)}, u32[]{:S(2)}) copy-start(bf16[512,384]{1,0:T(8,128)(2,1)S(1)} %multiply_convert_fusion.refs_0_) | copy-start | bytes 1179652
  100.8 66.9 %copy-start.9 = (bf16[64,512]{1,0:T(8,128)(2,1)S(1)}, bf16[64,512]{1,0:T(8,128)(2,1)}, u32[]{:S(2)}) copy-start(bf16[64,512]{1,0:T(8,128)(2,1)} %get-tuple-element.20) | copy-start | bytes 196612
  100.8 11.6 %collective-permute-start.9 = (bf16[512,384]{1,0:T(8,128)(2,1)S(1)}, bf16[512,384]{1,0:T(8,128)(2,1)S(1)}, u32[]{:S(2)}, u32[]{:S(2)}) collective-permute-start(bf16[512,384]{1,0:T(8,128)(2,1)S(1)} %multiply_convert_fusion.refs_0_), channel_id=1, source_target_pairs={{0,64},{64,128},{128,192},{192,0},{1,65},{65,129},{129,193},{193,1... | collective-permute-start | bytes 1179656 | tf_op jit(solution)/shard_map/ppermute | solution.py:152
  100.9 17.9 %collective-permute-start.10 = (bf16[512,384]{1,0:T(8,128)(2,1)S(1)}, bf16[512,384]{1,0:T(8,128)(2,1)S(1)}, u32[]{:S(2)}, u32[]{:S(2)}) collective-permute-start(bf16[512,384]{1,0:T(8,128)(2,1)S(1)} %multiply_convert_fusion.refs_0_), channel_id=1, source_target_pairs={{0,128},{64,192},{128,0},{192,64},{1,129},{65,193},{129,1},{193,65... | collective-permute-start | bytes 1179656 | tf_op jit(solution)/shard_map/ppermute | solution.py:152
  102.5 17.9 %collective-permute-start.11 = (bf16[512,384]{1,0:T(8,128)(2,1)S(1)}, bf16[512,384]{1,0:T(8,128)(2,1)S(1)}, u32[]{:S(2)}, u32[]{:S(2)}) collective-permute-start(bf16[512,384]{1,0:T(8,128)(2,1)S(1)} %multiply_convert_fusion.refs_0_), channel_id=1, source_target_pairs={{0,192},{64,0},{128,64},{192,128},{1,193},{65,1},{129,65},{193,129... | collective-permute-start | bytes 1179656 | tf_op jit(solution)/shard_map/ppermute | solution.py:152
  112.4 8.1 %copy-start.6 = (bf16[512,384]{1,0:T(8,128)(2,1)}, bf16[512,384]{1,0:T(8,128)(2,1)S(1)}, u32[]{:S(2)}) copy-start(bf16[512,384]{1,0:T(8,128)(2,1)S(1)} %collective-permute-done.9.refs_1_) | copy-start | bytes 1179652
  118.8 1.6 copy-start.7
  (1 other events, 0.8 us)

commit v7 on v6

--- a/solution.py
+++ b/solution.py
@@ -81,31 +81,89 @@
     )(section, routing.T, gate_weights.T, tokens, tokens)
 
 
-def split_down(section, w_down, sections):
+def split_down(section, w_down, pieces, sections):
     _, hid, width = w_down.shape
     quarter = width // sections
-    count = sections - 1
+    count = len(pieces)
 
     def kernel(s_ref, *refs):
         for src, out in zip(refs[:count], refs[count:]):
             out[...] = src[0]
 
-    def columns(d):
-        return pl.BlockSpec((1, hid, quarter), lambda i, at: (0, 0, lax.rem(at[0] + d, sections)))
+    def columns(d, part, parts):
+        return pl.BlockSpec(
+            (1, hid // parts, quarter), lambda i, at: (0, part, lax.rem(at[0] + d, sections))
+        )
 
     return pl.pallas_call(
         kernel,
         grid_spec=pltpu.PrefetchScalarGridSpec(
             num_scalar_prefetch=1,
             grid=(1,),
-            in_specs=[columns(d + 1) for d in range(count)],
-            out_specs=[pl.BlockSpec((hid, quarter), lambda i, at: (0, 0))] * count,
-        ),
-        out_shape=[jax.ShapeDtypeStruct((hid, quarter), BF)] * count,
-        compiler_params=PARAMS,
-        cost_estimate=cost(0, 4 * count * hid * quarter),
+            in_specs=[columns(*p) for p in pieces],
+            out_specs=[
+                pl.BlockSpec((hid // parts, quarter), lambda i, at: (0, 0)) for _, _, parts in pieces
+            ],
+        ),
+        out_shape=[jax.ShapeDtypeStruct((hid // parts, quarter), BF) for _, _, parts in pieces],
+        compiler_params=PARAMS,
+        cost_estimate=cost(0, 4 * (sections - 1) * hid * quarter),
         name="split_down",
     )(section, *([w_down] * count))
+
+
+def gate_up(section, blocks, starts, w_gate, w_up, sections, total=None, last=False):
+    rows = sum(p.shape[0] for p in blocks[0])
+    hid = w_gate.shape[2]
+    n = len(blocks)
+    flat = [p for parts in blocks for p in parts]
+    counts = [len(parts) for parts in blocks]
+    widths = [parts[0].shape[1] for parts in blocks]
+
+    def kernel(s_ref, *refs):
+        refs = list(refs)
+        xs = [[refs.pop(0) for _ in range(c)] for c in counts]
+        gs = [refs.pop(0) for _ in range(n)]
+        us = [refs.pop(0) for _ in range(n)]
+        acc = refs.pop(0)[...] if total is not None else None
+        for x, g, u in zip(xs, gs, us):
+            block = x[0][...] if len(x) == 1 else jnp.concatenate([p[...] for p in x], axis=0)
+            term = dot(block, jnp.concatenate([g[0], u[0]], axis=1))
+            acc = term if acc is None else acc + term
+        if not last:
+            refs[0][...] = acc
+            return
+        gate, up = acc[:, :hid], acc[:, hid:]
+        refs[0][...] = (gate / (1.0 + jnp.exp(-gate)) * up).astype(BF)
+
+    def weights(start, width):
+        if isinstance(start, tuple):
+            return pl.BlockSpec(
+                (1, width, hid), lambda i, at: (0, lax.rem(at[0] + start[0], sections), 0)
+            )
+        return pl.BlockSpec((1, width, hid), lambda i, at: (0, start, 0))
+
+    def whole(v):
+        return pl.BlockSpec(v.shape, lambda i, at: (0, 0))
+
+    w_specs = [weights(st, w) for st, w in zip(starts, widths)]
+    extra = [] if total is None else [total]
+    shape = jax.ShapeDtypeStruct((rows, hid), BF) if last else jax.ShapeDtypeStruct((rows, 2 * hid), F32)
+    return pl.pallas_call(
+        kernel,
+        grid_spec=pltpu.PrefetchScalarGridSpec(
+            num_scalar_prefetch=1,
+            grid=(1,),
+            in_specs=[whole(v) for v in flat] + w_specs + w_specs + [whole(v) for v in extra],
+            out_specs=whole(shape),
+        ),
+        out_shape=shape,
+        compiler_params=PARAMS,
+        cost_estimate=cost(
+            4 * rows * hid * sum(widths), 2 * sum(widths) * (rows + 2 * hid) + 8 * rows * hid
+        ),
+        name="gate_up",
+    )(section, *flat, *([w_gate] * n), *([w_up] * n), *extra)
 
 
 def project(section, hiddens, downs, w_down, sections):
@@ -116,11 +174,10 @@
     tiles = quarter // tile
 
     def kernel(s_ref, *refs):
-        hs, ws, out = refs[:n], refs[n : 2 * n], refs[2 * n]
-        total = dot(hs[0][...], ws[0][0])
-        for h, w in zip(hs[1:], ws[1:]):
-            total = total + dot(h[...], w[...])
-        out[...] = total.astype(BF)
+        hs, ws, out = refs[:n], refs[n:-1], refs[-1]
+        hidden = jnp.concatenate([h[...] for h in hs], axis=1)
+        columns = jnp.concatenate([ws[0][0]] + [w[...] for w in ws[1:]], axis=0)
+        out[...] = dot(hidden, columns).astype(BF)
 
     return pl.pallas_call(
         kernel,
@@ -129,7 +186,7 @@
             grid=(tiles,),
             in_specs=[pl.BlockSpec((rows, hid), lambda i, at: (0, 0))] * n
             + [pl.BlockSpec((1, hid, tile), lambda i, at: (0, 0, at[0] * tiles + i))]
-            + [pl.BlockSpec((hid, tile), lambda i, at: (0, i))] * (n - 1),
+            + [pl.BlockSpec((d.shape[0], tile), lambda i, at: (0, i)) for d in downs],
             out_specs=pl.BlockSpec((rows, tile), lambda i, at: (0, i)),
         ),
         out_shape=jax.ShapeDtypeStruct((rows, quarter), BF),
@@ -163,8 +220,10 @@
             v.reshape(experts, cap, w), ED, split_axis=0, concat_axis=0, tiled=True
         ).reshape(rows, w)
 
-    cut = split_down(s.reshape(1), w_down, sections)
-    downs = [send(c, d + 1) for d, c in enumerate(cut)]
+    pieces = [(1, 0, 1), (2, 0, 2), (2, 1, 2), (3, 0, 1)]
+    cut = split_down(s.reshape(1), w_down, pieces, sections)
+    downs = [send(c, p[0]) for c, p in zip(cut, pieces)]
+
     share = quarter - quarter // 8
     outgoing, straight, spread = make_slots(
         s.reshape(1), tokens, routing, gate_weights, cap, experts, share
@@ -173,30 +232,41 @@
     rows = experts * cap
     half = rows // 2
 
-    def k_rows(block, start):
-        g = lax.dynamic_slice_in_dim(w_gate[0], start, block.shape[1], axis=0)
-        u = lax.dynamic_slice_in_dim(w_up[0], start, block.shape[1], axis=0)
-        return dot(block, g), dot(block, u)
-
-    def k_part(halves, d):
-        return k_rows(jnp.concatenate(halves, axis=0), lax.rem(s + d, sections) * share)
-
-    a, b = received[:half], received[half:]
-    r_a, l_b = to_right(a), to_left(b)
-    gate, up = k_part((a, b), 0)
-    a_later, b_later, straight, gate, up, *downs = lax.optimization_barrier(
-        (a, b, straight, gate, up, *downs)
-    )
-    r_b, l_a = to_right(b_later), to_left(a_later)
-    across = (to_right(r_a), to_left(l_b))
+    straight, received, downs[0], downs[1], downs[3] = lax.optimization_barrier(
+        (straight, received, downs[0], downs[1], downs[3])
+    )
+    from_left, from_right = to_right(received), to_left(received)
     straight = exchange(straight)
-    parts = [k_part(halves, d) for halves, d in (((r_a, r_b), 3), ((l_a, l_b), 1))]
-    parts.append(k_rows(straight, share * sections))
-    parts.append(k_part(across, 2))
-    for g, u in parts:
-        gate, up = gate + g, up + u
-    hidden = (jax.nn.silu(gate) * up).astype(BF)
-    hiddens = [hidden] + [send(hidden, d + 1) for d in range(len(downs))]
+    at = s.reshape(1)
+    total = gate_up(at, [(received,)], [(0,)], w_gate, w_up, sections)
+    from_left, from_right, total, *downs = lax.optimization_barrier(
+        (from_left, from_right, total, *downs)
+    )
+    pass_r, pass_l = from_left[:half], from_right[half:]
+    across = (to_right(pass_r), to_left(pass_l))
+    from_left, from_right, pass_r, pass_l = lax.optimization_barrier(
+        (from_left, from_right, pass_r, pass_l)
+    )
+    total = gate_up(
+        at,
+        [(from_left,), (from_right,)],
+        [(sections - 1,), (1,)],
+        w_gate,
+        w_up,
+        sections,
+        total,
+    )
+    hidden = gate_up(
+        at,
+        [(straight,), across],
+        [width // straight.shape[1] - 1, (2,)],
+        w_gate,
+        w_up,
+        sections,
+        total,
+        last=True,
+    )
+    hiddens = [hidden] + [send(hidden, d) for d in range(1, sections)]
     returned = exchange(project(s.reshape(1), hiddens, downs, w_down, sections))
     both = dot(spread, returned)
     return (both[:toks] + both[toks:]).astype(BF)

time: 170 us -> 165 us (0.971)
  matrix products: 22 us -> 0.3 us
  Pallas kernels: 11.8 us -> 25.6 us
  waiting for transfers between devices: 48.3 us -> 61.7 us
  starting transfers between devices: 40.1 us -> 35.2 us
  local copies, waits for them, and re-layouts: 5.12 us -> 2.56 us
  blocking collectives: 40.5 us -> 38.8 us
    ppermute x12 -> x11, waiting for transfers between devices: 27.9 us -> 61.7 us  [send(): lax.ppermute(v, 'section', [(k, (k + d) % sections) for k in range(sectio...]
    dot_general x11 -> x1, matrix products: 22 us -> 0.3 us  [dot(): return jnp.dot(a, b, preferred_element_type=F32)]
    all_to_all x2, waiting for transfers between devices: 20.4 us -> 0.01 us  [exchange(): lax.all_to_all(v.reshape(experts, cap, w), ED, split_axis=0, concat_axis=...]
    pallas_call x0 -> x3, Pallas kernels: none -> 14.2 us  [gate_up(): pl.pallas_call(kernel, grid_spec=pltpu.PrefetchScalarGridSpec(num_scalar_...]
    ppermute x12 -> x11, starting transfers between devices: 16.1 us -> 10.3 us  [send(): lax.ppermute(v, 'section', [(k, (k + d) % sections) for k in range(sectio...]
    all_to_all x1, blocking collectives: 40.5 us -> 38.8 us  [exchange(): lax.all_to_all(v.reshape(experts, cap, w), ED, split_axis=0, concat_axis=...]
  transfers between devices with their start and end apart: 14 -> 13, of which waited for: 8 -> 7; matrix products, arithmetic and copies ran while one was open for 11% -> 0% of each run, Pallas kernels for 0% -> 6%
where the time goes in v7:
time: 165 us
  waiting for transfers between devices  61.7 us (37%)
  blocking collectives  38.8 us (24%)
  starting transfers between devices  35.2 us (21%)
  Pallas kernels  25.6 us (16%)
  local copies, waits for them, and re-layouts  2.56 us (2%)
    ppermute x11, waiting for transfers between devices, send(): lax.ppermute(v, 'section', [(k, (k + d) % sections) for k in range(sectio...  61.7 us
    all_to_all x1, blocking collectives, exchange(): lax.all_to_all(v.reshape(experts, cap, w), ED, split_axis=0, concat_axis=...  38.8 us
    all_to_all x2, starting transfers between devices, exchange(): lax.all_to_all(v.reshape(experts, cap, w), ED, split_axis=0, concat_axis=...  24.9 us
    pallas_call x3, Pallas kernels, gate_up(): pl.pallas_call(kernel, grid_spec=pltpu.PrefetchScalarGridSpec(num_scalar_...  14.2 us
    ppermute x11, starting transfers between devices, send(): lax.ppermute(v, 'section', [(k, (k + d) % sections) for k in range(sectio...  10.3 us
    pallas_call x1, Pallas kernels, project(): pl.pallas_call(kernel, grid_spec=pltpu.PrefetchScalarGridSpec(num_scalar_...  5.65 us
  transfers between devices with their start and end apart: 13, of which 7 were waited for; matrix products, arithmetic and copies ran while one was open for 0% of the time, Pallas kernels for 6%

profile of v7, /device:TPU:1, one launch (start us, length us, event | category | flops | bytes accessed | tf_op | source)
XLA Modules:
  0.0 165.0 jit_solution(6658969633420130368)
XLA Ops:
  0.0 3.1 %split_down.1 = (bf16[384,1024]{1,0:T(8,128)(2,1)}, bf16[192,1024]{1,0:T(8,128)(2,1)}, bf16[192,1024]{1,0:T(8,128)(2,1)}, bf16[384,1024]{1,0:T(8,128)(2,1)}) custom-call(s32[1]{0:T(128)} %bitcast.s_ref, bf16[1,384,4096]{2,1,0:T(8,128)(2,1)} %refs_4_.5, bf16[1,384,4096]{2,1,0:T(8,128)(2,1)} %refs_4_.5, bf16[1,384,4096]{2,1,0:T(8,128)(2,1)} %refs_4_.5, ...), custom_call_target="tpu_custom_call" | custom-call | bytes 4718592 | tf_op jit(solution)/shard_map/split_down/pallas_call | solution.py:98
  3.1 2.7 %slots.1 = (bf16[512,896]{1,0:T(8,128)(2,1)}, bf16[512,512]{1,0:T(8,128)(2,1)}, bf16[64,512]{1,0:T(8,128)(2,1)}) custom-call(s32[1]{0:T(128)} %bitcast.s_ref, s32[8,32]{1,0:T(8,128)} %bitcast.19, f32[8,32]{1,0:T(8,128)} %bitcast.20, bf16[32,4096]{1,0:T(8,128)(2,1)} %refs_1_.3, bf16[32,4096]{1,0:T(8,128)(2,1)} %refs_1_.3), custom_call_target="tpu_custom_call" | custom-call | flops 46137344 | bytes 1441792 | tf_op jit(solution)/shard_map/slots/pallas_call | solution.py:62
  5.8 13.2 %all-to-all-start = ((bf16[64,8,896]{2,1,0:T(8,128)(2,1)}), bf16[64,8,896]{2,1,0:T(8,128)(2,1)S(1)}, u32[]{:S(2)}, u32[]{:S(2)}) async-start(bf16[64,8,896]{2,1,0:T(8,128)(2,1)} %bitcast.17), calls=%async_computation | async-start | bytes 1835008 | tf_op jit(solution)/shard_map/all_to_all | solution.py:219
  19.0 1.3 collective-permute-start
  20.3 1.5 collective-permute-start.2
  21.7 1.5 collective-permute-start.1
  23.3 25.3 %collective-permute-done.1.refs_6_ = bf16[192,1024]{1,0:T(8,128)(2,1)S(1)} collective-permute-done((bf16[192,1024]{1,0:T(8,128)(2,1)}, bf16[192,1024]{1,0:T(8,128)(2,1)S(1)}, u32[]{:S(2)}, u32[]{:S(2)}) %collective-permute-start.1) | collective-permute-done | bytes 393248 | tf_op jit(solution)/shard_map/ppermute | solution.py:209
  49.3 0.9 copy-done.4
  50.2 1.2 collective-permute-start.4
  51.8 11.8 %all-to-all-start.1 = ((bf16[64,8,512]{2,1,0:T(8,128)(2,1)}), bf16[64,8,512]{2,1,0:T(8,128)(2,1)S(1)}, u32[]{:S(2)}, u32[]{:S(2)}) async-start(bf16[64,8,512]{2,1,0:T(8,128)(2,1)} %bitcast.18), calls=%async_computation.1 | async-start | bytes 1048576 | tf_op jit(solution)/shard_map/all_to_all | solution.py:219
  63.6 1.1 collective-permute-start.5
  64.7 3.7 %gate_up.3.refs_6_ = f32[512,768]{1,0:T(8,128)} custom-call(s32[1]{0:T(128)} %bitcast.s_ref, bf16[512,896]{1,0:T(8,128)(2,1)} %bitcast.15, bf16[1,4096,384]{2,1,0:T(8,128)(2,1)} %refs_4_.4, bf16[1,4096,384]{2,1,0:T(8,128)(2,1)} %refs_6_.1), custom_call_target="tpu_custom_call" | custom-call | flops 704643072 | bytes 3866624 | tf_op jit(solution)/shard_map/gate_up/pallas_call | solution.py:152
  68.5 11.4 %collective-permute-done.5.refs_7_ = bf16[192,1024]{1,0:T(8,128)(2,1)S(1)} collective-permute-done((bf16[192,1024]{1,0:T(8,128)(2,1)}, bf16[192,1024]{1,0:T(8,128)(2,1)S(1)}, u32[]{:S(2)}, u32[]{:S(2)}) %collective-permute-start.5) | collective-permute-done | bytes 393248 | tf_op jit(solution)/shard_map/ppermute | solution.py:209
  80.0 1.9 %collective-permute-start.7 = (bf16[256,896]{1,0:T(8,128)(2,1)S(1)}, bf16[256,896]{1,0:T(8,128)(2,1)}, u32[]{:S(2)}, u32[]{:S(2)}) collective-permute-start(bf16[256,896]{1,0:T(8,128)(2,1)S(1)} %slice.13), channel_id=1, source_target_pairs={{0,192},{64,0},{128,64},{192,128},{1,193},{65,1},{129,65},{193,129... | collective-permute-start | bytes 1376264 | tf_op jit(solution)/shard_map/ppermute | solution.py:209
  81.9 5.7 %gate_up.4.refs_7_ = f32[512,768]{1,0:T(8,128)} custom-call(s32[1]{0:T(128)} %bitcast.s_ref, bf16[512,896]{1,0:T(8,128)(2,1)} %copy-done.3, bf16[512,896]{1,0:T(8,128)(2,1)} %copy-done.2, bf16[1,4096,384]{2,1,0:T(8,128)(2,1)} %refs_4_.4, bf16[1,4096,384]{2,1,0:T(8,128)(2,1)} %refs_4_.4, bf16[1,4096,384]{2,1,0:T(8,128)(2,1)} %refs_6_.1, ...), custom_call_target="tpu_custom_call" | custom-call | flops 1409286144 | bytes 6160384 | tf_op jit(solution)/shard_map/gate_up/pallas_call | solution.py:152
  87.6 1.8 %collective-permute-done.7.refs_2_ = bf16[256,896]{1,0:T(8,128)(2,1)} collective-permute-done((bf16[256,896]{1,0:T(8,128)(2,1)S(1)}, bf16[256,896]{1,0:T(8,128)(2,1)}, u32[]{:S(2)}, u32[]{:S(2)}) %collective-permute-start.7) | collective-permute-done | bytes 458784 | tf_op jit(solution)/shard_map/ppermute | solution.py:209
  89.5 3.2 %collective-permute-done.6.refs_1_ = bf16[256,896]{1,0:T(8,128)(2,1)} collective-permute-done((bf16[256,896]{1,0:T(8,128)(2,1)S(1)}, bf16[256,896]{1,0:T(8,128)(2,1)}, u32[]{:S(2)}, u32[]{:S(2)}) %collective-permute-start.6) | collective-permute-done | bytes 458784 | tf_op jit(solution)/shard_map/ppermute | solution.py:209
  92.7 4.7 %gate_up.5.refs_0_ = bf16[512,384]{1,0:T(8,128)(2,1)} custom-call(s32[1]{0:T(128)} %bitcast.s_ref, bf16[512,512]{1,0:T(8,128)(2,1)} %bitcast.16, bf16[256,896]{1,0:T(8,128)(2,1)} %collective-permute-done.6.refs_1_, bf16[256,896]{1,0:T(8,128)(2,1)} %collective-permute-done.7.refs_2_, bf16[1,4096,384]{2,1,0:T(8,128)(2,1)} %refs_4_.4, ...), custom_call_target="tpu_custom_call" | custom-call | flops 1107296256 | bytes 5177344 | tf_op jit(solution)/shard_map/gate_up/pallas_call | solution.py:152
  97.7 1.2 collective-permute-start.8
  98.9 5.9 %collective-permute-done.10.refs_3_ = bf16[512,384]{1,0:T(8,128)(2,1)S(1)} collective-permute-done((bf16[512,384]{1,0:T(8,128)(2,1)}, bf16[512,384]{1,0:T(8,128)(2,1)S(1)}, u32[]{:S(2)}, u32[]{:S(2)}) %collective-permute-start.10) | collective-permute-done | bytes 393248 | tf_op jit(solution)/shard_map/ppermute | solution.py:209
  104.8 1.9 %collective-permute-done.9.refs_2_ = bf16[512,384]{1,0:T(8,128)(2,1)S(1)} collective-permute-done((bf16[512,384]{1,0:T(8,128)(2,1)}, bf16[512,384]{1,0:T(8,128)(2,1)S(1)}, u32[]{:S(2)}, u32[]{:S(2)}) %collective-permute-start.9) | collective-permute-done | bytes 393248 | tf_op jit(solution)/shard_map/ppermute | solution.py:209
  106.7 12.1 %collective-permute-done.8.refs_1_ = bf16[512,384]{1,0:T(8,128)(2,1)S(1)} collective-permute-done((bf16[512,384]{1,0:T(8,128)(2,1)}, bf16[512,384]{1,0:T(8,128)(2,1)S(1)}, u32[]{:S(2)}, u32[]{:S(2)}) %collective-permute-start.8) | collective-permute-done | bytes 393248 | tf_op jit(solution)/shard_map/ppermute | solution.py:209
  119.6 5.7 %down.1 = bf16[512,1024]{1,0:T(8,128)(2,1)} custom-call(s32[1]{0:T(128)} %bitcast.s_ref, bf16[512,384]{1,0:T(8,128)(2,1)} %gate_up.5.refs_0_, bf16[512,384]{1,0:T(8,128)(2,1)} %copy-done.9, bf16[512,384]{1,0:T(8,128)(2,1)} %copy-done.8, bf16[512,384]{1,0:T(8,128)(2,1)} %copy-done.7, bf16[1,384,4096]{2,1,0:T(8,128)(2,1)} %refs_4_.5, ...), custom_call_target="tpu_custom_call" | custom-call | flops 1610612736 | bytes 4718592 | tf_op jit(solution)/shard_map/down/pallas_call | solution.py:182
  125.2 38.8 %all_to_all.15 = bf16[64,8,1024]{2,1,0:T(8,128)(2,1)S(1)} all-to-all(bf16[64,8,1024]{2,1,0:T(8,128)(2,1)} %bitcast.12), channel_id=1, replica_groups=mesh['section'=4,'expert'=32,'dp'=2] {'expert','dp'}, dimensions={0} | all-to-all | bytes 2097152 | tf_op jit(solution)/shard_map/all_to_all | solution.py:219
  (35 shorter events, 3.3 us)
Async XLA Ops:
  5.8 44.4 %all-to-all-start = ((bf16[64,8,896]{2,1,0:T(8,128)(2,1)}), bf16[64,8,896]{2,1,0:T(8,128)(2,1)S(1)}, u32[]{:S(2)}, u32[]{:S(2)}) async-start(bf16[64,8,896]{2,1,0:T(8,128)(2,1)} %bitcast.17), calls=%async_computation | async-start | bytes 1835008 | tf_op jit(solution)/shard_map/all_to_all | solution.py:219
  19.0 29.6 %collective-permute-start = (bf16[384,1024]{1,0:T(8,128)(2,1)}, bf16[384,1024]{1,0:T(8,128)(2,1)S(1)}, u32[]{:S(2)}, u32[]{:S(2)}) collective-permute-start(bf16[384,1024]{1,0:T(8,128)(2,1)} %get-tuple-element.30), channel_id=1, source_target_pairs={{0,64},{64,128},{128,192},{192,0},{1,65},{65,129},{129,193},{193,1... | collective-permute-start | bytes 2359304 | tf_op jit(solution)/shard_map/ppermute | solution.py:209
  20.3 30.0 %collective-permute-start.2 = (bf16[384,1024]{1,0:T(8,128)(2,1)}, bf16[384,1024]{1,0:T(8,128)(2,1)}, u32[]{:S(2)}, u32[]{:S(2)}) collective-permute-start(bf16[384,1024]{1,0:T(8,128)(2,1)} %get-tuple-element.33), channel_id=1, source_target_pairs={{0,192},{64,0},{128,64},{192,128},{1,193},{65,1},{129,65},{193,129... | collective-permute-start | bytes 2359304 | tf_op jit(solution)/shard_map/ppermute | solution.py:209
  21.7 26.8 %collective-permute-start.1 = (bf16[192,1024]{1,0:T(8,128)(2,1)}, bf16[192,1024]{1,0:T(8,128)(2,1)S(1)}, u32[]{:S(2)}, u32[]{:S(2)}) collective-permute-start(bf16[192,1024]{1,0:T(8,128)(2,1)} %get-tuple-element.31), channel_id=1, source_target_pairs={{0,128},{64,192},{128,0},{192,64},{1,129},{65,193},{129,1},{193,65... | collective-permute-start | bytes 1179656 | tf_op jit(solution)/shard_map/ppermute | solution.py:209
  48.5 0.8 copy-start.5
  49.3 0.9 copy-start.4
  50.2 14.5 %copy-start = (bf16[64,8,896]{2,1,0:T(8,128)(2,1)}, bf16[64,8,896]{2,1,0:T(8,128)(2,1)S(1)}, u32[]{:S(2)}) copy-start(bf16[64,8,896]{2,1,0:T(8,128)(2,1)S(1)} %all-to-all-done) | copy-start | bytes 2752516
  50.2 29.7 %collective-permute-start.4 = (bf16[512,896]{1,0:T(8,128)(2,1)S(1)}, bf16[512,896]{1,0:T(8,128)(2,1)S(1)}, u32[]{:S(2)}, u32[]{:S(2)}) collective-permute-start(bf16[512,896]{1,0:T(8,128)(2,1)S(1)} %bitcast.13), channel_id=1, source_target_pairs={{0,192},{64,0},{128,64},{192,128},{1,193},{65,1},{129,65},{193,129... | collective-permute-start | bytes 2752520 | tf_op jit(solution)/shard_map/ppermute | solution.py:209
  51.4 28.5 %collective-permute-start.3 = (bf16[512,896]{1,0:T(8,128)(2,1)S(1)}, bf16[512,896]{1,0:T(8,128)(2,1)S(1)}, u32[]{:S(2)}, u32[]{:S(2)}) collective-permute-start(bf16[512,896]{1,0:T(8,128)(2,1)S(1)} %bitcast.14), channel_id=1, source_target_pairs={{0,64},{64,128},{128,192},{192,0},{1,65},{65,129},{129,193},{193,1... | collective-permute-start | bytes 2752520 | tf_op jit(solution)/shard_map/ppermute | solution.py:209
  51.8 35.9 %all-to-all-start.1 = ((bf16[64,8,512]{2,1,0:T(8,128)(2,1)}), bf16[64,8,512]{2,1,0:T(8,128)(2,1)S(1)}, u32[]{:S(2)}, u32[]{:S(2)}) async-start(bf16[64,8,512]{2,1,0:T(8,128)(2,1)} %bitcast.18), calls=%async_computation.1 | async-start | bytes 1048576 | tf_op jit(solution)/shard_map/all_to_all | solution.py:219
  63.6 16.3 %collective-permute-start.5 = (bf16[192,1024]{1,0:T(8,128)(2,1)}, bf16[192,1024]{1,0:T(8,128)(2,1)S(1)}, u32[]{:S(2)}, u32[]{:S(2)}) collective-permute-start(bf16[192,1024]{1,0:T(8,128)(2,1)} %get-tuple-element.32), channel_id=1, source_target_pairs={{0,128},{64,192},{128,0},{192,64},{1,129},{65,193},{129,1},{193,65... | collective-permute-start | bytes 1179656 | tf_op jit(solution)/shard_map/ppermute | solution.py:209
  79.9 2.0 %copy-start.6 = (bf16[192,1024]{1,0:T(8,128)(2,1)}, bf16[192,1024]{1,0:T(8,128)(2,1)S(1)}, u32[]{:S(2)}) copy-start(bf16[192,1024]{1,0:T(8,128)(2,1)S(1)} %collective-permute-done.5.refs_7_) | copy-start | bytes 1179652
  79.9 2.0 %copy-start.2 = (bf16[512,896]{1,0:T(8,128)(2,1)}, bf16[512,896]{1,0:T(8,128)(2,1)S(1)}, u32[]{:S(2)}) copy-start(bf16[512,896]{1,0:T(8,128)(2,1)S(1)} %collective-permute-done.4.refs_1_) | copy-start | bytes 2752516
  79.9 2.0 %copy-start.3 = (bf16[512,896]{1,0:T(8,128)(2,1)}, bf16[512,896]{1,0:T(8,128)(2,1)S(1)}, u32[]{:S(2)}) copy-start(bf16[512,896]{1,0:T(8,128)(2,1)S(1)} %collective-permute-done.3.refs_0_) | copy-start | bytes 2752516
  80.0 9.5 %collective-permute-start.7 = (bf16[256,896]{1,0:T(8,128)(2,1)S(1)}, bf16[256,896]{1,0:T(8,128)(2,1)}, u32[]{:S(2)}, u32[]{:S(2)}) collective-permute-start(bf16[256,896]{1,0:T(8,128)(2,1)S(1)} %slice.13), channel_id=1, source_target_pairs={{0,192},{64,0},{128,64},{192,128},{1,193},{65,1},{129,65},{193,129... | collective-permute-start | bytes 1376264 | tf_op jit(solution)/shard_map/ppermute | solution.py:209
  81.9 10.8 %collective-permute-start.6 = (bf16[256,896]{1,0:T(8,128)(2,1)S(1)}, bf16[256,896]{1,0:T(8,128)(2,1)}, u32[]{:S(2)}, u32[]{:S(2)}) collective-permute-start(bf16[256,896]{1,0:T(8,128)(2,1)S(1)} %slice.12), channel_id=1, source_target_pairs={{0,64},{64,128},{128,192},{192,0},{1,65},{65,129},{129,193},{193,1... | collective-permute-start | bytes 1376264 | tf_op jit(solution)/shard_map/ppermute | solution.py:209
  87.6 5.1 %copy-start.1 = (bf16[64,8,512]{2,1,0:T(8,128)(2,1)}, bf16[64,8,512]{2,1,0:T(8,128)(2,1)S(1)}, u32[]{:S(2)}) copy-start(bf16[64,8,512]{2,1,0:T(8,128)(2,1)S(1)} %all-to-all-done.1) | copy-start | bytes 1572868
  97.4 66.6 %copy-start.10 = (bf16[64,512]{1,0:T(8,128)(2,1)S(1)}, bf16[64,512]{1,0:T(8,128)(2,1)}, u32[]{:S(2)}) copy-start(bf16[64,512]{1,0:T(8,128)(2,1)} %get-tuple-element.27) | copy-start | bytes 196612
  97.4 7.4 %collective-permute-start.10 = (bf16[512,384]{1,0:T(8,128)(2,1)}, bf16[512,384]{1,0:T(8,128)(2,1)S(1)}, u32[]{:S(2)}, u32[]{:S(2)}) collective-permute-start(bf16[512,384]{1,0:T(8,128)(2,1)} %gate_up.5.refs_0_), channel_id=1, source_target_pairs={{0,192},{64,0},{128,64},{192,128},{1,193},{65,1},{129,65},{193,129... | collective-permute-start | bytes 1179656 | tf_op jit(solution)/shard_map/ppermute | solution.py:209
  97.7 9.0 %collective-permute-start.9 = (bf16[512,384]{1,0:T(8,128)(2,1)}, bf16[512,384]{1,0:T(8,128)(2,1)S(1)}, u32[]{:S(2)}, u32[]{:S(2)}) collective-permute-start(bf16[512,384]{1,0:T(8,128)(2,1)} %gate_up.5.refs_0_), channel_id=1, source_target_pairs={{0,128},{64,192},{128,0},{192,64},{1,129},{65,193},{129,1},{193,65... | collective-permute-start | bytes 1179656 | tf_op jit(solution)/shard_map/ppermute | solution.py:209
  97.7 21.1 %collective-permute-start.8 = (bf16[512,384]{1,0:T(8,128)(2,1)}, bf16[512,384]{1,0:T(8,128)(2,1)S(1)}, u32[]{:S(2)}, u32[]{:S(2)}) collective-permute-start(bf16[512,384]{1,0:T(8,128)(2,1)} %gate_up.5.refs_0_), channel_id=1, source_target_pairs={{0,64},{64,128},{128,192},{192,0},{1,65},{65,129},{129,193},{193,1... | collective-permute-start | bytes 1179656 | tf_op jit(solution)/shard_map/ppermute | solution.py:209
  104.8 14.0 %copy-start.7 = (bf16[512,384]{1,0:T(8,128)(2,1)}, bf16[512,384]{1,0:T(8,128)(2,1)S(1)}, u32[]{:S(2)}) copy-start(bf16[512,384]{1,0:T(8,128)(2,1)S(1)} %collective-permute-done.10.refs_3_) | copy-start | bytes 1179652
  106.7 12.1 %copy-start.8 = (bf16[512,384]{1,0:T(8,128)(2,1)}, bf16[512,384]{1,0:T(8,128)(2,1)S(1)}, u32[]{:S(2)}) copy-start(bf16[512,384]{1,0:T(8,128)(2,1)S(1)} %collective-permute-done.9.refs_2_) | copy-start | bytes 1179652
  118.8 0.8 copy-start.9

commit v8 on v4

v8 whole, which is shorter than its diff:
```python
import jax
import jax.numpy as jnp
from jax import lax
from jax.experimental import pallas as pl
from jax.experimental.pallas import tpu as pltpu
from jax.sharding import PartitionSpec as P

ED = ("expert", "dp")
BF = jnp.bfloat16
F32 = jnp.float32
ANY = pl.BlockSpec(memory_space=pl.ANY)
PARAMS = pltpu.CompilerParams(vmem_limit_bytes=56 * 1024 * 1024)


def dot(a, b):
    return jnp.dot(a, b, preferred_element_type=F32)


def cost(flops, read):
    return pl.CostEstimate(flops=flops, bytes_accessed=read, transcendentals=0)


def first(section, tokens, routing, gate_weights, w_down, cap, experts, sections):
    toks, fanout = routing.shape
    slots = experts * cap
    _, hid, width = w_down.shape
    quarter = width // sections
    count = sections - 1

    def kernel(s_ref, routing_ref, weights_ref, tokens_ref, down_ref, *refs):
        rows_ref, spread_ref = refs[:2]
        cuts, bufs = refs[2 : 2 + count], refs[2 + count]
        in_sem, out_sem = refs[3 + count], refs[4 + count]
        ins, outs = [], []
        for d in range(count):
            start = pl.multiple_of(lax.rem(s_ref[0] + d + 1, sections) * quarter, 128)
            ins.append(
                pltpu.make_async_copy(
                    down_ref.at[0, :, pl.ds(start, quarter)], bufs.at[d], in_sem.at[d]
                )
            )
            outs.append(pltpu.make_async_copy(bufs.at[d], cuts[d], out_sem.at[d]))
        for c in ins:
            c.start()
        slot = lax.broadcasted_iota(jnp.int32, (toks, slots), 1)
        expert, order = lax.div(slot, cap), lax.rem(slot, cap)
        named = jnp.zeros((toks, slots), F32)
        weight = jnp.zeros((toks, slots), F32)
        routes, gates = routing_ref[...].T, weights_ref[...].T
        for k in range(fanout):
            hit = routes[:, k : k + 1] == expert
            named = jnp.where(hit, 1.0, named)
            weight = jnp.where(hit, gates[:, k : k + 1], weight)
        for c_in, c_out in zip(ins, outs):
            c_in.wait()
            c_out.start()
        before = (
            lax.broadcasted_iota(jnp.int32, (toks, toks), 0)
            > lax.broadcasted_iota(jnp.int32, (toks, toks), 1)
        )
        earlier = dot(jnp.where(before, 1.0, 0.0).astype(BF), named.astype(BF))
        place = jnp.where(earlier == order.astype(F32), named, 0.0)
        rows_ref[...] = lax.dot_general(
            place.astype(BF),
            tokens_ref[...],
            (((0,), (0,)), ((), ())),
            preferred_element_type=F32,
        ).astype(BF)
        spread = place * weight
        high = spread.astype(BF)
        spread_ref[...] = jnp.concatenate([high, (spread - high.astype(F32)).astype(BF)], axis=0)
        for c in outs:
            c.wait()

    def whole(*shape):
        return pl.BlockSpec(shape, lambda i, s: (0, 0))

    rows, spread, *cut = pl.pallas_call(
        kernel,
        grid_spec=pltpu.PrefetchScalarGridSpec(
            num_scalar_prefetch=1,
            grid=(1,),
            in_specs=[
                whole(fanout, toks),
                whole(fanout, toks),
                pl.BlockSpec((toks, quarter), lambda i, s: (0, s[0])),
                ANY,
            ],
            out_specs=[whole(slots, quarter), whole(2 * toks, slots)] + [ANY] * count,
            scratch_shapes=[
                pltpu.VMEM((count, hid, quarter), BF),
                pltpu.SemaphoreType.DMA((count,)),
                pltpu.SemaphoreType.DMA((count,)),
            ],
        ),
        out_shape=[
            jax.ShapeDtypeStruct((slots, quarter), BF),
            jax.ShapeDtypeStruct((2 * toks, slots), BF),
        ]
        + [jax.ShapeDtypeStruct((hid, quarter), BF)] * count,
        compiler_params=PARAMS,
        cost_estimate=cost(
            2 * slots * toks * quarter, 2 * slots * quarter + 4 * count * hid * quarter
        ),
        name="first",
    )(section, routing.T, gate_weights.T, tokens, w_down)
    return rows, spread, cut


def on_device(tokens, routing, gate_weights, w_gate, w_up, w_down):
    toks, width = tokens.shape
    fanout = routing.shape[1]
    experts = lax.axis_size(ED)
    sections = lax.axis_size("section")
    cap = min(toks, max(2, 2 * toks * fanout // experts))
    quarter = width // sections
    s = lax.axis_index("section").astype(jnp.int32)

    def send(v, d):
        return lax.ppermute(v, "section", [(k, (k + d) % sections) for k in range(sections)])

    def to_right(v):
        return send(v, 1)

    def to_left(v):
        return send(v, sections - 1)

    def exchange(v):
        rows, w = v.shape
        return lax.all_to_all(
            v.reshape(experts, cap, w), ED, split_axis=0, concat_axis=0, tiled=True
        ).reshape(rows, w)

    outgoing, spread, cut = first(
        s.reshape(1), tokens, routing, gate_weights, w_down, cap, experts, sections
    )
    downs = [send(c, d + 1) for d, c in enumerate(cut)]
    received = exchange(outgoing)
    rows = experts * cap
    half = rows // 2

    def k_part(halves, d):
        block = jnp.concatenate(halves, axis=0)
        start = lax.rem(s + d, sections) * quarter
        g = lax.dynamic_slice_in_dim(w_gate[0], start, quarter, axis=0)
        u = lax.dynamic_slice_in_dim(w_up[0], start, quarter, axis=0)
        return dot(block, g), dot(block, u)

    a, b = received[:half], received[half:]
    r_a, l_b = to_right(a), to_left(b)
    gate, up = k_part((a, b), 0)
    a_later, b_later, gate, up, *downs = lax.optimization_barrier((a, b, gate, up, *downs))
    r_b, l_a = to_right(b_later), to_left(a_later)
    across = (to_right(r_a), to_left(l_b))
    for halves, d in (((r_a, r_b), 3), ((l_a, l_b), 1), (across, 2)):
        g, u = k_part(halves, d)
        gate, up = gate + g, up + u
    hidden = (jax.nn.silu(gate) * up).astype(BF)
    out = dot(hidden, lax.dynamic_slice_in_dim(w_down[0], s * quarter, quarter, axis=1))
    for d, down in enumerate(downs):
        out = out + dot(send(hidden, d + 1), down)
    returned = exchange(out.astype(BF))
    both = dot(spread, returned)
    return (both[:toks] + both[toks:]).astype(BF)


def solution(mesh):
    placed = (
        P(ED, None),
        P(ED, None),
        P(ED, None),
        P(ED, None, "section"),
        P(ED, None, "section"),
        P(ED, "section", None),
    )
    return jax.shard_map(
        on_device,
        mesh=mesh,
        in_specs=placed,
        out_specs=P(ED, "section"),
        check_vma=False,
    )
```

time: 245 us -> 158 us (0.64)
  Pallas kernels: 75.2 us -> 4.64 us
  waiting for transfers between devices: 65.7 us -> 56.4 us
  blocking collectives: 45.3 us -> 39.1 us
    pallas_call x2 -> x1, Pallas kernels: 75.2 us -> 4.64 us  [first(): pl.pallas_call(kernel, grid_spec=pltpu.PrefetchScalarGridSpec(num_scalar_...]
    ppermute x12, waiting for transfers between devices: 65.7 us -> 33.4 us  [send(): lax.ppermute(v, 'section', [(k, (k + d) % sections) for k in range(sectio...]
    all_to_all x1, waiting for transfers between devices: 0.01 us -> 23 us  [exchange(): lax.all_to_all(v.reshape(experts, cap, w), ED, split_axis=0, concat_axis=...]
    all_to_all x1, blocking collectives: 45.3 us -> 39.1 us  [exchange(): lax.all_to_all(v.reshape(experts, cap, w), ED, split_axis=0, concat_axis=...]
    unnamed x13, local copies, waits for them, and re-layouts: 5.08 us -> 2.57 us
  transfers between devices with their start and end apart: 13 -> 13, of which waited for: 8 -> 6; matrix products, arithmetic and copies ran while one was open for 7% -> 14% of each run, Pallas kernels for 0% -> 0%
where the time goes in v8:
time: 158 us; the launch traced here: 157 us
  waiting for transfers between devices  56.4 us (36%)
  blocking collectives  39.1 us (25%)
  starting transfers between devices  30.1 us (19%)
  matrix products  20.2 us (13%)
  local copies, waits for them, and re-layouts  5.97 us (4%)
  Pallas kernels  4.64 us (3%)
    all_to_all x1, blocking collectives, exchange(): lax.all_to_all(v.reshape(experts, cap, w), ED, split_axis=0, concat_axis=...  39.1 us
    ppermute x12, waiting for transfers between devices, send(): lax.ppermute(v, 'section', [(k, (k + d) % sections) for k in range(sectio...  33.4 us
    all_to_all x1, waiting for transfers between devices, exchange(): lax.all_to_all(v.reshape(experts, cap, w), ED, split_axis=0, concat_axis=...  23 us
    dot_general x13, matrix products, dot(): return jnp.dot(a, b, preferred_element_type=F32)  20.2 us
    ppermute x12, starting transfers between devices, send(): lax.ppermute(v, 'section', [(k, (k + d) % sections) for k in range(sectio...  16.8 us
    all_to_all x1, starting transfers between devices, exchange(): lax.all_to_all(v.reshape(experts, cap, w), ED, split_axis=0, concat_axis=...  13.4 us
    pallas_call x1, Pallas kernels, first(): pl.pallas_call(kernel, grid_spec=pltpu.PrefetchScalarGridSpec(num_scalar_...  4.64 us
  transfers between devices with their start and end apart: 13, of which 6 were waited for; matrix products, arithmetic and copies ran while one was open for 14% of the time, Pallas kernels for 0%

profile of v8, /device:TPU:1, one launch (start us, length us, event | category | flops | bytes accessed | tf_op | source)
XLA Modules:
  0.0 157.2 jit_solution(1859712318758112450)
XLA Ops:
  0.0 4.6 %first.1 = (bf16[512,1024]{1,0:T(8,128)(2,1)}, bf16[64,512]{1,0:T(8,128)(2,1)}, bf16[384,1024]{1,0:T(8,128)(2,1)}, bf16[384,1024]{1,0:T(8,128)(2,1)}, bf16[384,1024]{1,0:T(8,128)(2,1)}) custom-call(s32[1]{0:T(128)} %bitcast.s_ref, s32[8,32]{1,0:T(8,128)} %bitcast.57, f32[8,32]{1,0:T(8,128)} %bitcast.58, bf16[32,4096]{1,0:T(8,128)(2,1)} %tokens_ref.1, ...), custom_call_target="tpu_custom_call" | custom-call | flops 33554432 | bytes 5767168 | tf_op jit(solution)/shard_map/first/pallas_call | solution.py:78
  4.7 13.4 %all-to-all-start = ((bf16[64,8,1024]{2,1,0:T(8,128)(2,1)}), bf16[64,8,1024]{2,1,0:T(8,128)(2,1)}, u32[]{:S(2)}, u32[]{:S(2)}) async-start(bf16[64,8,1024]{2,1,0:T(8,128)(2,1)} %bitcast.56), calls=%async_computation | async-start | bytes 2097152 | tf_op jit(solution)/shard_map/all_to_all | solution.py:130
  18.0 1.3 collective-permute-start
  19.3 2.5 %collective-permute-start.1 = (bf16[384,1024]{1,0:T(8,128)(2,1)}, bf16[384,1024]{1,0:T(8,128)(2,1)}, u32[]{:S(2)}, u32[]{:S(2)}) collective-permute-start(bf16[384,1024]{1,0:T(8,128)(2,1)} %get-tuple-element.20), channel_id=1, source_target_pairs={{0,128},{64,192},{128,0},{192,64},{1,129},{65,193},{129,1},{193,65... | collective-permute-start | bytes 2359304 | tf_op jit(solution)/shard_map/ppermute | solution.py:120
  22.9 23.0 %all-to-all-done = bf16[64,8,1024]{2,1,0:T(8,128)(2,1)} async-done(((bf16[64,8,1024]{2,1,0:T(8,128)(2,1)}), bf16[64,8,1024]{2,1,0:T(8,128)(2,1)}, u32[]{:S(2)}, u32[]{:S(2)}) %all-to-all-start) | async-done | bytes 1048608 | tf_op jit(solution)/shard_map/all_to_all | solution.py:130
  45.9 2.2 %slice_bitcast_fusion = (bf16[256,1024]{1,0:T(8,128)(2,1)}, bf16[256,1024]{1,0:T(8,128)(2,1)}) fusion(bf16[64,8,1024]{2,1,0:T(8,128)(2,1)} %all-to-all-done), kind=kLoop, calls=%fused_computation.33 | loop fusion | bytes 2097152 | tf_op jit(solution)/shard_map/slice | solution.py:149
  48.2 2.5 %collective-permute-start.6 = (bf16[256,1024]{1,0:T(8,128)(2,1)}, bf16[256,1024]{1,0:T(8,128)(2,1)}, u32[]{:S(2)}, u32[]{:S(2)}) collective-permute-start(bf16[256,1024]{1,0:T(8,128)(2,1)} %get-tuple-element.23), channel_id=1, source_target_pairs={{0,192},{64,0},{128,64},{192,128},{1,193},{65,1},{129,65},{193,129... | collective-permute-start | bytes 1572872 | tf_op jit(solution)/shard_map/ppermute | solution.py:120
  50.6 3.0 %fusion.15 = f32[512,384]{1,0:T(8,128)} fusion(bf16[1,4096,384]{2,1,0:T(8,128)(2,1)} %param.10, s32[]{:T(128)S(6)} %select_n.19, bf16[256,1024]{1,0:T(8,128)(2,1)} %get-tuple-element.23, bf16[256,1024]{1,0:T(8,128)(2,1)} %get-tuple-element.24), kind=kOutput, calls=%fused_computation.19 | convolution fusion | flops 404750336 | bytes 2621444 | tf_op jit(solution)/shard_map/dot_general | solution.py:16
  53.7 2.8 %fusion.17 = f32[512,384]{1,0:T(8,128)} fusion(bf16[1,4096,384]{2,1,0:T(8,128)(2,1)S(1)} %copy-done, s32[]{:T(128)S(6)} %select_n.19, bf16[256,1024]{1,0:T(8,128)(2,1)} %get-tuple-element.23, bf16[256,1024]{1,0:T(8,128)(2,1)} %get-tuple-element.24), kind=kOutput, calls=%fused_computation.21 | convolution fusion | flops 404750336 | bytes 2621444 | tf_op jit(solution)/shard_map/dot_general | solution.py:16
  56.5 2.8 %collective-permute-start.5 = (bf16[256,1024]{1,0:T(8,128)(2,1)}, bf16[256,1024]{1,0:T(8,128)(2,1)}, u32[]{:S(2)}, u32[]{:S(2)}) collective-permute-start(bf16[256,1024]{1,0:T(8,128)(2,1)} %get-tuple-element.24), channel_id=1, source_target_pairs={{0,192},{64,0},{128,64},{192,128},{1,193},{65,1},{129,65},{193,129... | collective-permute-start | bytes 1572872 | tf_op jit(solution)/shard_map/ppermute | solution.py:120
  59.3 7.4 %collective-permute-done.6 = bf16[256,1024]{1,0:T(8,128)(2,1)} collective-permute-done((bf16[256,1024]{1,0:T(8,128)(2,1)}, bf16[256,1024]{1,0:T(8,128)(2,1)}, u32[]{:S(2)}, u32[]{:S(2)}) %collective-permute-start.6) | collective-permute-done | bytes 524320 | tf_op jit(solution)/shard_map/ppermute | solution.py:120
  66.7 3.4 %collective-permute-start.8 = (bf16[256,1024]{1,0:T(8,128)(2,1)}, bf16[256,1024]{1,0:T(8,128)(2,1)S(1)}, u32[]{:S(2)}, u32[]{:S(2)}) collective-permute-start(bf16[256,1024]{1,0:T(8,128)(2,1)} %collective-permute-done.6), channel_id=1, source_target_pairs={{0,192},{64,0},{128,64},{192,128},{1,193},{65,1},{129,65},{193,129... | collective-permute-start | bytes 1572872 | tf_op jit(solution)/shard_map/ppermute | solution.py:120
  71.3 6.7 %collective-permute-done.5 = bf16[256,1024]{1,0:T(8,128)(2,1)} collective-permute-done((bf16[256,1024]{1,0:T(8,128)(2,1)}, bf16[256,1024]{1,0:T(8,128)(2,1)}, u32[]{:S(2)}, u32[]{:S(2)}) %collective-permute-start.5) | collective-permute-done | bytes 524320 | tf_op jit(solution)/shard_map/ppermute | solution.py:120
  80.1 2.0 %fusion.6 = f32[512,384]{1,0:T(8,128)S(1)} fusion(bf16[512,1024]{1,0:T(8,128)(2,1)S(1)} %constant_dynamic-update-slice_fusion.2, bf16[1,4096,384]{2,1,0:T(8,128)(2,1)} %param.10, s32[]{:T(128)S(6)} %select_n.21), kind=kOutput, calls=%fused_computation.10 | convolution fusion | flops 402653184 | bytes 2621444 | tf_op jit(solution)/shard_map/dot_general | solution.py:16
  84.4 5.7 %collective-permute-done.7 = bf16[256,1024]{1,0:T(8,128)(2,1)S(1)} collective-permute-done((bf16[256,1024]{1,0:T(8,128)(2,1)}, bf16[256,1024]{1,0:T(8,128)(2,1)S(1)}, u32[]{:S(2)}, u32[]{:S(2)}) %collective-permute-start.7) | collective-permute-done | bytes 524320 | tf_op jit(solution)/shard_map/ppermute | solution.py:120
  91.3 1.6 %multiply_convert_fusion = bf16[512,384]{1,0:T(8,128)(2,1)} fusion(f32[512,384]{1,0:T(8,128)S(1)} %convolution_add_fusion.1, bf16[512,1024]{1,0:T(8,128)(2,1)S(1)} %constant_dynamic-update-slice_fusion.4, bf16[1,4096,384]{2,1,0:T(8,128)(2,1)S(1)} %copy-done.2, s32[]{:T(128)S(6)} %select_n.22, f32[512,384]{1,0:T(8,128)S(1)} %fusion.6, ...), kind=kOutput, calls=%fused_computation.24 | convolution fusion | flops 404422656 | bytes 5373956 | tf_op jit(solution)/shard_map/dot_general | solution.py:16
  93.2 2.3 %collective-permute-start.11 = (bf16[512,384]{1,0:T(8,128)(2,1)}, bf16[512,384]{1,0:T(8,128)(2,1)S(1)}, u32[]{:S(2)}, u32[]{:S(2)}) collective-permute-start(bf16[512,384]{1,0:T(8,128)(2,1)} %multiply_convert_fusion), channel_id=1, source_target_pairs={{0,192},{64,0},{128,64},{192,128},{1,193},{65,1},{129,65},{193,129... | collective-permute-start | bytes 1179656 | tf_op jit(solution)/shard_map/ppermute | solution.py:120
  96.1 2.0 %fusion.3 = f32[512,1024]{1,0:T(8,128)S(1)} fusion(bf16[512,384]{1,0:T(8,128)(2,1)} %multiply_convert_fusion, bf16[1,384,4096]{2,1,0:T(8,128)(2,1)} %down_ref.1, s32[]{:T(128)S(6)} %select_n.23), kind=kOutput, calls=%fused_computation.7 | convolution fusion | flops 402653184 | bytes 3276804 | tf_op jit(solution)/shard_map/dot_general | solution.py:16
  98.0 5.9 %collective-permute-done.9 = bf16[512,384]{1,0:T(8,128)(2,1)S(1)} collective-permute-done((bf16[512,384]{1,0:T(8,128)(2,1)}, bf16[512,384]{1,0:T(8,128)(2,1)S(1)}, u32[]{:S(2)}, u32[]{:S(2)}) %collective-permute-start.9) | collective-permute-done | bytes 393248 | tf_op jit(solution)/shard_map/ppermute | solution.py:120
  104.0 1.8 %fusion.42 = f32[512,1024]{1,0:T(8,128)S(1)} fusion(bf16[512,384]{1,0:T(8,128)(2,1)S(1)} %collective-permute-done.9, bf16[384,1024]{1,0:T(8,128)(2,1)} %collective-permute-done), kind=kOutput, calls=%fused_computation.54 | convolution fusion | flops 402653184 | bytes 3276800 | tf_op jit(solution)/shard_map/dot_general | solution.py:16
  105.8 7.6 %collective-permute-done.10 = bf16[512,384]{1,0:T(8,128)(2,1)S(1)} collective-permute-done((bf16[512,384]{1,0:T(8,128)(2,1)}, bf16[512,384]{1,0:T(8,128)(2,1)S(1)}, u32[]{:S(2)}, u32[]{:S(2)}) %collective-permute-start.10) | collective-permute-done | bytes 393248 | tf_op jit(solution)/shard_map/ppermute | solution.py:120
  113.4 1.8 %fusion.43 = f32[512,1024]{1,0:T(8,128)S(1)} fusion(bf16[512,384]{1,0:T(8,128)(2,1)S(1)} %collective-permute-done.10, bf16[384,1024]{1,0:T(8,128)(2,1)} %collective-permute-done.1), kind=kOutput, calls=%fused_computation.55 | convolution fusion | flops 402653184 | bytes 3276800 | tf_op jit(solution)/shard_map/dot_general | solution.py:16
  115.3 1.9 %fusion = bf16[64,8,1024]{2,1,0:T(8,128)(2,1)S(1)} fusion(f32[512,1024]{1,0:T(8,128)S(1)} %fusion.43, f32[512,1024]{1,0:T(8,128)S(1)} %fusion.3, f32[512,1024]{1,0:T(8,128)S(1)} %fusion.42, bf16[512,384]{1,0:T(8,128)(2,1)S(1)} %collective-permute-done.11, bf16[384,1024]{1,0:T(8,128)(2,1)} %collective-permute-done.2), kind=kOutput, calls=%fused_computation.3 | convolution fusion | flops 404750336 | bytes 8519680 | tf_op jit(solution)/shard_map/dot_general | solution.py:16
  117.2 39.1 %all_to_all.10 = bf16[64,8,1024]{2,1,0:T(8,128)(2,1)S(1)} all-to-all(bf16[64,8,1024]{2,1,0:T(8,128)(2,1)S(1)} %fusion), channel_id=1, replica_groups=mesh['section'=4,'expert'=32,'dp'=2] {'expert','dp'}, dimensions={0} | all-to-all | bytes 2097152 | tf_op jit(solution)/shard_map/all_to_all | solution.py:130
  (35 shorter events, 9.7 us)
Async XLA Ops:
  0.0 53.7 %copy-start = (bf16[1,4096,384]{2,1,0:T(8,128)(2,1)S(1)}, bf16[1,4096,384]{2,1,0:T(8,128)(2,1)}, u32[]{:S(2)}) copy-start(bf16[1,4096,384]{2,1,0:T(8,128)(2,1)} %param.9) | copy-start | bytes 9437188
  4.7 41.3 %all-to-all-start = ((bf16[64,8,1024]{2,1,0:T(8,128)(2,1)}), bf16[64,8,1024]{2,1,0:T(8,128)(2,1)}, u32[]{:S(2)}, u32[]{:S(2)}) async-start(bf16[64,8,1024]{2,1,0:T(8,128)(2,1)} %bitcast.56), calls=%async_computation | async-start | bytes 2097152 | tf_op jit(solution)/shard_map/all_to_all | solution.py:130
  18.0 38.5 %collective-permute-start = (bf16[384,1024]{1,0:T(8,128)(2,1)}, bf16[384,1024]{1,0:T(8,128)(2,1)}, u32[]{:S(2)}, u32[]{:S(2)}) collective-permute-start(bf16[384,1024]{1,0:T(8,128)(2,1)} %get-tuple-element.19), channel_id=1, source_target_pairs={{0,64},{64,128},{128,192},{192,0},{1,65},{65,129},{129,193},{193,1... | collective-permute-start | bytes 2359304 | tf_op jit(solution)/shard_map/ppermute | solution.py:120
  19.3 37.2 %collective-permute-start.1 = (bf16[384,1024]{1,0:T(8,128)(2,1)}, bf16[384,1024]{1,0:T(8,128)(2,1)}, u32[]{:S(2)}, u32[]{:S(2)}) collective-permute-start(bf16[384,1024]{1,0:T(8,128)(2,1)} %get-tuple-element.20), channel_id=1, source_target_pairs={{0,128},{64,192},{128,0},{192,64},{1,129},{65,193},{129,1},{193,65... | collective-permute-start | bytes 2359304 | tf_op jit(solution)/shard_map/ppermute | solution.py:120
  21.8 34.8 %collective-permute-start.2 = (bf16[384,1024]{1,0:T(8,128)(2,1)}, bf16[384,1024]{1,0:T(8,128)(2,1)}, u32[]{:S(2)}, u32[]{:S(2)}) collective-permute-start(bf16[384,1024]{1,0:T(8,128)(2,1)} %get-tuple-element.21), channel_id=1, source_target_pairs={{0,192},{64,0},{128,64},{192,128},{1,193},{65,1},{129,65},{193,129... | collective-permute-start | bytes 2359304 | tf_op jit(solution)/shard_map/ppermute | solution.py:120
  48.2 18.6 %collective-permute-start.6 = (bf16[256,1024]{1,0:T(8,128)(2,1)}, bf16[256,1024]{1,0:T(8,128)(2,1)}, u32[]{:S(2)}, u32[]{:S(2)}) collective-permute-start(bf16[256,1024]{1,0:T(8,128)(2,1)} %get-tuple-element.23), channel_id=1, source_target_pairs={{0,192},{64,0},{128,64},{192,128},{1,193},{65,1},{129,65},{193,129... | collective-permute-start | bytes 1572872 | tf_op jit(solution)/shard_map/ppermute | solution.py:120
  50.6 19.5 %collective-permute-start.3 = (bf16[256,1024]{1,0:T(8,128)(2,1)}, bf16[256,1024]{1,0:T(8,128)(2,1)}, u32[]{:S(2)}, u32[]{:S(2)}) collective-permute-start(bf16[256,1024]{1,0:T(8,128)(2,1)} %get-tuple-element.24), channel_id=1, source_target_pairs={{0,64},{64,128},{128,192},{192,0},{1,65},{65,129},{129,193},{193,1... | collective-permute-start | bytes 1572872 | tf_op jit(solution)/shard_map/ppermute | solution.py:120
  56.5 21.4 %collective-permute-start.5 = (bf16[256,1024]{1,0:T(8,128)(2,1)}, bf16[256,1024]{1,0:T(8,128)(2,1)}, u32[]{:S(2)}, u32[]{:S(2)}) collective-permute-start(bf16[256,1024]{1,0:T(8,128)(2,1)} %get-tuple-element.24), channel_id=1, source_target_pairs={{0,192},{64,0},{128,64},{192,128},{1,193},{65,1},{129,65},{193,129... | collective-permute-start | bytes 1572872 | tf_op jit(solution)/shard_map/ppermute | solution.py:120
  59.3 23.6 %collective-permute-start.4 = (bf16[256,1024]{1,0:T(8,128)(2,1)}, bf16[256,1024]{1,0:T(8,128)(2,1)S(1)}, u32[]{:S(2)}, u32[]{:S(2)}) collective-permute-start(bf16[256,1024]{1,0:T(8,128)(2,1)} %get-tuple-element.23), channel_id=1, source_target_pairs={{0,64},{64,128},{128,192},{192,0},{1,65},{65,129},{129,193},{193,1... | collective-permute-start | bytes 1572872 | tf_op jit(solution)/shard_map/ppermute | solution.py:120
  66.7 23.4 %collective-permute-start.8 = (bf16[256,1024]{1,0:T(8,128)(2,1)}, bf16[256,1024]{1,0:T(8,128)(2,1)S(1)}, u32[]{:S(2)}, u32[]{:S(2)}) collective-permute-start(bf16[256,1024]{1,0:T(8,128)(2,1)} %collective-permute-done.6), channel_id=1, source_target_pairs={{0,192},{64,0},{128,64},{192,128},{1,193},{65,1},{129,65},{193,129... | collective-permute-start | bytes 1572872 | tf_op jit(solution)/shard_map/ppermute | solution.py:120
  70.1 19.9 %collective-permute-start.7 = (bf16[256,1024]{1,0:T(8,128)(2,1)}, bf16[256,1024]{1,0:T(8,128)(2,1)S(1)}, u32[]{:S(2)}, u32[]{:S(2)}) collective-permute-start(bf16[256,1024]{1,0:T(8,128)(2,1)} %collective-permute-done.3), channel_id=1, source_target_pairs={{0,64},{64,128},{128,192},{192,0},{1,65},{65,129},{129,193},{193,1... | collective-permute-start | bytes 1572872 | tf_op jit(solution)/shard_map/ppermute | solution.py:120
  80.1 2.8 %copy-start.2 = (bf16[1,4096,384]{2,1,0:T(8,128)(2,1)S(1)}, bf16[1,4096,384]{2,1,0:T(8,128)(2,1)}, u32[]{:S(2)}) copy-start(bf16[1,4096,384]{2,1,0:T(8,128)(2,1)} %param.10) | copy-start | bytes 9437188
  82.9 7.3 %copy-start.1 = (f32[512,384]{1,0:T(8,128)S(1)}, f32[512,384]{1,0:T(8,128)}, u32[]{:S(2)}) copy-start(f32[512,384]{1,0:T(8,128)} %fusion.17) | copy-start | bytes 2359300
  90.1 1.1 copy-start.4
  92.8 11.1 %collective-permute-start.9 = (bf16[512,384]{1,0:T(8,128)(2,1)}, bf16[512,384]{1,0:T(8,128)(2,1)S(1)}, u32[]{:S(2)}, u32[]{:S(2)}) collective-permute-start(bf16[512,384]{1,0:T(8,128)(2,1)} %multiply_convert_fusion), channel_id=1, source_target_pairs={{0,64},{64,128},{128,192},{192,0},{1,65},{65,129},{129,193},{193,1... | collective-permute-start | bytes 1179656 | tf_op jit(solution)/shard_map/ppermute | solution.py:120
  93.2 22.1 %collective-permute-start.11 = (bf16[512,384]{1,0:T(8,128)(2,1)}, bf16[512,384]{1,0:T(8,128)(2,1)S(1)}, u32[]{:S(2)}, u32[]{:S(2)}) collective-permute-start(bf16[512,384]{1,0:T(8,128)(2,1)} %multiply_convert_fusion), channel_id=1, source_target_pairs={{0,192},{64,0},{128,64},{192,128},{1,193},{65,1},{129,65},{193,129... | collective-permute-start | bytes 1179656 | tf_op jit(solution)/shard_map/ppermute | solution.py:120
  95.5 17.9 %collective-permute-start.10 = (bf16[512,384]{1,0:T(8,128)(2,1)}, bf16[512,384]{1,0:T(8,128)(2,1)S(1)}, u32[]{:S(2)}, u32[]{:S(2)}) collective-permute-start(bf16[512,384]{1,0:T(8,128)(2,1)} %multiply_convert_fusion), channel_id=1, source_target_pairs={{0,128},{64,192},{128,0},{192,64},{1,129},{65,193},{129,1},{193,65... | collective-permute-start | bytes 1179656 | tf_op jit(solution)/shard_map/ppermute | solution.py:120
  115.3 41.0 %copy-start.3 = (bf16[64,512]{1,0:T(8,128)(2,1)S(1)}, bf16[64,512]{1,0:T(8,128)(2,1)}, u32[]{:S(2)}) copy-start(bf16[64,512]{1,0:T(8,128)(2,1)} %get-tuple-element.17) | copy-start | bytes 196612

commit v9 on v8

--- a/solution.py
+++ b/solution.py
@@ -42,33 +42,27 @@
             outs.append(pltpu.make_async_copy(bufs.at[d], cuts[d], out_sem.at[d]))
         for c in ins:
             c.start()
-        slot = lax.broadcasted_iota(jnp.int32, (toks, slots), 1)
+        slot = lax.broadcasted_iota(jnp.int32, (slots, toks), 0)
         expert, order = lax.div(slot, cap), lax.rem(slot, cap)
-        named = jnp.zeros((toks, slots), F32)
-        weight = jnp.zeros((toks, slots), F32)
-        routes, gates = routing_ref[...].T, weights_ref[...].T
+        named = jnp.zeros((slots, toks), F32)
+        weight = jnp.zeros((slots, toks), F32)
         for k in range(fanout):
-            hit = routes[:, k : k + 1] == expert
+            hit = routing_ref[k : k + 1, :] == expert
             named = jnp.where(hit, 1.0, named)
-            weight = jnp.where(hit, gates[:, k : k + 1], weight)
+            weight = jnp.where(hit, weights_ref[k : k + 1, :], weight)
         for c_in, c_out in zip(ins, outs):
             c_in.wait()
             c_out.start()
         before = (
             lax.broadcasted_iota(jnp.int32, (toks, toks), 0)
-            > lax.broadcasted_iota(jnp.int32, (toks, toks), 1)
+            < lax.broadcasted_iota(jnp.int32, (toks, toks), 1)
         )
-        earlier = dot(jnp.where(before, 1.0, 0.0).astype(BF), named.astype(BF))
+        earlier = dot(named.astype(BF), jnp.where(before, 1.0, 0.0).astype(BF))
         place = jnp.where(earlier == order.astype(F32), named, 0.0)
-        rows_ref[...] = lax.dot_general(
-            place.astype(BF),
-            tokens_ref[...],
-            (((0,), (0,)), ((), ())),
-            preferred_element_type=F32,
-        ).astype(BF)
+        rows_ref[...] = dot(place.astype(BF), tokens_ref[...]).astype(BF)
         spread = place * weight
         high = spread.astype(BF)
-        spread_ref[...] = jnp.concatenate([high, (spread - high.astype(F32)).astype(BF)], axis=0)
+        spread_ref[...] = jnp.concatenate([high, (spread - high.astype(F32)).astype(BF)], axis=1)
         for c in outs:
             c.wait()
 
@@ -86,7 +80,7 @@
                 pl.BlockSpec((toks, quarter), lambda i, s: (0, s[0])),
                 ANY,
             ],
-            out_specs=[whole(slots, quarter), whole(2 * toks, slots)] + [ANY] * count,
+            out_specs=[whole(slots, quarter), whole(slots, 2 * toks)] + [ANY] * count,
             scratch_shapes=[
                 pltpu.VMEM((count, hid, quarter), BF),
                 pltpu.SemaphoreType.DMA((count,)),
@@ -95,7 +89,7 @@
         ),
         out_shape=[
             jax.ShapeDtypeStruct((slots, quarter), BF),
-            jax.ShapeDtypeStruct((2 * toks, slots), BF),
+            jax.ShapeDtypeStruct((slots, 2 * toks), BF),
         ]
         + [jax.ShapeDtypeStruct((hid, quarter), BF)] * count,
         compiler_params=PARAMS,
@@ -156,11 +150,16 @@
         g, u = k_part(halves, d)
         gate, up = gate + g, up + u
     hidden = (jax.nn.silu(gate) * up).astype(BF)
+    near = [send(hidden, d) for d in (1, sections - 1)]
     out = dot(hidden, lax.dynamic_slice_in_dim(w_down[0], s * quarter, quarter, axis=1))
-    for d, down in enumerate(downs):
-        out = out + dot(send(hidden, d + 1), down)
+    far = send(lax.optimization_barrier((hidden, out))[0], 2)
+    for block, down in zip(near, (downs[0], downs[2])):
+        out = out + dot(block, down)
+    out = out + dot(far, downs[1])
     returned = exchange(out.astype(BF))
-    both = dot(spread, returned)
+    both = lax.dot_general(
+        spread, returned, (((0,), (0,)), ((), ())), preferred_element_type=F32
+    )
     return (both[:toks] + both[toks:]).astype(BF)
 
 

time: 158 us -> 158 us (level)
  waiting for transfers between devices: 56.4 us -> 54.5 us
    ppermute x12, waiting for transfers between devices: 33.4 us -> 31.5 us  [send(): lax.ppermute(v, 'section', [(k, (k + d) % sections) for k in range(sectio...]
    dot_general x13 -> x12, matrix products: 20.2 us -> 19.9 us  [dot(): return jnp.dot(a, b, preferred_element_type=F32)]
where the time goes in v9:
time: 158 us; the launch traced here: 157 us
  waiting for transfers between devices  54.5 us (34%)
  blocking collectives  40.2 us (25%)
  starting transfers between devices  30.2 us (19%)
  matrix products  20.2 us (13%)
  local copies, waits for them, and re-layouts  5.96 us (4%)
  Pallas kernels  4.68 us (3%)
    all_to_all x1, blocking collectives, exchange(): lax.all_to_all(v.reshape(experts, cap, w), ED, split_axis=0, concat_axis=...  40.2 us
    ppermute x12, waiting for transfers between devices, send(): lax.ppermute(v, 'section', [(k, (k + d) % sections) for k in range(sectio...  31.5 us
    all_to_all x1, waiting for transfers between devices, exchange(): lax.all_to_all(v.reshape(experts, cap, w), ED, split_axis=0, concat_axis=...  23 us
    dot_general x12, matrix products, dot(): return jnp.dot(a, b, preferred_element_type=F32)  19.9 us
    ppermute x12, starting transfers between devices, send(): lax.ppermute(v, 'section', [(k, (k + d) % sections) for k in range(sectio...  16.9 us
    all_to_all x1, starting transfers between devices, exchange(): lax.all_to_all(v.reshape(experts, cap, w), ED, split_axis=0, concat_axis=...  13.4 us
    pallas_call x1, Pallas kernels, first(): pl.pallas_call(kernel, grid_spec=pltpu.PrefetchScalarGridSpec(num_scalar_...  4.68 us
  transfers between devices with their start and end apart: 13, of which 6 were waited for; matrix products, arithmetic and copies ran while one was open for 14% of the time, Pallas kernels for 0%

profile of v9, /device:TPU:1, one launch (start us, length us, event | category | flops | bytes accessed | tf_op | source)
XLA Modules:
  0.0 156.6 jit_solution(15881637410543310661)
XLA Ops:
  0.0 4.7 %first.1 = (bf16[512,1024]{1,0:T(8,128)(2,1)}, bf16[512,64]{1,0:T(8,128)(2,1)}, bf16[384,1024]{1,0:T(8,128)(2,1)}, bf16[384,1024]{1,0:T(8,128)(2,1)}, bf16[384,1024]{1,0:T(8,128)(2,1)}) custom-call(s32[1]{0:T(128)} %bitcast.s_ref, s32[8,32]{1,0:T(8,128)} %bitcast.57, f32[8,32]{1,0:T(8,128)} %bitcast.58, bf16[32,4096]{1,0:T(8,128)(2,1)} %tokens_ref.1, ...), custom_call_target="tpu_custom_call" | custom-call | flops 33554432 | bytes 5767168 | tf_op jit(solution)/shard_map/first/pallas_call | solution.py:72
  4.7 13.4 %all-to-all-start = ((bf16[64,8,1024]{2,1,0:T(8,128)(2,1)}), bf16[64,8,1024]{2,1,0:T(8,128)(2,1)}, u32[]{:S(2)}, u32[]{:S(2)}) async-start(bf16[64,8,1024]{2,1,0:T(8,128)(2,1)} %bitcast.56), calls=%async_computation | async-start | bytes 2097152 | tf_op jit(solution)/shard_map/all_to_all | solution.py:124
  18.1 1.3 collective-permute-start
  19.3 2.5 %collective-permute-start.1 = (bf16[384,1024]{1,0:T(8,128)(2,1)}, bf16[384,1024]{1,0:T(8,128)(2,1)}, u32[]{:S(2)}, u32[]{:S(2)}) collective-permute-start(bf16[384,1024]{1,0:T(8,128)(2,1)} %get-tuple-element.21), channel_id=1, source_target_pairs={{0,128},{64,192},{128,0},{192,64},{1,129},{65,193},{129,1},{193,65... | collective-permute-start | bytes 2359304 | tf_op jit(solution)/shard_map/ppermute | solution.py:114
  23.0 23.0 %all-to-all-done = bf16[64,8,1024]{2,1,0:T(8,128)(2,1)} async-done(((bf16[64,8,1024]{2,1,0:T(8,128)(2,1)}), bf16[64,8,1024]{2,1,0:T(8,128)(2,1)}, u32[]{:S(2)}, u32[]{:S(2)}) %all-to-all-start) | async-done | bytes 1048608 | tf_op jit(solution)/shard_map/all_to_all | solution.py:124
  46.0 2.2 %slice_bitcast_fusion = (bf16[256,1024]{1,0:T(8,128)(2,1)}, bf16[256,1024]{1,0:T(8,128)(2,1)}) fusion(bf16[64,8,1024]{2,1,0:T(8,128)(2,1)} %all-to-all-done), kind=kLoop, calls=%fused_computation.33 | loop fusion | bytes 2097152 | tf_op jit(solution)/shard_map/slice | solution.py:143
  48.2 2.5 %collective-permute-start.6 = (bf16[256,1024]{1,0:T(8,128)(2,1)}, bf16[256,1024]{1,0:T(8,128)(2,1)}, u32[]{:S(2)}, u32[]{:S(2)}) collective-permute-start(bf16[256,1024]{1,0:T(8,128)(2,1)} %get-tuple-element.24), channel_id=1, source_target_pairs={{0,192},{64,0},{128,64},{192,128},{1,193},{65,1},{129,65},{193,129... | collective-permute-start | bytes 1572872 | tf_op jit(solution)/shard_map/ppermute | solution.py:114
  50.7 3.0 %fusion.15 = f32[512,384]{1,0:T(8,128)} fusion(bf16[1,4096,384]{2,1,0:T(8,128)(2,1)} %param.10, s32[]{:T(128)S(6)} %select_n.19, bf16[256,1024]{1,0:T(8,128)(2,1)} %get-tuple-element.24, bf16[256,1024]{1,0:T(8,128)(2,1)} %get-tuple-element.25), kind=kOutput, calls=%fused_computation.19 | convolution fusion | flops 404750336 | bytes 2621444 | tf_op jit(solution)/shard_map/dot_general | solution.py:16
  53.7 2.8 %fusion.17 = f32[512,384]{1,0:T(8,128)} fusion(bf16[1,4096,384]{2,1,0:T(8,128)(2,1)S(1)} %copy-done, s32[]{:T(128)S(6)} %select_n.19, bf16[256,1024]{1,0:T(8,128)(2,1)} %get-tuple-element.24, bf16[256,1024]{1,0:T(8,128)(2,1)} %get-tuple-element.25), kind=kOutput, calls=%fused_computation.21 | convolution fusion | flops 404750336 | bytes 2621444 | tf_op jit(solution)/shard_map/dot_general | solution.py:16
  56.6 2.8 %collective-permute-start.5 = (bf16[256,1024]{1,0:T(8,128)(2,1)}, bf16[256,1024]{1,0:T(8,128)(2,1)}, u32[]{:S(2)}, u32[]{:S(2)}) collective-permute-start(bf16[256,1024]{1,0:T(8,128)(2,1)} %get-tuple-element.25), channel_id=1, source_target_pairs={{0,192},{64,0},{128,64},{192,128},{1,193},{65,1},{129,65},{193,129... | collective-permute-start | bytes 1572872 | tf_op jit(solution)/shard_map/ppermute | solution.py:114
  59.3 7.4 %collective-permute-done.6 = bf16[256,1024]{1,0:T(8,128)(2,1)} collective-permute-done((bf16[256,1024]{1,0:T(8,128)(2,1)}, bf16[256,1024]{1,0:T(8,128)(2,1)}, u32[]{:S(2)}, u32[]{:S(2)}) %collective-permute-start.6) | collective-permute-done | bytes 524320 | tf_op jit(solution)/shard_map/ppermute | solution.py:114
  66.8 3.4 %collective-permute-start.8 = (bf16[256,1024]{1,0:T(8,128)(2,1)}, bf16[256,1024]{1,0:T(8,128)(2,1)S(1)}, u32[]{:S(2)}, u32[]{:S(2)}) collective-permute-start(bf16[256,1024]{1,0:T(8,128)(2,1)} %collective-permute-done.6), channel_id=1, source_target_pairs={{0,192},{64,0},{128,64},{192,128},{1,193},{65,1},{129,65},{193,129... | collective-permute-start | bytes 1572872 | tf_op jit(solution)/shard_map/ppermute | solution.py:114
  71.3 6.7 %collective-permute-done.5 = bf16[256,1024]{1,0:T(8,128)(2,1)} collective-permute-done((bf16[256,1024]{1,0:T(8,128)(2,1)}, bf16[256,1024]{1,0:T(8,128)(2,1)}, u32[]{:S(2)}, u32[]{:S(2)}) %collective-permute-start.5) | collective-permute-done | bytes 524320 | tf_op jit(solution)/shard_map/ppermute | solution.py:114
  80.2 2.0 %fusion.6 = f32[512,384]{1,0:T(8,128)S(1)} fusion(bf16[512,1024]{1,0:T(8,128)(2,1)S(1)} %constant_dynamic-update-slice_fusion.2, bf16[1,4096,384]{2,1,0:T(8,128)(2,1)} %param.10, s32[]{:T(128)S(6)} %select_n.21), kind=kOutput, calls=%fused_computation.10 | convolution fusion | flops 402653184 | bytes 2621444 | tf_op jit(solution)/shard_map/dot_general | solution.py:16
  84.4 5.7 %collective-permute-done.7 = bf16[256,1024]{1,0:T(8,128)(2,1)S(1)} collective-permute-done((bf16[256,1024]{1,0:T(8,128)(2,1)}, bf16[256,1024]{1,0:T(8,128)(2,1)S(1)}, u32[]{:S(2)}, u32[]{:S(2)}) %collective-permute-start.7) | collective-permute-done | bytes 524320 | tf_op jit(solution)/shard_map/ppermute | solution.py:114
  91.3 1.6 %multiply_convert_fusion = bf16[512,384]{1,0:T(8,128)(2,1)} fusion(f32[512,384]{1,0:T(8,128)S(1)} %convolution_add_fusion.1, bf16[512,1024]{1,0:T(8,128)(2,1)S(1)} %constant_dynamic-update-slice_fusion.4, bf16[1,4096,384]{2,1,0:T(8,128)(2,1)S(1)} %copy-done.2, s32[]{:T(128)S(6)} %select_n.22, f32[512,384]{1,0:T(8,128)S(1)} %fusion.6, ...), kind=kOutput, calls=%fused_computation.24 | convolution fusion | flops 404422656 | bytes 5373956 | tf_op jit(solution)/shard_map/dot_general | solution.py:16
  93.3 2.3 %collective-permute-start.10 = (bf16[512,384]{1,0:T(8,128)(2,1)}, bf16[512,384]{1,0:T(8,128)(2,1)S(1)}, u32[]{:S(2)}, u32[]{:S(2)}) collective-permute-start(bf16[512,384]{1,0:T(8,128)(2,1)} %multiply_convert_fusion), channel_id=1, source_target_pairs={{0,192},{64,0},{128,64},{192,128},{1,193},{65,1},{129,65},{193,129... | collective-permute-start | bytes 1179656 | tf_op jit(solution)/shard_map/ppermute | solution.py:114
  95.6 2.0 %fusion.3 = f32[512,1024]{1,0:T(8,128)S(1)} fusion(bf16[512,384]{1,0:T(8,128)(2,1)} %multiply_convert_fusion, bf16[1,384,4096]{2,1,0:T(8,128)(2,1)} %down_ref.1, s32[]{:T(128)S(6)} %select_n.23), kind=kOutput, calls=%fused_computation.7 | convolution fusion | flops 402653184 | bytes 3276804 | tf_op jit(solution)/shard_map/dot_general | solution.py:16
  98.2 5.8 %collective-permute-done.9 = bf16[512,384]{1,0:T(8,128)(2,1)S(1)} collective-permute-done((bf16[512,384]{1,0:T(8,128)(2,1)}, bf16[512,384]{1,0:T(8,128)(2,1)S(1)}, u32[]{:S(2)}, u32[]{:S(2)}) %collective-permute-start.9) | collective-permute-done | bytes 393248 | tf_op jit(solution)/shard_map/ppermute | solution.py:114
  104.0 1.8 %fusion.42 = f32[512,1024]{1,0:T(8,128)S(1)} fusion(bf16[512,384]{1,0:T(8,128)(2,1)S(1)} %collective-permute-done.9, bf16[384,1024]{1,0:T(8,128)(2,1)} %collective-permute-done), kind=kOutput, calls=%fused_computation.54 | convolution fusion | flops 402653184 | bytes 3276800 | tf_op jit(solution)/shard_map/dot_general | solution.py:16
  105.8 1.8 %fusion.43 = f32[512,1024]{1,0:T(8,128)S(1)} fusion(bf16[512,384]{1,0:T(8,128)(2,1)S(1)} %collective-permute-done.10, bf16[384,1024]{1,0:T(8,128)(2,1)} %collective-permute-done.2), kind=kOutput, calls=%fused_computation.55 | convolution fusion | flops 402653184 | bytes 3276800 | tf_op jit(solution)/shard_map/dot_general | solution.py:16
  107.7 5.8 %collective-permute-done.11 = bf16[512,384]{1,0:T(8,128)(2,1)S(1)} collective-permute-done((bf16[512,384]{1,0:T(8,128)(2,1)}, bf16[512,384]{1,0:T(8,128)(2,1)S(1)}, u32[]{:S(2)}, u32[]{:S(2)}) %collective-permute-start.11) | collective-permute-done | bytes 393248 | tf_op jit(solution)/shard_map/ppermute | solution.py:114
  113.5 1.9 %fusion = bf16[64,8,1024]{2,1,0:T(8,128)(2,1)S(1)} fusion(f32[512,1024]{1,0:T(8,128)S(1)} %fusion.43, f32[512,1024]{1,0:T(8,128)S(1)} %fusion.3, f32[512,1024]{1,0:T(8,128)S(1)} %fusion.42, bf16[512,384]{1,0:T(8,128)(2,1)S(1)} %collective-permute-done.11, bf16[384,1024]{1,0:T(8,128)(2,1)} %collective-permute-done.1), kind=kOutput, calls=%fused_computation.3 | convolution fusion | flops 404750336 | bytes 8519680 | tf_op jit(solution)/shard_map/dot_general | solution.py:16
  115.4 40.2 %all_to_all.10 = bf16[64,8,1024]{2,1,0:T(8,128)(2,1)S(1)} all-to-all(bf16[64,8,1024]{2,1,0:T(8,128)(2,1)S(1)} %fusion), channel_id=1, replica_groups=mesh['section'=4,'expert'=32,'dp'=2] {'expert','dp'}, dimensions={0} | all-to-all | bytes 2097152 | tf_op jit(solution)/shard_map/all_to_all | solution.py:124
  (35 shorter events, 9.8 us)
Async XLA Ops:
  0.0 53.7 %copy-start = (bf16[1,4096,384]{2,1,0:T(8,128)(2,1)S(1)}, bf16[1,4096,384]{2,1,0:T(8,128)(2,1)}, u32[]{:S(2)}) copy-start(bf16[1,4096,384]{2,1,0:T(8,128)(2,1)} %param.9) | copy-start | bytes 9437188
  4.7 41.3 %all-to-all-start = ((bf16[64,8,1024]{2,1,0:T(8,128)(2,1)}), bf16[64,8,1024]{2,1,0:T(8,128)(2,1)}, u32[]{:S(2)}, u32[]{:S(2)}) async-start(bf16[64,8,1024]{2,1,0:T(8,128)(2,1)} %bitcast.56), calls=%async_computation | async-start | bytes 2097152 | tf_op jit(solution)/shard_map/all_to_all | solution.py:124
  18.1 38.5 %collective-permute-start = (bf16[384,1024]{1,0:T(8,128)(2,1)}, bf16[384,1024]{1,0:T(8,128)(2,1)}, u32[]{:S(2)}, u32[]{:S(2)}) collective-permute-start(bf16[384,1024]{1,0:T(8,128)(2,1)} %get-tuple-element.20), channel_id=1, source_target_pairs={{0,64},{64,128},{128,192},{192,0},{1,65},{65,129},{129,193},{193,1... | collective-permute-start | bytes 2359304 | tf_op jit(solution)/shard_map/ppermute | solution.py:114
  19.3 37.2 %collective-permute-start.1 = (bf16[384,1024]{1,0:T(8,128)(2,1)}, bf16[384,1024]{1,0:T(8,128)(2,1)}, u32[]{:S(2)}, u32[]{:S(2)}) collective-permute-start(bf16[384,1024]{1,0:T(8,128)(2,1)} %get-tuple-element.21), channel_id=1, source_target_pairs={{0,128},{64,192},{128,0},{192,64},{1,129},{65,193},{129,1},{193,65... | collective-permute-start | bytes 2359304 | tf_op jit(solution)/shard_map/ppermute | solution.py:114
  21.8 34.8 %collective-permute-start.2 = (bf16[384,1024]{1,0:T(8,128)(2,1)}, bf16[384,1024]{1,0:T(8,128)(2,1)}, u32[]{:S(2)}, u32[]{:S(2)}) collective-permute-start(bf16[384,1024]{1,0:T(8,128)(2,1)} %get-tuple-element.22), channel_id=1, source_target_pairs={{0,192},{64,0},{128,64},{192,128},{1,193},{65,1},{129,65},{193,129... | collective-permute-start | bytes 2359304 | tf_op jit(solution)/shard_map/ppermute | solution.py:114
  48.2 18.6 %collective-permute-start.6 = (bf16[256,1024]{1,0:T(8,128)(2,1)}, bf16[256,1024]{1,0:T(8,128)(2,1)}, u32[]{:S(2)}, u32[]{:S(2)}) collective-permute-start(bf16[256,1024]{1,0:T(8,128)(2,1)} %get-tuple-element.24), channel_id=1, source_target_pairs={{0,192},{64,0},{128,64},{192,128},{1,193},{65,1},{129,65},{193,129... | collective-permute-start | bytes 1572872 | tf_op jit(solution)/shard_map/ppermute | solution.py:114
  50.7 19.5 %collective-permute-start.3 = (bf16[256,1024]{1,0:T(8,128)(2,1)}, bf16[256,1024]{1,0:T(8,128)(2,1)}, u32[]{:S(2)}, u32[]{:S(2)}) collective-permute-start(bf16[256,1024]{1,0:T(8,128)(2,1)} %get-tuple-element.25), channel_id=1, source_target_pairs={{0,64},{64,128},{128,192},{192,0},{1,65},{65,129},{129,193},{193,1... | collective-permute-start | bytes 1572872 | tf_op jit(solution)/shard_map/ppermute | solution.py:114
  56.6 21.4 %collective-permute-start.5 = (bf16[256,1024]{1,0:T(8,128)(2,1)}, bf16[256,1024]{1,0:T(8,128)(2,1)}, u32[]{:S(2)}, u32[]{:S(2)}) collective-permute-start(bf16[256,1024]{1,0:T(8,128)(2,1)} %get-tuple-element.25), channel_id=1, source_target_pairs={{0,192},{64,0},{128,64},{192,128},{1,193},{65,1},{129,65},{193,129... | collective-permute-start | bytes 1572872 | tf_op jit(solution)/shard_map/ppermute | solution.py:114
  59.3 23.6 %collective-permute-start.4 = (bf16[256,1024]{1,0:T(8,128)(2,1)}, bf16[256,1024]{1,0:T(8,128)(2,1)S(1)}, u32[]{:S(2)}, u32[]{:S(2)}) collective-permute-start(bf16[256,1024]{1,0:T(8,128)(2,1)} %get-tuple-element.24), channel_id=1, source_target_pairs={{0,64},{64,128},{128,192},{192,0},{1,65},{65,129},{129,193},{193,1... | collective-permute-start | bytes 1572872 | tf_op jit(solution)/shard_map/ppermute | solution.py:114
  66.8 23.4 %collective-permute-start.8 = (bf16[256,1024]{1,0:T(8,128)(2,1)}, bf16[256,1024]{1,0:T(8,128)(2,1)S(1)}, u32[]{:S(2)}, u32[]{:S(2)}) collective-permute-start(bf16[256,1024]{1,0:T(8,128)(2,1)} %collective-permute-done.6), channel_id=1, source_target_pairs={{0,192},{64,0},{128,64},{192,128},{1,193},{65,1},{129,65},{193,129... | collective-permute-start | bytes 1572872 | tf_op jit(solution)/shard_map/ppermute | solution.py:114
  70.2 19.9 %collective-permute-start.7 = (bf16[256,1024]{1,0:T(8,128)(2,1)}, bf16[256,1024]{1,0:T(8,128)(2,1)S(1)}, u32[]{:S(2)}, u32[]{:S(2)}) collective-permute-start(bf16[256,1024]{1,0:T(8,128)(2,1)} %collective-permute-done.3), channel_id=1, source_target_pairs={{0,64},{64,128},{128,192},{192,0},{1,65},{65,129},{129,193},{193,1... | collective-permute-start | bytes 1572872 | tf_op jit(solution)/shard_map/ppermute | solution.py:114
  80.2 2.8 %copy-start.2 = (bf16[1,4096,384]{2,1,0:T(8,128)(2,1)S(1)}, bf16[1,4096,384]{2,1,0:T(8,128)(2,1)}, u32[]{:S(2)}) copy-start(bf16[1,4096,384]{2,1,0:T(8,128)(2,1)} %param.10) | copy-start | bytes 9437188
  83.0 7.3 %copy-start.1 = (f32[512,384]{1,0:T(8,128)S(1)}, f32[512,384]{1,0:T(8,128)}, u32[]{:S(2)}) copy-start(f32[512,384]{1,0:T(8,128)} %fusion.17) | copy-start | bytes 2359300
  90.2 1.1 copy-start.4
  92.9 11.1 %collective-permute-start.9 = (bf16[512,384]{1,0:T(8,128)(2,1)}, bf16[512,384]{1,0:T(8,128)(2,1)S(1)}, u32[]{:S(2)}, u32[]{:S(2)}) collective-permute-start(bf16[512,384]{1,0:T(8,128)(2,1)} %multiply_convert_fusion), channel_id=1, source_target_pairs={{0,64},{64,128},{128,192},{192,0},{1,65},{65,129},{129,193},{193,1... | collective-permute-start | bytes 1179656 | tf_op jit(solution)/shard_map/ppermute | solution.py:114
  93.3 12.6 %collective-permute-start.10 = (bf16[512,384]{1,0:T(8,128)(2,1)}, bf16[512,384]{1,0:T(8,128)(2,1)S(1)}, u32[]{:S(2)}, u32[]{:S(2)}) collective-permute-start(bf16[512,384]{1,0:T(8,128)(2,1)} %multiply_convert_fusion), channel_id=1, source_target_pairs={{0,192},{64,0},{128,64},{192,128},{1,193},{65,1},{129,65},{193,129... | collective-permute-start | bytes 1179656 | tf_op jit(solution)/shard_map/ppermute | solution.py:114
  97.5 16.0 %collective-permute-start.11 = (bf16[512,384]{1,0:T(8,128)(2,1)}, bf16[512,384]{1,0:T(8,128)(2,1)S(1)}, u32[]{:S(2)}, u32[]{:S(2)}) collective-permute-start(bf16[512,384]{1,0:T(8,128)(2,1)} %multiply_convert_fusion), channel_id=1, source_target_pairs={{0,128},{64,192},{128,0},{192,64},{1,129},{65,193},{129,1},{193,65... | collective-permute-start | bytes 1179656 | tf_op jit(solution)/shard_map/ppermute | solution.py:114
  107.7 47.9 %copy-start.3 = (bf16[512,64]{1,0:T(8,128)(2,1)S(1)}, bf16[512,64]{1,0:T(8,128)(2,1)}, u32[]{:S(2)}) copy-start(bf16[512,64]{1,0:T(8,128)(2,1)} %get-tuple-element.18) | copy-start | bytes 196612

commit v10 on v9

--- a/solution.py
+++ b/solution.py
@@ -150,12 +150,15 @@
         g, u = k_part(halves, d)
         gate, up = gate + g, up + u
     hidden = (jax.nn.silu(gate) * up).astype(BF)
-    near = [send(hidden, d) for d in (1, sections - 1)]
+    a, b = hidden[:half], hidden[half:]
+    r_a, l_b = to_right(a), to_left(b)
     out = dot(hidden, lax.dynamic_slice_in_dim(w_down[0], s * quarter, quarter, axis=1))
-    far = send(lax.optimization_barrier((hidden, out))[0], 2)
-    for block, down in zip(near, (downs[0], downs[2])):
-        out = out + dot(block, down)
-    out = out + dot(far, downs[1])
+    a_later, b_later, _ = lax.optimization_barrier((a, b, out))
+    r_b, l_a = to_right(b_later), to_left(a_later)
+    across = jnp.concatenate([to_right(r_a), to_left(l_b)], axis=0)
+    out = out + dot(jnp.concatenate([r_a, r_b], axis=0), downs[0])
+    out = out + dot(jnp.concatenate([l_a, l_b], axis=0), downs[2])
+    out = out + dot(across, downs[1])
     returned = exchange(out.astype(BF))
     both = lax.dot_general(
         spread, returned, (((0,), (0,)), ((), ())), preferred_element_type=F32

time: 158 us -> 152 us (0.962)
  waiting for transfers between devices: 54.5 us -> 46.3 us
  starting transfers between devices: 30.2 us -> 33.9 us
    ppermute x12 -> x15, waiting for transfers between devices: 31.5 us -> 23.3 us  [send(): lax.ppermute(v, 'section', [(k, (k + d) % sections) for k in range(sectio...]
    ppermute x12 -> x15, starting transfers between devices: 16.9 us -> 20.5 us  [send(): lax.ppermute(v, 'section', [(k, (k + d) % sections) for k in range(sectio...]
  transfers between devices with their start and end apart: 13 -> 16, of which waited for: 6 -> 7; matrix products, arithmetic and copies ran while one was open for 14% -> 14% of each run, Pallas kernels for 0% -> 0%
where the time goes in v10:
time: 152 us; the launch traced here: 151 us
  waiting for transfers between devices  46.3 us (30%)
  blocking collectives  40 us (26%)
  starting transfers between devices  33.9 us (22%)
  matrix products  19.3 us (13%)
  local copies, waits for them, and re-layouts  6 us (4%)
  Pallas kernels  4.66 us (3%)
    all_to_all x1, blocking collectives, exchange(): lax.all_to_all(v.reshape(experts, cap, w), ED, split_axis=0, concat_axis=...  40 us
    ppermute x15, waiting for transfers between devices, send(): lax.ppermute(v, 'section', [(k, (k + d) % sections) for k in range(sectio...  23.3 us
    all_to_all x1, waiting for transfers between devices, exchange(): lax.all_to_all(v.reshape(experts, cap, w), ED, split_axis=0, concat_axis=...  23 us
    ppermute x15, starting transfers between devices, send(): lax.ppermute(v, 'section', [(k, (k + d) % sections) for k in range(sectio...  20.5 us
    dot_general x12, matrix products, dot(): return jnp.dot(a, b, preferred_element_type=F32)  19 us
    all_to_all x1, starting transfers between devices, exchange(): lax.all_to_all(v.reshape(experts, cap, w), ED, split_axis=0, concat_axis=...  13.4 us
    pallas_call x1, Pallas kernels, first(): pl.pallas_call(kernel, grid_spec=pltpu.PrefetchScalarGridSpec(num_scalar_...  4.66 us
  transfers between devices with their start and end apart: 16, of which 7 were waited for; matrix products, arithmetic and copies ran while one was open for 14% of the time, Pallas kernels for 0%

profile of v10, /device:TPU:1, one launch (start us, length us, event | category | flops | bytes accessed | tf_op | source)
XLA Modules:
  0.0 151.0 jit_solution(9955915015434014052)
XLA Ops:
  0.0 4.7 %first.1 = (bf16[512,1024]{1,0:T(8,128)(2,1)}, bf16[512,64]{1,0:T(8,128)(2,1)}, bf16[384,1024]{1,0:T(8,128)(2,1)}, bf16[384,1024]{1,0:T(8,128)(2,1)}, bf16[384,1024]{1,0:T(8,128)(2,1)}) custom-call(s32[1]{0:T(128)} %bitcast.s_ref, s32[8,32]{1,0:T(8,128)} %bitcast.54, f32[8,32]{1,0:T(8,128)} %bitcast.55, bf16[32,4096]{1,0:T(8,128)(2,1)} %tokens_ref.1, ...), custom_call_target="tpu_custom_call" | custom-call | flops 33554432 | bytes 5767168 | tf_op jit(solution)/shard_map/first/pallas_call | solution.py:72
  4.7 13.4 %all-to-all-start = ((bf16[64,8,1024]{2,1,0:T(8,128)(2,1)}), bf16[64,8,1024]{2,1,0:T(8,128)(2,1)}, u32[]{:S(2)}, u32[]{:S(2)}) async-start(bf16[64,8,1024]{2,1,0:T(8,128)(2,1)} %bitcast.53), calls=%async_computation | async-start | bytes 2097152 | tf_op jit(solution)/shard_map/all_to_all | solution.py:124
  18.0 1.3 collective-permute-start
  19.3 2.5 %collective-permute-start.1 = (bf16[384,1024]{1,0:T(8,128)(2,1)}, bf16[384,1024]{1,0:T(8,128)(2,1)}, u32[]{:S(2)}, u32[]{:S(2)}) collective-permute-start(bf16[384,1024]{1,0:T(8,128)(2,1)} %get-tuple-element.22), channel_id=1, source_target_pairs={{0,128},{64,192},{128,0},{192,64},{1,129},{65,193},{129,1},{193,65... | collective-permute-start | bytes 2359304 | tf_op jit(solution)/shard_map/ppermute | solution.py:114
  21.8 1.2 collective-permute-start.2
  22.9 23.0 %all-to-all-done = bf16[64,8,1024]{2,1,0:T(8,128)(2,1)} async-done(((bf16[64,8,1024]{2,1,0:T(8,128)(2,1)}), bf16[64,8,1024]{2,1,0:T(8,128)(2,1)}, u32[]{:S(2)}, u32[]{:S(2)}) %all-to-all-start) | async-done | bytes 1048608 | tf_op jit(solution)/shard_map/all_to_all | solution.py:124
  45.9 2.2 %slice_bitcast_fusion = (bf16[256,1024]{1,0:T(8,128)(2,1)}, bf16[256,1024]{1,0:T(8,128)(2,1)}) fusion(bf16[64,8,1024]{2,1,0:T(8,128)(2,1)} %all-to-all-done), kind=kLoop, calls=%fused_computation.33 | loop fusion | bytes 2097152 | tf_op jit(solution)/shard_map/slice | solution.py:143
  48.2 2.5 %collective-permute-start.6 = (bf16[256,1024]{1,0:T(8,128)(2,1)}, bf16[256,1024]{1,0:T(8,128)(2,1)}, u32[]{:S(2)}, u32[]{:S(2)}) collective-permute-start(bf16[256,1024]{1,0:T(8,128)(2,1)} %get-tuple-element.25), channel_id=1, source_target_pairs={{0,192},{64,0},{128,64},{192,128},{1,193},{65,1},{129,65},{193,129... | collective-permute-start | bytes 1572872 | tf_op jit(solution)/shard_map/ppermute | solution.py:114
  50.7 3.0 %fusion.15 = f32[512,384]{1,0:T(8,128)} fusion(bf16[1,4096,384]{2,1,0:T(8,128)(2,1)} %param.10, s32[]{:T(128)S(6)} %select_n.19, bf16[256,1024]{1,0:T(8,128)(2,1)} %get-tuple-element.25, bf16[256,1024]{1,0:T(8,128)(2,1)} %get-tuple-element.26), kind=kOutput, calls=%fused_computation.19 | convolution fusion | flops 404750336 | bytes 2621444 | tf_op jit(solution)/shard_map/dot_general | solution.py:16
  53.7 2.8 %fusion.17 = f32[512,384]{1,0:T(8,128)} fusion(bf16[1,4096,384]{2,1,0:T(8,128)(2,1)S(1)} %copy-done, s32[]{:T(128)S(6)} %select_n.19, bf16[256,1024]{1,0:T(8,128)(2,1)} %get-tuple-element.25, bf16[256,1024]{1,0:T(8,128)(2,1)} %get-tuple-element.26), kind=kOutput, calls=%fused_computation.21 | convolution fusion | flops 404750336 | bytes 2621444 | tf_op jit(solution)/shard_map/dot_general | solution.py:16
  56.5 2.8 %collective-permute-start.5 = (bf16[256,1024]{1,0:T(8,128)(2,1)}, bf16[256,1024]{1,0:T(8,128)(2,1)}, u32[]{:S(2)}, u32[]{:S(2)}) collective-permute-start(bf16[256,1024]{1,0:T(8,128)(2,1)} %get-tuple-element.26), channel_id=1, source_target_pairs={{0,192},{64,0},{128,64},{192,128},{1,193},{65,1},{129,65},{193,129... | collective-permute-start | bytes 1572872 | tf_op jit(solution)/shard_map/ppermute | solution.py:114
  59.3 7.5 %collective-permute-done.6 = bf16[256,1024]{1,0:T(8,128)(2,1)} collective-permute-done((bf16[256,1024]{1,0:T(8,128)(2,1)}, bf16[256,1024]{1,0:T(8,128)(2,1)}, u32[]{:S(2)}, u32[]{:S(2)}) %collective-permute-start.6) | collective-permute-done | bytes 524320 | tf_op jit(solution)/shard_map/ppermute | solution.py:114
  66.8 3.4 %collective-permute-start.8 = (bf16[256,1024]{1,0:T(8,128)(2,1)}, bf16[256,1024]{1,0:T(8,128)(2,1)S(1)}, u32[]{:S(2)}, u32[]{:S(2)}) collective-permute-start(bf16[256,1024]{1,0:T(8,128)(2,1)} %collective-permute-done.6), channel_id=1, source_target_pairs={{0,192},{64,0},{128,64},{192,128},{1,193},{65,1},{129,65},{193,129... | collective-permute-start | bytes 1572872 | tf_op jit(solution)/shard_map/ppermute | solution.py:114
  71.3 6.7 %collective-permute-done.5 = bf16[256,1024]{1,0:T(8,128)(2,1)} collective-permute-done((bf16[256,1024]{1,0:T(8,128)(2,1)}, bf16[256,1024]{1,0:T(8,128)(2,1)}, u32[]{:S(2)}, u32[]{:S(2)}) %collective-permute-start.5) | collective-permute-done | bytes 524320 | tf_op jit(solution)/shard_map/ppermute | solution.py:114
  80.2 2.0 %fusion.6 = f32[512,384]{1,0:T(8,128)S(1)} fusion(bf16[512,1024]{1,0:T(8,128)(2,1)S(1)} %constant_dynamic-update-slice_fusion.2, bf16[1,4096,384]{2,1,0:T(8,128)(2,1)} %param.10, s32[]{:T(128)S(6)} %select_n.21), kind=kOutput, calls=%fused_computation.10 | convolution fusion | flops 402653184 | bytes 2621444 | tf_op jit(solution)/shard_map/dot_general | solution.py:16
  84.4 5.7 %collective-permute-done.7 = bf16[256,1024]{1,0:T(8,128)(2,1)S(1)} collective-permute-done((bf16[256,1024]{1,0:T(8,128)(2,1)}, bf16[256,1024]{1,0:T(8,128)(2,1)S(1)}, u32[]{:S(2)}, u32[]{:S(2)}) %collective-permute-start.7) | collective-permute-done | bytes 524320 | tf_op jit(solution)/shard_map/ppermute | solution.py:114
  92.6 2.3 %collective-permute-start.12 = (bf16[256,384]{1,0:T(8,128)(2,1)S(1)}, bf16[256,384]{1,0:T(8,128)(2,1)S(1)}, u32[]{:S(2)}, u32[]{:S(2)}) collective-permute-start(bf16[256,384]{1,0:T(8,128)(2,1)S(1)} %get-tuple-element.28), channel_id=1, source_target_pairs={{0,192},{64,0},{128,64},{192,128},{1,193},{65,1},{129,65},{193,129... | collective-permute-start | bytes 589832 | tf_op jit(solution)/shard_map/ppermute | solution.py:114
  94.9 1.8 %fusion.3 = f32[512,1024]{1,0:T(8,128)S(1)} fusion(bf16[512,384]{1,0:T(8,128)(2,1)S(1)} %multiply_convert_fusion, bf16[1,384,4096]{2,1,0:T(8,128)(2,1)} %down_ref.1, s32[]{:T(128)S(6)} %select_n.23), kind=kOutput, calls=%fused_computation.7 | convolution fusion | flops 402653184 | bytes 3276804 | tf_op jit(solution)/shard_map/dot_general | solution.py:16
  98.9 2.7 %collective-permute-start.14 = (bf16[256,384]{1,0:T(8,128)(2,1)S(1)}, bf16[256,384]{1,0:T(8,128)(2,1)S(1)}, u32[]{:S(2)}, u32[]{:S(2)}) collective-permute-start(bf16[256,384]{1,0:T(8,128)(2,1)S(1)} %collective-permute-done.12), channel_id=1, source_target_pairs={{0,192},{64,0},{128,64},{192,128},{1,193},{65,1},{129,65},{193,129... | collective-permute-start | bytes 589832 | tf_op jit(solution)/shard_map/ppermute | solution.py:114
  102.4 1.8 %fusion.32 = f32[512,1024]{1,0:T(8,128)S(1)} fusion(bf16[384,1024]{1,0:T(8,128)(2,1)} %collective-permute-done.2, bf16[256,384]{1,0:T(8,128)(2,1)S(1)} %collective-permute-done.12, bf16[256,384]{1,0:T(8,128)(2,1)S(1)} %collective-permute-done.11), kind=kOutput, calls=%fused_computation.39 | convolution fusion | flops 403439616 | bytes 3276800 | tf_op jit(solution)/shard_map/dot_general | solution.py:16
  104.3 1.8 %fusion.28 = f32[512,1024]{1,0:T(8,128)S(1)} fusion(bf16[384,1024]{1,0:T(8,128)(2,1)} %collective-permute-done, bf16[256,384]{1,0:T(8,128)(2,1)S(1)} %collective-permute-done.10, bf16[256,384]{1,0:T(8,128)(2,1)S(1)} %collective-permute-done.9), kind=kOutput, calls=%fused_computation.35 | convolution fusion | flops 403439616 | bytes 3276800 | tf_op jit(solution)/shard_map/dot_general | solution.py:16
  106.1 2.0 %collective-permute-done.13 = bf16[256,384]{1,0:T(8,128)(2,1)S(1)} collective-permute-done((bf16[256,384]{1,0:T(8,128)(2,1)S(1)}, bf16[256,384]{1,0:T(8,128)(2,1)S(1)}, u32[]{:S(2)}, u32[]{:S(2)}) %collective-permute-start.13) | collective-permute-done | bytes 196640 | tf_op jit(solution)/shard_map/ppermute | solution.py:114
  108.2 1.9 %fusion = bf16[64,8,1024]{2,1,0:T(8,128)(2,1)S(1)} fusion(bf16[384,1024]{1,0:T(8,128)(2,1)} %collective-permute-done.1, f32[512,1024]{1,0:T(8,128)S(1)} %fusion.32, f32[512,1024]{1,0:T(8,128)S(1)} %fusion.3, f32[512,1024]{1,0:T(8,128)S(1)} %fusion.28, bf16[256,384]{1,0:T(8,128)(2,1)S(1)} %collective-permute-done.14, ...), kind=kOutput, calls=%fused_computation.1 | convolution fusion | flops 405536768 | bytes 8519680 | tf_op jit(solution)/shard_map/dot_general | solution.py:16
  110.1 40.0 %all_to_all.10 = bf16[64,8,1024]{2,1,0:T(8,128)(2,1)S(1)} all-to-all(bf16[64,8,1024]{2,1,0:T(8,128)(2,1)S(1)} %fusion), channel_id=1, replica_groups=mesh['section'=4,'expert'=32,'dp'=2] {'expert','dp'}, dimensions={0} | all-to-all | bytes 2097152 | tf_op jit(solution)/shard_map/all_to_all | solution.py:124
  (42 shorter events, 11.9 us)
Async XLA Ops:
  0.0 53.7 %copy-start = (bf16[1,4096,384]{2,1,0:T(8,128)(2,1)S(1)}, bf16[1,4096,384]{2,1,0:T(8,128)(2,1)}, u32[]{:S(2)}) copy-start(bf16[1,4096,384]{2,1,0:T(8,128)(2,1)} %param.9) | copy-start | bytes 9437188
  4.7 41.3 %all-to-all-start = ((bf16[64,8,1024]{2,1,0:T(8,128)(2,1)}), bf16[64,8,1024]{2,1,0:T(8,128)(2,1)}, u32[]{:S(2)}, u32[]{:S(2)}) async-start(bf16[64,8,1024]{2,1,0:T(8,128)(2,1)} %bitcast.53), calls=%async_computation | async-start | bytes 2097152 | tf_op jit(solution)/shard_map/all_to_all | solution.py:124
  18.0 38.5 %collective-permute-start = (bf16[384,1024]{1,0:T(8,128)(2,1)}, bf16[384,1024]{1,0:T(8,128)(2,1)}, u32[]{:S(2)}, u32[]{:S(2)}) collective-permute-start(bf16[384,1024]{1,0:T(8,128)(2,1)} %get-tuple-element.21), channel_id=1, source_target_pairs={{0,64},{64,128},{128,192},{192,0},{1,65},{65,129},{129,193},{193,1... | collective-permute-start | bytes 2359304 | tf_op jit(solution)/shard_map/ppermute | solution.py:114
  19.3 37.2 %collective-permute-start.1 = (bf16[384,1024]{1,0:T(8,128)(2,1)}, bf16[384,1024]{1,0:T(8,128)(2,1)}, u32[]{:S(2)}, u32[]{:S(2)}) collective-permute-start(bf16[384,1024]{1,0:T(8,128)(2,1)} %get-tuple-element.22), channel_id=1, source_target_pairs={{0,128},{64,192},{128,0},{192,64},{1,129},{65,193},{129,1},{193,65... | collective-permute-start | bytes 2359304 | tf_op jit(solution)/shard_map/ppermute | solution.py:114
  21.8 34.8 %collective-permute-start.2 = (bf16[384,1024]{1,0:T(8,128)(2,1)}, bf16[384,1024]{1,0:T(8,128)(2,1)}, u32[]{:S(2)}, u32[]{:S(2)}) collective-permute-start(bf16[384,1024]{1,0:T(8,128)(2,1)} %get-tuple-element.23), channel_id=1, source_target_pairs={{0,192},{64,0},{128,64},{192,128},{1,193},{65,1},{129,65},{193,129... | collective-permute-start | bytes 2359304 | tf_op jit(solution)/shard_map/ppermute | solution.py:114
  48.2 18.6 %collective-permute-start.6 = (bf16[256,1024]{1,0:T(8,128)(2,1)}, bf16[256,1024]{1,0:T(8,128)(2,1)}, u32[]{:S(2)}, u32[]{:S(2)}) collective-permute-start(bf16[256,1024]{1,0:T(8,128)(2,1)} %get-tuple-element.25), channel_id=1, source_target_pairs={{0,192},{64,0},{128,64},{192,128},{1,193},{65,1},{129,65},{193,129... | collective-permute-start | bytes 1572872 | tf_op jit(solution)/shard_map/ppermute | solution.py:114
  50.7 19.5 %collective-permute-start.3 = (bf16[256,1024]{1,0:T(8,128)(2,1)}, bf16[256,1024]{1,0:T(8,128)(2,1)}, u32[]{:S(2)}, u32[]{:S(2)}) collective-permute-start(bf16[256,1024]{1,0:T(8,128)(2,1)} %get-tuple-element.26), channel_id=1, source_target_pairs={{0,64},{64,128},{128,192},{192,0},{1,65},{65,129},{129,193},{193,1... | collective-permute-start | bytes 1572872 | tf_op jit(solution)/shard_map/ppermute | solution.py:114
  56.5 21.4 %collective-permute-start.5 = (bf16[256,1024]{1,0:T(8,128)(2,1)}, bf16[256,1024]{1,0:T(8,128)(2,1)}, u32[]{:S(2)}, u32[]{:S(2)}) collective-permute-start(bf16[256,1024]{1,0:T(8,128)(2,1)} %get-tuple-element.26), channel_id=1, source_target_pairs={{0,192},{64,0},{128,64},{192,128},{1,193},{65,1},{129,65},{193,129... | collective-permute-start | bytes 1572872 | tf_op jit(solution)/shard_map/ppermute | solution.py:114
  59.3 23.6 %collective-permute-start.4 = (bf16[256,1024]{1,0:T(8,128)(2,1)}, bf16[256,1024]{1,0:T(8,128)(2,1)S(1)}, u32[]{:S(2)}, u32[]{:S(2)}) collective-permute-start(bf16[256,1024]{1,0:T(8,128)(2,1)} %get-tuple-element.25), channel_id=1, source_target_pairs={{0,64},{64,128},{128,192},{192,0},{1,65},{65,129},{129,193},{193,1... | collective-permute-start | bytes 1572872 | tf_op jit(solution)/shard_map/ppermute | solution.py:114
  66.8 23.4 %collective-permute-start.8 = (bf16[256,1024]{1,0:T(8,128)(2,1)}, bf16[256,1024]{1,0:T(8,128)(2,1)S(1)}, u32[]{:S(2)}, u32[]{:S(2)}) collective-permute-start(bf16[256,1024]{1,0:T(8,128)(2,1)} %collective-permute-done.6), channel_id=1, source_target_pairs={{0,192},{64,0},{128,64},{192,128},{1,193},{65,1},{129,65},{193,129... | collective-permute-start | bytes 1572872 | tf_op jit(solution)/shard_map/ppermute | solution.py:114
  70.2 19.9 %collective-permute-start.7 = (bf16[256,1024]{1,0:T(8,128)(2,1)}, bf16[256,1024]{1,0:T(8,128)(2,1)S(1)}, u32[]{:S(2)}, u32[]{:S(2)}) collective-permute-start(bf16[256,1024]{1,0:T(8,128)(2,1)} %collective-permute-done.3), channel_id=1, source_target_pairs={{0,64},{64,128},{128,192},{192,0},{1,65},{65,129},{129,193},{193,1... | collective-permute-start | bytes 1572872 | tf_op jit(solution)/shard_map/ppermute | solution.py:114
  80.1 2.8 %copy-start.2 = (bf16[1,4096,384]{2,1,0:T(8,128)(2,1)S(1)}, bf16[1,4096,384]{2,1,0:T(8,128)(2,1)}, u32[]{:S(2)}) copy-start(bf16[1,4096,384]{2,1,0:T(8,128)(2,1)} %param.10) | copy-start | bytes 9437188
  83.0 7.3 %copy-start.1 = (f32[512,384]{1,0:T(8,128)S(1)}, f32[512,384]{1,0:T(8,128)}, u32[]{:S(2)}) copy-start(f32[512,384]{1,0:T(8,128)} %fusion.17) | copy-start | bytes 2359300
  90.1 1.1 copy-start.4
  92.2 6.8 %collective-permute-start.9 = (bf16[256,384]{1,0:T(8,128)(2,1)S(1)}, bf16[256,384]{1,0:T(8,128)(2,1)S(1)}, u32[]{:S(2)}, u32[]{:S(2)}) collective-permute-start(bf16[256,384]{1,0:T(8,128)(2,1)S(1)} %get-tuple-element.30), channel_id=1, source_target_pairs={{0,64},{64,128},{128,192},{192,0},{1,65},{65,129},{129,193},{193,1... | collective-permute-start | bytes 589832 | tf_op jit(solution)/shard_map/ppermute | solution.py:114
  92.6 6.3 %collective-permute-start.12 = (bf16[256,384]{1,0:T(8,128)(2,1)S(1)}, bf16[256,384]{1,0:T(8,128)(2,1)S(1)}, u32[]{:S(2)}, u32[]{:S(2)}) collective-permute-start(bf16[256,384]{1,0:T(8,128)(2,1)S(1)} %get-tuple-element.28), channel_id=1, source_target_pairs={{0,192},{64,0},{128,64},{192,128},{1,193},{65,1},{129,65},{193,129... | collective-permute-start | bytes 589832 | tf_op jit(solution)/shard_map/ppermute | solution.py:114
  96.8 5.6 %collective-permute-start.11 = (bf16[256,384]{1,0:T(8,128)(2,1)S(1)}, bf16[256,384]{1,0:T(8,128)(2,1)S(1)}, u32[]{:S(2)}, u32[]{:S(2)}) collective-permute-start(bf16[256,384]{1,0:T(8,128)(2,1)S(1)} %get-tuple-element.30), channel_id=1, source_target_pairs={{0,192},{64,0},{128,64},{192,128},{1,193},{65,1},{129,65},{193,129... | collective-permute-start | bytes 589832 | tf_op jit(solution)/shard_map/ppermute | solution.py:114
  97.7 6.6 %collective-permute-start.10 = (bf16[256,384]{1,0:T(8,128)(2,1)S(1)}, bf16[256,384]{1,0:T(8,128)(2,1)S(1)}, u32[]{:S(2)}, u32[]{:S(2)}) collective-permute-start(bf16[256,384]{1,0:T(8,128)(2,1)S(1)} %get-tuple-element.28), channel_id=1, source_target_pairs={{0,64},{64,128},{128,192},{192,0},{1,65},{65,129},{129,193},{193,1... | collective-permute-start | bytes 589832 | tf_op jit(solution)/shard_map/ppermute | solution.py:114
  98.9 9.2 %collective-permute-start.13 = (bf16[256,384]{1,0:T(8,128)(2,1)S(1)}, bf16[256,384]{1,0:T(8,128)(2,1)S(1)}, u32[]{:S(2)}, u32[]{:S(2)}) collective-permute-start(bf16[256,384]{1,0:T(8,128)(2,1)S(1)} %collective-permute-done.9), channel_id=1, source_target_pairs={{0,64},{64,128},{128,192},{192,0},{1,65},{65,129},{129,193},{193,1... | collective-permute-start | bytes 589832 | tf_op jit(solution)/shard_map/ppermute | solution.py:114
  98.9 9.2 %collective-permute-start.14 = (bf16[256,384]{1,0:T(8,128)(2,1)S(1)}, bf16[256,384]{1,0:T(8,128)(2,1)S(1)}, u32[]{:S(2)}, u32[]{:S(2)}) collective-permute-start(bf16[256,384]{1,0:T(8,128)(2,1)S(1)} %collective-permute-done.12), channel_id=1, source_target_pairs={{0,192},{64,0},{128,64},{192,128},{1,193},{65,1},{129,65},{193,129... | collective-permute-start | bytes 589832 | tf_op jit(solution)/shard_map/ppermute | solution.py:114
  106.1 43.9 %copy-start.3 = (bf16[512,64]{1,0:T(8,128)(2,1)S(1)}, bf16[512,64]{1,0:T(8,128)(2,1)}, u32[]{:S(2)}) copy-start(bf16[512,64]{1,0:T(8,128)(2,1)} %get-tuple-element.19) | copy-start | bytes 196612

commit v11 on v10

--- a/solution.py
+++ b/solution.py
@@ -27,21 +27,39 @@
     quarter = width // sections
     count = sections - 1
 
-    def kernel(s_ref, routing_ref, weights_ref, tokens_ref, down_ref, *refs):
-        rows_ref, spread_ref = refs[:2]
-        cuts, bufs = refs[2 : 2 + count], refs[2 + count]
-        in_sem, out_sem = refs[3 + count], refs[4 + count]
+    parts = 2
+    piece = hid // parts
+
+    def kernel(s_ref, routing_hbm, weights_hbm, tokens_hbm, down_hbm, *refs):
+        rows_hbm, spread_hbm = refs[:2]
+        cuts = refs[2 : 2 + count]
+        (bufs, routing_ref, weights_ref, tokens_ref, rows_ref, spread_ref) = refs[2 + count : -3]
+        in_sem, out_sem, small_sem = refs[-3:]
+
+        def columns(d):
+            start = lax.rem(s_ref[0] + d, sections) * quarter
+            return pl.ds(pl.multiple_of(start, 128), quarter)
+
+        small = [
+            pltpu.make_async_copy(routing_hbm, routing_ref, small_sem.at[0]),
+            pltpu.make_async_copy(weights_hbm, weights_ref, small_sem.at[1]),
+            pltpu.make_async_copy(tokens_hbm.at[:, columns(0)], tokens_ref, small_sem.at[2]),
+        ]
         ins, outs = [], []
         for d in range(count):
-            start = pl.multiple_of(lax.rem(s_ref[0] + d + 1, sections) * quarter, 128)
-            ins.append(
-                pltpu.make_async_copy(
-                    down_ref.at[0, :, pl.ds(start, quarter)], bufs.at[d], in_sem.at[d]
+            for p in range(parts):
+                n = d * parts + p
+                at = pl.ds(p * piece, piece)
+                ins.append(
+                    pltpu.make_async_copy(
+                        down_hbm.at[0, at, columns(d + 1)], bufs.at[n], in_sem.at[n]
+                    )
                 )
-            )
-            outs.append(pltpu.make_async_copy(bufs.at[d], cuts[d], out_sem.at[d]))
-        for c in ins:
+                outs.append(pltpu.make_async_copy(bufs.at[n], cuts[d].at[at, :], out_sem.at[n]))
+        for c in small + ins:
             c.start()
+        for c in small:
+            c.wait()
         slot = lax.broadcasted_iota(jnp.int32, (slots, toks), 0)
         expert, order = lax.div(slot, cap), lax.rem(slot, cap)
         named = jnp.zeros((slots, toks), F32)
@@ -50,9 +68,6 @@
             hit = routing_ref[k : k + 1, :] == expert
             named = jnp.where(hit, 1.0, named)
             weight = jnp.where(hit, weights_ref[k : k + 1, :], weight)
-        for c_in, c_out in zip(ins, outs):
-            c_in.wait()
-            c_out.start()
         before = (
             lax.broadcasted_iota(jnp.int32, (toks, toks), 0)
             < lax.broadcasted_iota(jnp.int32, (toks, toks), 1)
@@ -60,38 +75,39 @@
         earlier = dot(named.astype(BF), jnp.where(before, 1.0, 0.0).astype(BF))
         place = jnp.where(earlier == order.astype(F32), named, 0.0)
         rows_ref[...] = dot(place.astype(BF), tokens_ref[...]).astype(BF)
+        rows_out = pltpu.make_async_copy(rows_ref, rows_hbm, small_sem.at[3])
+        rows_out.start()
+        for c_in, c_out in zip(ins, outs):
+            c_in.wait()
+            c_out.start()
         spread = place * weight
         high = spread.astype(BF)
         spread_ref[...] = jnp.concatenate([high, (spread - high.astype(F32)).astype(BF)], axis=1)
-        for c in outs:
+        spread_out = pltpu.make_async_copy(spread_ref, spread_hbm, small_sem.at[4])
+        spread_out.start()
+        for c in outs + [rows_out, spread_out]:
             c.wait()
-
-    def whole(*shape):
-        return pl.BlockSpec(shape, lambda i, s: (0, 0))
 
     rows, spread, *cut = pl.pallas_call(
         kernel,
-        grid_spec=pltpu.PrefetchScalarGridSpec(
-            num_scalar_prefetch=1,
-            grid=(1,),
-            in_specs=[
-                whole(fanout, toks),
-                whole(fanout, toks),
-                pl.BlockSpec((toks, quarter), lambda i, s: (0, s[0])),
-                ANY,
-            ],
-            out_specs=[whole(slots, quarter), whole(slots, 2 * toks)] + [ANY] * count,
-            scratch_shapes=[
-                pltpu.VMEM((count, hid, quarter), BF),
-                pltpu.SemaphoreType.DMA((count,)),
-                pltpu.SemaphoreType.DMA((count,)),
-            ],
-        ),
+        in_specs=[pl.BlockSpec(memory_space=pltpu.SMEM)] + [ANY] * 4,
+        out_specs=[ANY] * (2 + count),
         out_shape=[
             jax.ShapeDtypeStruct((slots, quarter), BF),
             jax.ShapeDtypeStruct((slots, 2 * toks), BF),
         ]
         + [jax.ShapeDtypeStruct((hid, quarter), BF)] * count,
+        scratch_shapes=[
+            pltpu.VMEM((count * parts, piece, quarter), BF),
+            pltpu.VMEM((fanout, toks), jnp.int32),
+            pltpu.VMEM((fanout, toks), F32),
+            pltpu.VMEM((toks, quarter), BF),
+            pltpu.VMEM((slots, quarter), BF),
+            pltpu.VMEM((slots, 2 * toks), BF),
+            pltpu.SemaphoreType.DMA((count * parts,)),
+            pltpu.SemaphoreType.DMA((count * parts,)),
+            pltpu.SemaphoreType.DMA((5,)),
+        ],
         compiler_params=PARAMS,
         cost_estimate=cost(
             2 * slots * toks * quarter, 2 * slots * quarter + 4 * count * hid * quarter

time: 152 us -> 151 us (level)
  no operation moved by 1% of the time
where the time goes in v11:
time: 151 us
  waiting for transfers between devices  46.3 us (31%)
  blocking collectives  40 us (26%)
  starting transfers between devices  33.9 us (22%)
  matrix products  19.3 us (13%)
  local copies, waits for them, and re-layouts  6 us (4%)
  Pallas kernels  4.26 us (3%)
    all_to_all x1, blocking collectives, exchange(): lax.all_to_all(v.reshape(experts, cap, w), ED, split_axis=0, concat_axis=...  40 us
    ppermute x15, waiting for transfers between devices, send(): lax.ppermute(v, 'section', [(k, (k + d) % sections) for k in range(sectio...  23.3 us
    all_to_all x1, waiting for transfers between devices, exchange(): lax.all_to_all(v.reshape(experts, cap, w), ED, split_axis=0, concat_axis=...  23 us
    ppermute x15, starting transfers between devices, send(): lax.ppermute(v, 'section', [(k, (k + d) % sections) for k in range(sectio...  20.5 us
    dot_general x12, matrix products, dot(): return jnp.dot(a, b, preferred_element_type=F32)  19 us
    all_to_all x1, starting transfers between devices, exchange(): lax.all_to_all(v.reshape(experts, cap, w), ED, split_axis=0, concat_axis=...  13.4 us
    pallas_call x1, Pallas kernels, first(): pl.pallas_call(kernel, in_specs=[pl.BlockSpec(memory_space=pltpu.SMEM)] +...  4.26 us
  transfers between devices with their start and end apart: 16, of which 7 were waited for; matrix products, arithmetic and copies ran while one was open for 14% of the time, Pallas kernels for 0%

profile of v11, /device:TPU:1, one launch (start us, length us, event | category | flops | bytes accessed | tf_op | source)
XLA Modules:
  0.0 150.6 jit_solution(3271418385995404391)
XLA Ops:
  0.0 4.3 %first.1 = (bf16[512,1024]{1,0:T(8,128)(2,1)}, bf16[512,64]{1,0:T(8,128)(2,1)}, bf16[384,1024]{1,0:T(8,128)(2,1)}, bf16[384,1024]{1,0:T(8,128)(2,1)}, bf16[384,1024]{1,0:T(8,128)(2,1)}) custom-call(s32[1]{0:T(128)} %bitcast.s_ref, s32[8,32]{1,0:T(8,128)} %bitcast.54, f32[8,32]{1,0:T(8,128)} %bitcast.55, bf16[32,4096]{1,0:T(8,128)(2,1)} %tokens_hbm.1, ...), custom_call_target="tpu_custom_call" | custom-call | flops 33554432 | bytes 5767168 | tf_op jit(solution)/shard_map/first/pallas_call | solution.py:91
  4.3 13.4 %all-to-all-start = ((bf16[64,8,1024]{2,1,0:T(8,128)(2,1)}), bf16[64,8,1024]{2,1,0:T(8,128)(2,1)}, u32[]{:S(2)}, u32[]{:S(2)}) async-start(bf16[64,8,1024]{2,1,0:T(8,128)(2,1)} %bitcast.53), calls=%async_computation | async-start | bytes 2097152 | tf_op jit(solution)/shard_map/all_to_all | solution.py:140
  17.6 1.3 collective-permute-start
  18.9 2.4 %collective-permute-start.1 = (bf16[384,1024]{1,0:T(8,128)(2,1)}, bf16[384,1024]{1,0:T(8,128)(2,1)}, u32[]{:S(2)}, u32[]{:S(2)}) collective-permute-start(bf16[384,1024]{1,0:T(8,128)(2,1)} %get-tuple-element.22), channel_id=1, source_target_pairs={{0,128},{64,192},{128,0},{192,64},{1,129},{65,193},{129,1},{193,65... | collective-permute-start | bytes 2359304 | tf_op jit(solution)/shard_map/ppermute | solution.py:130
  21.4 1.2 collective-permute-start.2
  22.5 23.0 %all-to-all-done = bf16[64,8,1024]{2,1,0:T(8,128)(2,1)} async-done(((bf16[64,8,1024]{2,1,0:T(8,128)(2,1)}), bf16[64,8,1024]{2,1,0:T(8,128)(2,1)}, u32[]{:S(2)}, u32[]{:S(2)}) %all-to-all-start) | async-done | bytes 1048608 | tf_op jit(solution)/shard_map/all_to_all | solution.py:140
  45.5 2.2 %slice_bitcast_fusion = (bf16[256,1024]{1,0:T(8,128)(2,1)}, bf16[256,1024]{1,0:T(8,128)(2,1)}) fusion(bf16[64,8,1024]{2,1,0:T(8,128)(2,1)} %all-to-all-done), kind=kLoop, calls=%fused_computation.33 | loop fusion | bytes 2097152 | tf_op jit(solution)/shard_map/slice | solution.py:159
  47.8 2.5 %collective-permute-start.6 = (bf16[256,1024]{1,0:T(8,128)(2,1)}, bf16[256,1024]{1,0:T(8,128)(2,1)}, u32[]{:S(2)}, u32[]{:S(2)}) collective-permute-start(bf16[256,1024]{1,0:T(8,128)(2,1)} %get-tuple-element.25), channel_id=1, source_target_pairs={{0,192},{64,0},{128,64},{192,128},{1,193},{65,1},{129,65},{193,129... | collective-permute-start | bytes 1572872 | tf_op jit(solution)/shard_map/ppermute | solution.py:130
  50.3 3.0 %fusion.15 = f32[512,384]{1,0:T(8,128)} fusion(bf16[1,4096,384]{2,1,0:T(8,128)(2,1)} %param.10, s32[]{:T(128)S(6)} %select_n.19, bf16[256,1024]{1,0:T(8,128)(2,1)} %get-tuple-element.25, bf16[256,1024]{1,0:T(8,128)(2,1)} %get-tuple-element.26), kind=kOutput, calls=%fused_computation.19 | convolution fusion | flops 404750336 | bytes 2621444 | tf_op jit(solution)/shard_map/dot_general | solution.py:16
  53.3 2.8 %fusion.17 = f32[512,384]{1,0:T(8,128)} fusion(bf16[1,4096,384]{2,1,0:T(8,128)(2,1)S(1)} %copy-done, s32[]{:T(128)S(6)} %select_n.19, bf16[256,1024]{1,0:T(8,128)(2,1)} %get-tuple-element.25, bf16[256,1024]{1,0:T(8,128)(2,1)} %get-tuple-element.26), kind=kOutput, calls=%fused_computation.21 | convolution fusion | flops 404750336 | bytes 2621444 | tf_op jit(solution)/shard_map/dot_general | solution.py:16
  56.1 2.8 %collective-permute-start.5 = (bf16[256,1024]{1,0:T(8,128)(2,1)}, bf16[256,1024]{1,0:T(8,128)(2,1)}, u32[]{:S(2)}, u32[]{:S(2)}) collective-permute-start(bf16[256,1024]{1,0:T(8,128)(2,1)} %get-tuple-element.26), channel_id=1, source_target_pairs={{0,192},{64,0},{128,64},{192,128},{1,193},{65,1},{129,65},{193,129... | collective-permute-start | bytes 1572872 | tf_op jit(solution)/shard_map/ppermute | solution.py:130
  58.9 7.5 %collective-permute-done.6 = bf16[256,1024]{1,0:T(8,128)(2,1)} collective-permute-done((bf16[256,1024]{1,0:T(8,128)(2,1)}, bf16[256,1024]{1,0:T(8,128)(2,1)}, u32[]{:S(2)}, u32[]{:S(2)}) %collective-permute-start.6) | collective-permute-done | bytes 524320 | tf_op jit(solution)/shard_map/ppermute | solution.py:130
  66.3 3.4 %collective-permute-start.8 = (bf16[256,1024]{1,0:T(8,128)(2,1)}, bf16[256,1024]{1,0:T(8,128)(2,1)S(1)}, u32[]{:S(2)}, u32[]{:S(2)}) collective-permute-start(bf16[256,1024]{1,0:T(8,128)(2,1)} %collective-permute-done.6), channel_id=1, source_target_pairs={{0,192},{64,0},{128,64},{192,128},{1,193},{65,1},{129,65},{193,129... | collective-permute-start | bytes 1572872 | tf_op jit(solution)/shard_map/ppermute | solution.py:130
  70.9 6.7 %collective-permute-done.5 = bf16[256,1024]{1,0:T(8,128)(2,1)} collective-permute-done((bf16[256,1024]{1,0:T(8,128)(2,1)}, bf16[256,1024]{1,0:T(8,128)(2,1)}, u32[]{:S(2)}, u32[]{:S(2)}) %collective-permute-start.5) | collective-permute-done | bytes 524320 | tf_op jit(solution)/shard_map/ppermute | solution.py:130
  79.8 2.0 %fusion.6 = f32[512,384]{1,0:T(8,128)S(1)} fusion(bf16[512,1024]{1,0:T(8,128)(2,1)S(1)} %constant_dynamic-update-slice_fusion.2, bf16[1,4096,384]{2,1,0:T(8,128)(2,1)} %param.10, s32[]{:T(128)S(6)} %select_n.21), kind=kOutput, calls=%fused_computation.10 | convolution fusion | flops 402653184 | bytes 2621444 | tf_op jit(solution)/shard_map/dot_general | solution.py:16
  84.0 5.7 %collective-permute-done.7 = bf16[256,1024]{1,0:T(8,128)(2,1)S(1)} collective-permute-done((bf16[256,1024]{1,0:T(8,128)(2,1)}, bf16[256,1024]{1,0:T(8,128)(2,1)S(1)}, u32[]{:S(2)}, u32[]{:S(2)}) %collective-permute-start.7) | collective-permute-done | bytes 524320 | tf_op jit(solution)/shard_map/ppermute | solution.py:130
  92.2 2.3 %collective-permute-start.12 = (bf16[256,384]{1,0:T(8,128)(2,1)S(1)}, bf16[256,384]{1,0:T(8,128)(2,1)S(1)}, u32[]{:S(2)}, u32[]{:S(2)}) collective-permute-start(bf16[256,384]{1,0:T(8,128)(2,1)S(1)} %get-tuple-element.28), channel_id=1, source_target_pairs={{0,192},{64,0},{128,64},{192,128},{1,193},{65,1},{129,65},{193,129... | collective-permute-start | bytes 589832 | tf_op jit(solution)/shard_map/ppermute | solution.py:130
  94.5 1.8 %fusion.3 = f32[512,1024]{1,0:T(8,128)S(1)} fusion(bf16[512,384]{1,0:T(8,128)(2,1)S(1)} %multiply_convert_fusion, bf16[1,384,4096]{2,1,0:T(8,128)(2,1)} %down_hbm.1, s32[]{:T(128)S(6)} %select_n.23), kind=kOutput, calls=%fused_computation.7 | convolution fusion | flops 402653184 | bytes 3276804 | tf_op jit(solution)/shard_map/dot_general | solution.py:16
  98.5 2.7 %collective-permute-start.14 = (bf16[256,384]{1,0:T(8,128)(2,1)S(1)}, bf16[256,384]{1,0:T(8,128)(2,1)S(1)}, u32[]{:S(2)}, u32[]{:S(2)}) collective-permute-start(bf16[256,384]{1,0:T(8,128)(2,1)S(1)} %collective-permute-done.12), channel_id=1, source_target_pairs={{0,192},{64,0},{128,64},{192,128},{1,193},{65,1},{129,65},{193,129... | collective-permute-start | bytes 589832 | tf_op jit(solution)/shard_map/ppermute | solution.py:130
  102.0 1.8 %fusion.32 = f32[512,1024]{1,0:T(8,128)S(1)} fusion(bf16[384,1024]{1,0:T(8,128)(2,1)} %collective-permute-done.2, bf16[256,384]{1,0:T(8,128)(2,1)S(1)} %collective-permute-done.12, bf16[256,384]{1,0:T(8,128)(2,1)S(1)} %collective-permute-done.11), kind=kOutput, calls=%fused_computation.39 | convolution fusion | flops 403439616 | bytes 3276800 | tf_op jit(solution)/shard_map/dot_general | solution.py:16
  103.9 1.8 %fusion.28 = f32[512,1024]{1,0:T(8,128)S(1)} fusion(bf16[384,1024]{1,0:T(8,128)(2,1)} %collective-permute-done, bf16[256,384]{1,0:T(8,128)(2,1)S(1)} %collective-permute-done.10, bf16[256,384]{1,0:T(8,128)(2,1)S(1)} %collective-permute-done.9), kind=kOutput, calls=%fused_computation.35 | convolution fusion | flops 403439616 | bytes 3276800 | tf_op jit(solution)/shard_map/dot_general | solution.py:16
  105.7 2.0 %collective-permute-done.13 = bf16[256,384]{1,0:T(8,128)(2,1)S(1)} collective-permute-done((bf16[256,384]{1,0:T(8,128)(2,1)S(1)}, bf16[256,384]{1,0:T(8,128)(2,1)S(1)}, u32[]{:S(2)}, u32[]{:S(2)}) %collective-permute-start.13) | collective-permute-done | bytes 196640 | tf_op jit(solution)/shard_map/ppermute | solution.py:130
  107.8 1.9 %fusion = bf16[64,8,1024]{2,1,0:T(8,128)(2,1)S(1)} fusion(bf16[384,1024]{1,0:T(8,128)(2,1)} %collective-permute-done.1, f32[512,1024]{1,0:T(8,128)S(1)} %fusion.32, f32[512,1024]{1,0:T(8,128)S(1)} %fusion.3, f32[512,1024]{1,0:T(8,128)S(1)} %fusion.28, bf16[256,384]{1,0:T(8,128)(2,1)S(1)} %collective-permute-done.14, ...), kind=kOutput, calls=%fused_computation.1 | convolution fusion | flops 405536768 | bytes 8519680 | tf_op jit(solution)/shard_map/dot_general | solution.py:16
  109.7 40.0 %all_to_all.10 = bf16[64,8,1024]{2,1,0:T(8,128)(2,1)S(1)} all-to-all(bf16[64,8,1024]{2,1,0:T(8,128)(2,1)S(1)} %fusion), channel_id=1, replica_groups=mesh['section'=4,'expert'=32,'dp'=2] {'expert','dp'}, dimensions={0} | all-to-all | bytes 2097152 | tf_op jit(solution)/shard_map/all_to_all | solution.py:140
  (42 shorter events, 11.9 us)
Async XLA Ops:
  0.0 53.3 %copy-start = (bf16[1,4096,384]{2,1,0:T(8,128)(2,1)S(1)}, bf16[1,4096,384]{2,1,0:T(8,128)(2,1)}, u32[]{:S(2)}) copy-start(bf16[1,4096,384]{2,1,0:T(8,128)(2,1)} %param.9) | copy-start | bytes 9437188
  4.3 41.3 %all-to-all-start = ((bf16[64,8,1024]{2,1,0:T(8,128)(2,1)}), bf16[64,8,1024]{2,1,0:T(8,128)(2,1)}, u32[]{:S(2)}, u32[]{:S(2)}) async-start(bf16[64,8,1024]{2,1,0:T(8,128)(2,1)} %bitcast.53), calls=%async_computation | async-start | bytes 2097152 | tf_op jit(solution)/shard_map/all_to_all | solution.py:140
  17.6 38.5 %collective-permute-start = (bf16[384,1024]{1,0:T(8,128)(2,1)}, bf16[384,1024]{1,0:T(8,128)(2,1)}, u32[]{:S(2)}, u32[]{:S(2)}) collective-permute-start(bf16[384,1024]{1,0:T(8,128)(2,1)} %get-tuple-element.21), channel_id=1, source_target_pairs={{0,64},{64,128},{128,192},{192,0},{1,65},{65,129},{129,193},{193,1... | collective-permute-start | bytes 2359304 | tf_op jit(solution)/shard_map/ppermute | solution.py:130
  18.9 37.2 %collective-permute-start.1 = (bf16[384,1024]{1,0:T(8,128)(2,1)}, bf16[384,1024]{1,0:T(8,128)(2,1)}, u32[]{:S(2)}, u32[]{:S(2)}) collective-permute-start(bf16[384,1024]{1,0:T(8,128)(2,1)} %get-tuple-element.22), channel_id=1, source_target_pairs={{0,128},{64,192},{128,0},{192,64},{1,129},{65,193},{129,1},{193,65... | collective-permute-start | bytes 2359304 | tf_op jit(solution)/shard_map/ppermute | solution.py:130
  21.4 34.8 %collective-permute-start.2 = (bf16[384,1024]{1,0:T(8,128)(2,1)}, bf16[384,1024]{1,0:T(8,128)(2,1)}, u32[]{:S(2)}, u32[]{:S(2)}) collective-permute-start(bf16[384,1024]{1,0:T(8,128)(2,1)} %get-tuple-element.23), channel_id=1, source_target_pairs={{0,192},{64,0},{128,64},{192,128},{1,193},{65,1},{129,65},{193,129... | collective-permute-start | bytes 2359304 | tf_op jit(solution)/shard_map/ppermute | solution.py:130
  47.8 18.6 %collective-permute-start.6 = (bf16[256,1024]{1,0:T(8,128)(2,1)}, bf16[256,1024]{1,0:T(8,128)(2,1)}, u32[]{:S(2)}, u32[]{:S(2)}) collective-permute-start(bf16[256,1024]{1,0:T(8,128)(2,1)} %get-tuple-element.25), channel_id=1, source_target_pairs={{0,192},{64,0},{128,64},{192,128},{1,193},{65,1},{129,65},{193,129... | collective-permute-start | bytes 1572872 | tf_op jit(solution)/shard_map/ppermute | solution.py:130
  50.3 19.5 %collective-permute-start.3 = (bf16[256,1024]{1,0:T(8,128)(2,1)}, bf16[256,1024]{1,0:T(8,128)(2,1)}, u32[]{:S(2)}, u32[]{:S(2)}) collective-permute-start(bf16[256,1024]{1,0:T(8,128)(2,1)} %get-tuple-element.26), channel_id=1, source_target_pairs={{0,64},{64,128},{128,192},{192,0},{1,65},{65,129},{129,193},{193,1... | collective-permute-start | bytes 1572872 | tf_op jit(solution)/shard_map/ppermute | solution.py:130
  56.1 21.4 %collective-permute-start.5 = (bf16[256,1024]{1,0:T(8,128)(2,1)}, bf16[256,1024]{1,0:T(8,128)(2,1)}, u32[]{:S(2)}, u32[]{:S(2)}) collective-permute-start(bf16[256,1024]{1,0:T(8,128)(2,1)} %get-tuple-element.26), channel_id=1, source_target_pairs={{0,192},{64,0},{128,64},{192,128},{1,193},{65,1},{129,65},{193,129... | collective-permute-start | bytes 1572872 | tf_op jit(solution)/shard_map/ppermute | solution.py:130
  58.9 23.6 %collective-permute-start.4 = (bf16[256,1024]{1,0:T(8,128)(2,1)}, bf16[256,1024]{1,0:T(8,128)(2,1)S(1)}, u32[]{:S(2)}, u32[]{:S(2)}) collective-permute-start(bf16[256,1024]{1,0:T(8,128)(2,1)} %get-tuple-element.25), channel_id=1, source_target_pairs={{0,64},{64,128},{128,192},{192,0},{1,65},{65,129},{129,193},{193,1... | collective-permute-start | bytes 1572872 | tf_op jit(solution)/shard_map/ppermute | solution.py:130
  66.3 23.4 %collective-permute-start.8 = (bf16[256,1024]{1,0:T(8,128)(2,1)}, bf16[256,1024]{1,0:T(8,128)(2,1)S(1)}, u32[]{:S(2)}, u32[]{:S(2)}) collective-permute-start(bf16[256,1024]{1,0:T(8,128)(2,1)} %collective-permute-done.6), channel_id=1, source_target_pairs={{0,192},{64,0},{128,64},{192,128},{1,193},{65,1},{129,65},{193,129... | collective-permute-start | bytes 1572872 | tf_op jit(solution)/shard_map/ppermute | solution.py:130
  69.8 19.9 %collective-permute-start.7 = (bf16[256,1024]{1,0:T(8,128)(2,1)}, bf16[256,1024]{1,0:T(8,128)(2,1)S(1)}, u32[]{:S(2)}, u32[]{:S(2)}) collective-permute-start(bf16[256,1024]{1,0:T(8,128)(2,1)} %collective-permute-done.3), channel_id=1, source_target_pairs={{0,64},{64,128},{128,192},{192,0},{1,65},{65,129},{129,193},{193,1... | collective-permute-start | bytes 1572872 | tf_op jit(solution)/shard_map/ppermute | solution.py:130
  79.7 2.8 %copy-start.2 = (bf16[1,4096,384]{2,1,0:T(8,128)(2,1)S(1)}, bf16[1,4096,384]{2,1,0:T(8,128)(2,1)}, u32[]{:S(2)}) copy-start(bf16[1,4096,384]{2,1,0:T(8,128)(2,1)} %param.10) | copy-start | bytes 9437188
  82.5 7.3 %copy-start.1 = (f32[512,384]{1,0:T(8,128)S(1)}, f32[512,384]{1,0:T(8,128)}, u32[]{:S(2)}) copy-start(f32[512,384]{1,0:T(8,128)} %fusion.17) | copy-start | bytes 2359300
  89.7 1.1 copy-start.4
  91.8 6.8 %collective-permute-start.9 = (bf16[256,384]{1,0:T(8,128)(2,1)S(1)}, bf16[256,384]{1,0:T(8,128)(2,1)S(1)}, u32[]{:S(2)}, u32[]{:S(2)}) collective-permute-start(bf16[256,384]{1,0:T(8,128)(2,1)S(1)} %get-tuple-element.30), channel_id=1, source_target_pairs={{0,64},{64,128},{128,192},{192,0},{1,65},{65,129},{129,193},{193,1... | collective-permute-start | bytes 589832 | tf_op jit(solution)/shard_map/ppermute | solution.py:130
  92.2 6.3 %collective-permute-start.12 = (bf16[256,384]{1,0:T(8,128)(2,1)S(1)}, bf16[256,384]{1,0:T(8,128)(2,1)S(1)}, u32[]{:S(2)}, u32[]{:S(2)}) collective-permute-start(bf16[256,384]{1,0:T(8,128)(2,1)S(1)} %get-tuple-element.28), channel_id=1, source_target_pairs={{0,192},{64,0},{128,64},{192,128},{1,193},{65,1},{129,65},{193,129... | collective-permute-start | bytes 589832 | tf_op jit(solution)/shard_map/ppermute | solution.py:130
  96.4 5.6 %collective-permute-start.11 = (bf16[256,384]{1,0:T(8,128)(2,1)S(1)}, bf16[256,384]{1,0:T(8,128)(2,1)S(1)}, u32[]{:S(2)}, u32[]{:S(2)}) collective-permute-start(bf16[256,384]{1,0:T(8,128)(2,1)S(1)} %get-tuple-element.30), channel_id=1, source_target_pairs={{0,192},{64,0},{128,64},{192,128},{1,193},{65,1},{129,65},{193,129... | collective-permute-start | bytes 589832 | tf_op jit(solution)/shard_map/ppermute | solution.py:130
  97.3 6.6 %collective-permute-start.10 = (bf16[256,384]{1,0:T(8,128)(2,1)S(1)}, bf16[256,384]{1,0:T(8,128)(2,1)S(1)}, u32[]{:S(2)}, u32[]{:S(2)}) collective-permute-start(bf16[256,384]{1,0:T(8,128)(2,1)S(1)} %get-tuple-element.28), channel_id=1, source_target_pairs={{0,64},{64,128},{128,192},{192,0},{1,65},{65,129},{129,193},{193,1... | collective-permute-start | bytes 589832 | tf_op jit(solution)/shard_map/ppermute | solution.py:130
  98.5 9.2 %collective-permute-start.13 = (bf16[256,384]{1,0:T(8,128)(2,1)S(1)}, bf16[256,384]{1,0:T(8,128)(2,1)S(1)}, u32[]{:S(2)}, u32[]{:S(2)}) collective-permute-start(bf16[256,384]{1,0:T(8,128)(2,1)S(1)} %collective-permute-done.9), channel_id=1, source_target_pairs={{0,64},{64,128},{128,192},{192,0},{1,65},{65,129},{129,193},{193,1... | collective-permute-start | bytes 589832 | tf_op jit(solution)/shard_map/ppermute | solution.py:130
  98.5 9.2 %collective-permute-start.14 = (bf16[256,384]{1,0:T(8,128)(2,1)S(1)}, bf16[256,384]{1,0:T(8,128)(2,1)S(1)}, u32[]{:S(2)}, u32[]{:S(2)}) collective-permute-start(bf16[256,384]{1,0:T(8,128)(2,1)S(1)} %collective-permute-done.12), channel_id=1, source_target_pairs={{0,192},{64,0},{128,64},{192,128},{1,193},{65,1},{129,65},{193,129... | collective-permute-start | bytes 589832 | tf_op jit(solution)/shard_map/ppermute | solution.py:130
  105.7 43.9 %copy-start.3 = (bf16[512,64]{1,0:T(8,128)(2,1)S(1)}, bf16[512,64]{1,0:T(8,128)(2,1)}, u32[]{:S(2)}) copy-start(bf16[512,64]{1,0:T(8,128)(2,1)} %get-tuple-element.19) | copy-start | bytes 196612

commit v12 on v11

--- a/solution.py
+++ b/solution.py
@@ -172,8 +172,10 @@
     a_later, b_later, _ = lax.optimization_barrier((a, b, out))
     r_b, l_a = to_right(b_later), to_left(a_later)
     across = jnp.concatenate([to_right(r_a), to_left(l_b)], axis=0)
-    out = out + dot(jnp.concatenate([r_a, r_b], axis=0), downs[0])
-    out = out + dot(jnp.concatenate([l_a, l_b], axis=0), downs[2])
+    near = jnp.concatenate(
+        [jnp.concatenate([r_a, r_b], axis=0), jnp.concatenate([l_a, l_b], axis=0)], axis=1
+    )
+    out = out + dot(near, jnp.concatenate([downs[0], downs[2]], axis=0))
     out = out + dot(across, downs[1])
     returned = exchange(out.astype(BF))
     both = lax.dot_general(

time: 151 us -> 151 us (level)
    dot_general x12 -> x11, matrix products: 19 us -> 17.5 us  [dot(): return jnp.dot(a, b, preferred_element_type=F32)]
  transfers between devices with their start and end apart: 16 -> 16, of which waited for: 7 -> 6; matrix products, arithmetic and copies ran while one was open for 14% -> 13% of each run, Pallas kernels for 0% -> 0%
where the time goes in v12:
time: 151 us; the launch traced here: 150 us
  waiting for transfers between devices  45 us (30%)
  blocking collectives  40.3 us (27%)
  starting transfers between devices  35.1 us (23%)
  matrix products  17.8 us (12%)
  local copies, waits for them, and re-layouts  7.17 us (5%)
  Pallas kernels  4.26 us (3%)
    all_to_all x1, blocking collectives, exchange(): lax.all_to_all(v.reshape(experts, cap, w), ED, split_axis=0, concat_axis=...  40.3 us
    all_to_all x1, waiting for transfers between devices, exchange(): lax.all_to_all(v.reshape(experts, cap, w), ED, split_axis=0, concat_axis=...  23 us
    ppermute x15, waiting for transfers between devices, send(): lax.ppermute(v, 'section', [(k, (k + d) % sections) for k in range(sectio...  22 us
    ppermute x15, starting transfers between devices, send(): lax.ppermute(v, 'section', [(k, (k + d) % sections) for k in range(sectio...  21.7 us
    dot_general x11, matrix products, dot(): return jnp.dot(a, b, preferred_element_type=F32)  17.5 us
    all_to_all x1, starting transfers between devices, exchange(): lax.all_to_all(v.reshape(experts, cap, w), ED, split_axis=0, concat_axis=...  13.4 us
    pallas_call x1, Pallas kernels, first(): pl.pallas_call(kernel, in_specs=[pl.BlockSpec(memory_space=pltpu.SMEM)] +...  4.26 us
    unnamed x13, local copies, waits for them, and re-layouts  3.74 us
  transfers between devices with their start and end apart: 16, of which 6 were waited for; matrix products, arithmetic and copies ran while one was open for 13% of the time, Pallas kernels for 0%

profile of v12, /device:TPU:1, one launch (start us, length us, event | category | flops | bytes accessed | tf_op | source)
XLA Modules:
  0.0 150.4 jit_solution(169797231700232995)
XLA Ops:
  0.0 4.3 %first.1 = (bf16[512,1024]{1,0:T(8,128)(2,1)}, bf16[512,64]{1,0:T(8,128)(2,1)}, bf16[384,1024]{1,0:T(8,128)(2,1)}, bf16[384,1024]{1,0:T(8,128)(2,1)}, bf16[384,1024]{1,0:T(8,128)(2,1)}) custom-call(s32[1]{0:T(128)} %bitcast.s_ref, s32[8,32]{1,0:T(8,128)} %bitcast.52, f32[8,32]{1,0:T(8,128)} %bitcast.53, bf16[32,4096]{1,0:T(8,128)(2,1)} %tokens_hbm.1, ...), custom_call_target="tpu_custom_call" | custom-call | flops 33554432 | bytes 5767168 | tf_op jit(solution)/shard_map/first/pallas_call | solution.py:91
  4.3 13.4 %all-to-all-start = ((bf16[64,8,1024]{2,1,0:T(8,128)(2,1)}), bf16[64,8,1024]{2,1,0:T(8,128)(2,1)}, u32[]{:S(2)}, u32[]{:S(2)}) async-start(bf16[64,8,1024]{2,1,0:T(8,128)(2,1)} %bitcast.51), calls=%async_computation | async-start | bytes 2097152 | tf_op jit(solution)/shard_map/all_to_all | solution.py:140
  17.6 1.3 collective-permute-start
  18.9 2.4 %collective-permute-start.1 = (bf16[384,1024]{1,0:T(8,128)(2,1)}, bf16[384,1024]{1,0:T(8,128)(2,1)}, u32[]{:S(2)}, u32[]{:S(2)}) collective-permute-start(bf16[384,1024]{1,0:T(8,128)(2,1)} %get-tuple-element.22), channel_id=1, source_target_pairs={{0,128},{64,192},{128,0},{192,64},{1,129},{65,193},{129,1},{193,65... | collective-permute-start | bytes 2359304 | tf_op jit(solution)/shard_map/ppermute | solution.py:130
  21.4 1.2 collective-permute-start.2
  22.5 23.0 %all-to-all-done = bf16[64,8,1024]{2,1,0:T(8,128)(2,1)} async-done(((bf16[64,8,1024]{2,1,0:T(8,128)(2,1)}), bf16[64,8,1024]{2,1,0:T(8,128)(2,1)}, u32[]{:S(2)}, u32[]{:S(2)}) %all-to-all-start) | async-done | bytes 1048608 | tf_op jit(solution)/shard_map/all_to_all | solution.py:140
  45.5 2.2 %slice_bitcast_fusion = (bf16[256,1024]{1,0:T(8,128)(2,1)}, bf16[256,1024]{1,0:T(8,128)(2,1)}) fusion(bf16[64,8,1024]{2,1,0:T(8,128)(2,1)} %all-to-all-done), kind=kLoop, calls=%fused_computation.44 | loop fusion | bytes 2097152 | tf_op jit(solution)/shard_map/slice | solution.py:159
  47.8 2.5 %collective-permute-start.6 = (bf16[256,1024]{1,0:T(8,128)(2,1)}, bf16[256,1024]{1,0:T(8,128)(2,1)}, u32[]{:S(2)}, u32[]{:S(2)}) collective-permute-start(bf16[256,1024]{1,0:T(8,128)(2,1)} %get-tuple-element.25), channel_id=1, source_target_pairs={{0,192},{64,0},{128,64},{192,128},{1,193},{65,1},{129,65},{193,129... | collective-permute-start | bytes 1572872 | tf_op jit(solution)/shard_map/ppermute | solution.py:130
  50.3 3.0 %fusion.26 = f32[512,384]{1,0:T(8,128)} fusion(bf16[1,4096,384]{2,1,0:T(8,128)(2,1)} %param.10, s32[]{:T(128)S(6)} %select_n.19, bf16[256,1024]{1,0:T(8,128)(2,1)} %get-tuple-element.25, bf16[256,1024]{1,0:T(8,128)(2,1)} %get-tuple-element.26), kind=kOutput, calls=%fused_computation.30 | convolution fusion | flops 404750336 | bytes 2621444 | tf_op jit(solution)/shard_map/dot_general | solution.py:16
  53.3 2.8 %fusion.28 = f32[512,384]{1,0:T(8,128)} fusion(bf16[1,4096,384]{2,1,0:T(8,128)(2,1)S(1)} %copy-done, s32[]{:T(128)S(6)} %select_n.19, bf16[256,1024]{1,0:T(8,128)(2,1)} %get-tuple-element.25, bf16[256,1024]{1,0:T(8,128)(2,1)} %get-tuple-element.26), kind=kOutput, calls=%fused_computation.32 | convolution fusion | flops 404750336 | bytes 2621444 | tf_op jit(solution)/shard_map/dot_general | solution.py:16
  56.1 2.8 %collective-permute-start.5 = (bf16[256,1024]{1,0:T(8,128)(2,1)}, bf16[256,1024]{1,0:T(8,128)(2,1)}, u32[]{:S(2)}, u32[]{:S(2)}) collective-permute-start(bf16[256,1024]{1,0:T(8,128)(2,1)} %get-tuple-element.26), channel_id=1, source_target_pairs={{0,192},{64,0},{128,64},{192,128},{1,193},{65,1},{129,65},{193,129... | collective-permute-start | bytes 1572872 | tf_op jit(solution)/shard_map/ppermute | solution.py:130
  58.9 7.5 %collective-permute-done.6 = bf16[256,1024]{1,0:T(8,128)(2,1)} collective-permute-done((bf16[256,1024]{1,0:T(8,128)(2,1)}, bf16[256,1024]{1,0:T(8,128)(2,1)}, u32[]{:S(2)}, u32[]{:S(2)}) %collective-permute-start.6) | collective-permute-done | bytes 524320 | tf_op jit(solution)/shard_map/ppermute | solution.py:130
  66.3 3.4 %collective-permute-start.8 = (bf16[256,1024]{1,0:T(8,128)(2,1)}, bf16[256,1024]{1,0:T(8,128)(2,1)S(1)}, u32[]{:S(2)}, u32[]{:S(2)}) collective-permute-start(bf16[256,1024]{1,0:T(8,128)(2,1)} %collective-permute-done.6), channel_id=1, source_target_pairs={{0,192},{64,0},{128,64},{192,128},{1,193},{65,1},{129,65},{193,129... | collective-permute-start | bytes 1572872 | tf_op jit(solution)/shard_map/ppermute | solution.py:130
  70.9 6.7 %collective-permute-done.5 = bf16[256,1024]{1,0:T(8,128)(2,1)} collective-permute-done((bf16[256,1024]{1,0:T(8,128)(2,1)}, bf16[256,1024]{1,0:T(8,128)(2,1)}, u32[]{:S(2)}, u32[]{:S(2)}) %collective-permute-start.5) | collective-permute-done | bytes 524320 | tf_op jit(solution)/shard_map/ppermute | solution.py:130
  79.7 1.9 %fusion.17 = f32[512,384]{1,0:T(8,128)S(1)} fusion(bf16[512,1024]{1,0:T(8,128)(2,1)S(1)} %constant_dynamic-update-slice_fusion.2, bf16[1,4096,384]{2,1,0:T(8,128)(2,1)} %param.10, s32[]{:T(128)S(6)} %select_n.21), kind=kOutput, calls=%fused_computation.21 | convolution fusion | flops 402653184 | bytes 2621444 | tf_op jit(solution)/shard_map/dot_general | solution.py:16
  84.9 4.8 %collective-permute-done.7 = bf16[256,1024]{1,0:T(8,128)(2,1)S(1)} collective-permute-done((bf16[256,1024]{1,0:T(8,128)(2,1)}, bf16[256,1024]{1,0:T(8,128)(2,1)S(1)}, u32[]{:S(2)}, u32[]{:S(2)}) %collective-permute-start.7) | collective-permute-done | bytes 524320 | tf_op jit(solution)/shard_map/ppermute | solution.py:130
  92.6 2.0 %collective-permute-start.12 = (bf16[256,384]{1,0:T(8,128)(2,1)S(1)}, bf16[256,384]{1,0:T(8,128)(2,1)S(1)}, u32[]{:S(2)}, u32[]{:S(2)}) collective-permute-start(bf16[256,384]{1,0:T(8,128)(2,1)S(1)} %get-tuple-element.28), channel_id=1, source_target_pairs={{0,192},{64,0},{128,64},{192,128},{1,193},{65,1},{129,65},{193,129... | collective-permute-start | bytes 589832 | tf_op jit(solution)/shard_map/ppermute | solution.py:130
  94.6 1.8 %fusion.14 = f32[512,1024]{1,0:T(8,128)S(1)} fusion(bf16[512,384]{1,0:T(8,128)(2,1)S(1)} %multiply_convert_fusion, bf16[1,384,4096]{2,1,0:T(8,128)(2,1)} %down_hbm.1, s32[]{:T(128)S(6)} %select_n.23), kind=kOutput, calls=%fused_computation.18 | convolution fusion | flops 402653184 | bytes 3276804 | tf_op jit(solution)/shard_map/dot_general | solution.py:16
  96.5 2.7 %collective-permute-start.11 = (bf16[256,384]{1,0:T(8,128)(2,1)S(1)}, bf16[256,384]{1,0:T(8,128)(2,1)S(1)}, u32[]{:S(2)}, u32[]{:S(2)}) collective-permute-start(bf16[256,384]{1,0:T(8,128)(2,1)S(1)} %get-tuple-element.29), channel_id=1, source_target_pairs={{0,192},{64,0},{128,64},{192,128},{1,193},{65,1},{129,65},{193,129... | collective-permute-start | bytes 589832 | tf_op jit(solution)/shard_map/ppermute | solution.py:130
  99.2 2.7 %collective-permute-start.14 = (bf16[256,384]{1,0:T(8,128)(2,1)S(1)}, bf16[256,384]{1,0:T(8,128)(2,1)S(1)}, u32[]{:S(2)}, u32[]{:S(2)}) collective-permute-start(bf16[256,384]{1,0:T(8,128)(2,1)S(1)} %collective-permute-done.12), channel_id=1, source_target_pairs={{0,192},{64,0},{128,64},{192,128},{1,193},{65,1},{129,65},{193,129... | collective-permute-start | bytes 589832 | tf_op jit(solution)/shard_map/ppermute | solution.py:130
  102.6 2.4 %fusion = f32[512,1024]{1,0:T(8,128)S(1)} fusion(bf16[384,1024]{1,0:T(8,128)(2,1)} %collective-permute-done.2, bf16[384,1024]{1,0:T(8,128)(2,1)} %collective-permute-done, bf16[256,384]{1,0:T(8,128)(2,1)S(1)} %collective-permute-done.12, bf16[256,384]{1,0:T(8,128)(2,1)S(1)} %collective-permute-done.11, bf16[256,384]{1,0:T(8,128)(2,1)S(1)} %collective-permute-done.10, ...), kind=kOutput, calls=%fused_computation.1 | convolution fusion | flops 811597824 | bytes 4456448 | tf_op jit(solution)/shard_map/dot_general | solution.py:16
  105.0 2.3 %collective-permute-done.13 = bf16[256,384]{1,0:T(8,128)(2,1)S(1)} collective-permute-done((bf16[256,384]{1,0:T(8,128)(2,1)S(1)}, bf16[256,384]{1,0:T(8,128)(2,1)S(1)}, u32[]{:S(2)}, u32[]{:S(2)}) %collective-permute-start.13) | collective-permute-done | bytes 196640 | tf_op jit(solution)/shard_map/ppermute | solution.py:130
  107.3 1.9 %fusion.4 = bf16[64,8,1024]{2,1,0:T(8,128)(2,1)S(1)} fusion(bf16[384,1024]{1,0:T(8,128)(2,1)} %collective-permute-done.1, f32[512,1024]{1,0:T(8,128)S(1)} %fusion.14, f32[512,1024]{1,0:T(8,128)S(1)} %fusion, bf16[256,384]{1,0:T(8,128)(2,1)S(1)} %collective-permute-done.14, bf16[256,384]{1,0:T(8,128)(2,1)S(1)} %collective-permute-done.13), kind=kOutput, calls=%fused_computation.5 | convolution fusion | flops 405012480 | bytes 6422528 | tf_op jit(solution)/shard_map/dot_general | solution.py:16
  109.2 40.3 %all_to_all.10 = bf16[64,8,1024]{2,1,0:T(8,128)(2,1)S(1)} all-to-all(bf16[64,8,1024]{2,1,0:T(8,128)(2,1)S(1)} %fusion.4), channel_id=1, replica_groups=mesh['section'=4,'expert'=32,'dp'=2] {'expert','dp'}, dimensions={0} | all-to-all | bytes 2097152 | tf_op jit(solution)/shard_map/all_to_all | solution.py:140
  (41 shorter events, 11.2 us)
Async XLA Ops:
  0.0 53.3 %copy-start = (bf16[1,4096,384]{2,1,0:T(8,128)(2,1)S(1)}, bf16[1,4096,384]{2,1,0:T(8,128)(2,1)}, u32[]{:S(2)}) copy-start(bf16[1,4096,384]{2,1,0:T(8,128)(2,1)} %param.9) | copy-start | bytes 9437188
  4.3 41.3 %all-to-all-start = ((bf16[64,8,1024]{2,1,0:T(8,128)(2,1)}), bf16[64,8,1024]{2,1,0:T(8,128)(2,1)}, u32[]{:S(2)}, u32[]{:S(2)}) async-start(bf16[64,8,1024]{2,1,0:T(8,128)(2,1)} %bitcast.51), calls=%async_computation | async-start | bytes 2097152 | tf_op jit(solution)/shard_map/all_to_all | solution.py:140
  17.6 38.5 %collective-permute-start = (bf16[384,1024]{1,0:T(8,128)(2,1)}, bf16[384,1024]{1,0:T(8,128)(2,1)}, u32[]{:S(2)}, u32[]{:S(2)}) collective-permute-start(bf16[384,1024]{1,0:T(8,128)(2,1)} %get-tuple-element.21), channel_id=1, source_target_pairs={{0,64},{64,128},{128,192},{192,0},{1,65},{65,129},{129,193},{193,1... | collective-permute-start | bytes 2359304 | tf_op jit(solution)/shard_map/ppermute | solution.py:130
  18.9 37.2 %collective-permute-start.1 = (bf16[384,1024]{1,0:T(8,128)(2,1)}, bf16[384,1024]{1,0:T(8,128)(2,1)}, u32[]{:S(2)}, u32[]{:S(2)}) collective-permute-start(bf16[384,1024]{1,0:T(8,128)(2,1)} %get-tuple-element.22), channel_id=1, source_target_pairs={{0,128},{64,192},{128,0},{192,64},{1,129},{65,193},{129,1},{193,65... | collective-permute-start | bytes 2359304 | tf_op jit(solution)/shard_map/ppermute | solution.py:130
  21.4 34.8 %collective-permute-start.2 = (bf16[384,1024]{1,0:T(8,128)(2,1)}, bf16[384,1024]{1,0:T(8,128)(2,1)}, u32[]{:S(2)}, u32[]{:S(2)}) collective-permute-start(bf16[384,1024]{1,0:T(8,128)(2,1)} %get-tuple-element.23), channel_id=1, source_target_pairs={{0,192},{64,0},{128,64},{192,128},{1,193},{65,1},{129,65},{193,129... | collective-permute-start | bytes 2359304 | tf_op jit(solution)/shard_map/ppermute | solution.py:130
  47.8 18.6 %collective-permute-start.6 = (bf16[256,1024]{1,0:T(8,128)(2,1)}, bf16[256,1024]{1,0:T(8,128)(2,1)}, u32[]{:S(2)}, u32[]{:S(2)}) collective-permute-start(bf16[256,1024]{1,0:T(8,128)(2,1)} %get-tuple-element.25), channel_id=1, source_target_pairs={{0,192},{64,0},{128,64},{192,128},{1,193},{65,1},{129,65},{193,129... | collective-permute-start | bytes 1572872 | tf_op jit(solution)/shard_map/ppermute | solution.py:130
  50.3 19.5 %collective-permute-start.3 = (bf16[256,1024]{1,0:T(8,128)(2,1)}, bf16[256,1024]{1,0:T(8,128)(2,1)}, u32[]{:S(2)}, u32[]{:S(2)}) collective-permute-start(bf16[256,1024]{1,0:T(8,128)(2,1)} %get-tuple-element.26), channel_id=1, source_target_pairs={{0,64},{64,128},{128,192},{192,0},{1,65},{65,129},{129,193},{193,1... | collective-permute-start | bytes 1572872 | tf_op jit(solution)/shard_map/ppermute | solution.py:130
  56.1 21.4 %collective-permute-start.5 = (bf16[256,1024]{1,0:T(8,128)(2,1)}, bf16[256,1024]{1,0:T(8,128)(2,1)}, u32[]{:S(2)}, u32[]{:S(2)}) collective-permute-start(bf16[256,1024]{1,0:T(8,128)(2,1)} %get-tuple-element.26), channel_id=1, source_target_pairs={{0,192},{64,0},{128,64},{192,128},{1,193},{65,1},{129,65},{193,129... | collective-permute-start | bytes 1572872 | tf_op jit(solution)/shard_map/ppermute | solution.py:130
  58.9 23.4 %collective-permute-start.4 = (bf16[256,1024]{1,0:T(8,128)(2,1)}, bf16[256,1024]{1,0:T(8,128)(2,1)S(1)}, u32[]{:S(2)}, u32[]{:S(2)}) collective-permute-start(bf16[256,1024]{1,0:T(8,128)(2,1)} %get-tuple-element.25), channel_id=1, source_target_pairs={{0,64},{64,128},{128,192},{192,0},{1,65},{65,129},{129,193},{193,1... | collective-permute-start | bytes 1572872 | tf_op jit(solution)/shard_map/ppermute | solution.py:130
  66.3 23.4 %collective-permute-start.8 = (bf16[256,1024]{1,0:T(8,128)(2,1)}, bf16[256,1024]{1,0:T(8,128)(2,1)S(1)}, u32[]{:S(2)}, u32[]{:S(2)}) collective-permute-start(bf16[256,1024]{1,0:T(8,128)(2,1)} %collective-permute-done.6), channel_id=1, source_target_pairs={{0,192},{64,0},{128,64},{192,128},{1,193},{65,1},{129,65},{193,129... | collective-permute-start | bytes 1572872 | tf_op jit(solution)/shard_map/ppermute | solution.py:130
  69.8 19.9 %collective-permute-start.7 = (bf16[256,1024]{1,0:T(8,128)(2,1)}, bf16[256,1024]{1,0:T(8,128)(2,1)S(1)}, u32[]{:S(2)}, u32[]{:S(2)}) collective-permute-start(bf16[256,1024]{1,0:T(8,128)(2,1)} %collective-permute-done.3), channel_id=1, source_target_pairs={{0,64},{64,128},{128,192},{192,0},{1,65},{65,129},{129,193},{193,1... | collective-permute-start | bytes 1572872 | tf_op jit(solution)/shard_map/ppermute | solution.py:130
  81.6 1.9 %copy-start.2 = (bf16[1,4096,384]{2,1,0:T(8,128)(2,1)S(1)}, bf16[1,4096,384]{2,1,0:T(8,128)(2,1)}, u32[]{:S(2)}) copy-start(bf16[1,4096,384]{2,1,0:T(8,128)(2,1)} %param.10) | copy-start | bytes 9437188
  84.2 5.6 %copy-start.1 = (f32[512,384]{1,0:T(8,128)S(1)}, f32[512,384]{1,0:T(8,128)}, u32[]{:S(2)}) copy-start(f32[512,384]{1,0:T(8,128)} %fusion.28) | copy-start | bytes 2359300
  89.8 1.1 copy-start.4
  91.8 7.4 %collective-permute-start.9 = (bf16[256,384]{1,0:T(8,128)(2,1)S(1)}, bf16[256,384]{1,0:T(8,128)(2,1)S(1)}, u32[]{:S(2)}, u32[]{:S(2)}) collective-permute-start(bf16[256,384]{1,0:T(8,128)(2,1)S(1)} %get-tuple-element.29), channel_id=1, source_target_pairs={{0,64},{64,128},{128,192},{192,0},{1,65},{65,129},{129,193},{193,1... | collective-permute-start | bytes 589832 | tf_op jit(solution)/shard_map/ppermute | solution.py:130
  92.6 6.6 %collective-permute-start.12 = (bf16[256,384]{1,0:T(8,128)(2,1)S(1)}, bf16[256,384]{1,0:T(8,128)(2,1)S(1)}, u32[]{:S(2)}, u32[]{:S(2)}) collective-permute-start(bf16[256,384]{1,0:T(8,128)(2,1)S(1)} %get-tuple-element.28), channel_id=1, source_target_pairs={{0,192},{64,0},{128,64},{192,128},{1,193},{65,1},{129,65},{193,129... | collective-permute-start | bytes 589832 | tf_op jit(solution)/shard_map/ppermute | solution.py:130
  96.4 6.2 %collective-permute-start.10 = (bf16[256,384]{1,0:T(8,128)(2,1)S(1)}, bf16[256,384]{1,0:T(8,128)(2,1)S(1)}, u32[]{:S(2)}, u32[]{:S(2)}) collective-permute-start(bf16[256,384]{1,0:T(8,128)(2,1)S(1)} %get-tuple-element.28), channel_id=1, source_target_pairs={{0,64},{64,128},{128,192},{192,0},{1,65},{65,129},{129,193},{193,1... | collective-permute-start | bytes 589832 | tf_op jit(solution)/shard_map/ppermute | solution.py:130
  96.5 6.1 %collective-permute-start.11 = (bf16[256,384]{1,0:T(8,128)(2,1)S(1)}, bf16[256,384]{1,0:T(8,128)(2,1)S(1)}, u32[]{:S(2)}, u32[]{:S(2)}) collective-permute-start(bf16[256,384]{1,0:T(8,128)(2,1)S(1)} %get-tuple-element.29), channel_id=1, source_target_pairs={{0,192},{64,0},{128,64},{192,128},{1,193},{65,1},{129,65},{193,129... | collective-permute-start | bytes 589832 | tf_op jit(solution)/shard_map/ppermute | solution.py:130
  99.2 8.1 %collective-permute-start.13 = (bf16[256,384]{1,0:T(8,128)(2,1)S(1)}, bf16[256,384]{1,0:T(8,128)(2,1)S(1)}, u32[]{:S(2)}, u32[]{:S(2)}) collective-permute-start(bf16[256,384]{1,0:T(8,128)(2,1)S(1)} %collective-permute-done.9), channel_id=1, source_target_pairs={{0,64},{64,128},{128,192},{192,0},{1,65},{65,129},{129,193},{193,1... | collective-permute-start | bytes 589832 | tf_op jit(solution)/shard_map/ppermute | solution.py:130
  99.2 8.1 %collective-permute-start.14 = (bf16[256,384]{1,0:T(8,128)(2,1)S(1)}, bf16[256,384]{1,0:T(8,128)(2,1)S(1)}, u32[]{:S(2)}, u32[]{:S(2)}) collective-permute-start(bf16[256,384]{1,0:T(8,128)(2,1)S(1)} %collective-permute-done.12), channel_id=1, source_target_pairs={{0,192},{64,0},{128,64},{192,128},{1,193},{65,1},{129,65},{193,129... | collective-permute-start | bytes 589832 | tf_op jit(solution)/shard_map/ppermute | solution.py:130
  109.2 40.3 %copy-start.3 = (bf16[512,64]{1,0:T(8,128)(2,1)S(1)}, bf16[512,64]{1,0:T(8,128)(2,1)}, u32[]{:S(2)}) copy-start(bf16[512,64]{1,0:T(8,128)(2,1)} %get-tuple-element.19) | copy-start | bytes 196612

commit v13 on v12

--- a/solution.py
+++ b/solution.py
@@ -176,7 +176,7 @@
         [jnp.concatenate([r_a, r_b], axis=0), jnp.concatenate([l_a, l_b], axis=0)], axis=1
     )
     out = out + dot(near, jnp.concatenate([downs[0], downs[2]], axis=0))
-    out = out + dot(across, downs[1])
+    out = lax.optimization_barrier(out) + dot(across, downs[1])
     returned = exchange(out.astype(BF))
     both = lax.dot_general(
         spread, returned, (((0,), (0,)), ((), ())), preferred_element_type=F32

time: 151 us -> 151 us (level)
  no operation moved by 1% of the time
where the time goes in v13:
time: 151 us; the launch traced here: 150 us
  waiting for transfers between devices  44.9 us (30%)
  blocking collectives  40.3 us (27%)
  starting transfers between devices  35.1 us (23%)
  matrix products  17.8 us (12%)
  local copies, waits for them, and re-layouts  7.17 us (5%)
  Pallas kernels  4.26 us (3%)
    all_to_all x1, blocking collectives, exchange(): lax.all_to_all(v.reshape(experts, cap, w), ED, split_axis=0, concat_axis=...  40.3 us
    all_to_all x1, waiting for transfers between devices, exchange(): lax.all_to_all(v.reshape(experts, cap, w), ED, split_axis=0, concat_axis=...  23 us
    ppermute x15, waiting for transfers between devices, send(): lax.ppermute(v, 'section', [(k, (k + d) % sections) for k in range(sectio...  21.9 us
    ppermute x15, starting transfers between devices, send(): lax.ppermute(v, 'section', [(k, (k + d) % sections) for k in range(sectio...  21.7 us
    dot_general x11, matrix products, dot(): return jnp.dot(a, b, preferred_element_type=F32)  17.5 us
    all_to_all x1, starting transfers between devices, exchange(): lax.all_to_all(v.reshape(experts, cap, w), ED, split_axis=0, concat_axis=...  13.4 us
    pallas_call x1, Pallas kernels, first(): pl.pallas_call(kernel, in_specs=[pl.BlockSpec(memory_space=pltpu.SMEM)] +...  4.26 us
    unnamed x13, local copies, waits for them, and re-layouts  3.74 us
  transfers between devices with their start and end apart: 16, of which 6 were waited for; matrix products, arithmetic and copies ran while one was open for 13% of the time, Pallas kernels for 0%

profile of v13, /device:TPU:1, one launch (start us, length us, event | category | flops | bytes accessed | tf_op | source)
XLA Modules:
  0.0 150.4 jit_solution(2076393871235961713)
XLA Ops:
  0.0 4.3 %first.1 = (bf16[512,1024]{1,0:T(8,128)(2,1)}, bf16[512,64]{1,0:T(8,128)(2,1)}, bf16[384,1024]{1,0:T(8,128)(2,1)}, bf16[384,1024]{1,0:T(8,128)(2,1)}, bf16[384,1024]{1,0:T(8,128)(2,1)}) custom-call(s32[1]{0:T(128)} %bitcast.s_ref, s32[8,32]{1,0:T(8,128)} %bitcast.52, f32[8,32]{1,0:T(8,128)} %bitcast.53, bf16[32,4096]{1,0:T(8,128)(2,1)} %tokens_hbm.1, ...), custom_call_target="tpu_custom_call" | custom-call | flops 33554432 | bytes 5767168 | tf_op jit(solution)/shard_map/first/pallas_call | solution.py:91
  4.3 13.4 %all-to-all-start = ((bf16[64,8,1024]{2,1,0:T(8,128)(2,1)}), bf16[64,8,1024]{2,1,0:T(8,128)(2,1)}, u32[]{:S(2)}, u32[]{:S(2)}) async-start(bf16[64,8,1024]{2,1,0:T(8,128)(2,1)} %bitcast.51), calls=%async_computation | async-start | bytes 2097152 | tf_op jit(solution)/shard_map/all_to_all | solution.py:140
  17.6 1.3 collective-permute-start
  18.9 2.4 %collective-permute-start.1 = (bf16[384,1024]{1,0:T(8,128)(2,1)}, bf16[384,1024]{1,0:T(8,128)(2,1)}, u32[]{:S(2)}, u32[]{:S(2)}) collective-permute-start(bf16[384,1024]{1,0:T(8,128)(2,1)} %get-tuple-element.22), channel_id=1, source_target_pairs={{0,128},{64,192},{128,0},{192,64},{1,129},{65,193},{129,1},{193,65... | collective-permute-start | bytes 2359304 | tf_op jit(solution)/shard_map/ppermute | solution.py:130
  21.4 1.2 collective-permute-start.2
  22.5 23.0 %all-to-all-done = bf16[64,8,1024]{2,1,0:T(8,128)(2,1)} async-done(((bf16[64,8,1024]{2,1,0:T(8,128)(2,1)}), bf16[64,8,1024]{2,1,0:T(8,128)(2,1)}, u32[]{:S(2)}, u32[]{:S(2)}) %all-to-all-start) | async-done | bytes 1048608 | tf_op jit(solution)/shard_map/all_to_all | solution.py:140
  45.5 2.2 %slice_bitcast_fusion = (bf16[256,1024]{1,0:T(8,128)(2,1)}, bf16[256,1024]{1,0:T(8,128)(2,1)}) fusion(bf16[64,8,1024]{2,1,0:T(8,128)(2,1)} %all-to-all-done), kind=kLoop, calls=%fused_computation.44 | loop fusion | bytes 2097152 | tf_op jit(solution)/shard_map/slice | solution.py:159
  47.8 2.5 %collective-permute-start.6 = (bf16[256,1024]{1,0:T(8,128)(2,1)}, bf16[256,1024]{1,0:T(8,128)(2,1)}, u32[]{:S(2)}, u32[]{:S(2)}) collective-permute-start(bf16[256,1024]{1,0:T(8,128)(2,1)} %get-tuple-element.25), channel_id=1, source_target_pairs={{0,192},{64,0},{128,64},{192,128},{1,193},{65,1},{129,65},{193,129... | collective-permute-start | bytes 1572872 | tf_op jit(solution)/shard_map/ppermute | solution.py:130
  50.3 3.0 %fusion.25 = f32[512,384]{1,0:T(8,128)} fusion(bf16[1,4096,384]{2,1,0:T(8,128)(2,1)} %param.10, s32[]{:T(128)S(6)} %select_n.19, bf16[256,1024]{1,0:T(8,128)(2,1)} %get-tuple-element.25, bf16[256,1024]{1,0:T(8,128)(2,1)} %get-tuple-element.26), kind=kOutput, calls=%fused_computation.30 | convolution fusion | flops 404750336 | bytes 2621444 | tf_op jit(solution)/shard_map/dot_general | solution.py:16
  53.3 2.8 %fusion.27 = f32[512,384]{1,0:T(8,128)} fusion(bf16[1,4096,384]{2,1,0:T(8,128)(2,1)S(1)} %copy-done, s32[]{:T(128)S(6)} %select_n.19, bf16[256,1024]{1,0:T(8,128)(2,1)} %get-tuple-element.25, bf16[256,1024]{1,0:T(8,128)(2,1)} %get-tuple-element.26), kind=kOutput, calls=%fused_computation.32 | convolution fusion | flops 404750336 | bytes 2621444 | tf_op jit(solution)/shard_map/dot_general | solution.py:16
  56.1 2.8 %collective-permute-start.5 = (bf16[256,1024]{1,0:T(8,128)(2,1)}, bf16[256,1024]{1,0:T(8,128)(2,1)}, u32[]{:S(2)}, u32[]{:S(2)}) collective-permute-start(bf16[256,1024]{1,0:T(8,128)(2,1)} %get-tuple-element.26), channel_id=1, source_target_pairs={{0,192},{64,0},{128,64},{192,128},{1,193},{65,1},{129,65},{193,129... | collective-permute-start | bytes 1572872 | tf_op jit(solution)/shard_map/ppermute | solution.py:130
  58.9 7.5 %collective-permute-done.6 = bf16[256,1024]{1,0:T(8,128)(2,1)} collective-permute-done((bf16[256,1024]{1,0:T(8,128)(2,1)}, bf16[256,1024]{1,0:T(8,128)(2,1)}, u32[]{:S(2)}, u32[]{:S(2)}) %collective-permute-start.6) | collective-permute-done | bytes 524320 | tf_op jit(solution)/shard_map/ppermute | solution.py:130
  66.3 3.4 %collective-permute-start.8 = (bf16[256,1024]{1,0:T(8,128)(2,1)}, bf16[256,1024]{1,0:T(8,128)(2,1)S(1)}, u32[]{:S(2)}, u32[]{:S(2)}) collective-permute-start(bf16[256,1024]{1,0:T(8,128)(2,1)} %collective-permute-done.6), channel_id=1, source_target_pairs={{0,192},{64,0},{128,64},{192,128},{1,193},{65,1},{129,65},{193,129... | collective-permute-start | bytes 1572872 | tf_op jit(solution)/shard_map/ppermute | solution.py:130
  70.9 6.7 %collective-permute-done.5 = bf16[256,1024]{1,0:T(8,128)(2,1)} collective-permute-done((bf16[256,1024]{1,0:T(8,128)(2,1)}, bf16[256,1024]{1,0:T(8,128)(2,1)}, u32[]{:S(2)}, u32[]{:S(2)}) %collective-permute-start.5) | collective-permute-done | bytes 524320 | tf_op jit(solution)/shard_map/ppermute | solution.py:130
  79.7 1.9 %fusion.16 = f32[512,384]{1,0:T(8,128)S(1)} fusion(bf16[512,1024]{1,0:T(8,128)(2,1)S(1)} %constant_dynamic-update-slice_fusion.2, bf16[1,4096,384]{2,1,0:T(8,128)(2,1)} %param.10, s32[]{:T(128)S(6)} %select_n.21), kind=kOutput, calls=%fused_computation.21 | convolution fusion | flops 402653184 | bytes 2621444 | tf_op jit(solution)/shard_map/dot_general | solution.py:16
  84.9 4.8 %collective-permute-done.7 = bf16[256,1024]{1,0:T(8,128)(2,1)S(1)} collective-permute-done((bf16[256,1024]{1,0:T(8,128)(2,1)}, bf16[256,1024]{1,0:T(8,128)(2,1)S(1)}, u32[]{:S(2)}, u32[]{:S(2)}) %collective-permute-start.7) | collective-permute-done | bytes 524320 | tf_op jit(solution)/shard_map/ppermute | solution.py:130
  92.6 2.0 %collective-permute-start.12 = (bf16[256,384]{1,0:T(8,128)(2,1)S(1)}, bf16[256,384]{1,0:T(8,128)(2,1)S(1)}, u32[]{:S(2)}, u32[]{:S(2)}) collective-permute-start(bf16[256,384]{1,0:T(8,128)(2,1)S(1)} %get-tuple-element.28), channel_id=1, source_target_pairs={{0,192},{64,0},{128,64},{192,128},{1,193},{65,1},{129,65},{193,129... | collective-permute-start | bytes 589832 | tf_op jit(solution)/shard_map/ppermute | solution.py:130
  94.6 1.8 %fusion.13 = f32[512,1024]{1,0:T(8,128)S(1)} fusion(bf16[512,384]{1,0:T(8,128)(2,1)S(1)} %multiply_convert_fusion, bf16[1,384,4096]{2,1,0:T(8,128)(2,1)} %down_hbm.1, s32[]{:T(128)S(6)} %select_n.23), kind=kOutput, calls=%fused_computation.18 | convolution fusion | flops 402653184 | bytes 3276804 | tf_op jit(solution)/shard_map/dot_general | solution.py:16
  96.5 2.7 %collective-permute-start.11 = (bf16[256,384]{1,0:T(8,128)(2,1)S(1)}, bf16[256,384]{1,0:T(8,128)(2,1)S(1)}, u32[]{:S(2)}, u32[]{:S(2)}) collective-permute-start(bf16[256,384]{1,0:T(8,128)(2,1)S(1)} %get-tuple-element.29), channel_id=1, source_target_pairs={{0,192},{64,0},{128,64},{192,128},{1,193},{65,1},{129,65},{193,129... | collective-permute-start | bytes 589832 | tf_op jit(solution)/shard_map/ppermute | solution.py:130
  99.2 2.7 %collective-permute-start.14 = (bf16[256,384]{1,0:T(8,128)(2,1)S(1)}, bf16[256,384]{1,0:T(8,128)(2,1)S(1)}, u32[]{:S(2)}, u32[]{:S(2)}) collective-permute-start(bf16[256,384]{1,0:T(8,128)(2,1)S(1)} %collective-permute-done.12), channel_id=1, source_target_pairs={{0,192},{64,0},{128,64},{192,128},{1,193},{65,1},{129,65},{193,129... | collective-permute-start | bytes 589832 | tf_op jit(solution)/shard_map/ppermute | solution.py:130
  102.6 2.4 %convolution_add_fusion = f32[512,1024]{1,0:T(8,128)S(1)} fusion(f32[512,1024]{1,0:T(8,128)S(1)} %fusion.13, bf16[384,1024]{1,0:T(8,128)(2,1)} %collective-permute-done.2, bf16[384,1024]{1,0:T(8,128)(2,1)} %collective-permute-done, bf16[256,384]{1,0:T(8,128)(2,1)S(1)} %collective-permute-done.12, bf16[256,384]{1,0:T(8,128)(2,1)S(1)} %collective-permute-done.11, ...), kind=kOutput, calls=%fused_computation.1 | convolution fusion | flops 812122112 | bytes 6553600 | tf_op jit(solution)/shard_map/dot_general | solution.py:16
  105.0 2.3 %collective-permute-done.13 = bf16[256,384]{1,0:T(8,128)(2,1)S(1)} collective-permute-done((bf16[256,384]{1,0:T(8,128)(2,1)S(1)}, bf16[256,384]{1,0:T(8,128)(2,1)S(1)}, u32[]{:S(2)}, u32[]{:S(2)}) %collective-permute-start.13) | collective-permute-done | bytes 196640 | tf_op jit(solution)/shard_map/ppermute | solution.py:130
  107.3 1.9 %fusion.3 = bf16[64,8,1024]{2,1,0:T(8,128)(2,1)S(1)} fusion(f32[512,1024]{1,0:T(8,128)S(1)} %convolution_add_fusion, bf16[384,1024]{1,0:T(8,128)(2,1)} %collective-permute-done.1, bf16[256,384]{1,0:T(8,128)(2,1)S(1)} %collective-permute-done.14, bf16[256,384]{1,0:T(8,128)(2,1)S(1)} %collective-permute-done.13), kind=kOutput, calls=%fused_computation.5 | convolution fusion | flops 404488192 | bytes 4325376 | tf_op jit(solution)/shard_map/dot_general | solution.py:16
  109.2 40.3 %all_to_all.10 = bf16[64,8,1024]{2,1,0:T(8,128)(2,1)S(1)} all-to-all(bf16[64,8,1024]{2,1,0:T(8,128)(2,1)S(1)} %fusion.3), channel_id=1, replica_groups=mesh['section'=4,'expert'=32,'dp'=2] {'expert','dp'}, dimensions={0} | all-to-all | bytes 2097152 | tf_op jit(solution)/shard_map/all_to_all | solution.py:140
  (41 shorter events, 11.2 us)
Async XLA Ops:
  0.0 53.3 %copy-start = (bf16[1,4096,384]{2,1,0:T(8,128)(2,1)S(1)}, bf16[1,4096,384]{2,1,0:T(8,128)(2,1)}, u32[]{:S(2)}) copy-start(bf16[1,4096,384]{2,1,0:T(8,128)(2,1)} %param.9) | copy-start | bytes 9437188
  4.3 41.3 %all-to-all-start = ((bf16[64,8,1024]{2,1,0:T(8,128)(2,1)}), bf16[64,8,1024]{2,1,0:T(8,128)(2,1)}, u32[]{:S(2)}, u32[]{:S(2)}) async-start(bf16[64,8,1024]{2,1,0:T(8,128)(2,1)} %bitcast.51), calls=%async_computation | async-start | bytes 2097152 | tf_op jit(solution)/shard_map/all_to_all | solution.py:140
  17.6 38.5 %collective-permute-start = (bf16[384,1024]{1,0:T(8,128)(2,1)}, bf16[384,1024]{1,0:T(8,128)(2,1)}, u32[]{:S(2)}, u32[]{:S(2)}) collective-permute-start(bf16[384,1024]{1,0:T(8,128)(2,1)} %get-tuple-element.21), channel_id=1, source_target_pairs={{0,64},{64,128},{128,192},{192,0},{1,65},{65,129},{129,193},{193,1... | collective-permute-start | bytes 2359304 | tf_op jit(solution)/shard_map/ppermute | solution.py:130
  18.9 37.2 %collective-permute-start.1 = (bf16[384,1024]{1,0:T(8,128)(2,1)}, bf16[384,1024]{1,0:T(8,128)(2,1)}, u32[]{:S(2)}, u32[]{:S(2)}) collective-permute-start(bf16[384,1024]{1,0:T(8,128)(2,1)} %get-tuple-element.22), channel_id=1, source_target_pairs={{0,128},{64,192},{128,0},{192,64},{1,129},{65,193},{129,1},{193,65... | collective-permute-start | bytes 2359304 | tf_op jit(solution)/shard_map/ppermute | solution.py:130
  21.4 34.8 %collective-permute-start.2 = (bf16[384,1024]{1,0:T(8,128)(2,1)}, bf16[384,1024]{1,0:T(8,128)(2,1)}, u32[]{:S(2)}, u32[]{:S(2)}) collective-permute-start(bf16[384,1024]{1,0:T(8,128)(2,1)} %get-tuple-element.23), channel_id=1, source_target_pairs={{0,192},{64,0},{128,64},{192,128},{1,193},{65,1},{129,65},{193,129... | collective-permute-start | bytes 2359304 | tf_op jit(solution)/shard_map/ppermute | solution.py:130
  47.8 18.6 %collective-permute-start.6 = (bf16[256,1024]{1,0:T(8,128)(2,1)}, bf16[256,1024]{1,0:T(8,128)(2,1)}, u32[]{:S(2)}, u32[]{:S(2)}) collective-permute-start(bf16[256,1024]{1,0:T(8,128)(2,1)} %get-tuple-element.25), channel_id=1, source_target_pairs={{0,192},{64,0},{128,64},{192,128},{1,193},{65,1},{129,65},{193,129... | collective-permute-start | bytes 1572872 | tf_op jit(solution)/shard_map/ppermute | solution.py:130
  50.3 19.5 %collective-permute-start.3 = (bf16[256,1024]{1,0:T(8,128)(2,1)}, bf16[256,1024]{1,0:T(8,128)(2,1)}, u32[]{:S(2)}, u32[]{:S(2)}) collective-permute-start(bf16[256,1024]{1,0:T(8,128)(2,1)} %get-tuple-element.26), channel_id=1, source_target_pairs={{0,64},{64,128},{128,192},{192,0},{1,65},{65,129},{129,193},{193,1... | collective-permute-start | bytes 1572872 | tf_op jit(solution)/shard_map/ppermute | solution.py:130
  56.1 21.4 %collective-permute-start.5 = (bf16[256,1024]{1,0:T(8,128)(2,1)}, bf16[256,1024]{1,0:T(8,128)(2,1)}, u32[]{:S(2)}, u32[]{:S(2)}) collective-permute-start(bf16[256,1024]{1,0:T(8,128)(2,1)} %get-tuple-element.26), channel_id=1, source_target_pairs={{0,192},{64,0},{128,64},{192,128},{1,193},{65,1},{129,65},{193,129... | collective-permute-start | bytes 1572872 | tf_op jit(solution)/shard_map/ppermute | solution.py:130
  58.9 23.4 %collective-permute-start.4 = (bf16[256,1024]{1,0:T(8,128)(2,1)}, bf16[256,1024]{1,0:T(8,128)(2,1)S(1)}, u32[]{:S(2)}, u32[]{:S(2)}) collective-permute-start(bf16[256,1024]{1,0:T(8,128)(2,1)} %get-tuple-element.25), channel_id=1, source_target_pairs={{0,64},{64,128},{128,192},{192,0},{1,65},{65,129},{129,193},{193,1... | collective-permute-start | bytes 1572872 | tf_op jit(solution)/shard_map/ppermute | solution.py:130
  66.3 23.4 %collective-permute-start.8 = (bf16[256,1024]{1,0:T(8,128)(2,1)}, bf16[256,1024]{1,0:T(8,128)(2,1)S(1)}, u32[]{:S(2)}, u32[]{:S(2)}) collective-permute-start(bf16[256,1024]{1,0:T(8,128)(2,1)} %collective-permute-done.6), channel_id=1, source_target_pairs={{0,192},{64,0},{128,64},{192,128},{1,193},{65,1},{129,65},{193,129... | collective-permute-start | bytes 1572872 | tf_op jit(solution)/shard_map/ppermute | solution.py:130
  69.8 19.9 %collective-permute-start.7 = (bf16[256,1024]{1,0:T(8,128)(2,1)}, bf16[256,1024]{1,0:T(8,128)(2,1)S(1)}, u32[]{:S(2)}, u32[]{:S(2)}) collective-permute-start(bf16[256,1024]{1,0:T(8,128)(2,1)} %collective-permute-done.3), channel_id=1, source_target_pairs={{0,64},{64,128},{128,192},{192,0},{1,65},{65,129},{129,193},{193,1... | collective-permute-start | bytes 1572872 | tf_op jit(solution)/shard_map/ppermute | solution.py:130
  81.6 1.9 %copy-start.2 = (bf16[1,4096,384]{2,1,0:T(8,128)(2,1)S(1)}, bf16[1,4096,384]{2,1,0:T(8,128)(2,1)}, u32[]{:S(2)}) copy-start(bf16[1,4096,384]{2,1,0:T(8,128)(2,1)} %param.10) | copy-start | bytes 9437188
  84.2 5.6 %copy-start.1 = (f32[512,384]{1,0:T(8,128)S(1)}, f32[512,384]{1,0:T(8,128)}, u32[]{:S(2)}) copy-start(f32[512,384]{1,0:T(8,128)} %fusion.27) | copy-start | bytes 2359300
  89.8 1.1 copy-start.4
  91.8 7.4 %collective-permute-start.9 = (bf16[256,384]{1,0:T(8,128)(2,1)S(1)}, bf16[256,384]{1,0:T(8,128)(2,1)S(1)}, u32[]{:S(2)}, u32[]{:S(2)}) collective-permute-start(bf16[256,384]{1,0:T(8,128)(2,1)S(1)} %get-tuple-element.29), channel_id=1, source_target_pairs={{0,64},{64,128},{128,192},{192,0},{1,65},{65,129},{129,193},{193,1... | collective-permute-start | bytes 589832 | tf_op jit(solution)/shard_map/ppermute | solution.py:130
  92.6 6.6 %collective-permute-start.12 = (bf16[256,384]{1,0:T(8,128)(2,1)S(1)}, bf16[256,384]{1,0:T(8,128)(2,1)S(1)}, u32[]{:S(2)}, u32[]{:S(2)}) collective-permute-start(bf16[256,384]{1,0:T(8,128)(2,1)S(1)} %get-tuple-element.28), channel_id=1, source_target_pairs={{0,192},{64,0},{128,64},{192,128},{1,193},{65,1},{129,65},{193,129... | collective-permute-start | bytes 589832 | tf_op jit(solution)/shard_map/ppermute | solution.py:130
  96.4 6.2 %collective-permute-start.10 = (bf16[256,384]{1,0:T(8,128)(2,1)S(1)}, bf16[256,384]{1,0:T(8,128)(2,1)S(1)}, u32[]{:S(2)}, u32[]{:S(2)}) collective-permute-start(bf16[256,384]{1,0:T(8,128)(2,1)S(1)} %get-tuple-element.28), channel_id=1, source_target_pairs={{0,64},{64,128},{128,192},{192,0},{1,65},{65,129},{129,193},{193,1... | collective-permute-start | bytes 589832 | tf_op jit(solution)/shard_map/ppermute | solution.py:130
  96.5 6.1 %collective-permute-start.11 = (bf16[256,384]{1,0:T(8,128)(2,1)S(1)}, bf16[256,384]{1,0:T(8,128)(2,1)S(1)}, u32[]{:S(2)}, u32[]{:S(2)}) collective-permute-start(bf16[256,384]{1,0:T(8,128)(2,1)S(1)} %get-tuple-element.29), channel_id=1, source_target_pairs={{0,192},{64,0},{128,64},{192,128},{1,193},{65,1},{129,65},{193,129... | collective-permute-start | bytes 589832 | tf_op jit(solution)/shard_map/ppermute | solution.py:130
  99.2 8.1 %collective-permute-start.13 = (bf16[256,384]{1,0:T(8,128)(2,1)S(1)}, bf16[256,384]{1,0:T(8,128)(2,1)S(1)}, u32[]{:S(2)}, u32[]{:S(2)}) collective-permute-start(bf16[256,384]{1,0:T(8,128)(2,1)S(1)} %collective-permute-done.9), channel_id=1, source_target_pairs={{0,64},{64,128},{128,192},{192,0},{1,65},{65,129},{129,193},{193,1... | collective-permute-start | bytes 589832 | tf_op jit(solution)/shard_map/ppermute | solution.py:130
  99.2 8.1 %collective-permute-start.14 = (bf16[256,384]{1,0:T(8,128)(2,1)S(1)}, bf16[256,384]{1,0:T(8,128)(2,1)S(1)}, u32[]{:S(2)}, u32[]{:S(2)}) collective-permute-start(bf16[256,384]{1,0:T(8,128)(2,1)S(1)} %collective-permute-done.12), channel_id=1, source_target_pairs={{0,192},{64,0},{128,64},{192,128},{1,193},{65,1},{129,65},{193,129... | collective-permute-start | bytes 589832 | tf_op jit(solution)/shard_map/ppermute | solution.py:130
  109.1 40.3 %copy-start.3 = (bf16[512,64]{1,0:T(8,128)(2,1)S(1)}, bf16[512,64]{1,0:T(8,128)(2,1)}, u32[]{:S(2)}) copy-start(bf16[512,64]{1,0:T(8,128)(2,1)} %get-tuple-element.19) | copy-start | bytes 196612
